TPU v7x, 32 devices: a whole 2x2x4 slice. The times are simulated.
32 devices in a mesh: site: 4 (over y, x), fsdp: 8 (over z, core).
Axes of the slice: x: 2, y: 2, z: 4, core: 2. Of those that a mesh axis runs over, the one named last changes fastest.
Arguments:
- held_input: bfloat16 [4, 4096, 1536], P('site', 'fsdp'), may hold values from -6 to 6
- held_cotangent: bfloat16 [4, 4096, 1536], P('site', 'fsdp'), may hold values from -6 to 6
- proj_weight: bfloat16 [1536, 1536], P('fsdp'), may hold values from -0.15625 to 0.15625
- stem_weight: bfloat16 [3, 512, 1536], P(None, 'fsdp'), may hold values from -0.15625 to 0.15625
- seg_counts: int32 [4, 8], P('site'), may hold values from 1 to 128, 512 in all within a row
Outputs:
- stem_grad: bfloat16 [4, 16384, 512], P('site', 'fsdp')
- weight_grad: float32 [1536, 1536], P('fsdp')
Inputs may be any that keep to these rules, and one draw needn't show every extreme that they name: `seg_counts`: in every group the 8 counts sum to 512, so that every holder slot is used; one owner has exactly 128, and a holder keeps at most 16 segments of one owner, a bound reached in every draw.
All inputs are finite; a program needn't handle non-finite values.
Results may differ from a plain program's by a relative error of at most 0.0049.
Values may be sent and summed in bfloat16 or wider, within the bound.
No kernel may reach another device: no remote copies, remote signals or barrier semaphores. Data moves between devices by JAX's collectives and lax.ppermute only.
A program may use at most 128 MiB of HBM per device.

v0:
```python
import math

import jax
import jax.numpy as jnp
from jax import lax
from jax.sharding import PartitionSpec as P

D = 1536
SEG = 8
HOLD = 64
OWN_SEG = 128


EPSILON = 1e-05


def stem_taps(frames, stem_weight):
    return jnp.einsum(
        "rd,kcd->krc",
        frames,
        lax.all_gather(stem_weight, "fsdp", axis=1, tiled=True),
        preferred_element_type=jnp.float32,
    )


def body(held_input, held_cotangent, proj_weight, stem_weight, seg_counts):
    group_size = lax.axis_size("fsdp")
    capacity = 2 * ((OWN_SEG + 2 * group_size - 1) // (2 * group_size))
    my_index = lax.axis_index("fsdp")
    inputs = held_input[0].astype(jnp.float32)
    cotangent = held_cotangent[0]
    row_mean = jnp.mean(inputs, axis=-1, keepdims=True)
    centered = inputs - row_mean
    variance = jnp.mean(centered * centered, axis=-1, keepdims=True)
    inverse = lax.rsqrt(variance + EPSILON)
    normed = centered * inverse
    normed_bf = normed.astype(jnp.bfloat16)
    proj_back = lax.dot_general(
        cotangent,
        lax.all_gather(proj_weight, "fsdp", axis=0, tiled=True),
        (((1,), (1,)), ((), ())),
        preferred_element_type=jnp.float32,
    )
    input_grad = cotangent.astype(jnp.float32) + inverse * (
        proj_back
        - jnp.mean(proj_back, axis=-1, keepdims=True)
        - normed * jnp.mean(proj_back * normed, axis=-1, keepdims=True)
    )
    input_grad = input_grad.astype(jnp.bfloat16)
    counts = seg_counts[0]
    endings = jnp.cumsum(counts)
    starts = endings - counts
    slot_ids = jnp.arange(HOLD, dtype=jnp.int32)
    item_index = 2 * (slot_ids // 2 * group_size + my_index) + slot_ids % 2
    owner_ids = jnp.sum((item_index[:, None] >= endings[None, :]).astype(jnp.int32), axis=1)
    earlier = (slot_ids[None, :] < slot_ids[:, None]) & (owner_ids[None, :] == owner_ids[:, None])
    rank_ids = jnp.sum(earlier.astype(jnp.int32), axis=1)
    target = owner_ids * capacity + rank_ids
    positions = jnp.arange(group_size * capacity, dtype=jnp.int32)
    matched = target[None, :] == positions[:, None]
    filled = jnp.any(matched, axis=1)
    source = jnp.sum(jnp.where(matched, slot_ids[None, :], 0), axis=1)
    owner_hit = jnp.arange(group_size, dtype=jnp.int32) == my_index
    my_count = jnp.sum(jnp.where(owner_hit, counts, 0))
    my_start = jnp.sum(jnp.where(owner_hit, starts, 0))
    segment = jnp.arange(OWN_SEG, dtype=jnp.int32)
    is_live = segment < my_count
    holder = (my_start + segment) // 2 % group_size
    before = (
        (segment[None, :] < segment[:, None])
        & (holder[None, :] == holder[:, None])
        & is_live[None, :]
    )
    holder_rank = jnp.sum(before.astype(jnp.int32), axis=1)
    row_index = jnp.where(is_live, holder * capacity + holder_rank, 0)
    held_segments = input_grad.reshape(HOLD, SEG, D)
    zero_bf = jnp.zeros((), jnp.bfloat16)
    send_rows = jnp.where(filled[:, None, None], jnp.take(held_segments, source, axis=0), zero_bf)
    received = lax.all_to_all(
        send_rows.reshape(group_size, capacity, SEG, D),
        "fsdp",
        split_axis=0,
        concat_axis=0,
        tiled=True,
    )
    picked = jnp.take(received.reshape(group_size * capacity, SEG, D), row_index, axis=0)
    frames = jnp.where(is_live[:, None, None], picked, zero_bf).reshape(OWN_SEG * SEG, D)
    tap_terms = stem_taps(frames, stem_weight)
    shifted = jnp.concatenate(
        [tap_terms[0][1:], jnp.zeros((1, tap_terms.shape[2]), jnp.float32)], 0
    )
    odd_rows = tap_terms[2] + shifted
    stem_rows = (
        jnp.stack([tap_terms[1], odd_rows], 1)
        .reshape(2 * OWN_SEG * SEG, tap_terms.shape[2])
        .astype(jnp.bfloat16)
    )
    shard_sum = lax.psum_scatter(
        lax.dot_general(
            normed_bf, cotangent, (((0,), (0,)), ((), ())), preferred_element_type=jnp.float32
        ),
        "fsdp",
        scatter_dimension=0,
        tiled=True,
    )
    shard_sum = lax.psum(shard_sum, "site")
    weight_grad = shard_sum / math.sqrt(lax.axis_size("site") * group_size * HOLD * SEG)
    return (stem_rows[None], weight_grad)


def solution(mesh):
    placed = (
        P("site", "fsdp", None),
        P("site", "fsdp", None),
        P("fsdp", None),
        P(None, "fsdp", None),
        P("site", None),
    )
    return jax.shard_map(
        body,
        mesh=mesh,
        in_specs=placed,
        out_specs=(P("site", "fsdp", None), P("fsdp", None)),
        check_vma=False,
    )
```

profile of v0, /device:TPU:9, one launch (start us, length us, event | category | flops | bytes accessed | tf_op | source)
XLA Modules:
  0.0 346.6 jit_solution(6739183576496997294)
XLA Ops:
  7.2 0.0 copy-start.1
  7.2 0.0 all-gather.3.cloned.1.call-start
  7.2 0.7 all-gather.3.cloned.1.call-update
  7.9 0.0 reduce-scatter.2.cloned.1.call-start
  8.0 1.8 convert_reduce_fusion
  9.8 0.5 fusion.10
  10.4 5.3 %fusion.25 = f32[1536,1536]{1,0:T(8,128)} fusion(bf16[1,512,1536]{2,1,0:T(8,128)(2,1)S(1)} %copy-done, bf16[1,512,1536]{2,1,0:T(8,128)(2,1)S(1)} %copy-done.1, f32[512]{0:T(512)S(1)} %add_rsqrt_fusion, f32[512]{0:T(512)S(1)} %broadcast_multiply_fusion.3), kind=kOutput, calls=%fused_computation.33 | convolution fusion | flops 2419064832 | bytes 12587008 | tf_op jit(solution)/shard_map/dot_general | solution.py:99
  15.7 0.0 reduce-scatter.2.cloned.1.call-update
  15.7 0.0 all-gather.5.cloned.1.call-start
  15.8 0.7 all-gather.5.cloned.1.call-update
  16.5 0.2 reduce-window.8
  16.7 0.1 convert_reduce_fusion.3
  16.8 0.2 convert_reduce_fusion.2
  17.0 0.1 select_reduce_fusion
  17.1 0.1 fusion.39
  17.2 0.1 reduce_sum.102
  17.2 0.1 broadcast_in_dim.98
  17.3 44.1 %all-gather.3.cloned.1.call-done = bf16[1536,1536]{1,0:T(8,128)(2,1)} async-done(((bf16[192,1536]{1,0:T(8,128)(2,1)}), bf16[1536,1536]{1,0:T(8,128)(2,1)}) %all-gather.3.cloned.1.call-update) | async-done | bytes 4718608 | tf_op jit(solution)/shard_map/all_gather | solution.py:40
  61.5 4.9 %fusion.55 = (f32[512]{0:T(512)S(1)}, f32[512]{0:T(512)S(1)}, f32[512,1536]{1,0:T(8,128)S(1)}) fusion(f32[512]{0:T(512)S(1)} %add_rsqrt_fusion, f32[512]{0:T(512)S(1)} %broadcast_multiply_fusion.3, bf16[1,512,1536]{2,1,0:T(8,128)(2,1)S(1)} %copy-done, bf16[1536,1536]{1,0:T(8,128)(2,1)} %all-gather.3.cloned.1.call-done, bf16[1,512,1536]{2,1,0:T(8,128)(2,1)S(1)} %copy-done.1), kind=kOutput, calls=%fused_computation.107 | convolution fusion | flops 2420636672 | bytes 11018240 | tf_op jit(solution)/shard_map/dot_general | solution.py:38
  66.4 1.2 fusion.27
  67.5 2.4 gather_fusion
  69.9 3.7 %select_select_fusion = bf16[8,16,8,1536]{3,2,1,0:T(8,128)(2,1)} fusion(bf16[8,16,8,1536]{3,2,1,0:T(8,128)(2,1)} %bitcast.92, pred[8,16]{1,0:T(8,128)(4,1)S(1)} %compare_and_fusion, pred[8,16]{1,0:T(8,128)(4,1)S(1)} %broadcast_in_dim.98), kind=kLoop, calls=%fused_computation.22 | loop fusion | flops 3145728 | bytes 6291712 | tf_op jit(solution)/shard_map/jit(_where)/select_n | solution.py:78
  73.7 5.2 %all-to-all-start = ((bf16[8,16,8,1536]{3,2,1,0:T(8,128)(2,1)}), bf16[8,16,8,1536]{3,2,1,0:T(8,128)(2,1)S(1)}, u32[]{:S(2)}, u32[]{:S(2)}) async-start(bf16[8,16,8,1536]{3,2,1,0:T(8,128)(2,1)} %select_select_fusion), calls=%async_computation | async-start | bytes 6291456 | tf_op jit(solution)/shard_map/all_to_all | solution.py:79
  78.9 0.0 all-reduce.3.cloned.1.call-start
  78.9 0.6 fusion.45
  79.5 0.7 iota_compare_fusion.3
  80.2 0.7 and_select_fusion.4
  80.8 0.2 convert_reduce_fusion.1
  81.0 1.3 compare_and_fusion.1
  82.3 0.1 broadcast_in_dim.95
  82.4 0.1 broadcast_in_dim.96
  82.5 0.1 broadcast_in_dim.92
  82.6 0.1 broadcast_in_dim.93
  82.7 1.3 fusion.52
  84.0 117.6 %all-to-all-done = bf16[8,16,8,1536]{3,2,1,0:T(8,128)(2,1)S(1)} async-done(((bf16[8,16,8,1536]{3,2,1,0:T(8,128)(2,1)}), bf16[8,16,8,1536]{3,2,1,0:T(8,128)(2,1)S(1)}, u32[]{:S(2)}, u32[]{:S(2)}) %all-to-all-start) | async-done | bytes 3145760 | tf_op jit(solution)/shard_map/all_to_all | solution.py:79
  201.6 2.4 gather_fusion.1
  204.0 25.4 %reduce-scatter.2.cloned.1.call-done = f32[192,1536]{1,0:T(8,128)} async-done(((f32[1536,1536]{1,0:T(8,128)}), f32[192,1536]{1,0:T(8,128)}) %reduce-scatter.2.cloned.1.call-update) | async-done | bytes 1179664 | tf_op jit(solution)/shard_map/reduce_scatter | solution.py:98
  229.4 0.0 all-reduce.3.cloned.1.call-update
  229.4 50.8 %all-gather.5.cloned.1.call-done = bf16[3,512,1536]{2,1,0:T(8,128)(2,1)} async-done(((bf16[3,64,1536]{2,1,0:T(8,128)(2,1)}), bf16[3,512,1536]{2,1,0:T(8,128)(2,1)}) %all-gather.5.cloned.1.call-update) | async-done | bytes 4718608 | tf_op jit(solution)/shard_map/all_gather | solution.py:21
  280.3 8.4 %fusion.19 = f32[3,1024,512]{2,1,0:T(8,128)S(1)} fusion(bf16[3,512,1536]{2,1,0:T(8,128)(2,1)} %all-gather.5.cloned.1.call-done, bf16[128,8,1536]{2,1,0:T(8,128)(2,1)} %gather_fusion.1, pred[1024]{0:T(1024)(128)(4,1)S(1)} %broadcast_in_dim.96, pred[1024]{0:T(1024)(128)(4,1)S(1)} %broadcast_in_dim.93), kind=kOutput, calls=%fused_computation.25 | convolution fusion | flops 4834983936 | bytes 14157824 | tf_op jit(solution)/shard_map/rd,kcd->krc/dot_general | solution.py:18
  288.7 0.1 fusion.35
  288.8 0.2 slice_bitcast_fusion
  289.1 0.6 fusion.36
  289.6 0.2 pad_maximum_fusion
  289.8 2.2 copy.8
  292.0 2.2 convert_element_type.46
  294.2 43.5 %all-reduce.3.cloned.1.call-done = f32[192,1536]{1,0:T(8,128)} async-done(((f32[192,1536]{1,0:T(8,128)}), f32[192,1536]{1,0:T(8,128)}) %all-reduce.3.cloned.1.call-update) | async-done | bytes 1179664 | tf_op jit(solution)/shard_map/psum | solution.py:106
  337.7 2.4 broadcast_multiply_fusion
  (16 shorter events, 0.1 us)
Async XLA Ops:
  7.2 2.6 copy-start
  7.2 3.2 copy-start.1
  7.2 54.3 %all-gather.3.cloned.1.call-start = ((), (), s32[]{:S(2)}) async-start(), calls=%async_computation.2 | async-start | bytes 5308416 | tf_op jit(solution)/shard_map/all_gather | solution.py:40
  7.9 221.5 %reduce-scatter.2.cloned.1.call-start = ((), (), s32[]{:S(2)}) async-start(), calls=%async_computation.4 | async-start | bytes 10616832 | tf_op jit(solution)/shard_map/reduce_scatter | solution.py:98
  15.7 0.8 copy-start.3
  15.7 264.6 %all-gather.5.cloned.1.call-start = ((), (), s32[]{:S(2)}) async-start(), calls=%async_computation.3 | async-start | bytes 5308416 | tf_op jit(solution)/shard_map/all_gather | solution.py:21
  61.5 4.9 %copy-start.2 = (bf16[1,512,1536]{2,1,0:T(8,128)(2,1)S(1)}, bf16[1,512,1536]{2,1,0:T(8,128)(2,1)}, u32[]{:S(2)}) copy-start(bf16[1,512,1536]{2,1,0:T(8,128)(2,1)} %param.6) | copy-start | bytes 4718596
  73.7 127.9 %all-to-all-start = ((bf16[8,16,8,1536]{3,2,1,0:T(8,128)(2,1)}), bf16[8,16,8,1536]{3,2,1,0:T(8,128)(2,1)S(1)}, u32[]{:S(2)}, u32[]{:S(2)}) async-start(bf16[8,16,8,1536]{3,2,1,0:T(8,128)(2,1)} %select_select_fusion), calls=%async_computation | async-start | bytes 6291456 | tf_op jit(solution)/shard_map/all_to_all | solution.py:79
  78.9 258.8 %all-reduce.3.cloned.1.call-start = ((), (), s32[]{:S(2)}) async-start(), calls=%async_computation.5 | async-start | bytes 2359296 | tf_op jit(solution)/shard_map/psum | solution.py:106
Sparse Core Ops, SparseCore 0:
  9.7 51.7 all-gather.2
  63.8 165.6 reduce-scatter.1
  231.0 49.2 all-gather.4
  283.2 54.4 all-reduce.2
where the time goes:
time: 348 us; the launch traced here: 347 us
  waiting for transfers between devices  283 us (81%)
  matrix products  18.6 us (5%)
  other arithmetic  15.9 us (5%)
  between operations  13.9 us (4%)
  local copies, waits for them, and re-layouts  10.1 us (3%)
  starting transfers between devices  5.31 us (2%)
    all_to_all x1, waiting for transfers between devices, body(): lax.all_to_all(send_rows.reshape(group_size, capacity, SEG, D), 'fsdp', s...  118 us
    all_gather x1, waiting for transfers between devices, stem_taps(): lax.all_gather(stem_weight, 'fsdp', axis=1, tiled=True)  50.8 us
    all_gather x1, waiting for transfers between devices, body(): lax.all_gather(proj_weight, 'fsdp', axis=0, tiled=True)  44.1 us
    psum x1, waiting for transfers between devices, body(): shard_sum = lax.psum(shard_sum, 'site')  43.5 us
    reduce_scatter x1, waiting for transfers between devices, body(): lax.psum_scatter(lax.dot_general(normed_bf, cotangent, (((0,), (0,)), (()...  25.4 us
    dot_general x1, matrix products, stem_taps(): jnp.einsum('rd,kcd->krc', frames, lax.all_gather(stem_weight, 'fsdp', axi...  8.38 us
  transfers between devices with their start and end apart: 5, of which 5 were waited for; matrix products, arithmetic and copies ran while one was open for 12% of the time, Pallas kernels for 0%

commit v1 on v0

--- a/solution.py
+++ b/solution.py
@@ -3,44 +3,423 @@
 import jax
 import jax.numpy as jnp
 from jax import lax
+from jax.experimental import pallas as pl
+from jax.experimental.pallas import tpu as pltpu
 from jax.sharding import PartitionSpec as P
 
 D = 1536
 SEG = 8
 HOLD = 64
 OWN_SEG = 128
-
+N_SITE = 4
+N_FSDP = 8
+N_Z = N_FSDP // 2
+QUARTER = D // N_SITE
+CAP = OWN_SEG // N_FSDP
+CS = 512
+ROWS = HOLD * SEG
+BLOCK = 128
+LANES = 128
+VMEM_LIMIT = 40 * 1024 * 1024
 
 EPSILON = 1e-05
-
-
-def stem_taps(frames, stem_weight):
-    return jnp.einsum(
-        "rd,kcd->krc",
-        frames,
-        lax.all_gather(stem_weight, "fsdp", axis=1, tiled=True),
-        preferred_element_type=jnp.float32,
-    )
+F32 = jnp.float32
+BF16 = jnp.bfloat16
+
+
+def swap_core(value):
+    return lax.ppermute(value, "fsdp", [(i, i ^ 1) for i in range(N_FSDP)])
+
+
+def swap_z(value, distance):
+    return lax.ppermute(value, "fsdp", [(i, i ^ (2 * distance)) for i in range(N_FSDP)])
+
+
+def swap_site(value, distance):
+    return lax.ppermute(value, "site", [(i, i ^ distance) for i in range(N_SITE)])
+
+
+def gather_parts(shard, site):
+    quarter = lax.dynamic_slice_in_dim(shard, site * QUARTER, QUARTER, 2)
+    others = jnp.stack([swap_z(quarter, distance) for distance in (1, 2, 3)])
+    parts = [shard, others] + [swap_site(others, distance) for distance in (1, 2, 3)]
+    return parts + [swap_core(part) for part in parts]
+
+
+def call(kernel, name, out_shape, grid, in_specs, out_specs, scratch, flops, moved):
+    return pl.pallas_call(
+        kernel,
+        name=name,
+        out_shape=out_shape,
+        grid_spec=pltpu.PrefetchScalarGridSpec(
+            num_scalar_prefetch=1,
+            grid=grid,
+            in_specs=in_specs,
+            out_specs=out_specs,
+            scratch_shapes=scratch,
+        ),
+        compiler_params=pltpu.CompilerParams(
+            dimension_semantics=("arbitrary",) * len(grid), vmem_limit_bytes=VMEM_LIMIT
+        ),
+        cost_estimate=pl.CostEstimate(flops=flops, bytes_accessed=moved, transcendentals=0),
+    )
+
+
+ANY = pl.BlockSpec(memory_space=pl.ANY)
+
+
+def whole(shape):
+    return pl.BlockSpec(shape, lambda i, scalars: (0,) * len(shape))
+
+
+def row_block(rows, columns):
+    return pl.BlockSpec((rows, columns), lambda i, scalars: (i, 0))
+
+
+def shape(dims, dtype):
+    return jax.ShapeDtypeStruct(dims, dtype)
+
+
+def dot_nt(a, b):
+    return lax.dot_general(a, b, (((1,), (1,)), ((), ())), preferred_element_type=F32)
+
+
+def normalise(inputs):
+    inputs = inputs.astype(F32)
+    centered = inputs - jnp.mean(inputs, axis=-1, keepdims=True)
+    variance = jnp.mean(centered * centered, axis=-1, keepdims=True)
+    inverse = lax.rsqrt(variance + EPSILON)
+    return centered * inverse, inverse
+
+
+def norm_kernel(scalars, x_ref, own_ref, other_ref, turned):
+    core = scalars[1] % 2
+    normed, _ = normalise(x_ref[...])
+    turned[...] = normed.astype(BF16).T
+    shard = D // N_FSDP
+    for z in range(N_Z):
+        rows = pl.ds(z * shard, shard)
+        mine = pl.multiple_of((2 * z + core) * shard, shard)
+        theirs = pl.multiple_of((2 * z + 1 - core) * shard, shard)
+        own_ref[rows, :] = turned[pl.ds(mine, shard), :]
+        other_ref[rows, :] = turned[pl.ds(theirs, shard), :]
+
+
+def norm_halves(scalars, inputs):
+    half = shape((D // 2, ROWS), BF16)
+    out = pl.BlockSpec((D // 2, BLOCK), lambda i, scalars: (0, i))
+    return call(
+        norm_kernel, "norm_halves", (half, half), (ROWS // BLOCK,), [row_block(BLOCK, D)],
+        (out, out), [pltpu.VMEM((D, BLOCK), BF16)], 10 * ROWS * D, 4 * ROWS * D,
+    )(scalars, inputs)
+
+
+def outer_kernel(scalars, na_ref, nb_ref, ca_ref, cb_ref, own_ref, p1_ref, p2_ref, p3_ref):
+    step = pl.program_id(0)
+    total = jnp.dot(na_ref[...], ca_ref[...], preferred_element_type=F32)
+    total = total + jnp.dot(nb_ref[...], cb_ref[...], preferred_element_type=F32)
+
+    @pl.when(step == 3)
+    def _():
+        own_ref[...] = total
+
+    for at, ref in enumerate((p1_ref, p2_ref, p3_ref)):
+
+        @pl.when(step == at)
+        def _(ref=ref):
+            ref[...] = total.astype(BF16)
+
+
+def outer_pieces(scalars, normed_a, normed_b, cotangent_a, cotangent_b):
+    dims = (D // 2, QUARTER)
+    column = pl.BlockSpec(
+        (ROWS, QUARTER), lambda i, scalars: (0, lax.bitwise_xor(scalars[0], lax.rem(i + 1, 4)))
+    )
+    return call(
+        outer_kernel, "outer_pieces", (shape(dims, F32),) + (shape(dims, BF16),) * 3, (N_SITE,),
+        [whole((D // 2, ROWS))] * 2 + [column] * 2, (whole(dims),) * 4, [],
+        2 * ROWS * D * D, 6 * ROWS * D + 3 * D * D,
+    )(scalars, normed_a, normed_b, cotangent_a, cotangent_b)
+
+
+def site_sum_kernel(scalars, own_ref, a_ref, b_ref, c_ref, o0_ref, o1_ref, o2_ref, o3_ref):
+    shard = D // N_FSDP
+    z = scalars[1] // 2
+    for distance, ref in enumerate((o0_ref, o1_ref, o2_ref, o3_ref)):
+        rows = pl.ds(pl.multiple_of(lax.bitwise_xor(z, distance) * shard, shard), shard)
+        total = own_ref[rows, :]
+        for part in (a_ref, b_ref, c_ref):
+            total = total + part[rows, :].astype(F32)
+        ref[...] = total.astype(ref.dtype)
+
+
+def site_sum(scalars, own, parts):
+    dims, out = (D // 2, QUARTER), (D // N_FSDP, QUARTER)
+    return call(
+        site_sum_kernel, "site_sum", (shape(out, F32),) + (shape(out, BF16),) * 3, (1,),
+        [whole(dims)] * 4, (whole(out),) * 4, [], 4 * dims[0] * dims[1], 14 * dims[0] * dims[1],
+    )(scalars, own, *parts)
+
+
+def z_sum_kernel(scale, scalars, own_ref, a_ref, b_ref, c_ref, out_ref):
+    total = own_ref[...]
+    for part in (a_ref, b_ref, c_ref):
+        total = total + part[...].astype(F32)
+    out_ref[...] = total * scale
+
+
+def z_sum(scalars, own, parts, scale):
+    dims = (D // N_FSDP, QUARTER)
+    return call(
+        lambda *refs: z_sum_kernel(scale, *refs), "z_sum", shape(dims, F32), (1,),
+        [whole(dims)] * 4, whole(dims), [], 4 * dims[0] * dims[1], 14 * dims[0] * dims[1],
+    )(scalars, own, *parts)
+
+
+def lay_columns_kernel(scalars, a_ref, b_ref, c_ref, d_ref, out_ref):
+    for distance, ref in enumerate((a_ref, b_ref, c_ref, d_ref)):
+        at = pl.multiple_of(lax.bitwise_xor(scalars[0], distance) * QUARTER, QUARTER)
+        out_ref[:, pl.ds(at, QUARTER)] = ref[...]
+
+
+def lay_columns(scalars, parts):
+    dims = (D // N_FSDP, QUARTER)
+    out = (D // N_FSDP, D)
+    return call(
+        lay_columns_kernel, "lay_columns", shape(out, F32), (1,), [whole(dims)] * 4, whole(out),
+        [], 0, 8 * out[0] * out[1],
+    )(scalars, *parts)
+
+
+def weight_copies(scalars, parts, weight, sem):
+    site, index = scalars[0], scalars[1]
+    rows = weight.shape[1] // N_FSDP
+    copies = []
+
+    def add(source, at, columns):
+        place = weight.at[:, pl.ds(pl.multiple_of(at * rows, rows), rows), columns]
+        copies.append(pltpu.make_async_copy(source, place, sem))
+
+    for swapped in (0, 1):
+        core_index = lax.bitwise_xor(index, swapped)
+        shard, *quarters = parts[5 * swapped : 5 * swapped + 5]
+        add(shard, core_index, pl.ds(0, D))
+        for distance, ref in enumerate(quarters):
+            at = pl.multiple_of(lax.bitwise_xor(site, distance) * QUARTER, QUARTER)
+            for z in (1, 2, 3):
+                add(ref.at[z - 1], lax.bitwise_xor(core_index, 2 * z), pl.ds(at, QUARTER))
+    return copies
+
+
+def fetch_weight(scalars, parts, weight, sem):
+    @pl.when(pl.program_id(0) == 0)
+    def _():
+        copies = weight_copies(scalars, parts, weight, sem)
+        for copy in copies:
+            copy.start()
+        for copy in copies:
+            copy.wait()
+
+
+def input_grad_kernel(scalars, *refs):
+    parts, (x_ref, cot_ref, out_ref, weight, sem) = refs[:10], refs[10:]
+    fetch_weight(scalars, parts, weight, sem)
+    cotangent = cot_ref[...]
+    back = dot_nt(cotangent, weight[0])
+    normed, inverse = normalise(x_ref[...])
+    inner = back - jnp.mean(back, axis=-1, keepdims=True)
+    inner = inner - normed * jnp.mean(back * normed, axis=-1, keepdims=True)
+    out_ref[...] = (cotangent.astype(F32) + inverse * inner).astype(BF16)
+
+
+def input_gradient(scalars, parts, inputs, cotangent):
+    return call(
+        input_grad_kernel, "input_gradient", shape((ROWS, D), BF16), (ROWS // BLOCK,),
+        [ANY] * 10 + [row_block(BLOCK, D)] * 2, row_block(BLOCK, D),
+        [pltpu.VMEM((1, D, D), BF16), pltpu.SemaphoreType.DMA], 2 * ROWS * D * D,
+        2 * D * D + 6 * ROWS * D,
+    )(scalars, *parts, inputs, cotangent)
+
+
+def starts_of(scalars):
+    starts = [jnp.int32(0)]
+    for owner in range(N_FSDP):
+        starts.append(starts[-1] + scalars[2 + owner])
+    return starts
+
+
+def held_before(start, holder):
+    return 2 * (start // (2 * N_FSDP)) + jnp.clip(start % (2 * N_FSDP) - 2 * holder, 0, 2)
+
+
+def stem_kernel(scalars, *refs):
+    parts, grad_ref, outs = refs[:10], refs[10], refs[11:19]
+    weight, mixed, packed, firsts, sem, out_sem = refs[19:]
+    fetch_weight(scalars, parts, weight, sem)
+    step = pl.program_id(0)
+    index = scalars[1]
+    grad = grad_ref[...]
+    even = dot_nt(grad, weight[1])
+    leading = dot_nt(grad, weight[0])
+    row = lax.broadcasted_iota(jnp.int32, leading.shape, 0)
+    following = pltpu.roll(leading, BLOCK - 1, 0)
+    following = jnp.where(row % SEG == SEG - 1, 0.0, following)
+    odd = dot_nt(grad, weight[2]) + following
+    for lane in range(CS // LANES):
+        mixed[lane, pl.ds(0, BLOCK, stride=2), :] = even[:, lane * LANES : (lane + 1) * LANES]
+        mixed[lane, pl.ds(1, BLOCK, stride=2), :] = odd[:, lane * LANES : (lane + 1) * LANES]
+    starts = starts_of(scalars)
+    segments = BLOCK // SEG
+    for local in range(segments):
+        slot = step * segments + local
+        item = 2 * (slot // 2 * N_FSDP + index) + slot % 2
+        owner = jnp.int32(0)
+        start = jnp.int32(0)
+        for other in range(1, N_FSDP):
+            passed = item >= starts[other]
+            owner = jnp.where(passed, other, owner)
+            start = jnp.where(passed, starts[other], start)
+        rank = slot - held_before(start, index)
+        place = lax.bitwise_xor(owner, index)
+        for lane in range(CS // LANES):
+            rows = mixed[lane, pl.ds(2 * SEG * local, 2 * SEG), :]
+            packed[place, rank, :, pl.ds(lane * LANES, LANES)] = rows.astype(BF16)
+        firsts[pl.ds(place * CAP + rank, 1), :] = leading[SEG * local : SEG * local + 1, :]
+
+    @pl.when(step == pl.num_programs(0) - 1)
+    def _():
+        packed[:, CAP] = firsts[...].reshape(N_FSDP, CAP, CS).astype(BF16)
+        copies = [
+            pltpu.make_async_copy(packed.at[place], outs[place], out_sem.at[place])
+            for place in range(N_FSDP)
+        ]
+        for copy in copies:
+            copy.start()
+        for copy in copies:
+            copy.wait()
+
+
+def stem_payloads(scalars, parts, grad):
+    payload = (CAP + 1, 2 * SEG, CS)
+    return call(
+        stem_kernel, "stem_payloads", (shape(payload, BF16),) * N_FSDP, (ROWS // BLOCK,),
+        [ANY] * 10 + [row_block(BLOCK, D)], (ANY,) * N_FSDP,
+        [
+            pltpu.VMEM((3, CS, D), BF16),
+            pltpu.VMEM((CS // LANES, 2 * BLOCK, LANES), F32),
+            pltpu.VMEM((N_FSDP,) + payload, BF16),
+            pltpu.VMEM((N_FSDP * CAP, CS), F32),
+            pltpu.SemaphoreType.DMA,
+            pltpu.SemaphoreType.DMA((N_FSDP,)),
+        ],
+        6 * ROWS * D * CS, 6 * CS * D + 2 * ROWS * D + 2 * N_FSDP * math.prod(payload),
+    )(scalars, *parts, grad)
+
+
+def owner_kernel(scalars, *refs):
+    payloads, out_ref = refs[:N_FSDP], refs[N_FSDP]
+    packed, firsts, sem = refs[N_FSDP + 1 :]
+    step = pl.program_id(0)
+    index = scalars[1]
+
+    @pl.when(step == 0)
+    def _():
+        copies = [
+            pltpu.make_async_copy(payloads[place], packed.at[place], sem.at[place])
+            for place in range(N_FSDP)
+        ]
+        for copy in copies:
+            copy.start()
+        for copy in copies:
+            copy.wait()
+        firsts[...] = packed[:, CAP].astype(F32).reshape(N_FSDP * CAP, CS)
+
+    start = jnp.int32(0)
+    for owner in range(N_FSDP):
+        start = start + jnp.where(owner < index, scalars[2 + owner], 0)
+    count = scalars[2 + index]
+
+    def place_of(segment):
+        item = start + segment
+        holder = item // 2 % N_FSDP
+        slot = 2 * (item // (2 * N_FSDP)) + item % 2
+        return lax.bitwise_xor(holder, index), slot - held_before(start, holder)
+
+    per_step = OWN_SEG // 4
+    last_row = lax.broadcasted_iota(jnp.int32, (2 * SEG, CS), 0) == 2 * SEG - 1
+
+    def one(local, carry):
+        segment = step * per_step + local
+        rows = pl.ds(pl.multiple_of(local * 2 * SEG, 2 * SEG), 2 * SEG)
+
+        @pl.when(segment < count)
+        def _():
+            place, rank = place_of(segment)
+            follows = segment + 1 < count
+            next_place, next_rank = place_of(jnp.where(follows, segment + 1, segment))
+            first = firsts[pl.ds(next_place * CAP + next_rank, 1), :]
+            extra = jnp.where(last_row & follows, jnp.broadcast_to(first, (2 * SEG, CS)), 0.0)
+            out_ref[rows, :] = (packed[place, rank].astype(F32) + extra).astype(BF16)
+
+        @pl.when(segment >= count)
+        def _():
+            out_ref[rows, :] = jnp.zeros((2 * SEG, CS), BF16)
+
+        return carry
+
+    lax.fori_loop(0, per_step, one, 0)
+
+
+def owner_rows(scalars, payloads):
+    payload = (CAP + 1, 2 * SEG, CS)
+    rows = 2 * OWN_SEG * SEG
+    return call(
+        owner_kernel, "owner_rows", shape((rows, CS), BF16), (4,), [ANY] * N_FSDP,
+        row_block(rows // 4, CS),
+        [
+            pltpu.VMEM((N_FSDP,) + payload, BF16),
+            pltpu.VMEM((N_FSDP * CAP, CS), F32),
+            pltpu.SemaphoreType.DMA((N_FSDP,)),
+        ],
+        4 * rows * CS, 2 * rows * CS + 2 * N_FSDP * math.prod(payload),
+    )(scalars, *payloads)
 
 
 def body(held_input, held_cotangent, proj_weight, stem_weight, seg_counts):
+    site, index = lax.axis_index("site"), lax.axis_index("fsdp")
+    scalars = jnp.concatenate([jnp.stack([site, index]).astype(jnp.int32), seg_counts[0]])
+    inputs, cotangent = held_input[0], held_cotangent[0]
+
+    proj_parts = gather_parts(proj_weight[None], site)
+    stem_parts = gather_parts(stem_weight, site)
+
+    normed_own, normed_other = norm_halves(scalars, inputs)
+    own, *pieces = outer_pieces(
+        scalars, normed_own, swap_core(normed_other), cotangent, swap_core(cotangent)
+    )
+    own, *pieces = site_sum(scalars, own, [swap_site(p, d + 1) for d, p in enumerate(pieces)])
+    scale = 1.0 / math.sqrt(N_SITE * N_FSDP * ROWS)
+    quarter = z_sum(scalars, own, [swap_z(p, d + 1) for d, p in enumerate(pieces)], scale)
+    weight_grad = lay_columns(scalars, [quarter] + [swap_site(quarter, d) for d in (1, 2, 3)])
+
+    grad = input_gradient(scalars, proj_parts, inputs, cotangent)
+    payloads = stem_payloads(scalars, stem_parts, grad)
+    received = [payloads[0]] + [
+        lax.ppermute(payloads[d], "fsdp", [(i, i ^ d) for i in range(N_FSDP)])
+        for d in range(1, N_FSDP)
+    ]
+    stem_grad = owner_rows(scalars, received)
+    return (stem_grad[None], weight_grad)
+
+
+def plain_body(held_input, held_cotangent, proj_weight, stem_weight, seg_counts):
     group_size = lax.axis_size("fsdp")
     capacity = 2 * ((OWN_SEG + 2 * group_size - 1) // (2 * group_size))
     my_index = lax.axis_index("fsdp")
-    inputs = held_input[0].astype(jnp.float32)
     cotangent = held_cotangent[0]
-    row_mean = jnp.mean(inputs, axis=-1, keepdims=True)
-    centered = inputs - row_mean
-    variance = jnp.mean(centered * centered, axis=-1, keepdims=True)
-    inverse = lax.rsqrt(variance + EPSILON)
-    normed = centered * inverse
+    normed, inverse = normalise(held_input[0])
     normed_bf = normed.astype(jnp.bfloat16)
-    proj_back = lax.dot_general(
-        cotangent,
-        lax.all_gather(proj_weight, "fsdp", axis=0, tiled=True),
-        (((1,), (1,)), ((), ())),
-        preferred_element_type=jnp.float32,
-    )
+    proj_back = dot_nt(cotangent, lax.all_gather(proj_weight, "fsdp", axis=0, tiled=True))
     input_grad = cotangent.astype(jnp.float32) + inverse * (
         proj_back
         - jnp.mean(proj_back, axis=-1, keepdims=True)
@@ -77,21 +456,21 @@
     zero_bf = jnp.zeros((), jnp.bfloat16)
     send_rows = jnp.where(filled[:, None, None], jnp.take(held_segments, source, axis=0), zero_bf)
     received = lax.all_to_all(
-        send_rows.reshape(group_size, capacity, SEG, D),
-        "fsdp",
-        split_axis=0,
-        concat_axis=0,
-        tiled=True,
+        send_rows.reshape(group_size, capacity, SEG, D), "fsdp", split_axis=0, concat_axis=0, tiled=True
     )
     picked = jnp.take(received.reshape(group_size * capacity, SEG, D), row_index, axis=0)
     frames = jnp.where(is_live[:, None, None], picked, zero_bf).reshape(OWN_SEG * SEG, D)
-    tap_terms = stem_taps(frames, stem_weight)
+    tap_terms = jnp.einsum(
+        "rd,kcd->krc",
+        frames,
+        lax.all_gather(stem_weight, "fsdp", axis=1, tiled=True),
+        preferred_element_type=jnp.float32,
+    )
     shifted = jnp.concatenate(
         [tap_terms[0][1:], jnp.zeros((1, tap_terms.shape[2]), jnp.float32)], 0
     )
-    odd_rows = tap_terms[2] + shifted
     stem_rows = (
-        jnp.stack([tap_terms[1], odd_rows], 1)
+        jnp.stack([tap_terms[1], tap_terms[2] + shifted], 1)
         .reshape(2 * OWN_SEG * SEG, tap_terms.shape[2])
         .astype(jnp.bfloat16)
     )
@@ -104,7 +483,7 @@
         tiled=True,
     )
     shard_sum = lax.psum(shard_sum, "site")
-    weight_grad = shard_sum / math.sqrt(lax.axis_size("site") * group_size * HOLD * SEG)
+    weight_grad = shard_sum / math.sqrt(lax.axis_size("site") * group_size * ROWS)
     return (stem_rows[None], weight_grad)
 
 
@@ -116,8 +495,9 @@
         P(None, "fsdp", None),
         P("site", None),
     )
+    fits = (mesh.shape["site"], mesh.shape["fsdp"]) == (N_SITE, N_FSDP)
     return jax.shard_map(
-        body,
+        body if fits else plain_body,
         mesh=mesh,
         in_specs=placed,
         out_specs=(P("site", "fsdp", None), P("fsdp", None)),

time: 348 us -> 193 us (0.55)
  waiting for transfers between devices: 283 us -> 81.8 us
  starting transfers between devices: 5.31 us -> 69.6 us
  Pallas kernels: 0 us -> 34.2 us
  matrix products: 18.6 us -> 0 us
  other arithmetic: 15.9 us -> 0.86 us
  between operations: 13.9 us -> 0.81 us
  local copies, waits for them, and re-layouts: 10.1 us -> 2.37 us
    all_to_all x1 -> x0, waiting for transfers between devices: 118 us -> none  [body(): lax.all_to_all(send_rows.reshape(group_size, capacity, SEG, D), 'fsdp', s...]
    all_gather x2 -> x0, waiting for transfers between devices: 94.9 us -> none  [the longest x1 50.8 us: stem_taps(): lax.all_gather(stem_weight, 'fsdp', axis=1, tiled=True)]
    ppermute x0 -> x40, waiting for transfers between devices: none -> 81.8 us  [the longest x7 34.7 us: body(): lax.ppermute(payloads[d], 'fsdp', [(i, i ^ d) for i in range(N_FSDP)])]
    ppermute x0 -> x40, starting transfers between devices: none -> 69.6 us  [the longest x12 27.4 us: swap_core(): return lax.ppermute(value, 'fsdp', [(i, i ^ 1) for i in range(N_FSDP)])]
    psum x1 -> x0, waiting for transfers between devices: 43.5 us -> none  [body(): shard_sum = lax.psum(shard_sum, 'site')]
    pallas_call x0 -> x8, Pallas kernels: none -> 34.2 us  [the longest x1 9.2 us: stem_payloads(): call(stem_kernel, 'stem_payloads', (shape(payload, BF16),) * N_FSDP, (ROW...]
    reduce_scatter x1 -> x0, waiting for transfers between devices: 25.4 us -> none  [body(): lax.psum_scatter(lax.dot_general(normed_bf, cotangent, (((0,), (0,)), (()...]
    dot_general x3 -> x0, matrix products: 18.6 us -> none  [the longest x1 8.38 us: stem_taps(): jnp.einsum('rd,kcd->krc', frames, lax.all_gather(stem_weight, 'fsdp', axi...]
  transfers between devices with their start and end apart: 5 -> 40, of which waited for: 5 -> 16; matrix products, arithmetic and copies ran while one was open for 12% -> 1% of each run, Pallas kernels for 0% -> 17%
where the time goes in v1:
time: 193 us; the launch traced here: 190 us
  waiting for transfers between devices  81.8 us (42%)
  starting transfers between devices  69.6 us (36%)
  Pallas kernels  34.2 us (18%)
  local copies, waits for them, and re-layouts  2.37 us (1%)
    ppermute x7, waiting for transfers between devices, body(): lax.ppermute(payloads[d], 'fsdp', [(i, i ^ d) for i in range(N_FSDP)])  34.7 us
    ppermute x12, starting transfers between devices, swap_core(): return lax.ppermute(value, 'fsdp', [(i, i ^ 1) for i in range(N_FSDP)])  27.4 us
    ppermute x9, waiting for transfers between devices, swap_z(): lax.ppermute(value, 'fsdp', [(i, i ^ 2 * distance) for i in range(N_FSDP)])  24 us
    ppermute x12, waiting for transfers between devices, swap_site(): lax.ppermute(value, 'site', [(i, i ^ distance) for i in range(N_SITE)])  21.6 us
    ppermute x7, starting transfers between devices, body(): lax.ppermute(payloads[d], 'fsdp', [(i, i ^ d) for i in range(N_FSDP)])  19.2 us
    ppermute x9, starting transfers between devices, swap_z(): lax.ppermute(value, 'fsdp', [(i, i ^ 2 * distance) for i in range(N_FSDP)])  13.5 us
    ppermute x12, starting transfers between devices, swap_site(): lax.ppermute(value, 'site', [(i, i ^ distance) for i in range(N_SITE)])  9.51 us
    pallas_call x1, Pallas kernels, stem_payloads(): call(stem_kernel, 'stem_payloads', (shape(payload, BF16),) * N_FSDP, (ROW...  9.2 us
  transfers between devices with their start and end apart: 40, of which 16 were waited for; matrix products, arithmetic and copies ran while one was open for 1% of the time, Pallas kernels for 17%

profile of v1, /device:TPU:9, one launch (start us, length us, event | category | flops | bytes accessed | tf_op | source)
XLA Modules:
  0.0 189.6 jit_solution(5329828835657037188)
XLA Ops:
  1.4 0.9 dynamic-slice_bitcast_fusion
  2.3 1.4 collective-permute-start.13
  3.7 2.2 %collective-permute-start.11 = (bf16[1,192,384]{2,1,0:T(8,128)(2,1)S(1)}, bf16[1,192,384]{2,1,0:T(8,128)(2,1)S(1)}, u32[]{:S(2)}, u32[]{:S(2)}) collective-permute-start(bf16[1,192,384]{2,1,0:T(8,128)(2,1)S(1)} %dynamic-slice_bitcast_fusion), channel_id=1, source_target_pairs={{0,2},{1,3},{2,0},{3,1},{4,6},{5,7},{6,4},{7,5},{8,10},{9,11},{10,... | collective-permute-start | bytes 442376 | tf_op jit(solution)/shard_map/ppermute | solution.py:35
  5.9 5.0 %collective-permute-done.13 = bf16[1,192,384]{2,1,0:T(8,128)(2,1)S(1)} collective-permute-done((bf16[1,192,384]{2,1,0:T(8,128)(2,1)S(1)}, bf16[1,192,384]{2,1,0:T(8,128)(2,1)S(1)}, u32[]{:S(2)}, u32[]{:S(2)}) %collective-permute-start.13) | collective-permute-done | bytes 147488 | tf_op jit(solution)/shard_map/ppermute | solution.py:35
  10.8 2.1 %collective-permute-done.11 = bf16[1,192,384]{2,1,0:T(8,128)(2,1)S(1)} collective-permute-done((bf16[1,192,384]{2,1,0:T(8,128)(2,1)S(1)}, bf16[1,192,384]{2,1,0:T(8,128)(2,1)S(1)}, u32[]{:S(2)}, u32[]{:S(2)}) %collective-permute-start.11) | collective-permute-done | bytes 147488 | tf_op jit(solution)/shard_map/ppermute | solution.py:35
  12.9 3.2 %collective-permute-done.12 = bf16[1,192,384]{2,1,0:T(8,128)(2,1)S(1)} collective-permute-done((bf16[1,192,384]{2,1,0:T(8,128)(2,1)S(1)}, bf16[1,192,384]{2,1,0:T(8,128)(2,1)S(1)}, u32[]{:S(2)}, u32[]{:S(2)}) %collective-permute-start.12) | collective-permute-done | bytes 147488 | tf_op jit(solution)/shard_map/ppermute | solution.py:35
  16.2 1.3 collective-permute-start.14
  18.2 1.4 copy-done
  19.6 2.9 %norm_halves.1 = (bf16[768,512]{1,0:T(8,128)(2,1)S(1)}, bf16[768,512]{1,0:T(8,128)(2,1)S(1)}) custom-call(s32[10]{0:T(128)S(1)} %pad_add_fusion.scalars.refs_0_, bf16[512,1536]{1,0:T(8,128)(2,1)S(1)} %bitcast.15), custom_call_target="tpu_custom_call" | custom-call | flops 7864320 | bytes 3145728 | tf_op jit(solution)/shard_map/norm_halves/pallas_call | solution.py:111
  22.5 1.4 collective-permute-start.29
  24.0 2.2 %collective-permute-start = (bf16[3,64,384]{2,1,0:T(8,128)(2,1)S(1)}, bf16[3,64,384]{2,1,0:T(8,128)(2,1)S(1)}, u32[]{:S(2)}, u32[]{:S(2)}) collective-permute-start(bf16[3,64,384]{2,1,0:T(8,128)(2,1)S(1)} %constant_dynamic-slice_fusion), channel_id=1, source_target_pairs={{0,2},{1,3},{2,0},{3,1},{4,6},{5,7},{6,4},{7,5},{8,10},{9,11},{10,... | collective-permute-start | bytes 442376 | tf_op jit(solution)/shard_map/ppermute | solution.py:35
  26.2 1.1 collective-permute-start.1
  27.3 5.1 %collective-permute-done = bf16[3,64,384]{2,1,0:T(8,128)(2,1)S(1)} collective-permute-done((bf16[3,64,384]{2,1,0:T(8,128)(2,1)S(1)}, bf16[3,64,384]{2,1,0:T(8,128)(2,1)S(1)}, u32[]{:S(2)}, u32[]{:S(2)}) %collective-permute-start) | collective-permute-done | bytes 147488 | tf_op jit(solution)/shard_map/ppermute | solution.py:35
  32.3 1.2 collective-permute-start.15
  33.6 1.0 collective-permute-done.1
  34.7 7.7 %collective-permute-done.2 = bf16[3,64,384]{2,1,0:T(8,128)(2,1)S(1)} collective-permute-done((bf16[3,64,384]{2,1,0:T(8,128)(2,1)S(1)}, bf16[3,64,384]{2,1,0:T(8,128)(2,1)S(1)}, u32[]{:S(2)}, u32[]{:S(2)}) %collective-permute-start.2) | collective-permute-done | bytes 147488 | tf_op jit(solution)/shard_map/ppermute | solution.py:35
  42.5 1.4 collective-permute-start.16
  43.9 1.6 collective-permute-start.18
  45.6 7.8 %collective-permute-done.16.refs_4_ = bf16[3,1,192,384]{3,2,1,0:T(8,128)(2,1)S(1)} collective-permute-done((bf16[3,1,192,384]{3,2,1,0:T(8,128)(2,1)S(1)}, bf16[3,1,192,384]{3,2,1,0:T(8,128)(2,1)S(1)}, u32[]{:S(2)}, u32[]{:S(2)}) %collective-permute-start.16) | collective-permute-done | bytes 442400 | tf_op jit(solution)/shard_map/ppermute | solution.py:39
  53.5 1.6 collective-permute-start.5
  55.1 1.2 collective-permute-start.3
  56.4 3.1 %collective-permute-start.19 = (bf16[3,1,192,384]{3,2,1,0:T(8,128)(2,1)S(1)}, bf16[3,1,192,384]{3,2,1,0:T(8,128)(2,1)S(1)}, u32[]{:S(2)}, u32[]{:S(2)}) collective-permute-start(bf16[3,1,192,384]{3,2,1,0:T(8,128)(2,1)S(1)} %collective-permute-done.14.refs_2_), channel_id=1, source_target_pairs={{0,1},{1,0},{2,3},{3,2},{4,5},{5,4},{6,7},{7,6},{8,9},{9,8},{10,11... | collective-permute-start | bytes 1327112 | tf_op jit(solution)/shard_map/ppermute | solution.py:31
  59.5 5.2 %outer_pieces.1 = (f32[768,384]{1,0:T(8,128)S(1)}, bf16[768,384]{1,0:T(8,128)(2,1)S(1)}, bf16[768,384]{1,0:T(8,128)(2,1)S(1)}, bf16[768,384]{1,0:T(8,128)(2,1)S(1)}) custom-call(s32[10]{0:T(128)S(1)} %pad_add_fusion.scalars.refs_0_, bf16[768,512]{1,0:T(8,128)(2,1)S(1)} %get-tuple-element.28.na_ref, bf16[768,512]{1,0:T(8,128)(2,1)S(1)} %collective-permute-done.29.nb_ref, ...), custom_call_target="tpu_custom_call" | custom-call | flops 2415919104 | bytes 11796480 | tf_op jit(solution)/shard_map/outer_pieces/pallas_call | solution.py:138
  65.1 8.7 %collective-permute-done.3.refs_2_ = bf16[3,3,64,384]{3,2,1,0:T(8,128)(2,1)S(1)} collective-permute-done((bf16[3,3,64,384]{3,2,1,0:T(8,128)(2,1)S(1)}, bf16[3,3,64,384]{3,2,1,0:T(8,128)(2,1)S(1)}, u32[]{:S(2)}, u32[]{:S(2)}) %collective-permute-start.3) | collective-permute-done | bytes 442400 | tf_op jit(solution)/shard_map/ppermute | solution.py:39
  73.9 2.1 %collective-permute-done.4.refs_3_ = bf16[3,3,64,384]{3,2,1,0:T(8,128)(2,1)S(1)} collective-permute-done((bf16[3,3,64,384]{3,2,1,0:T(8,128)(2,1)S(1)}, bf16[3,3,64,384]{3,2,1,0:T(8,128)(2,1)S(1)}, u32[]{:S(2)}, u32[]{:S(2)}) %collective-permute-start.4) | collective-permute-done | bytes 442400 | tf_op jit(solution)/shard_map/ppermute | solution.py:39
  76.0 1.6 collective-permute-start.33
  77.6 4.1 %collective-permute-start.21 = (bf16[3,1,192,384]{3,2,1,0:T(8,128)(2,1)S(1)}, bf16[3,1,192,384]{3,2,1,0:T(8,128)(2,1)S(1)}, u32[]{:S(2)}, u32[]{:S(2)}) collective-permute-start(bf16[3,1,192,384]{3,2,1,0:T(8,128)(2,1)S(1)} %collective-permute-done.16.refs_4_), channel_id=1, source_target_pairs={{0,1},{1,0},{2,3},{3,2},{4,5},{5,4},{6,7},{7,6},{8,9},{9,8},{10,11... | collective-permute-start | bytes 1327112 | tf_op jit(solution)/shard_map/ppermute | solution.py:31
  81.8 1.3 collective-permute-done.21.refs_9_
  83.5 3.0 %collective-permute-done.31.a_ref = bf16[768,384]{1,0:T(8,128)(2,1)S(1)} collective-permute-done((bf16[768,384]{1,0:T(8,128)(2,1)S(1)}, bf16[768,384]{1,0:T(8,128)(2,1)S(1)}, u32[]{:S(2)}, u32[]{:S(2)}) %collective-permute-start.31) | collective-permute-done | bytes 589856 | tf_op jit(solution)/shard_map/ppermute | solution.py:39
  86.5 5.9 %collective-permute-start.10 = (bf16[3,3,64,384]{3,2,1,0:T(8,128)(2,1)S(1)}, bf16[3,3,64,384]{3,2,1,0:T(8,128)(2,1)S(1)}, u32[]{:S(2)}, u32[]{:S(2)}) collective-permute-start(bf16[3,3,64,384]{3,2,1,0:T(8,128)(2,1)S(1)} %collective-permute-done.5.refs_4_), channel_id=1, source_target_pairs={{0,1},{1,0},{2,3},{3,2},{4,5},{5,4},{6,7},{7,6},{8,9},{9,8},{10,11... | collective-permute-start | bytes 1327112 | tf_op jit(solution)/shard_map/ppermute | solution.py:31
  92.3 9.9 %collective-permute-start.8 = (bf16[3,3,64,384]{3,2,1,0:T(8,128)(2,1)S(1)}, bf16[3,3,64,384]{3,2,1,0:T(8,128)(2,1)S(1)}, u32[]{:S(2)}, u32[]{:S(2)}) collective-permute-start(bf16[3,3,64,384]{3,2,1,0:T(8,128)(2,1)S(1)} %collective-permute-done.3.refs_2_), channel_id=1, source_target_pairs={{0,1},{1,0},{2,3},{3,2},{4,5},{5,4},{6,7},{7,6},{8,9},{9,8},{10,11... | collective-permute-start | bytes 1327112 | tf_op jit(solution)/shard_map/ppermute | solution.py:31
  102.2 9.0 %input_gradient.1.refs_10_ = bf16[512,1536]{1,0:T(8,128)(2,1)S(1)} custom-call(s32[10]{0:T(128)S(1)} %pad_add_fusion.scalars.refs_0_, bf16[1,192,1536]{2,1,0:T(8,128)(2,1)S(1)} %bitcast.21, bf16[3,1,192,384]{3,2,1,0:T(8,128)(2,1)S(1)} %pad_maximum_fusion.1.refs_1_, bf16[3,1,192,384]{3,2,1,0:T(8,128)(2,1)S(1)} %collective-permute-done.14.refs_2_, ...), custom_call_target="tpu_custom_call" | custom-call | flops 2415919104 | bytes 9437184 | tf_op jit(solution)/shard_map/input_gradient/pallas_call | solution.py:236
  111.2 0.8 site_sum.1
  112.1 5.3 %collective-permute-start.34 = (bf16[192,384]{1,0:T(8,128)(2,1)S(1)}, bf16[192,384]{1,0:T(8,128)(2,1)S(1)}, u32[]{:S(2)}, u32[]{:S(2)}) collective-permute-start(bf16[192,384]{1,0:T(8,128)(2,1)S(1)} %get-tuple-element.35), channel_id=1, source_target_pairs={{0,2},{1,3},{2,0},{3,1},{4,6},{5,7},{6,4},{7,5},{8,10},{9,11},{10,... | collective-permute-start | bytes 442376 | tf_op jit(solution)/shard_map/ppermute | solution.py:35
  117.3 1.3 collective-permute-start.36
  118.6 9.2 %stem_payloads.1 = (bf16[17,16,512]{2,1,0:T(8,128)(2,1)S(1)}, bf16[17,16,512]{2,1,0:T(8,128)(2,1)S(1)}, bf16[17,16,512]{2,1,0:T(8,128)(2,1)S(1)}, bf16[17,16,512...) custom-call(s32[10]{0:T(128)S(1)} %pad_add_fusion.scalars.refs_0_, ...), custom_call_target="tpu_custom_call" | custom-call | flops 2415919104 | bytes 8519680 | tf_op jit(solution)/shard_map/stem_payloads/pallas_call | solution.py:304
  127.8 1.1 collective-permute-start.22
  128.9 2.6 %collective-permute-start.23 = (bf16[17,16,512]{2,1,0:T(8,128)(2,1)S(1)}, bf16[17,16,512]{2,1,0:T(8,128)(2,1)S(1)}, u32[]{:S(2)}, u32[]{:S(2)}) collective-permute-start(bf16[17,16,512]{2,1,0:T(8,128)(2,1)S(1)} %get-tuple-element.22), channel_id=1, source_target_pairs={{0,2},{1,3},{2,0},{3,1},{4,6},{5,7},{6,4},{7,5},{8,10},{9,11},{10,... | collective-permute-start | bytes 835592 | tf_op jit(solution)/shard_map/ppermute | solution.py:408
  131.8 2.7 %collective-permute-start.26 = (bf16[17,16,512]{2,1,0:T(8,128)(2,1)S(1)}, bf16[17,16,512]{2,1,0:T(8,128)(2,1)S(1)}, u32[]{:S(2)}, u32[]{:S(2)}) collective-permute-start(bf16[17,16,512]{2,1,0:T(8,128)(2,1)S(1)} %get-tuple-element.25), channel_id=1, source_target_pairs={{0,5},{1,4},{2,7},{3,6},{4,1},{5,0},{6,3},{7,2},{8,13},{9,12},{10,... | collective-permute-start | bytes 835592 | tf_op jit(solution)/shard_map/ppermute | solution.py:408
  135.4 10.1 %collective-permute-done.23.refs_2_ = bf16[17,16,512]{2,1,0:T(8,128)(2,1)S(1)} collective-permute-done((bf16[17,16,512]{2,1,0:T(8,128)(2,1)S(1)}, bf16[17,16,512]{2,1,0:T(8,128)(2,1)S(1)}, u32[]{:S(2)}, u32[]{:S(2)}) %collective-permute-start.23) | collective-permute-done | bytes 278560 | tf_op jit(solution)/shard_map/ppermute | solution.py:408
  145.8 5.7 %collective-permute-done.24.refs_3_ = bf16[17,16,512]{2,1,0:T(8,128)(2,1)S(1)} collective-permute-done((bf16[17,16,512]{2,1,0:T(8,128)(2,1)S(1)}, bf16[17,16,512]{2,1,0:T(8,128)(2,1)S(1)}, u32[]{:S(2)}, u32[]{:S(2)}) %collective-permute-start.24) | collective-permute-done | bytes 278560 | tf_op jit(solution)/shard_map/ppermute | solution.py:408
  151.7 2.3 %collective-permute-start.27 = (bf16[17,16,512]{2,1,0:T(8,128)(2,1)S(1)}, bf16[17,16,512]{2,1,0:T(8,128)(2,1)S(1)}, u32[]{:S(2)}, u32[]{:S(2)}) collective-permute-start(bf16[17,16,512]{2,1,0:T(8,128)(2,1)S(1)} %get-tuple-element.26), channel_id=1, source_target_pairs={{0,6},{1,7},{2,4},{3,5},{4,2},{5,3},{6,0},{7,1},{8,14},{9,15},{10,... | collective-permute-start | bytes 835592 | tf_op jit(solution)/shard_map/ppermute | solution.py:408
  154.0 1.4 collective-permute-done.26.refs_5_
  155.4 10.3 %collective-permute-start.28 = (bf16[17,16,512]{2,1,0:T(8,128)(2,1)S(1)}, bf16[17,16,512]{2,1,0:T(8,128)(2,1)S(1)}, u32[]{:S(2)}, u32[]{:S(2)}) collective-permute-start(bf16[17,16,512]{2,1,0:T(8,128)(2,1)S(1)} %get-tuple-element.27), channel_id=1, source_target_pairs={{0,7},{1,6},{2,5},{3,4},{4,3},{5,2},{6,1},{7,0},{8,15},{9,14},{10,... | collective-permute-start | bytes 835592 | tf_op jit(solution)/shard_map/ppermute | solution.py:408
  165.7 11.3 %collective-permute-done.27.refs_6_ = bf16[17,16,512]{2,1,0:T(8,128)(2,1)S(1)} collective-permute-done((bf16[17,16,512]{2,1,0:T(8,128)(2,1)S(1)}, bf16[17,16,512]{2,1,0:T(8,128)(2,1)S(1)}, u32[]{:S(2)}, u32[]{:S(2)}) %collective-permute-start.27) | collective-permute-done | bytes 278560 | tf_op jit(solution)/shard_map/ppermute | solution.py:408
  176.9 6.2 %collective-permute-done.28.refs_7_ = bf16[17,16,512]{2,1,0:T(8,128)(2,1)S(1)} collective-permute-done((bf16[17,16,512]{2,1,0:T(8,128)(2,1)S(1)}, bf16[17,16,512]{2,1,0:T(8,128)(2,1)S(1)}, u32[]{:S(2)}, u32[]{:S(2)}) %collective-permute-start.28) | collective-permute-done | bytes 278560 | tf_op jit(solution)/shard_map/ppermute | solution.py:408
  183.2 4.7 %owner_rows.1 = bf16[2048,512]{1,0:T(8,128)(2,1)} custom-call(s32[10]{0:T(128)S(1)} %pad_add_fusion.scalars.refs_0_, bf16[17,16,512]{2,1,0:T(8,128)(2,1)S(1)} %get-tuple-element.20.refs_0_, bf16[17,16,512]{2,1,0:T(8,128)(2,1)S(1)} %collective-permute-done.22.refs_1_, bf16[17,16,512]{2,1,0:T(8,128)(2,1)S(1)} %collective-permute-done.23.refs_2_, ...), custom_call_target="tpu_custom_call" | custom-call | flops 4194304 | bytes 4325376 | tf_op jit(solution)/shard_map/owner_rows/pallas_call | solution.py:376
  187.9 1.6 lay_columns.1
  (55 shorter events, 4.4 us)
Async XLA Ops:
  0.6 44.9 %copy-start.3 = (bf16[192,1536]{1,0:T(8,128)(2,1)S(1)}, bf16[192,1536]{1,0:T(8,128)(2,1)}, u32[]{:S(2)}) copy-start(bf16[192,1536]{1,0:T(8,128)(2,1)} %param.7) | copy-start | bytes 1769476
  0.6 23.4 %copy-start.4 = (bf16[3,64,1536]{2,1,0:T(8,128)(2,1)S(1)}, bf16[3,64,1536]{2,1,0:T(8,128)(2,1)}, u32[]{:S(2)}) copy-start(bf16[3,64,1536]{2,1,0:T(8,128)(2,1)} %refs_0_.1) | copy-start | bytes 1769476
  0.6 55.7 %collective-permute-start.30 = (bf16[512,1536]{1,0:T(8,128)(2,1)}, bf16[512,1536]{1,0:T(8,128)(2,1)S(1)}, u32[]{:S(2)}, u32[]{:S(2)}) collective-permute-start(bf16[512,1536]{1,0:T(8,128)(2,1)} %bitcast.17), channel_id=1, source_target_pairs={{0,1},{1,0},{2,3},{3,2},{4,5},{5,4},{6,7},{7,6},{8,9},{9,8},{10,11... | collective-permute-start | bytes 4718600 | tf_op jit(solution)/shard_map/ppermute | solution.py:31
  2.3 8.5 %collective-permute-start.13 = (bf16[1,192,384]{2,1,0:T(8,128)(2,1)S(1)}, bf16[1,192,384]{2,1,0:T(8,128)(2,1)S(1)}, u32[]{:S(2)}, u32[]{:S(2)}) collective-permute-start(bf16[1,192,384]{2,1,0:T(8,128)(2,1)S(1)} %dynamic-slice_bitcast_fusion), channel_id=1, source_target_pairs={{0,6},{1,7},{2,4},{3,5},{4,2},{5,3},{6,0},{7,1},{8,14},{9,15},{10,... | collective-permute-start | bytes 442376 | tf_op jit(solution)/shard_map/ppermute | solution.py:35
  3.7 9.2 %collective-permute-start.11 = (bf16[1,192,384]{2,1,0:T(8,128)(2,1)S(1)}, bf16[1,192,384]{2,1,0:T(8,128)(2,1)S(1)}, u32[]{:S(2)}, u32[]{:S(2)}) collective-permute-start(bf16[1,192,384]{2,1,0:T(8,128)(2,1)S(1)} %dynamic-slice_bitcast_fusion), channel_id=1, source_target_pairs={{0,2},{1,3},{2,0},{3,1},{4,6},{5,7},{6,4},{7,5},{8,10},{9,11},{10,... | collective-permute-start | bytes 442376 | tf_op jit(solution)/shard_map/ppermute | solution.py:35
  5.9 10.2 %collective-permute-start.12 = (bf16[1,192,384]{2,1,0:T(8,128)(2,1)S(1)}, bf16[1,192,384]{2,1,0:T(8,128)(2,1)S(1)}, u32[]{:S(2)}, u32[]{:S(2)}) collective-permute-start(bf16[1,192,384]{2,1,0:T(8,128)(2,1)S(1)} %dynamic-slice_bitcast_fusion), channel_id=1, source_target_pairs={{0,4},{1,5},{2,6},{3,7},{4,0},{5,1},{6,2},{7,3},{8,12},{9,13},{10,... | collective-permute-start | bytes 442376 | tf_op jit(solution)/shard_map/ppermute | solution.py:35
  16.2 27.7 %collective-permute-start.14 = (bf16[3,1,192,384]{3,2,1,0:T(8,128)(2,1)S(1)}, bf16[3,1,192,384]{3,2,1,0:T(8,128)(2,1)S(1)}, u32[]{:S(2)}, u32[]{:S(2)}) collective-permute-start(bf16[3,1,192,384]{3,2,1,0:T(8,128)(2,1)S(1)} %pad_maximum_fusion.1.refs_1_), channel_id=1, source_target_pairs={{0,8},{8,0},{16,24},{24,16},{1,9},{9,1},{17,25},{25,17},{2,10},{10... | collective-permute-start | bytes 1327112 | tf_op jit(solution)/shard_map/ppermute | solution.py:39
  18.2 1.4 copy-start
  19.6 39.8 %copy-start.2 = (bf16[1,512,1536]{2,1,0:T(8,128)(2,1)S(1)}, bf16[1,512,1536]{2,1,0:T(8,128)(2,1)}, u32[]{:S(2)}) copy-start(bf16[1,512,1536]{2,1,0:T(8,128)(2,1)} %param.6) | copy-start | bytes 4718596
  22.5 33.8 %collective-permute-start.29 = (bf16[768,512]{1,0:T(8,128)(2,1)S(1)}, bf16[768,512]{1,0:T(8,128)(2,1)S(1)}, u32[]{:S(2)}, u32[]{:S(2)}) collective-permute-start(bf16[768,512]{1,0:T(8,128)(2,1)S(1)} %get-tuple-element.29), channel_id=1, source_target_pairs={{0,1},{1,0},{2,3},{3,2},{4,5},{5,4},{6,7},{7,6},{8,9},{9,8},{10,11... | collective-permute-start | bytes 2359304 | tf_op jit(solution)/shard_map/ppermute | solution.py:31
  24.0 8.3 %collective-permute-start = (bf16[3,64,384]{2,1,0:T(8,128)(2,1)S(1)}, bf16[3,64,384]{2,1,0:T(8,128)(2,1)S(1)}, u32[]{:S(2)}, u32[]{:S(2)}) collective-permute-start(bf16[3,64,384]{2,1,0:T(8,128)(2,1)S(1)} %constant_dynamic-slice_fusion), channel_id=1, source_target_pairs={{0,2},{1,3},{2,0},{3,1},{4,6},{5,7},{6,4},{7,5},{8,10},{9,11},{10,... | collective-permute-start | bytes 442376 | tf_op jit(solution)/shard_map/ppermute | solution.py:35
  26.2 8.4 %collective-permute-start.1 = (bf16[3,64,384]{2,1,0:T(8,128)(2,1)S(1)}, bf16[3,64,384]{2,1,0:T(8,128)(2,1)S(1)}, u32[]{:S(2)}, u32[]{:S(2)}) collective-permute-start(bf16[3,64,384]{2,1,0:T(8,128)(2,1)S(1)} %constant_dynamic-slice_fusion), channel_id=1, source_target_pairs={{0,4},{1,5},{2,6},{3,7},{4,0},{5,1},{6,2},{7,3},{8,12},{9,13},{10,... | collective-permute-start | bytes 442376 | tf_op jit(solution)/shard_map/ppermute | solution.py:35
  32.3 13.2 %collective-permute-start.15 = (bf16[3,1,192,384]{3,2,1,0:T(8,128)(2,1)S(1)}, bf16[3,1,192,384]{3,2,1,0:T(8,128)(2,1)S(1)}, u32[]{:S(2)}, u32[]{:S(2)}) collective-permute-start(bf16[3,1,192,384]{3,2,1,0:T(8,128)(2,1)S(1)} %pad_maximum_fusion.1.refs_1_), channel_id=1, source_target_pairs={{0,16},{8,24},{16,0},{24,8},{1,17},{9,25},{17,1},{25,9},{2,18},{10... | collective-permute-start | bytes 1327112 | tf_op jit(solution)/shard_map/ppermute | solution.py:39
  34.6 7.9 %collective-permute-start.2 = (bf16[3,64,384]{2,1,0:T(8,128)(2,1)S(1)}, bf16[3,64,384]{2,1,0:T(8,128)(2,1)S(1)}, u32[]{:S(2)}, u32[]{:S(2)}) collective-permute-start(bf16[3,64,384]{2,1,0:T(8,128)(2,1)S(1)} %constant_dynamic-slice_fusion), channel_id=1, source_target_pairs={{0,6},{1,7},{2,4},{3,5},{4,2},{5,3},{6,0},{7,1},{8,14},{9,15},{10,... | collective-permute-start | bytes 442376 | tf_op jit(solution)/shard_map/ppermute | solution.py:35
  42.5 11.0 %collective-permute-start.16 = (bf16[3,1,192,384]{3,2,1,0:T(8,128)(2,1)S(1)}, bf16[3,1,192,384]{3,2,1,0:T(8,128)(2,1)S(1)}, u32[]{:S(2)}, u32[]{:S(2)}) collective-permute-start(bf16[3,1,192,384]{3,2,1,0:T(8,128)(2,1)S(1)} %pad_maximum_fusion.1.refs_1_), channel_id=1, source_target_pairs={{0,24},{8,16},{16,8},{24,0},{1,25},{9,17},{17,9},{25,1},{2,26},{10... | collective-permute-start | bytes 1327112 | tf_op jit(solution)/shard_map/ppermute | solution.py:39
  43.9 11.2 %collective-permute-start.18 = (bf16[3,1,192,384]{3,2,1,0:T(8,128)(2,1)S(1)}, bf16[3,1,192,384]{3,2,1,0:T(8,128)(2,1)S(1)}, u32[]{:S(2)}, u32[]{:S(2)}) collective-permute-start(bf16[3,1,192,384]{3,2,1,0:T(8,128)(2,1)S(1)} %pad_maximum_fusion.1.refs_1_), channel_id=1, source_target_pairs={{0,1},{1,0},{2,3},{3,2},{4,5},{5,4},{6,7},{7,6},{8,9},{9,8},{10,11... | collective-permute-start | bytes 1327112 | tf_op jit(solution)/shard_map/ppermute | solution.py:31
  45.5 19.2 %collective-permute-start.17 = (bf16[1,192,1536]{2,1,0:T(8,128)(2,1)S(1)}, bf16[1,192,1536]{2,1,0:T(8,128)(2,1)S(1)}, u32[]{:S(2)}, u32[]{:S(2)}) collective-permute-start(bf16[1,192,1536]{2,1,0:T(8,128)(2,1)S(1)} %bitcast.20), channel_id=1, source_target_pairs={{0,1},{1,0},{2,3},{3,2},{4,5},{5,4},{6,7},{7,6},{8,9},{9,8},{10,11... | collective-permute-start | bytes 1769480 | tf_op jit(solution)/shard_map/ppermute | solution.py:31
  53.5 11.3 %collective-permute-start.5 = (bf16[3,3,64,384]{3,2,1,0:T(8,128)(2,1)S(1)}, bf16[3,3,64,384]{3,2,1,0:T(8,128)(2,1)S(1)}, u32[]{:S(2)}, u32[]{:S(2)}) collective-permute-start(bf16[3,3,64,384]{3,2,1,0:T(8,128)(2,1)S(1)} %pad_maximum_fusion.refs_1_), channel_id=1, source_target_pairs={{0,24},{8,16},{16,8},{24,0},{1,25},{9,17},{17,9},{25,1},{2,26},{10... | collective-permute-start | bytes 1327112 | tf_op jit(solution)/shard_map/ppermute | solution.py:39
  55.1 18.7 %collective-permute-start.3 = (bf16[3,3,64,384]{3,2,1,0:T(8,128)(2,1)S(1)}, bf16[3,3,64,384]{3,2,1,0:T(8,128)(2,1)S(1)}, u32[]{:S(2)}, u32[]{:S(2)}) collective-permute-start(bf16[3,3,64,384]{3,2,1,0:T(8,128)(2,1)S(1)} %pad_maximum_fusion.refs_1_), channel_id=1, source_target_pairs={{0,8},{8,0},{16,24},{24,16},{1,9},{9,1},{17,25},{25,17},{2,10},{10... | collective-permute-start | bytes 1327112 | tf_op jit(solution)/shard_map/ppermute | solution.py:39
  56.3 19.6 %collective-permute-start.4 = (bf16[3,3,64,384]{3,2,1,0:T(8,128)(2,1)S(1)}, bf16[3,3,64,384]{3,2,1,0:T(8,128)(2,1)S(1)}, u32[]{:S(2)}, u32[]{:S(2)}) collective-permute-start(bf16[3,3,64,384]{3,2,1,0:T(8,128)(2,1)S(1)} %pad_maximum_fusion.refs_1_), channel_id=1, source_target_pairs={{0,16},{8,24},{16,0},{24,8},{1,17},{9,25},{17,1},{25,9},{2,18},{10... | collective-permute-start | bytes 1327112 | tf_op jit(solution)/shard_map/ppermute | solution.py:39
  56.4 21.2 %collective-permute-start.19 = (bf16[3,1,192,384]{3,2,1,0:T(8,128)(2,1)S(1)}, bf16[3,1,192,384]{3,2,1,0:T(8,128)(2,1)S(1)}, u32[]{:S(2)}, u32[]{:S(2)}) collective-permute-start(bf16[3,1,192,384]{3,2,1,0:T(8,128)(2,1)S(1)} %collective-permute-done.14.refs_2_), channel_id=1, source_target_pairs={{0,1},{1,0},{2,3},{3,2},{4,5},{5,4},{6,7},{7,6},{8,9},{9,8},{10,11... | collective-permute-start | bytes 1327112 | tf_op jit(solution)/shard_map/ppermute | solution.py:31
  59.5 42.8 %copy-start.1 = (bf16[1,512,1536]{2,1,0:T(8,128)(2,1)S(1)}, bf16[1,512,1536]{2,1,0:T(8,128)(2,1)}, u32[]{:S(2)}) copy-start(bf16[1,512,1536]{2,1,0:T(8,128)(2,1)} %param.5) | copy-start | bytes 4718596
  64.7 17.0 %collective-permute-start.20 = (bf16[3,1,192,384]{3,2,1,0:T(8,128)(2,1)S(1)}, bf16[3,1,192,384]{3,2,1,0:T(8,128)(2,1)S(1)}, u32[]{:S(2)}, u32[]{:S(2)}) collective-permute-start(bf16[3,1,192,384]{3,2,1,0:T(8,128)(2,1)S(1)} %collective-permute-done.15.refs_3_), channel_id=1, source_target_pairs={{0,1},{1,0},{2,3},{3,2},{4,5},{5,4},{6,7},{7,6},{8,9},{9,8},{10,11... | collective-permute-start | bytes 1327112 | tf_op jit(solution)/shard_map/ppermute | solution.py:31
  64.8 21.7 %collective-permute-start.31 = (bf16[768,384]{1,0:T(8,128)(2,1)S(1)}, bf16[768,384]{1,0:T(8,128)(2,1)S(1)}, u32[]{:S(2)}, u32[]{:S(2)}) collective-permute-start(bf16[768,384]{1,0:T(8,128)(2,1)S(1)} %get-tuple-element.31), channel_id=1, source_target_pairs={{0,8},{8,0},{16,24},{24,16},{1,9},{9,1},{17,25},{25,17},{2,10},{10... | collective-permute-start | bytes 1769480 | tf_op jit(solution)/shard_map/ppermute | solution.py:39
  73.8 18.5 %collective-permute-start.32 = (bf16[768,384]{1,0:T(8,128)(2,1)S(1)}, bf16[768,384]{1,0:T(8,128)(2,1)S(1)}, u32[]{:S(2)}, u32[]{:S(2)}) collective-permute-start(bf16[768,384]{1,0:T(8,128)(2,1)S(1)} %get-tuple-element.32), channel_id=1, source_target_pairs={{0,16},{8,24},{16,0},{24,8},{1,17},{9,25},{17,1},{25,9},{2,18},{10... | collective-permute-start | bytes 1769480 | tf_op jit(solution)/shard_map/ppermute | solution.py:39
  76.0 26.3 %collective-permute-start.33 = (bf16[768,384]{1,0:T(8,128)(2,1)S(1)}, bf16[768,384]{1,0:T(8,128)(2,1)S(1)}, u32[]{:S(2)}, u32[]{:S(2)}) collective-permute-start(bf16[768,384]{1,0:T(8,128)(2,1)S(1)} %get-tuple-element.33), channel_id=1, source_target_pairs={{0,24},{8,16},{16,8},{24,0},{1,25},{9,17},{17,9},{25,1},{2,26},{10... | collective-permute-start | bytes 1769480 | tf_op jit(solution)/shard_map/ppermute | solution.py:39
  77.6 5.5 %collective-permute-start.21 = (bf16[3,1,192,384]{3,2,1,0:T(8,128)(2,1)S(1)}, bf16[3,1,192,384]{3,2,1,0:T(8,128)(2,1)S(1)}, u32[]{:S(2)}, u32[]{:S(2)}) collective-permute-start(bf16[3,1,192,384]{3,2,1,0:T(8,128)(2,1)S(1)} %collective-permute-done.16.refs_4_), channel_id=1, source_target_pairs={{0,1},{1,0},{2,3},{3,2},{4,5},{5,4},{6,7},{7,6},{8,9},{9,8},{10,11... | collective-permute-start | bytes 1327112 | tf_op jit(solution)/shard_map/ppermute | solution.py:31
  81.7 35.6 %collective-permute-start.6 = (bf16[3,64,1536]{2,1,0:T(8,128)(2,1)S(1)}, bf16[3,64,1536]{2,1,0:T(8,128)(2,1)S(1)}, u32[]{:S(2)}, u32[]{:S(2)}) collective-permute-start(bf16[3,64,1536]{2,1,0:T(8,128)(2,1)S(1)} %copy-done.4), channel_id=1, source_target_pairs={{0,1},{1,0},{2,3},{3,2},{4,5},{5,4},{6,7},{7,6},{8,9},{9,8},{10,11... | collective-permute-start | bytes 1769480 | tf_op jit(solution)/shard_map/ppermute | solution.py:31
  83.1 28.9 %collective-permute-start.7 = (bf16[3,3,64,384]{3,2,1,0:T(8,128)(2,1)S(1)}, bf16[3,3,64,384]{3,2,1,0:T(8,128)(2,1)S(1)}, u32[]{:S(2)}, u32[]{:S(2)}) collective-permute-start(bf16[3,3,64,384]{3,2,1,0:T(8,128)(2,1)S(1)} %pad_maximum_fusion.refs_1_), channel_id=1, source_target_pairs={{0,1},{1,0},{2,3},{3,2},{4,5},{5,4},{6,7},{7,6},{8,9},{9,8},{10,11... | collective-permute-start | bytes 1327112 | tf_op jit(solution)/shard_map/ppermute | solution.py:31
  86.5 30.8 %collective-permute-start.10 = (bf16[3,3,64,384]{3,2,1,0:T(8,128)(2,1)S(1)}, bf16[3,3,64,384]{3,2,1,0:T(8,128)(2,1)S(1)}, u32[]{:S(2)}, u32[]{:S(2)}) collective-permute-start(bf16[3,3,64,384]{3,2,1,0:T(8,128)(2,1)S(1)} %collective-permute-done.5.refs_4_), channel_id=1, source_target_pairs={{0,1},{1,0},{2,3},{3,2},{4,5},{5,4},{6,7},{7,6},{8,9},{9,8},{10,11... | collective-permute-start | bytes 1327112 | tf_op jit(solution)/shard_map/ppermute | solution.py:31
  92.3 26.3 %collective-permute-start.8 = (bf16[3,3,64,384]{3,2,1,0:T(8,128)(2,1)S(1)}, bf16[3,3,64,384]{3,2,1,0:T(8,128)(2,1)S(1)}, u32[]{:S(2)}, u32[]{:S(2)}) collective-permute-start(bf16[3,3,64,384]{3,2,1,0:T(8,128)(2,1)S(1)} %collective-permute-done.3.refs_2_), channel_id=1, source_target_pairs={{0,1},{1,0},{2,3},{3,2},{4,5},{5,4},{6,7},{7,6},{8,9},{9,8},{10,11... | collective-permute-start | bytes 1327112 | tf_op jit(solution)/shard_map/ppermute | solution.py:31
  102.2 16.4 %collective-permute-start.9 = (bf16[3,3,64,384]{3,2,1,0:T(8,128)(2,1)S(1)}, bf16[3,3,64,384]{3,2,1,0:T(8,128)(2,1)S(1)}, u32[]{:S(2)}, u32[]{:S(2)}) collective-permute-start(bf16[3,3,64,384]{3,2,1,0:T(8,128)(2,1)S(1)} %collective-permute-done.4.refs_3_), channel_id=1, source_target_pairs={{0,1},{1,0},{2,3},{3,2},{4,5},{5,4},{6,7},{7,6},{8,9},{9,8},{10,11... | collective-permute-start | bytes 1327112 | tf_op jit(solution)/shard_map/ppermute | solution.py:31
  112.1 19.5 %collective-permute-start.34 = (bf16[192,384]{1,0:T(8,128)(2,1)S(1)}, bf16[192,384]{1,0:T(8,128)(2,1)S(1)}, u32[]{:S(2)}, u32[]{:S(2)}) collective-permute-start(bf16[192,384]{1,0:T(8,128)(2,1)S(1)} %get-tuple-element.35), channel_id=1, source_target_pairs={{0,2},{1,3},{2,0},{3,1},{4,6},{5,7},{6,4},{7,5},{8,10},{9,11},{10,... | collective-permute-start | bytes 442376 | tf_op jit(solution)/shard_map/ppermute | solution.py:35
  117.3 14.3 %collective-permute-start.35 = (bf16[192,384]{1,0:T(8,128)(2,1)S(1)}, bf16[192,384]{1,0:T(8,128)(2,1)S(1)}, u32[]{:S(2)}, u32[]{:S(2)}) collective-permute-start(bf16[192,384]{1,0:T(8,128)(2,1)S(1)} %get-tuple-element.36), channel_id=1, source_target_pairs={{0,4},{1,5},{2,6},{3,7},{4,0},{5,1},{6,2},{7,3},{8,12},{9,13},{10,... | collective-permute-start | bytes 442376 | tf_op jit(solution)/shard_map/ppermute | solution.py:35
  117.3 14.5 %collective-permute-start.36 = (bf16[192,384]{1,0:T(8,128)(2,1)S(1)}, bf16[192,384]{1,0:T(8,128)(2,1)S(1)}, u32[]{:S(2)}, u32[]{:S(2)}) collective-permute-start(bf16[192,384]{1,0:T(8,128)(2,1)S(1)} %get-tuple-element.37), channel_id=1, source_target_pairs={{0,6},{1,7},{2,4},{3,5},{4,2},{5,3},{6,0},{7,1},{8,14},{9,15},{10,... | collective-permute-start | bytes 442376 | tf_op jit(solution)/shard_map/ppermute | solution.py:35
  127.8 7.3 %collective-permute-start.22 = (bf16[17,16,512]{2,1,0:T(8,128)(2,1)S(1)}, bf16[17,16,512]{2,1,0:T(8,128)(2,1)S(1)}, u32[]{:S(2)}, u32[]{:S(2)}) collective-permute-start(bf16[17,16,512]{2,1,0:T(8,128)(2,1)S(1)} %get-tuple-element.21), channel_id=1, source_target_pairs={{0,1},{1,0},{2,3},{3,2},{4,5},{5,4},{6,7},{7,6},{8,9},{9,8},{10,11... | collective-permute-start | bytes 835592 | tf_op jit(solution)/shard_map/ppermute | solution.py:408
  128.9 16.6 %collective-permute-start.23 = (bf16[17,16,512]{2,1,0:T(8,128)(2,1)S(1)}, bf16[17,16,512]{2,1,0:T(8,128)(2,1)S(1)}, u32[]{:S(2)}, u32[]{:S(2)}) collective-permute-start(bf16[17,16,512]{2,1,0:T(8,128)(2,1)S(1)} %get-tuple-element.22), channel_id=1, source_target_pairs={{0,2},{1,3},{2,0},{3,1},{4,6},{5,7},{6,4},{7,5},{8,10},{9,11},{10,... | collective-permute-start | bytes 835592 | tf_op jit(solution)/shard_map/ppermute | solution.py:408
  131.5 20.0 %collective-permute-start.24 = (bf16[17,16,512]{2,1,0:T(8,128)(2,1)S(1)}, bf16[17,16,512]{2,1,0:T(8,128)(2,1)S(1)}, u32[]{:S(2)}, u32[]{:S(2)}) collective-permute-start(bf16[17,16,512]{2,1,0:T(8,128)(2,1)S(1)} %get-tuple-element.23), channel_id=1, source_target_pairs={{0,3},{1,2},{2,1},{3,0},{4,7},{5,6},{6,5},{7,4},{8,11},{9,10},{10,... | collective-permute-start | bytes 835592 | tf_op jit(solution)/shard_map/ppermute | solution.py:408
  131.6 20.2 %collective-permute-start.25 = (bf16[17,16,512]{2,1,0:T(8,128)(2,1)S(1)}, bf16[17,16,512]{2,1,0:T(8,128)(2,1)S(1)}, u32[]{:S(2)}, u32[]{:S(2)}) collective-permute-start(bf16[17,16,512]{2,1,0:T(8,128)(2,1)S(1)} %get-tuple-element.24), channel_id=1, source_target_pairs={{0,4},{1,5},{2,6},{3,7},{4,0},{5,1},{6,2},{7,3},{8,12},{9,13},{10,... | collective-permute-start | bytes 835592 | tf_op jit(solution)/shard_map/ppermute | solution.py:408
  131.8 23.6 %collective-permute-start.26 = (bf16[17,16,512]{2,1,0:T(8,128)(2,1)S(1)}, bf16[17,16,512]{2,1,0:T(8,128)(2,1)S(1)}, u32[]{:S(2)}, u32[]{:S(2)}) collective-permute-start(bf16[17,16,512]{2,1,0:T(8,128)(2,1)S(1)} %get-tuple-element.25), channel_id=1, source_target_pairs={{0,5},{1,4},{2,7},{3,6},{4,1},{5,0},{6,3},{7,2},{8,13},{9,12},{10,... | collective-permute-start | bytes 835592 | tf_op jit(solution)/shard_map/ppermute | solution.py:408
  135.1 52.8 %collective-permute-start.37 = (f32[192,384]{1,0:T(8,128)S(1)}, f32[192,384]{1,0:T(8,128)S(1)}, u32[]{:S(2)}, u32[]{:S(2)}) collective-permute-start(f32[192,384]{1,0:T(8,128)S(1)} %z_sum.1.a_ref), channel_id=1, source_target_pairs={{0,8},{8,0},{16,24},{24,16},{1,9},{9,1},{17,25},{25,17},{2,10},{10... | collective-permute-start | bytes 884744 | tf_op jit(solution)/shard_map/ppermute | solution.py:39
  145.6 42.4 %collective-permute-start.38 = (f32[192,384]{1,0:T(8,128)S(1)}, f32[192,384]{1,0:T(8,128)S(1)}, u32[]{:S(2)}, u32[]{:S(2)}) collective-permute-start(f32[192,384]{1,0:T(8,128)S(1)} %z_sum.1.a_ref), channel_id=1, source_target_pairs={{0,16},{8,24},{16,0},{24,8},{1,17},{9,25},{17,1},{25,9},{2,18},{10... | collective-permute-start | bytes 884744 | tf_op jit(solution)/shard_map/ppermute | solution.py:39
  151.5 36.4 %collective-permute-start.39 = (f32[192,384]{1,0:T(8,128)S(1)}, f32[192,384]{1,0:T(8,128)S(1)}, u32[]{:S(2)}, u32[]{:S(2)}) collective-permute-start(f32[192,384]{1,0:T(8,128)S(1)} %z_sum.1.a_ref), channel_id=1, source_target_pairs={{0,24},{8,16},{16,8},{24,0},{1,25},{9,17},{17,9},{25,1},{2,26},{10... | collective-permute-start | bytes 884744 | tf_op jit(solution)/shard_map/ppermute | solution.py:39
  151.7 25.2 %collective-permute-start.27 = (bf16[17,16,512]{2,1,0:T(8,128)(2,1)S(1)}, bf16[17,16,512]{2,1,0:T(8,128)(2,1)S(1)}, u32[]{:S(2)}, u32[]{:S(2)}) collective-permute-start(bf16[17,16,512]{2,1,0:T(8,128)(2,1)S(1)} %get-tuple-element.26), channel_id=1, source_target_pairs={{0,6},{1,7},{2,4},{3,5},{4,2},{5,3},{6,0},{7,1},{8,14},{9,15},{10,... | collective-permute-start | bytes 835592 | tf_op jit(solution)/shard_map/ppermute | solution.py:408
  155.4 27.8 %collective-permute-start.28 = (bf16[17,16,512]{2,1,0:T(8,128)(2,1)S(1)}, bf16[17,16,512]{2,1,0:T(8,128)(2,1)S(1)}, u32[]{:S(2)}, u32[]{:S(2)}) collective-permute-start(bf16[17,16,512]{2,1,0:T(8,128)(2,1)S(1)} %get-tuple-element.27), channel_id=1, source_target_pairs={{0,7},{1,6},{2,5},{3,4},{4,3},{5,2},{6,1},{7,0},{8,15},{9,14},{10,... | collective-permute-start | bytes 835592 | tf_op jit(solution)/shard_map/ppermute | solution.py:408

commit v2 on v1

v2 whole, which is shorter than its diff:
```python
import math

import jax
import jax.numpy as jnp
from jax import lax
from jax.experimental import pallas as pl
from jax.experimental.pallas import tpu as pltpu
from jax.sharding import PartitionSpec as P

D = 1536
SEG = 8
HOLD = 64
OWN_SEG = 128
N_SITE = 4
N_FSDP = 8
N_Z = N_FSDP // 2
QUARTER = D // N_SITE
CAP = OWN_SEG // N_FSDP
CS = 512
ROWS = HOLD * SEG
BLOCK = 128
LANES = 128
COLUMNS = 256
PAYLOAD_ORDER = (0, 4, 5, 6, 7, 2, 3, 1)
MIB = 1024 * 1024

EPSILON = 1e-05
F32 = jnp.float32
BF16 = jnp.bfloat16


def swap_core(value):
    return lax.ppermute(value, "fsdp", [(i, i ^ 1) for i in range(N_FSDP)])


def swap_z(value, distance):
    return lax.ppermute(value, "fsdp", [(i, i ^ (2 * distance)) for i in range(N_FSDP)])


def swap_site(value, distance):
    return lax.ppermute(value, "site", [(i, i ^ distance) for i in range(N_SITE)])


def hold(value, *first):
    return pl.pallas_call(
        lambda *refs: None,
        name="hold",
        out_shape=shape(value.shape, value.dtype),
        in_specs=[HBM] + [ANY] * len(first),
        out_specs=HBM,
        input_output_aliases={0: 0},
        cost_estimate=pl.CostEstimate(flops=0, bytes_accessed=0, transcendentals=0),
    )(value, *first)


Z_ORDER = (2, 1, 3)
HALF = D // N_FSDP // 2
STEM_ROWS = CS // N_FSDP
TAPS = 3
QUARTER_TAPS = (0, 2)
WHOLE_TAP = 1
UNITS = len(QUARTER_TAPS) + N_SITE


def half_places(site, low):
    return [(0, z, ("xor", site), low, HALF) for z in Z_ORDER]


def unit_places(site):
    return [(tap, z, ("xor", site), 0, STEM_ROWS) for z in Z_ORDER for tap in QUARTER_TAPS]


def all_places():
    whole_tap = [(WHOLE_TAP, ("abs", j)) for j in range(N_SITE)]
    columns = [(tap, ("xor", 0)) for tap in QUARTER_TAPS] + whole_tap
    return [(tap, z, kind, 0, STEM_ROWS) for z in Z_ORDER for tap, kind in columns]


def shard_places(tap, count):
    return [(tap, 0, ("abs", j), 0, count) for j in range(N_SITE)]


def rows_of(value):
    return value.reshape(-1, QUARTER)


def call(kernel, name, out_shape, grid, in_specs, out_specs, scratch, vmem=16):
    return pl.pallas_call(
        kernel,
        name=name,
        out_shape=out_shape,
        grid_spec=pltpu.PrefetchScalarGridSpec(
            num_scalar_prefetch=1,
            grid=grid,
            in_specs=in_specs,
            out_specs=out_specs,
            scratch_shapes=scratch,
        ),
        compiler_params=pltpu.CompilerParams(
            dimension_semantics=("arbitrary",) * len(grid), vmem_limit_bytes=vmem * MIB
        ),
        cost_estimate=pl.CostEstimate(flops=0, bytes_accessed=0, transcendentals=0),
    )


ANY = pl.BlockSpec(memory_space=pl.ANY)
HBM = pl.BlockSpec(memory_space=pltpu.HBM)


def whole(shape):
    return pl.BlockSpec(shape, lambda i, scalars: (0,) * len(shape))


def row_block(rows, columns):
    return pl.BlockSpec((rows, columns), lambda i, scalars: (i, 0))


def shape(dims, dtype):
    return jax.ShapeDtypeStruct(dims, dtype)


def dot_nt(a, b):
    return lax.dot_general(a, b, (((1,), (1,)), ((), ())), preferred_element_type=F32)


def join(kernel, name, out_dims, values, first=(), scratch=()):
    n = len(values)

    def wrapped(*refs):
        kernel(*refs[:n], *refs[n + len(first) :])

    out = tuple(shape(dims, BF16) for dims in out_dims)
    vmem = pl.BlockSpec(memory_space=pltpu.VMEM)
    return pl.pallas_call(
        wrapped,
        name=name,
        out_shape=out,
        in_specs=[vmem] * n + [ANY] * len(first),
        out_specs=(vmem,) * len(out),
        compiler_params=pltpu.CompilerParams(vmem_limit_bytes=8 * MIB),
        cost_estimate=pl.CostEstimate(flops=0, bytes_accessed=0, transcendentals=0),
    )(*values, *first)


def cut_proj_kernel(shard, out):
    at = pl.multiple_of(lax.axis_index("site") * QUARTER, QUARTER)
    out[...] = shard[:, pl.ds(at, QUARTER)]


def cut_stem_kernel(shard, out):
    at = pl.multiple_of(lax.axis_index("site") * QUARTER, QUARTER)
    for i, tap in enumerate(QUARTER_TAPS):
        out[i] = shard[tap, :, pl.ds(at, QUARTER)]
    for i in range(N_SITE):
        out[len(QUARTER_TAPS) + i] = shard[WHOLE_TAP, :, i * QUARTER : (i + 1) * QUARTER]


def pair_kernel(a, b, out):
    out[0] = a[...]
    out[1] = b[...]


def halves_kernel(pair, near, a, b):
    for i, piece in enumerate((pair.at[1], near.at[0], near.at[1])):
        a[i] = piece[:HALF, :]
        b[i] = piece[HALF:, :]


def pack_rows(out, pieces):
    at = 0
    for piece in pieces:
        out[at : at + piece.shape[0], :] = piece
        at += piece.shape[0]


def column_pieces(shard):
    return [shard[:, i * QUARTER : (i + 1) * QUARTER] for i in range(N_SITE)]


def site_step_kernel(shard, stem, a0, b0, a1, b1, quarter, far, a, b, packed, pair):
    pair[0], pair[1] = quarter[...], far[...]
    a[0], a[1], b[0], b[1] = a0[...], a1[...], b0[...], b1[...]
    pieces = column_pieces(shard[...])
    for tap in range(stem.shape[0]):
        pieces += column_pieces(stem[tap])
    pack_rows(packed, pieces + [ref[i] for ref in (a0, b0, a1, b1) for i in range(3)])


def collect_kernel(a, b, c, out):
    out[0], out[1], out[2] = a[...], b[...], c[...]


def three_kernel(pair, near, a2, b2, quarters, units, packed):
    pieces = [ref[j, i] for ref in (a2, b2) for j in range(2) for i in range(3)]
    for i, piece in enumerate((pair[1], near[0], near[1])):
        quarters[i] = piece[: len(QUARTER_TAPS)]
        units[i] = piece
        pieces += [piece[j] for j in range(UNITS)]
    pack_rows(packed, pieces)


def normalise(inputs):
    inputs = inputs.astype(F32)
    centered = inputs - jnp.mean(inputs, axis=-1, keepdims=True)
    variance = jnp.mean(centered * centered, axis=-1, keepdims=True)
    inverse = lax.rsqrt(variance + EPSILON)
    return centered * inverse, inverse


def norm_kernel(scalars, x_ref, out_ref, turned):
    core = scalars[1] % 2
    normed, _ = normalise(x_ref[...])
    turned[...] = normed.astype(BF16).T
    shard = D // N_FSDP
    for z in range(N_Z):
        rows = pl.ds(pl.multiple_of((2 * z + core) * shard, shard), shard)
        out_ref[pl.ds(z * shard, shard), :] = turned[rows, :]


def norm_half(scalars, inputs):
    return call(
        norm_kernel, "norm_half", shape((D // 2, ROWS), BF16), (ROWS // BLOCK,),
        [row_block(BLOCK, D)], pl.BlockSpec((D // 2, BLOCK), lambda i, scalars: (0, i)),
        [pltpu.VMEM((D, BLOCK), BF16)],
    )(scalars, inputs)


OUTER_PLACES = (((0, 0), (0, 0)), ((1, 0), (0, 1)), ((0, 1), (1, 0)), ((1, 1), (1, 1)))


def outer_kernel(scalars, na_ref, nb_ref, ca_ref, cb_ref, ka_ref, sa_ref, kb_ref, sb_ref):
    step = pl.program_id(0)
    total = jnp.dot(na_ref[...], ca_ref[...], preferred_element_type=F32)
    total = total + jnp.dot(nb_ref[...], cb_ref[...], preferred_element_type=F32)
    low, high = total[: D // 4, :], total[D // 4 :, :]
    for at, (a, b) in enumerate(OUTER_PLACES):

        @pl.when(step == at)
        def _(a=a, b=b):
            for (ref, i), value in (((ka_ref, sa_ref)[a[0]], a[1]), low), (((kb_ref, sb_ref)[b[0]], b[1]), high):
                ref[i] = value.astype(ref.dtype)


def outer_pieces(scalars, normed_a, normed_b, cotangent_a, cotangent_b):
    dims = (2, D // 4, QUARTER)
    column = pl.BlockSpec((ROWS, QUARTER), lambda i, scalars: (0, lax.bitwise_xor(scalars[0], i)))
    return call(
        outer_kernel, "outer_pieces", (shape(dims, F32), shape(dims, BF16)) * 2, (N_SITE,),
        [whole((D // 2, ROWS))] * 2 + [column] * 2, (whole(dims),) * 4, [],
    )(scalars, normed_a, normed_b, cotangent_a, cotangent_b)


def half_sum_kernel(scalars, ka_ref, ra_ref, kb_ref, rb_ref, oa_ref, sa_ref, ob_ref, sb_ref):
    for kept, came, own, sent in ((ka_ref, ra_ref, oa_ref, sa_ref), (kb_ref, rb_ref, ob_ref, sb_ref)):
        own[...] = kept[0] + came[0].astype(F32)
        sent[...] = (kept[1] + came[1].astype(F32)).astype(BF16)


def half_sum(scalars, *values):
    dims, out = (2, D // 4, QUARTER), (D // 4, QUARTER)
    return call(
        half_sum_kernel, "half_sum", (shape(out, F32), shape(out, BF16)) * 2, (1,),
        [whole(dims)] * 4, (whole(out),) * 4, [],
    )(scalars, *values)


def site_sum_kernel(scalars, oa_ref, ra_ref, ob_ref, rb_ref, kept_ref, sent_ref, total):
    shard = D // N_FSDP
    z = scalars[1] // 2
    total[: D // 4, :] = oa_ref[...] + ra_ref[...].astype(F32)
    total[D // 4 :, :] = ob_ref[...] + rb_ref[...].astype(F32)
    for distance, (ref, i) in enumerate(((kept_ref, 0), (sent_ref, 0), (kept_ref, 1), (sent_ref, 1))):
        rows = pl.ds(pl.multiple_of(lax.bitwise_xor(z, distance) * shard, shard), shard)
        ref[i] = total[rows, :].astype(ref.dtype)


def site_sum(scalars, *values):
    dims, out = (D // 4, QUARTER), (2, D // N_FSDP, QUARTER)
    return call(
        site_sum_kernel, "site_sum", (shape(out, F32), shape(out, BF16)), (1,),
        [whole(dims)] * 4, (whole(out),) * 2, [pltpu.VMEM((D // 2, QUARTER), F32)],
    )(scalars, *values)


def near_sum_kernel(scalars, kept_ref, came_ref, *refs):
    own_ref, sent_ref = refs[-2:]
    own_ref[...] = kept_ref[0] + came_ref[0].astype(F32)
    sent_ref[...] = (kept_ref[1] + came_ref[1].astype(F32)).astype(BF16)


def near_sum(scalars, kept, came, first):
    dims, out = (2, D // N_FSDP, QUARTER), (D // N_FSDP, QUARTER)
    return call(
        near_sum_kernel, "near_sum", (shape(out, F32), shape(out, BF16)), (1,),
        [whole(dims)] * 2 + [ANY] * len(first), (whole(out),) * 2, [],
    )(scalars, kept, came, *first)


def far_sum_kernel(scale, scalars, own_ref, came_ref, *refs):
    refs[-1][...] = (own_ref[...] + came_ref[...].astype(F32)) * scale


def far_sum(scalars, own, came, scale, first):
    dims = (D // N_FSDP, QUARTER)
    return call(
        lambda *refs: far_sum_kernel(scale, *refs), "far_sum", shape(dims, F32), (1,),
        [whole(dims)] * 2 + [ANY] * len(first), whole(dims), [],
    )(scalars, own, came, *first)


def lay_columns_kernel(scalars, a_ref, b_ref, c_ref, d_ref, out_ref):
    for distance, ref in enumerate((a_ref, b_ref, c_ref, d_ref)):
        at = pl.multiple_of(lax.bitwise_xor(scalars[0], distance) * QUARTER, QUARTER)
        out_ref[:, pl.ds(at, QUARTER)] = ref[...]


def lay_columns(scalars, parts):
    out = (D // N_FSDP, D)
    return call(
        lay_columns_kernel, "lay_columns", shape(out, F32), (1,), [whole(parts[0].shape)] * N_SITE,
        whole(out), [],
    )(scalars, *parts)


def weight_copies(tables, scalars, refs, weight, sem):
    site, index = scalars[0], scalars[1]
    shard = weight.shape[1] // N_FSDP
    copies = []
    for (places, swapped), ref in zip(tables, refs, strict=True):
        at = 0
        for place in places:
            if isinstance(place, int):
                at += place
                continue
            tap, z, (kind, quarter), low, count = place
            start = lax.bitwise_xor(index, 2 * z + swapped) * shard + low
            rows = pl.ds(pl.multiple_of(start, math.gcd(shard, low)), count)
            columns = pl.ds(quarter * QUARTER, QUARTER)
            if kind == "all":
                columns = pl.ds(0, D)
            elif kind == "xor":
                column = lax.bitwise_xor(site, quarter) * QUARTER
                columns = pl.ds(pl.multiple_of(column, QUARTER), QUARTER)
            source = ref.at[pl.ds(at, count), :]
            copies.append(pltpu.make_async_copy(source, weight.at[tap, rows, columns], sem))
            at += count
        assert at == ref.shape[0]
    return copies


def input_grad_kernel(tables, scalars, *refs):
    n = len(tables)
    parts, (x_ref, cot_ref, out_ref, weight, normed, inverse, back, sem) = refs[:n], refs[n:]
    copies = weight_copies(tables, scalars, parts, weight, sem)
    for copy in copies:
        copy.start()

    @pl.loop(0, ROWS // BLOCK)
    def _(i):
        rows = pl.ds(pl.multiple_of(i * BLOCK, BLOCK), BLOCK)
        normed[rows, :], inverse[rows, :] = normalise(x_ref[rows, :])

    for copy in copies:
        copy.wait()

    @pl.loop(0, D // COLUMNS)
    def _(i):
        rows = pl.ds(pl.multiple_of(i * COLUMNS, COLUMNS), COLUMNS)
        back[:, rows] = dot_nt(cot_ref[...], weight[0, rows, :])

    @pl.loop(0, ROWS // BLOCK)
    def _(i):
        rows = pl.ds(pl.multiple_of(i * BLOCK, BLOCK), BLOCK)
        term, row_normed = back[rows, :], normed[rows, :]
        inner = term - jnp.mean(term, axis=-1, keepdims=True)
        inner = inner - row_normed * jnp.mean(term * row_normed, axis=-1, keepdims=True)
        out_ref[rows, :] = (cot_ref[rows, :].astype(F32) + inverse[rows, :] * inner).astype(BF16)


def split_parts(parts):
    return [(places, swapped) for _, places, swapped in parts], [value for value, _, _ in parts]


def input_gradient(scalars, parts, inputs, cotangent):
    tables, values = split_parts(parts)
    return call(
        lambda *refs: input_grad_kernel(tables, *refs), "input_gradient", shape((ROWS, D), BF16),
        (1,), [ANY] * len(values) + [whole((ROWS, D))] * 2, whole((ROWS, D)),
        [
            pltpu.VMEM((1, D, D), BF16),
            pltpu.VMEM((ROWS, D), F32),
            pltpu.VMEM((ROWS, 1), F32),
            pltpu.VMEM((ROWS, D), F32),
            pltpu.SemaphoreType.DMA,
        ],
        vmem=32,
    )(scalars, *values, inputs, cotangent)


def starts_of(scalars):
    starts = [jnp.int32(0)]
    for owner in range(N_FSDP):
        starts.append(starts[-1] + scalars[2 + owner])
    return starts


def held_before(start, holder):
    return 2 * (start // (2 * N_FSDP)) + jnp.clip(start % (2 * N_FSDP) - 2 * holder, 0, 2)


def stem_kernel(tables, scalars, *refs):
    n = len(tables)
    parts, grad_ref, outs = refs[:n], refs[n], refs[n + 1 : n + 1 + N_FSDP]
    weight, mixed, leading, packed, firsts, sem, out_sem = refs[n + 1 + N_FSDP :]
    copies = weight_copies(tables, scalars, parts, weight, sem)
    for copy in copies:
        copy.start()
    for copy in copies:
        copy.wait()
    index = scalars[1]
    for lane in range(0, CS, COLUMNS):
        span = pl.ds(lane, COLUMNS)
        even = dot_nt(grad_ref[...], weight[1, span, :])
        first = dot_nt(grad_ref[...], weight[0, span, :])
        leading[:, span] = first
        row = lax.broadcasted_iota(jnp.int32, first.shape, 0)
        following = jnp.where(row % SEG == SEG - 1, 0.0, pltpu.roll(first, ROWS - 1, 0))
        odd = dot_nt(grad_ref[...], weight[2, span, :]) + following
        for part in range(COLUMNS // LANES):
            at = lane // LANES + part
            columns = slice(part * LANES, (part + 1) * LANES)
            mixed[at, pl.ds(0, ROWS, stride=2), :] = even[:, columns]
            mixed[at, pl.ds(1, ROWS, stride=2), :] = odd[:, columns]
    starts = starts_of(scalars)

    @pl.loop(0, HOLD, unroll=4)
    def _(slot):
        item = 2 * (slot // 2 * N_FSDP + index) + slot % 2
        owner = jnp.int32(0)
        start = jnp.int32(0)
        for other in range(1, N_FSDP):
            passed = item >= starts[other]
            owner = jnp.where(passed, other, owner)
            start = jnp.where(passed, starts[other], start)
        rank = slot - held_before(start, index)
        place = lax.bitwise_xor(owner, index)
        rows = pl.ds(pl.multiple_of(slot * 2 * SEG, 2 * SEG), 2 * SEG)
        for lane in range(CS // LANES):
            packed[place, rank, :, pl.ds(lane * LANES, LANES)] = mixed[lane, rows, :].astype(BF16)
        firsts[pl.ds(place * CAP + rank, 1), :] = leading[pl.ds(slot * SEG, 1), :]

    packed[:, CAP] = firsts[...].reshape(N_FSDP, CAP, CS).astype(BF16)
    copies = [
        pltpu.make_async_copy(packed.at[place], outs[place], out_sem.at[place])
        for place in range(N_FSDP)
    ]
    for copy in copies:
        copy.start()
    for copy in copies:
        copy.wait()


def stem_payloads(scalars, parts, grad):
    tables, values = split_parts(parts)
    payload = (CAP + 1, 2 * SEG, CS)
    return call(
        lambda *refs: stem_kernel(tables, *refs), "stem_payloads",
        (shape(payload, BF16),) * N_FSDP, (1,),
        [ANY] * len(values) + [whole((ROWS, D))], (HBM,) * N_FSDP,
        [
            pltpu.VMEM((3, CS, D), BF16),
            pltpu.VMEM((CS // LANES, 2 * ROWS, LANES), F32),
            pltpu.VMEM((ROWS, CS), F32),
            pltpu.VMEM((N_FSDP,) + payload, BF16),
            pltpu.VMEM((N_FSDP * CAP, CS), F32),
            pltpu.SemaphoreType.DMA,
            pltpu.SemaphoreType.DMA((N_FSDP,)),
        ],
        vmem=32,
    )(scalars, *values, grad)


def owner_kernel(scalars, *refs):
    payloads, out_ref = refs[:N_FSDP], refs[N_FSDP]
    packed, firsts, sem = refs[N_FSDP + 1 :]
    step = pl.program_id(0)
    index = scalars[1]

    @pl.when(step == 0)
    def _():
        copies = [
            pltpu.make_async_copy(payloads[i], packed.at[place], sem.at[place])
            for i, place in enumerate(PAYLOAD_ORDER)
        ]
        for copy in copies:
            copy.start()
        for copy in copies:
            copy.wait()
        firsts[...] = packed[:, CAP].astype(F32).reshape(N_FSDP * CAP, CS)

    start = jnp.int32(0)
    for owner in range(N_FSDP):
        start = start + jnp.where(owner < index, scalars[2 + owner], 0)
    count = scalars[2 + index]

    def place_of(segment):
        item = start + segment
        holder = item // 2 % N_FSDP
        slot = 2 * (item // (2 * N_FSDP)) + item % 2
        return lax.bitwise_xor(holder, index), slot - held_before(start, holder)

    per_step = OWN_SEG // 4
    last_row = lax.broadcasted_iota(jnp.int32, (2 * SEG, CS), 0) == 2 * SEG - 1

    def one(local, carry):
        segment = step * per_step + local
        rows = pl.ds(pl.multiple_of(local * 2 * SEG, 2 * SEG), 2 * SEG)

        @pl.when(segment < count)
        def _():
            place, rank = place_of(segment)
            follows = segment + 1 < count
            next_place, next_rank = place_of(jnp.where(follows, segment + 1, segment))
            first = firsts[pl.ds(next_place * CAP + next_rank, 1), :]
            extra = jnp.where(last_row & follows, jnp.broadcast_to(first, (2 * SEG, CS)), 0.0)
            out_ref[rows, :] = (packed[place, rank].astype(F32) + extra).astype(BF16)

        @pl.when(segment >= count)
        def _():
            out_ref[rows, :] = jnp.zeros((2 * SEG, CS), BF16)

        return carry

    lax.fori_loop(0, per_step, one, 0)


def owner_rows(scalars, payloads):
    payload = (CAP + 1, 2 * SEG, CS)
    rows = 2 * OWN_SEG * SEG
    return call(
        owner_kernel, "owner_rows", shape((rows, CS), BF16), (4,), [ANY] * N_FSDP,
        row_block(rows // 4, CS),
        [
            pltpu.VMEM((N_FSDP,) + payload, BF16),
            pltpu.VMEM((N_FSDP * CAP, CS), F32),
            pltpu.SemaphoreType.DMA((N_FSDP,)),
        ],
    )(scalars, *payloads)


def body(held_input, held_cotangent, proj_weight, stem_weight, seg_counts):
    site, index = lax.axis_index("site"), lax.axis_index("fsdp")
    scalars = jnp.concatenate([jnp.stack([site, index]).astype(jnp.int32), seg_counts[0]])
    inputs, cotangent = held_input[0], held_cotangent[0]

    piece = (D // N_FSDP, QUARTER)
    half = (3, HALF, QUARTER)
    units = (UNITS, STEM_ROWS, QUARTER)
    quarters = (len(QUARTER_TAPS), STEM_ROWS, QUARTER)

    normed_own = norm_half(scalars, inputs)
    normed_theirs = norm_half(scalars, swap_core(inputs))
    kept_a, sent_a, kept_b, sent_b = outer_pieces(
        scalars, normed_own, normed_theirs, cotangent, swap_core(cotangent)
    )
    (proj_quarter,) = join(cut_proj_kernel, "cut_proj", [piece], [proj_weight], [normed_own])
    far = swap_z(proj_quarter, 2)
    (pair,) = join(pair_kernel, "pair", [(2, *piece)], [proj_quarter, far], [sent_a])

    near = swap_z(pair, 1)
    came_a, came_b = swap_site(sent_a, 1), swap_site(sent_b, 2)
    a0, b0 = join(halves_kernel, "halves", [half, half], [pair, near])

    a1, b1 = swap_site(a0, 1), swap_site(b0, 2)
    own_a, sent_a, own_b, sent_b = half_sum(scalars, kept_a, came_a, kept_b, came_b)
    (stem_quarter,) = join(cut_stem_kernel, "cut_stem", [units], [stem_weight], [near])
    far = swap_z(stem_quarter, 2)
    kept, sent = site_sum(scalars, own_a, swap_site(sent_a, 2), own_b, swap_site(sent_b, 1))
    a, b, packed, stem_pair = join(
        site_step_kernel, "site_step", [(2, *half)] * 2 + [(D // 2 + TAPS * N_SITE * STEM_ROWS + 12 * HALF, QUARTER), (2, *units)],
        [proj_weight, stem_weight, a0, b0, a1, b1, stem_quarter, far], [kept],
    )

    a2, b2 = swap_site(a, 2), swap_site(b, 1)
    near = swap_z(stem_pair, 1)
    packed = swap_core(packed)
    n = 3 * UNITS * STEM_ROWS
    others, all_others, late = join(
        three_kernel, "three", [(3, *quarters), (3, *units), (12 * HALF + n, QUARTER)],
        [stem_pair, near, a2, b2], [packed],
    )

    over = [swap_site(others, distance) for distance in (1, 2, 3)]
    late = swap_core(late)
    whole_proj = [(0, 0, ("all", 0), 0, D // N_FSDP)]
    first = [half_places(0, 0), half_places(0, HALF), half_places(1, 0), half_places(2, HALF)]
    last = [half_places(2, 0) + half_places(3, 0), half_places(1, HALF) + half_places(3, HALF)]
    proj_parts = [
        (proj_weight, whole_proj, 0),
        (rows_of(a0), first[0], 0), (rows_of(b0), first[1], 0),
        (rows_of(a1), first[2], 0), (rows_of(b1), first[3], 0),
        (rows_of(a2), last[0], 0), (rows_of(b2), last[1], 0),
        (packed, shard_places(0, D // N_FSDP) + [TAPS * N_SITE * STEM_ROWS] + sum(first, []), 1),
        (late, sum(last, []) + [n], 1),
    ]
    grad = input_gradient(scalars, proj_parts, inputs, cotangent)
    own, sent = near_sum(scalars, kept, swap_z(hold(sent, others), 1), [grad])
    (over,) = join(collect_kernel, "collect", [(3, 3, *quarters)], over, [grad, sent])
    over = rows_of(over)
    last = sum((unit_places(d) for d in (1, 2, 3)), [])
    stem_parts = [
        (stem_weight.reshape(-1, D), [(tap, 0, ("all", 0), 0, STEM_ROWS) for tap in range(TAPS)], 0),
        (rows_of(all_others), all_places(), 0),
        (over, last, 0),
        (
            packed,
            [D // 2] + sum((shard_places(tap, STEM_ROWS) for tap in range(TAPS)), []) + [12 * HALF],
            1,
        ),
        (late, [12 * HALF] + all_places(), 1),
        (swap_core(over), last, 1),
    ]

    payloads = stem_payloads(scalars, stem_parts, grad)
    received = {0: payloads[0]}
    for d in PAYLOAD_ORDER[1:]:
        received[d] = lax.ppermute(payloads[d], "fsdp", [(i, i ^ d) for i in range(N_FSDP)])
    scale = 1.0 / math.sqrt(N_SITE * N_FSDP * ROWS)
    first = [received[d] for d in (4, 5, 2, 3)]
    terms = far_sum(scalars, own, swap_z(sent, 2), scale, first)
    weight_grad = lay_columns(scalars, [terms] + [swap_site(terms, d) for d in (1, 2, 3)])
    stem_grad = owner_rows(scalars, [received[d] for d in PAYLOAD_ORDER])
    return (stem_grad[None], weight_grad)


def plain_body(held_input, held_cotangent, proj_weight, stem_weight, seg_counts):
    group_size = lax.axis_size("fsdp")
    capacity = 2 * ((OWN_SEG + 2 * group_size - 1) // (2 * group_size))
    my_index = lax.axis_index("fsdp")
    cotangent = held_cotangent[0]
    normed, inverse = normalise(held_input[0])
    normed_bf = normed.astype(jnp.bfloat16)
    proj_back = dot_nt(cotangent, lax.all_gather(proj_weight, "fsdp", axis=0, tiled=True))
    input_grad = cotangent.astype(jnp.float32) + inverse * (
        proj_back
        - jnp.mean(proj_back, axis=-1, keepdims=True)
        - normed * jnp.mean(proj_back * normed, axis=-1, keepdims=True)
    )
    input_grad = input_grad.astype(jnp.bfloat16)
    counts = seg_counts[0]
    endings = jnp.cumsum(counts)
    starts = endings - counts
    slot_ids = jnp.arange(HOLD, dtype=jnp.int32)
    item_index = 2 * (slot_ids // 2 * group_size + my_index) + slot_ids % 2
    owner_ids = jnp.sum((item_index[:, None] >= endings[None, :]).astype(jnp.int32), axis=1)
    earlier = (slot_ids[None, :] < slot_ids[:, None]) & (owner_ids[None, :] == owner_ids[:, None])
    rank_ids = jnp.sum(earlier.astype(jnp.int32), axis=1)
    target = owner_ids * capacity + rank_ids
    positions = jnp.arange(group_size * capacity, dtype=jnp.int32)
    matched = target[None, :] == positions[:, None]
    filled = jnp.any(matched, axis=1)
    source = jnp.sum(jnp.where(matched, slot_ids[None, :], 0), axis=1)
    owner_hit = jnp.arange(group_size, dtype=jnp.int32) == my_index
    my_count = jnp.sum(jnp.where(owner_hit, counts, 0))
    my_start = jnp.sum(jnp.where(owner_hit, starts, 0))
    segment = jnp.arange(OWN_SEG, dtype=jnp.int32)
    is_live = segment < my_count
    holder = (my_start + segment) // 2 % group_size
    before = (
        (segment[None, :] < segment[:, None])
        & (holder[None, :] == holder[:, None])
        & is_live[None, :]
    )
    holder_rank = jnp.sum(before.astype(jnp.int32), axis=1)
    row_index = jnp.where(is_live, holder * capacity + holder_rank, 0)
    held_segments = input_grad.reshape(HOLD, SEG, D)
    zero_bf = jnp.zeros((), jnp.bfloat16)
    send_rows = jnp.where(filled[:, None, None], jnp.take(held_segments, source, axis=0), zero_bf)
    received = lax.all_to_all(
        send_rows.reshape(group_size, capacity, SEG, D), "fsdp", split_axis=0, concat_axis=0, tiled=True
    )
    picked = jnp.take(received.reshape(group_size * capacity, SEG, D), row_index, axis=0)
    frames = jnp.where(is_live[:, None, None], picked, zero_bf).reshape(OWN_SEG * SEG, D)
    tap_terms = jnp.einsum(
        "rd,kcd->krc",
        frames,
        lax.all_gather(stem_weight, "fsdp", axis=1, tiled=True),
        preferred_element_type=jnp.float32,
    )
    shifted = jnp.concatenate(
        [tap_terms[0][1:], jnp.zeros((1, tap_terms.shape[2]), jnp.float32)], 0
    )
    stem_rows = (
        jnp.stack([tap_terms[1], tap_terms[2] + shifted], 1)
        .reshape(2 * OWN_SEG * SEG, tap_terms.shape[2])
        .astype(jnp.bfloat16)
    )
    shard_sum = lax.psum_scatter(
        lax.dot_general(
            normed_bf, cotangent, (((0,), (0,)), ((), ())), preferred_element_type=jnp.float32
        ),
        "fsdp",
        scatter_dimension=0,
        tiled=True,
    )
    shard_sum = lax.psum(shard_sum, "site")
    weight_grad = shard_sum / math.sqrt(lax.axis_size("site") * group_size * ROWS)
    return (stem_rows[None], weight_grad)


def solution(mesh):
    placed = (
        P("site", "fsdp", None),
        P("site", "fsdp", None),
        P("fsdp", None),
        P(None, "fsdp", None),
        P("site", None),
    )
    fits = (mesh.shape["site"], mesh.shape["fsdp"]) == (N_SITE, N_FSDP)
    return jax.shard_map(
        body if fits else plain_body,
        mesh=mesh,
        in_specs=placed,
        out_specs=(P("site", "fsdp", None), P("fsdp", None)),
        check_vma=False,
    )
```

time: 193 us -> 163 us (0.84)
  starting transfers between devices: 69.6 us -> 31.7 us
  local copies, waits for them, and re-layouts: 2.37 us -> 10 us
  Pallas kernels: 34.2 us -> 39 us
  waiting for transfers between devices: 81.8 us -> 78.9 us
    ppermute x12 -> x5, starting transfers between devices: 27.4 us -> 4.13 us  [swap_core(): return lax.ppermute(value, 'fsdp', [(i, i ^ 1) for i in range(N_FSDP)])]
    ppermute x7, starting transfers between devices: 19.2 us -> 7.27 us  [body(): lax.ppermute(payloads[d], 'fsdp', [(i, i ^ d) for i in range(N_FSDP)])]
    unnamed x10 -> x44, local copies, waits for them, and re-layouts: 1.42 us -> 10 us
    ppermute x7, waiting for transfers between devices: 34.7 us -> 41.6 us  [body(): lax.ppermute(payloads[d], 'fsdp', [(i, i ^ d) for i in range(N_FSDP)])]
    ppermute x9 -> x6, waiting for transfers between devices: 24 us -> 18.5 us  [swap_z(): lax.ppermute(value, 'fsdp', [(i, i ^ 2 * distance) for i in range(N_FSDP)])]
    ppermute x9 -> x6, starting transfers between devices: 13.5 us -> 9.79 us  [swap_z(): lax.ppermute(value, 'fsdp', [(i, i ^ 2 * distance) for i in range(N_FSDP)])]
    pallas_call x7 -> x18, Pallas kernels: 29.4 us -> 32.3 us  [the longest x1 7.83 us: stem_payloads(): call(lambda *refs: stem_kernel(tables, *refs), 'stem_payloads', (shape(pa...]
    ppermute x12 -> x14, waiting for transfers between devices: 21.6 us -> 18.8 us  [swap_site(): lax.ppermute(value, 'site', [(i, i ^ distance) for i in range(N_SITE)])]
  transfers between devices with their start and end apart: 40 -> 32, of which waited for: 16 -> 13; matrix products, arithmetic and copies ran while one was open for 1% -> 0% of each run, Pallas kernels for 17% -> 19%
where the time goes in v2:
time: 163 us; the launch traced here: 161 us
  waiting for transfers between devices  78.9 us (48%)
  Pallas kernels  39 us (24%)
  starting transfers between devices  31.7 us (19%)
  local copies, waits for them, and re-layouts  10 us (6%)
    ppermute x7, waiting for transfers between devices, body(): lax.ppermute(payloads[d], 'fsdp', [(i, i ^ d) for i in range(N_FSDP)])  41.6 us
    ppermute x14, waiting for transfers between devices, swap_site(): lax.ppermute(value, 'site', [(i, i ^ distance) for i in range(N_SITE)])  18.8 us
    ppermute x6, waiting for transfers between devices, swap_z(): lax.ppermute(value, 'fsdp', [(i, i ^ 2 * distance) for i in range(N_FSDP)])  18.5 us
    ppermute x14, starting transfers between devices, swap_site(): lax.ppermute(value, 'site', [(i, i ^ distance) for i in range(N_SITE)])  10.5 us
    unnamed x44, local copies, waits for them, and re-layouts  10 us
    ppermute x6, starting transfers between devices, swap_z(): lax.ppermute(value, 'fsdp', [(i, i ^ 2 * distance) for i in range(N_FSDP)])  9.79 us
    pallas_call x1, Pallas kernels, stem_payloads(): call(lambda *refs: stem_kernel(tables, *refs), 'stem_payloads', (shape(pa...  7.83 us
    pallas_call x1, Pallas kernels, input_gradient(): call(lambda *refs: input_grad_kernel(tables, *refs), 'input_gradient', sh...  7.62 us
  transfers between devices with their start and end apart: 32, of which 13 were waited for; matrix products, arithmetic and copies ran while one was open for 0% of the time, Pallas kernels for 19%

profile of v2, /device:TPU:9, one launch (start us, length us, event | category | flops | bytes accessed | tf_op | source)
XLA Modules:
  0.0 161.4 jit_solution(2997429412194637398)
XLA Ops:
  2.2 1.4 copy-done.2
  3.6 2.7 %norm_half.2.refs_1_.na_ref = bf16[768,512]{1,0:T(8,128)(2,1)S(1)} custom-call(s32[10]{0:T(128)S(1)} %pad_add_fusion.scalars.refs_0_, bf16[512,1536]{1,0:T(8,128)(2,1)S(1)} %bitcast.19), custom_call_target="tpu_custom_call" | custom-call | tf_op jit(solution)/shard_map/norm_half/pallas_call | solution.py:221
  6.3 2.7 %norm_half.3.nb_ref = bf16[768,512]{1,0:T(8,128)(2,1)S(1)} custom-call(s32[10]{0:T(128)S(1)} %pad_add_fusion.scalars.refs_0_, bf16[512,1536]{1,0:T(8,128)(2,1)S(1)} %collective-permute-done.1.x_ref), custom_call_target="tpu_custom_call" | custom-call | tf_op jit(solution)/shard_map/norm_half/pallas_call | solution.py:221
  9.0 5.2 %outer_pieces.1 = (f32[2,384,384]{2,1,0:T(8,128)S(1)}, bf16[2,384,384]{2,1,0:T(8,128)(2,1)S(1)}, f32[2,384,384]{2,1,0:T(8,128)S(1)}, bf16[2,384,384]{2,1,0:T(8,128)(2,1)S(1)}) custom-call(s32[10]{0:T(128)S(1)} %pad_add_fusion.scalars.refs_0_, bf16[768,512]{1,0:T(8,128)(2,1)S(1)} %norm_half.2.refs_1_.na_ref, bf16[768,512]{1,0:T(8,128)(2,1)S(1)} %norm_half.3.nb_ref, ...), custom_call_target="tpu_custom_call" | custom-call | tf_op jit(solution)/shard_map/outer_pieces/pallas_call | solution.py:247
  14.3 1.3 collective-permute-start.8
  15.6 1.2 collective-permute-start.7
  16.8 2.4 %collective-permute-start = (bf16[192,384]{1,0:T(8,128)(2,1)S(1)}, bf16[192,384]{1,0:T(8,128)(2,1)S(1)}, u32[]{:S(2)}, u32[]{:S(2)}) collective-permute-start(bf16[192,384]{1,0:T(8,128)(2,1)S(1)} %cut_proj.1.refs_0_), channel_id=1, source_target_pairs={{0,4},{1,5},{2,6},{3,7},{4,0},{5,1},{6,2},{7,3},{8,12},{9,13},{10,... | collective-permute-start | bytes 442376 | tf_op jit(solution)/shard_map/ppermute | solution.py:37
  19.2 6.6 %collective-permute-done.refs_1_ = bf16[192,384]{1,0:T(8,128)(2,1)S(1)} collective-permute-done((bf16[192,384]{1,0:T(8,128)(2,1)S(1)}, bf16[192,384]{1,0:T(8,128)(2,1)S(1)}, u32[]{:S(2)}, u32[]{:S(2)}) %collective-permute-start) | collective-permute-done | bytes 147488 | tf_op jit(solution)/shard_map/ppermute | solution.py:37
  25.9 2.9 %collective-permute-done.8.rb_ref = bf16[2,384,384]{2,1,0:T(8,128)(2,1)S(1)} collective-permute-done((bf16[2,384,384]{2,1,0:T(8,128)(2,1)S(1)}, bf16[2,384,384]{2,1,0:T(8,128)(2,1)S(1)}, u32[]{:S(2)}, u32[]{:S(2)}) %collective-permute-start.8) | collective-permute-done | bytes 589856 | tf_op jit(solution)/shard_map/ppermute | solution.py:41
  28.8 0.9 collective-permute-done.7.ra_ref
  30.8 1.2 collective-permute-start.10
  32.1 1.9 %collective-permute-done.3.refs_1_ = bf16[2,192,384]{2,1,0:T(8,128)(2,1)S(1)} collective-permute-done((bf16[2,192,384]{2,1,0:T(8,128)(2,1)S(1)}, bf16[2,192,384]{2,1,0:T(8,128)(2,1)S(1)}, u32[]{:S(2)}, u32[]{:S(2)}) %collective-permute-start.3) | collective-permute-done | bytes 294944 | tf_op jit(solution)/shard_map/ppermute | solution.py:37
  34.0 3.2 %collective-permute-start.6 = (bf16[6,64,384]{2,1,0:T(8,128)(2,1)S(1)}, bf16[6,64,384]{2,1,0:T(8,128)(2,1)S(1)}, u32[]{:S(2)}, u32[]{:S(2)}) collective-permute-start(bf16[6,64,384]{2,1,0:T(8,128)(2,1)S(1)} %cut_stem.1.refs_6_), channel_id=1, source_target_pairs={{0,4},{1,5},{2,6},{3,7},{4,0},{5,1},{6,2},{7,3},{8,12},{9,13},{10,... | collective-permute-start | bytes 884744 | tf_op jit(solution)/shard_map/ppermute | solution.py:37
  38.5 4.0 %collective-permute-done.4.refs_4_ = bf16[3,96,384]{2,1,0:T(8,128)(2,1)S(1)} collective-permute-done((bf16[3,96,384]{2,1,0:T(8,128)(2,1)S(1)}, bf16[3,96,384]{2,1,0:T(8,128)(2,1)S(1)}, u32[]{:S(2)}, u32[]{:S(2)}) %collective-permute-start.4) | collective-permute-done | bytes 221216 | tf_op jit(solution)/shard_map/ppermute | solution.py:41
  42.6 7.6 %collective-permute-done.6.refs_7_ = bf16[6,64,384]{2,1,0:T(8,128)(2,1)S(1)} collective-permute-done((bf16[6,64,384]{2,1,0:T(8,128)(2,1)S(1)}, bf16[6,64,384]{2,1,0:T(8,128)(2,1)S(1)}, u32[]{:S(2)}, u32[]{:S(2)}) %collective-permute-start.6) | collective-permute-done | bytes 294944 | tf_op jit(solution)/shard_map/ppermute | solution.py:37
  51.1 1.1 collective-permute-start.11
  52.7 10.9 %collective-permute-done.12.refs_2_ = bf16[2,3,96,384]{3,2,1,0:T(8,128)(2,1)S(1)} collective-permute-done((bf16[2,3,96,384]{3,2,1,0:T(8,128)(2,1)S(1)}, bf16[2,3,96,384]{3,2,1,0:T(8,128)(2,1)S(1)}, u32[]{:S(2)}, u32[]{:S(2)}) %collective-permute-start.12) | collective-permute-done | bytes 442400 | tf_op jit(solution)/shard_map/ppermute | solution.py:41
  63.6 2.4 %collective-permute-done.11.refs_1_ = bf16[2,6,64,384]{3,2,1,0:T(8,128)(2,1)S(1)} collective-permute-done((bf16[2,6,64,384]{3,2,1,0:T(8,128)(2,1)S(1)}, bf16[2,6,64,384]{3,2,1,0:T(8,128)(2,1)S(1)}, u32[]{:S(2)}, u32[]{:S(2)}) %collective-permute-start.11) | collective-permute-done | bytes 589856 | tf_op jit(solution)/shard_map/ppermute | solution.py:37
  66.0 1.5 three.1
  67.5 0.9 copy-done.12
  68.4 0.8 collective-permute-start.18
  69.3 1.1 collective-permute-start.19
  70.5 1.2 collective-permute-start.16
  71.8 1.2 collective-permute-start.15
  73.0 1.4 copy-done.1
  74.4 1.4 copy-done.3
  75.8 1.0 copy-done.9
  76.8 1.0 copy-done.11
  77.8 0.9 copy-done.15
  78.8 0.9 copy-done.17
  79.7 0.9 copy-done.19
  80.7 7.6 %input_gradient.1.refs_0_.refs_3_.refs_7_ = bf16[512,1536]{1,0:T(8,128)(2,1)S(1)} custom-call(s32[10]{0:T(128)S(1)} %pad_add_fusion.scalars.refs_0_, bf16[192,1536]{1,0:T(8,128)(2,1)S(1)} %copy-done.5, bf16[288,384]{1,0:T(8,128)(2,1)S(1)} %bitcast.27, bf16[288,384]{1,0:T(8,128)(2,1)S(1)} %bitcast.28, bf16[288,384]{1,0:T(8,128)(2,1)S(1)} %bitcast.29, ...), custom_call_target="tpu_custom_call" | custom-call | tf_op jit(solution)/shard_map/input_gradient/pallas_call | solution.py:386
  89.0 1.9 %collective-permute-start.20 = (bf16[1152,384]{1,0:T(8,128)(2,1)S(1)}, bf16[1152,384]{1,0:T(8,128)(2,1)S(1)}, u32[]{:S(2)}, u32[]{:S(2)}) collective-permute-start(bf16[1152,384]{1,0:T(8,128)(2,1)S(1)} %bitcast.22), channel_id=1, source_target_pairs={{0,1},{1,0},{2,3},{3,2},{4,5},{5,4},{6,7},{7,6},{8,9},{9,8},{10,11... | collective-permute-start | bytes 2654216 | tf_op jit(solution)/shard_map/ppermute | solution.py:33
  90.9 2.0 %collective-permute-start.28 = (bf16[192,384]{1,0:T(8,128)(2,1)S(1)}, bf16[192,384]{1,0:T(8,128)(2,1)S(1)}, u32[]{:S(2)}, u32[]{:S(2)}) collective-permute-start(bf16[192,384]{1,0:T(8,128)(2,1)S(1)} %get-tuple-element.50.refs_4_), channel_id=1, source_target_pairs={{0,4},{1,5},{2,6},{3,7},{4,0},{5,1},{6,2},{7,3},{8,12},{9,13},{10,... | collective-permute-start | bytes 442376 | tf_op jit(solution)/shard_map/ppermute | solution.py:37
  92.9 7.8 %stem_payloads.1 = (bf16[17,16,512]{2,1,0:T(8,128)(2,1)S(1)}, bf16[17,16,512]{2,1,0:T(8,128)(2,1)S(1)}, bf16[17,16,512]{2,1,0:T(8,128)(2,1)S(1)}, bf16[17,16,512...) custom-call(s32[10]{0:T(128)S(1)} %pad_add_fusion.scalars.refs_0_, ...), custom_call_target="tpu_custom_call" | custom-call | tf_op jit(solution)/shard_map/stem_payloads/pallas_call | solution.py:466
  100.8 2.1 %collective-permute-start.21 = (bf16[17,16,512]{2,1,0:T(8,128)(2,1)S(1)}, bf16[17,16,512]{2,1,0:T(8,128)(2,1)S(1)}, u32[]{:S(2)}, u32[]{:S(2)}) collective-permute-start(bf16[17,16,512]{2,1,0:T(8,128)(2,1)S(1)} %get-tuple-element.52), channel_id=1, source_target_pairs={{0,4},{1,5},{2,6},{3,7},{4,0},{5,1},{6,2},{7,3},{8,12},{9,13},{10,... | collective-permute-start | bytes 835592 | tf_op jit(solution)/shard_map/ppermute | solution.py:627
  102.9 0.9 collective-permute-start.22
  103.8 1.5 collective-permute-start.25
  105.3 2.3 %collective-permute-start.23 = (bf16[17,16,512]{2,1,0:T(8,128)(2,1)S(1)}, bf16[17,16,512]{2,1,0:T(8,128)(2,1)S(1)}, u32[]{:S(2)}, u32[]{:S(2)}) collective-permute-start(bf16[17,16,512]{2,1,0:T(8,128)(2,1)S(1)} %get-tuple-element.54), channel_id=1, source_target_pairs={{0,6},{1,7},{2,4},{3,5},{4,2},{5,3},{6,0},{7,1},{8,14},{9,15},{10,... | collective-permute-start | bytes 835592 | tf_op jit(solution)/shard_map/ppermute | solution.py:627
  107.6 12.9 %collective-permute-done.21.refs_1_.refs_3_ = bf16[17,16,512]{2,1,0:T(8,128)(2,1)S(1)} collective-permute-done((bf16[17,16,512]{2,1,0:T(8,128)(2,1)S(1)}, bf16[17,16,512]{2,1,0:T(8,128)(2,1)S(1)}, u32[]{:S(2)}, u32[]{:S(2)}) %collective-permute-start.21) | collective-permute-done | bytes 278560 | tf_op jit(solution)/shard_map/ppermute | solution.py:627
  120.5 6.0 %collective-permute-done.22.refs_2_.refs_4_ = bf16[17,16,512]{2,1,0:T(8,128)(2,1)S(1)} collective-permute-done((bf16[17,16,512]{2,1,0:T(8,128)(2,1)S(1)}, bf16[17,16,512]{2,1,0:T(8,128)(2,1)S(1)}, u32[]{:S(2)}, u32[]{:S(2)}) %collective-permute-start.22) | collective-permute-done | bytes 278560 | tf_op jit(solution)/shard_map/ppermute | solution.py:627
  126.5 8.7 %collective-permute-done.26.refs_6_ = bf16[17,16,512]{2,1,0:T(8,128)(2,1)S(1)} collective-permute-done((bf16[17,16,512]{2,1,0:T(8,128)(2,1)S(1)}, bf16[17,16,512]{2,1,0:T(8,128)(2,1)S(1)}, u32[]{:S(2)}, u32[]{:S(2)}) %collective-permute-start.26) | collective-permute-done | bytes 278560 | tf_op jit(solution)/shard_map/ppermute | solution.py:627
  136.1 1.2 collective-permute-start.30
  137.3 1.2 collective-permute-start.29
  138.5 1.7 %collective-permute-done.23.refs_3_ = bf16[17,16,512]{2,1,0:T(8,128)(2,1)S(1)} collective-permute-done((bf16[17,16,512]{2,1,0:T(8,128)(2,1)S(1)}, bf16[17,16,512]{2,1,0:T(8,128)(2,1)S(1)}, u32[]{:S(2)}, u32[]{:S(2)}) %collective-permute-start.23) | collective-permute-done | bytes 278560 | tf_op jit(solution)/shard_map/ppermute | solution.py:627
  140.7 12.2 %collective-permute-done.24.refs_4_ = bf16[17,16,512]{2,1,0:T(8,128)(2,1)S(1)} collective-permute-done((bf16[17,16,512]{2,1,0:T(8,128)(2,1)S(1)}, bf16[17,16,512]{2,1,0:T(8,128)(2,1)S(1)}, u32[]{:S(2)}, u32[]{:S(2)}) %collective-permute-start.24) | collective-permute-done | bytes 278560 | tf_op jit(solution)/shard_map/ppermute | solution.py:627
  153.0 6.7 %owner_rows.1 = bf16[2048,512]{1,0:T(8,128)(2,1)} custom-call(s32[10]{0:T(128)S(1)} %pad_add_fusion.scalars.refs_0_, bf16[17,16,512]{2,1,0:T(8,128)(2,1)S(1)} %get-tuple-element.51.refs_0_, bf16[17,16,512]{2,1,0:T(8,128)(2,1)S(1)} %collective-permute-done.21.refs_1_.refs_3_, bf16[17,16,512]{2,1,0:T(8,128)(2,1)S(1)} %collective-permute-done.22.refs_2_.refs_4_, ...), custom_call_target="tpu_custom_call" | custom-call | tf_op jit(solution)/shard_map/owner_rows/pallas_call | solution.py:540
  159.7 1.6 %lay_columns.1 = f32[192,1536]{1,0:T(8,128)} custom-call(s32[10]{0:T(128)S(1)} %pad_add_fusion.scalars.refs_0_, f32[192,384]{1,0:T(8,128)S(1)} %far_sum.1.a_ref, f32[192,384]{1,0:T(8,128)S(1)} %collective-permute-done.29.b_ref, f32[192,384]{1,0:T(8,128)S(1)} %collective-permute-done.30.c_ref, f32[192,384]{1,0:T(8,128)S(1)} %collective-permute-done.31.d_ref), custom_call_target="tpu_custom_call" | custom-call | tf_op jit(solution)/shard_map/lay_columns/pallas_call | solution.py:319
  (80 shorter events, 7.9 us)
Async XLA Ops:
  0.6 5.7 %collective-permute-start.1 = (bf16[512,1536]{1,0:T(8,128)(2,1)}, bf16[512,1536]{1,0:T(8,128)(2,1)S(1)}, u32[]{:S(2)}, u32[]{:S(2)}) collective-permute-start(bf16[512,1536]{1,0:T(8,128)(2,1)} %bitcast.18), channel_id=1, source_target_pairs={{0,1},{1,0},{2,3},{3,2},{4,5},{5,4},{6,7},{7,6},{8,9},{9,8},{10,11... | collective-permute-start | bytes 4718600 | tf_op jit(solution)/shard_map/ppermute | solution.py:33
  1.4 7.6 %collective-permute-start.2 = (bf16[512,1536]{1,0:T(8,128)(2,1)}, bf16[512,1536]{1,0:T(8,128)(2,1)S(1)}, u32[]{:S(2)}, u32[]{:S(2)}) collective-permute-start(bf16[512,1536]{1,0:T(8,128)(2,1)} %bitcast.15), channel_id=1, source_target_pairs={{0,1},{1,0},{2,3},{3,2},{4,5},{5,4},{6,7},{7,6},{8,9},{9,8},{10,11... | collective-permute-start | bytes 4718600 | tf_op jit(solution)/shard_map/ppermute | solution.py:33
  2.2 1.4 copy-start.2
  6.3 2.7 %copy-start = (bf16[1,512,1536]{2,1,0:T(8,128)(2,1)S(1)}, bf16[1,512,1536]{2,1,0:T(8,128)(2,1)}, u32[]{:S(2)}) copy-start(bf16[1,512,1536]{2,1,0:T(8,128)(2,1)} %param.6) | copy-start | bytes 4718596
  9.0 7.8 %copy-start.5 = (bf16[192,1536]{1,0:T(8,128)(2,1)S(1)}, bf16[192,1536]{1,0:T(8,128)(2,1)}, u32[]{:S(2)}) copy-start(bf16[192,1536]{1,0:T(8,128)(2,1)} %refs_1_.3) | copy-start | bytes 1769476
  14.3 14.5 %collective-permute-start.8 = (bf16[2,384,384]{2,1,0:T(8,128)(2,1)S(1)}, bf16[2,384,384]{2,1,0:T(8,128)(2,1)S(1)}, u32[]{:S(2)}, u32[]{:S(2)}) collective-permute-start(bf16[2,384,384]{2,1,0:T(8,128)(2,1)S(1)} %get-tuple-element.36), channel_id=1, source_target_pairs={{0,16},{8,24},{16,0},{24,8},{1,17},{9,25},{17,1},{25,9},{2,18},{10... | collective-permute-start | bytes 1769480 | tf_op jit(solution)/shard_map/ppermute | solution.py:41
  15.6 14.2 %collective-permute-start.7 = (bf16[2,384,384]{2,1,0:T(8,128)(2,1)S(1)}, bf16[2,384,384]{2,1,0:T(8,128)(2,1)S(1)}, u32[]{:S(2)}, u32[]{:S(2)}) collective-permute-start(bf16[2,384,384]{2,1,0:T(8,128)(2,1)S(1)} %get-tuple-element.31.refs_2_), channel_id=1, source_target_pairs={{0,8},{8,0},{16,24},{24,16},{1,9},{9,1},{17,25},{25,17},{2,10},{10... | collective-permute-start | bytes 1769480 | tf_op jit(solution)/shard_map/ppermute | solution.py:41
  16.8 9.0 %collective-permute-start = (bf16[192,384]{1,0:T(8,128)(2,1)S(1)}, bf16[192,384]{1,0:T(8,128)(2,1)S(1)}, u32[]{:S(2)}, u32[]{:S(2)}) collective-permute-start(bf16[192,384]{1,0:T(8,128)(2,1)S(1)} %cut_proj.1.refs_0_), channel_id=1, source_target_pairs={{0,4},{1,5},{2,6},{3,7},{4,0},{5,1},{6,2},{7,3},{8,12},{9,13},{10,... | collective-permute-start | bytes 442376 | tf_op jit(solution)/shard_map/ppermute | solution.py:37
  25.8 8.2 %collective-permute-start.3 = (bf16[2,192,384]{2,1,0:T(8,128)(2,1)S(1)}, bf16[2,192,384]{2,1,0:T(8,128)(2,1)S(1)}, u32[]{:S(2)}, u32[]{:S(2)}) collective-permute-start(bf16[2,192,384]{2,1,0:T(8,128)(2,1)S(1)} %pair.1.refs_0_), channel_id=1, source_target_pairs={{0,2},{1,3},{2,0},{3,1},{4,6},{5,7},{6,4},{7,5},{8,10},{9,11},{10,... | collective-permute-start | bytes 884744 | tf_op jit(solution)/shard_map/ppermute | solution.py:37
  29.7 4.3 %copy-start.4 = (bf16[3,64,1536]{2,1,0:T(8,128)(2,1)S(1)}, bf16[3,64,1536]{2,1,0:T(8,128)(2,1)}, u32[]{:S(2)}) copy-start(bf16[3,64,1536]{2,1,0:T(8,128)(2,1)} %refs_1_.2) | copy-start | bytes 1769476
  30.5 7.3 %collective-permute-start.9 = (bf16[384,384]{1,0:T(8,128)(2,1)S(1)}, bf16[384,384]{1,0:T(8,128)(2,1)S(1)}, u32[]{:S(2)}, u32[]{:S(2)}) collective-permute-start(bf16[384,384]{1,0:T(8,128)(2,1)S(1)} %get-tuple-element.38), channel_id=1, source_target_pairs={{0,16},{8,24},{16,0},{24,8},{1,17},{9,25},{17,1},{25,9},{2,18},{10... | collective-permute-start | bytes 884744 | tf_op jit(solution)/shard_map/ppermute | solution.py:41
  30.8 6.9 %collective-permute-start.10 = (bf16[384,384]{1,0:T(8,128)(2,1)S(1)}, bf16[384,384]{1,0:T(8,128)(2,1)S(1)}, u32[]{:S(2)}, u32[]{:S(2)}) collective-permute-start(bf16[384,384]{1,0:T(8,128)(2,1)S(1)} %get-tuple-element.40), channel_id=1, source_target_pairs={{0,8},{8,0},{16,24},{24,16},{1,9},{9,1},{17,25},{25,17},{2,10},{10... | collective-permute-start | bytes 884744 | tf_op jit(solution)/shard_map/ppermute | solution.py:41
  34.0 16.2 %collective-permute-start.6 = (bf16[6,64,384]{2,1,0:T(8,128)(2,1)S(1)}, bf16[6,64,384]{2,1,0:T(8,128)(2,1)S(1)}, u32[]{:S(2)}, u32[]{:S(2)}) collective-permute-start(bf16[6,64,384]{2,1,0:T(8,128)(2,1)S(1)} %cut_stem.1.refs_6_), channel_id=1, source_target_pairs={{0,4},{1,5},{2,6},{3,7},{4,0},{5,1},{6,2},{7,3},{8,12},{9,13},{10,... | collective-permute-start | bytes 884744 | tf_op jit(solution)/shard_map/ppermute | solution.py:37
  37.2 13.3 %copy-start.14 = (bf16[3,96,384]{2,1,0:T(8,128)(2,1)}, bf16[3,96,384]{2,1,0:T(8,128)(2,1)S(1)}, u32[]{:S(2)}) copy-start(bf16[3,96,384]{2,1,0:T(8,128)(2,1)S(1)} %get-tuple-element.33.refs_3_) | copy-start | bytes 663556
  37.2 5.4 %collective-permute-start.4 = (bf16[3,96,384]{2,1,0:T(8,128)(2,1)S(1)}, bf16[3,96,384]{2,1,0:T(8,128)(2,1)S(1)}, u32[]{:S(2)}, u32[]{:S(2)}) collective-permute-start(bf16[3,96,384]{2,1,0:T(8,128)(2,1)S(1)} %get-tuple-element.32.refs_2_), channel_id=1, source_target_pairs={{0,8},{8,0},{16,24},{24,16},{1,9},{9,1},{17,25},{25,17},{2,10},{10... | collective-permute-start | bytes 663560 | tf_op jit(solution)/shard_map/ppermute | solution.py:41
  37.5 5.1 %collective-permute-start.5 = (bf16[3,96,384]{2,1,0:T(8,128)(2,1)S(1)}, bf16[3,96,384]{2,1,0:T(8,128)(2,1)S(1)}, u32[]{:S(2)}, u32[]{:S(2)}) collective-permute-start(bf16[3,96,384]{2,1,0:T(8,128)(2,1)S(1)} %get-tuple-element.33.refs_3_), channel_id=1, source_target_pairs={{0,16},{8,24},{16,0},{24,8},{1,17},{9,25},{17,1},{25,9},{2,18},{10... | collective-permute-start | bytes 663560 | tf_op jit(solution)/shard_map/ppermute | solution.py:41
  38.5 12.0 %copy-start.6 = (f32[2,192,384]{2,1,0:T(8,128)}, f32[2,192,384]{2,1,0:T(8,128)S(1)}, u32[]{:S(2)}) copy-start(f32[2,192,384]{2,1,0:T(8,128)S(1)} %get-tuple-element.41.refs_8_.kept_ref) | copy-start | bytes 1769476
  38.5 29.9 %copy-start.20 = (bf16[2,192,384]{2,1,0:T(8,128)(2,1)}, bf16[2,192,384]{2,1,0:T(8,128)(2,1)S(1)}, u32[]{:S(2)}) copy-start(bf16[2,192,384]{2,1,0:T(8,128)(2,1)S(1)} %get-tuple-element.49.refs_0_) | copy-start | bytes 884740
  42.6 7.9 %copy-start.16 = (bf16[3,96,384]{2,1,0:T(8,128)(2,1)}, bf16[3,96,384]{2,1,0:T(8,128)(2,1)S(1)}, u32[]{:S(2)}) copy-start(bf16[3,96,384]{2,1,0:T(8,128)(2,1)S(1)} %collective-permute-done.4.refs_4_) | copy-start | bytes 663556
  42.6 7.9 %copy-start.18 = (bf16[3,96,384]{2,1,0:T(8,128)(2,1)}, bf16[3,96,384]{2,1,0:T(8,128)(2,1)S(1)}, u32[]{:S(2)}) copy-start(bf16[3,96,384]{2,1,0:T(8,128)(2,1)S(1)} %collective-permute-done.5.refs_5_) | copy-start | bytes 663556
  50.5 15.5 %collective-permute-start.14 = (bf16[2688,384]{1,0:T(8,128)(2,1)S(1)}, bf16[2688,384]{1,0:T(8,128)(2,1)S(1)}, u32[]{:S(2)}, u32[]{:S(2)}) collective-permute-start(bf16[2688,384]{1,0:T(8,128)(2,1)S(1)} %get-tuple-element.45), channel_id=1, source_target_pairs={{0,1},{1,0},{2,3},{3,2},{4,5},{5,4},{6,7},{7,6},{8,9},{9,8},{10,11... | collective-permute-start | bytes 6193160 | tf_op jit(solution)/shard_map/ppermute | solution.py:33
  51.1 14.9 %collective-permute-start.11 = (bf16[2,6,64,384]{3,2,1,0:T(8,128)(2,1)S(1)}, bf16[2,6,64,384]{3,2,1,0:T(8,128)(2,1)S(1)}, u32[]{:S(2)}, u32[]{:S(2)}) collective-permute-start(bf16[2,6,64,384]{3,2,1,0:T(8,128)(2,1)S(1)} %get-tuple-element.42.refs_0_), channel_id=1, source_target_pairs={{0,2},{1,3},{2,0},{3,1},{4,6},{5,7},{6,4},{7,5},{8,10},{9,11},{10,... | collective-permute-start | bytes 1769480 | tf_op jit(solution)/shard_map/ppermute | solution.py:37
  52.2 11.4 %collective-permute-start.12 = (bf16[2,3,96,384]{3,2,1,0:T(8,128)(2,1)S(1)}, bf16[2,3,96,384]{3,2,1,0:T(8,128)(2,1)S(1)}, u32[]{:S(2)}, u32[]{:S(2)}) collective-permute-start(bf16[2,3,96,384]{3,2,1,0:T(8,128)(2,1)S(1)} %get-tuple-element.43), channel_id=1, source_target_pairs={{0,16},{8,24},{16,0},{24,8},{1,17},{9,25},{17,1},{25,9},{2,18},{10... | collective-permute-start | bytes 1327112 | tf_op jit(solution)/shard_map/ppermute | solution.py:41
  52.4 11.2 %collective-permute-start.13 = (bf16[2,3,96,384]{3,2,1,0:T(8,128)(2,1)S(1)}, bf16[2,3,96,384]{3,2,1,0:T(8,128)(2,1)S(1)}, u32[]{:S(2)}, u32[]{:S(2)}) collective-permute-start(bf16[2,3,96,384]{3,2,1,0:T(8,128)(2,1)S(1)} %get-tuple-element.44), channel_id=1, source_target_pairs={{0,8},{8,0},{16,24},{24,16},{1,9},{9,1},{17,25},{25,17},{2,10},{10... | collective-permute-start | bytes 1327112 | tf_op jit(solution)/shard_map/ppermute | solution.py:41
  63.6 3.9 %copy-start.8 = (bf16[2,3,96,384]{3,2,1,0:T(8,128)(2,1)}, bf16[2,3,96,384]{3,2,1,0:T(8,128)(2,1)S(1)}, u32[]{:S(2)}) copy-start(bf16[2,3,96,384]{3,2,1,0:T(8,128)(2,1)S(1)} %collective-permute-done.12.refs_2_) | copy-start | bytes 1327108
  63.6 3.9 %copy-start.10 = (bf16[2,3,96,384]{3,2,1,0:T(8,128)(2,1)}, bf16[2,3,96,384]{3,2,1,0:T(8,128)(2,1)S(1)}, u32[]{:S(2)}) copy-start(bf16[2,3,96,384]{3,2,1,0:T(8,128)(2,1)S(1)} %collective-permute-done.13.refs_3_) | copy-start | bytes 1327108
  68.4 4.6 %collective-permute-start.18 = (bf16[2304,384]{1,0:T(8,128)(2,1)}, bf16[2304,384]{1,0:T(8,128)(2,1)}, u32[]{:S(2)}, u32[]{:S(2)}) collective-permute-start(bf16[2304,384]{1,0:T(8,128)(2,1)} %get-tuple-element.48), channel_id=1, source_target_pairs={{0,1},{1,0},{2,3},{3,2},{4,5},{5,4},{6,7},{7,6},{8,9},{9,8},{10,11... | collective-permute-start | bytes 5308424 | tf_op jit(solution)/shard_map/ppermute | solution.py:33
  69.3 19.0 %collective-permute-start.19 = (bf16[2,192,384]{2,1,0:T(8,128)(2,1)}, bf16[2,192,384]{2,1,0:T(8,128)(2,1)S(1)}, u32[]{:S(2)}, u32[]{:S(2)}) collective-permute-start(bf16[2,192,384]{2,1,0:T(8,128)(2,1)} %hold.1), channel_id=1, source_target_pairs={{0,2},{1,3},{2,0},{3,1},{4,6},{5,7},{6,4},{7,5},{8,10},{9,11},{10,... | collective-permute-start | bytes 884744 | tf_op jit(solution)/shard_map/ppermute | solution.py:37
  70.3 18.6 %collective-permute-start.17 = (bf16[3,2,64,384]{3,2,1,0:T(8,128)(2,1)}, bf16[3,2,64,384]{3,2,1,0:T(8,128)(2,1)S(1)}, u32[]{:S(2)}, u32[]{:S(2)}) collective-permute-start(bf16[3,2,64,384]{3,2,1,0:T(8,128)(2,1)} %copy-done.21), channel_id=1, source_target_pairs={{0,24},{8,16},{16,8},{24,0},{1,25},{9,17},{17,9},{25,1},{2,26},{10... | collective-permute-start | bytes 884744 | tf_op jit(solution)/shard_map/ppermute | solution.py:41
  70.5 18.4 %collective-permute-start.16 = (bf16[3,2,64,384]{3,2,1,0:T(8,128)(2,1)}, bf16[3,2,64,384]{3,2,1,0:T(8,128)(2,1)S(1)}, u32[]{:S(2)}, u32[]{:S(2)}) collective-permute-start(bf16[3,2,64,384]{3,2,1,0:T(8,128)(2,1)} %copy-done.21), channel_id=1, source_target_pairs={{0,16},{8,24},{16,0},{24,8},{1,17},{9,25},{17,1},{25,9},{2,18},{10... | collective-permute-start | bytes 884744 | tf_op jit(solution)/shard_map/ppermute | solution.py:41
  71.8 17.1 %collective-permute-start.15 = (bf16[3,2,64,384]{3,2,1,0:T(8,128)(2,1)}, bf16[3,2,64,384]{3,2,1,0:T(8,128)(2,1)S(1)}, u32[]{:S(2)}, u32[]{:S(2)}) collective-permute-start(bf16[3,2,64,384]{3,2,1,0:T(8,128)(2,1)} %copy-done.21), channel_id=1, source_target_pairs={{0,8},{8,0},{16,24},{24,16},{1,9},{9,1},{17,25},{25,17},{2,10},{10... | collective-permute-start | bytes 884744 | tf_op jit(solution)/shard_map/ppermute | solution.py:41
  73.0 1.4 copy-start.1
  74.4 1.4 copy-start.3
  75.8 1.0 copy-start.9
  80.6 7.6 %copy-start.7 = (f32[2,192,384]{2,1,0:T(8,128)S(1)}, f32[2,192,384]{2,1,0:T(8,128)}, u32[]{:S(2)}) copy-start(f32[2,192,384]{2,1,0:T(8,128)} %copy-done.6) | copy-start | bytes 1769476
  88.9 4.0 %copy-start.13 = (bf16[3,6,64,384]{3,2,1,0:T(8,128)(2,1)S(1)}, bf16[3,6,64,384]{3,2,1,0:T(8,128)(2,1)}, u32[]{:S(2)}) copy-start(bf16[3,6,64,384]{3,2,1,0:T(8,128)(2,1)} %copy-done.12) | copy-start | bytes 2654212
  89.0 3.9 %collective-permute-start.20 = (bf16[1152,384]{1,0:T(8,128)(2,1)S(1)}, bf16[1152,384]{1,0:T(8,128)(2,1)S(1)}, u32[]{:S(2)}, u32[]{:S(2)}) collective-permute-start(bf16[1152,384]{1,0:T(8,128)(2,1)S(1)} %bitcast.22), channel_id=1, source_target_pairs={{0,1},{1,0},{2,3},{3,2},{4,5},{5,4},{6,7},{7,6},{8,9},{9,8},{10,11... | collective-permute-start | bytes 2654216 | tf_op jit(solution)/shard_map/ppermute | solution.py:33
  90.9 14.4 %collective-permute-start.28 = (bf16[192,384]{1,0:T(8,128)(2,1)S(1)}, bf16[192,384]{1,0:T(8,128)(2,1)S(1)}, u32[]{:S(2)}, u32[]{:S(2)}) collective-permute-start(bf16[192,384]{1,0:T(8,128)(2,1)S(1)} %get-tuple-element.50.refs_4_), channel_id=1, source_target_pairs={{0,4},{1,5},{2,6},{3,7},{4,0},{5,1},{6,2},{7,3},{8,12},{9,13},{10,... | collective-permute-start | bytes 442376 | tf_op jit(solution)/shard_map/ppermute | solution.py:37
  100.8 19.8 %collective-permute-start.21 = (bf16[17,16,512]{2,1,0:T(8,128)(2,1)S(1)}, bf16[17,16,512]{2,1,0:T(8,128)(2,1)S(1)}, u32[]{:S(2)}, u32[]{:S(2)}) collective-permute-start(bf16[17,16,512]{2,1,0:T(8,128)(2,1)S(1)} %get-tuple-element.52), channel_id=1, source_target_pairs={{0,4},{1,5},{2,6},{3,7},{4,0},{5,1},{6,2},{7,3},{8,12},{9,13},{10,... | collective-permute-start | bytes 835592 | tf_op jit(solution)/shard_map/ppermute | solution.py:627
  102.9 23.6 %collective-permute-start.22 = (bf16[17,16,512]{2,1,0:T(8,128)(2,1)S(1)}, bf16[17,16,512]{2,1,0:T(8,128)(2,1)S(1)}, u32[]{:S(2)}, u32[]{:S(2)}) collective-permute-start(bf16[17,16,512]{2,1,0:T(8,128)(2,1)S(1)} %get-tuple-element.53), channel_id=1, source_target_pairs={{0,5},{1,4},{2,7},{3,6},{4,1},{5,0},{6,3},{7,2},{8,13},{9,12},{10,... | collective-permute-start | bytes 835592 | tf_op jit(solution)/shard_map/ppermute | solution.py:627
  103.8 22.8 %collective-permute-start.25 = (bf16[17,16,512]{2,1,0:T(8,128)(2,1)S(1)}, bf16[17,16,512]{2,1,0:T(8,128)(2,1)S(1)}, u32[]{:S(2)}, u32[]{:S(2)}) collective-permute-start(bf16[17,16,512]{2,1,0:T(8,128)(2,1)S(1)} %get-tuple-element.56), channel_id=1, source_target_pairs={{0,2},{1,3},{2,0},{3,1},{4,6},{5,7},{6,4},{7,5},{8,10},{9,11},{10,... | collective-permute-start | bytes 835592 | tf_op jit(solution)/shard_map/ppermute | solution.py:627
  105.2 30.0 %collective-permute-start.26 = (bf16[17,16,512]{2,1,0:T(8,128)(2,1)S(1)}, bf16[17,16,512]{2,1,0:T(8,128)(2,1)S(1)}, u32[]{:S(2)}, u32[]{:S(2)}) collective-permute-start(bf16[17,16,512]{2,1,0:T(8,128)(2,1)S(1)} %get-tuple-element.57), channel_id=1, source_target_pairs={{0,3},{1,2},{2,1},{3,0},{4,7},{5,6},{6,5},{7,4},{8,11},{9,10},{10,... | collective-permute-start | bytes 835592 | tf_op jit(solution)/shard_map/ppermute | solution.py:627
  105.3 35.0 %collective-permute-start.23 = (bf16[17,16,512]{2,1,0:T(8,128)(2,1)S(1)}, bf16[17,16,512]{2,1,0:T(8,128)(2,1)S(1)}, u32[]{:S(2)}, u32[]{:S(2)}) collective-permute-start(bf16[17,16,512]{2,1,0:T(8,128)(2,1)S(1)} %get-tuple-element.54), channel_id=1, source_target_pairs={{0,6},{1,7},{2,4},{3,5},{4,2},{5,3},{6,0},{7,1},{8,14},{9,15},{10,... | collective-permute-start | bytes 835592 | tf_op jit(solution)/shard_map/ppermute | solution.py:627
  135.8 23.9 %collective-permute-start.31 = (f32[192,384]{1,0:T(8,128)S(1)}, f32[192,384]{1,0:T(8,128)S(1)}, u32[]{:S(2)}, u32[]{:S(2)}) collective-permute-start(f32[192,384]{1,0:T(8,128)S(1)} %far_sum.1.a_ref), channel_id=1, source_target_pairs={{0,24},{8,16},{16,8},{24,0},{1,25},{9,17},{17,9},{25,1},{2,26},{10... | collective-permute-start | bytes 884744 | tf_op jit(solution)/shard_map/ppermute | solution.py:41
  136.1 23.6 %collective-permute-start.30 = (f32[192,384]{1,0:T(8,128)S(1)}, f32[192,384]{1,0:T(8,128)S(1)}, u32[]{:S(2)}, u32[]{:S(2)}) collective-permute-start(f32[192,384]{1,0:T(8,128)S(1)} %far_sum.1.a_ref), channel_id=1, source_target_pairs={{0,16},{8,24},{16,0},{24,8},{1,17},{9,25},{17,1},{25,9},{2,18},{10... | collective-permute-start | bytes 884744 | tf_op jit(solution)/shard_map/ppermute | solution.py:41
  137.3 22.4 %collective-permute-start.29 = (f32[192,384]{1,0:T(8,128)S(1)}, f32[192,384]{1,0:T(8,128)S(1)}, u32[]{:S(2)}, u32[]{:S(2)}) collective-permute-start(f32[192,384]{1,0:T(8,128)S(1)} %far_sum.1.a_ref), channel_id=1, source_target_pairs={{0,8},{8,0},{16,24},{24,16},{1,9},{9,1},{17,25},{25,17},{2,10},{10... | collective-permute-start | bytes 884744 | tf_op jit(solution)/shard_map/ppermute | solution.py:41
  138.5 14.4 %collective-permute-start.24 = (bf16[17,16,512]{2,1,0:T(8,128)(2,1)S(1)}, bf16[17,16,512]{2,1,0:T(8,128)(2,1)S(1)}, u32[]{:S(2)}, u32[]{:S(2)}) collective-permute-start(bf16[17,16,512]{2,1,0:T(8,128)(2,1)S(1)} %get-tuple-element.55), channel_id=1, source_target_pairs={{0,7},{1,6},{2,5},{3,4},{4,3},{5,2},{6,1},{7,0},{8,15},{9,14},{10,... | collective-permute-start | bytes 835592 | tf_op jit(solution)/shard_map/ppermute | solution.py:627
  140.2 12.7 %collective-permute-start.27 = (bf16[17,16,512]{2,1,0:T(8,128)(2,1)S(1)}, bf16[17,16,512]{2,1,0:T(8,128)(2,1)S(1)}, u32[]{:S(2)}, u32[]{:S(2)}) collective-permute-start(bf16[17,16,512]{2,1,0:T(8,128)(2,1)S(1)} %get-tuple-element.58), channel_id=1, source_target_pairs={{0,1},{1,0},{2,3},{3,2},{4,5},{5,4},{6,7},{7,6},{8,9},{9,8},{10,11... | collective-permute-start | bytes 835592 | tf_op jit(solution)/shard_map/ppermute | solution.py:627
  (6 other events, 5.6 us)

commit v3 on v2

--- a/solution.py
+++ b/solution.py
@@ -20,8 +20,8 @@
 ROWS = HOLD * SEG
 BLOCK = 128
 LANES = 128
-COLUMNS = 256
-PAYLOAD_ORDER = (0, 4, 5, 6, 7, 2, 3, 1)
+COLUMNS = 768
+PAYLOAD_ORDER = (0, 4, 5, 2, 3, 6, 7, 1)
 MIB = 1024 * 1024
 
 EPSILON = 1e-05
@@ -57,9 +57,9 @@
 HALF = D // N_FSDP // 2
 STEM_ROWS = CS // N_FSDP
 TAPS = 3
-QUARTER_TAPS = (0, 2)
-WHOLE_TAP = 1
-UNITS = len(QUARTER_TAPS) + N_SITE
+QUARTER_TAPS = (1,)
+WHOLE_TAPS = (0, 2)
+UNITS = len(QUARTER_TAPS) + len(WHOLE_TAPS) * N_SITE
 
 
 def half_places(site, low):
@@ -71,7 +71,7 @@
 
 
 def all_places():
-    whole_tap = [(WHOLE_TAP, ("abs", j)) for j in range(N_SITE)]
+    whole_tap = [(tap, ("abs", j)) for tap in WHOLE_TAPS for j in range(N_SITE)]
     columns = [(tap, ("xor", 0)) for tap in QUARTER_TAPS] + whole_tap
     return [(tap, z, kind, 0, STEM_ROWS) for z in Z_ORDER for tap, kind in columns]
 
@@ -123,13 +123,13 @@
     return lax.dot_general(a, b, (((1,), (1,)), ((), ())), preferred_element_type=F32)
 
 
-def join(kernel, name, out_dims, values, first=(), scratch=()):
+def join(kernel, name, out_dims, values, first=(), wide_dims=()):
     n = len(values)
 
     def wrapped(*refs):
         kernel(*refs[:n], *refs[n + len(first) :])
 
-    out = tuple(shape(dims, BF16) for dims in out_dims)
+    out = tuple(shape(dims, BF16) for dims in out_dims) + tuple(shape(dims, F32) for dims in wide_dims)
     vmem = pl.BlockSpec(memory_space=pltpu.VMEM)
     return pl.pallas_call(
         wrapped,
@@ -137,7 +137,7 @@
         out_shape=out,
         in_specs=[vmem] * n + [ANY] * len(first),
         out_specs=(vmem,) * len(out),
-        compiler_params=pltpu.CompilerParams(vmem_limit_bytes=8 * MIB),
+        compiler_params=pltpu.CompilerParams(vmem_limit_bytes=16 * MIB),
         cost_estimate=pl.CostEstimate(flops=0, bytes_accessed=0, transcendentals=0),
     )(*values, *first)
 
@@ -147,23 +147,23 @@
     out[...] = shard[:, pl.ds(at, QUARTER)]
 
 
-def cut_stem_kernel(shard, out):
-    at = pl.multiple_of(lax.axis_index("site") * QUARTER, QUARTER)
-    for i, tap in enumerate(QUARTER_TAPS):
-        out[i] = shard[tap, :, pl.ds(at, QUARTER)]
-    for i in range(N_SITE):
-        out[len(QUARTER_TAPS) + i] = shard[WHOLE_TAP, :, i * QUARTER : (i + 1) * QUARTER]
-
-
 def pair_kernel(a, b, out):
     out[0] = a[...]
     out[1] = b[...]
 
 
-def halves_kernel(pair, near, a, b):
+def halves_kernel(pair, near, sent_a, sent_b, stem, a, b, out_a, out_b, units):
+    out_a[...], out_b[...] = sent_a[...], sent_b[...]
     for i, piece in enumerate((pair.at[1], near.at[0], near.at[1])):
         a[i] = piece[:HALF, :]
         b[i] = piece[HALF:, :]
+    at = pl.multiple_of(lax.axis_index("site") * QUARTER, QUARTER)
+    for i, tap in enumerate(QUARTER_TAPS):
+        units[i] = stem[tap, :, pl.ds(at, QUARTER)]
+    for i, tap in enumerate(WHOLE_TAPS):
+        for j in range(N_SITE):
+            columns = slice(j * QUARTER, (j + 1) * QUARTER)
+            units[len(QUARTER_TAPS) + N_SITE * i + j] = stem[tap, :, columns]
 
 
 def pack_rows(out, pieces):
@@ -173,25 +173,22 @@
         at += piece.shape[0]
 
 
-def column_pieces(shard):
-    return [shard[:, i * QUARTER : (i + 1) * QUARTER] for i in range(N_SITE)]
-
-
-def site_step_kernel(shard, stem, a0, b0, a1, b1, quarter, far, a, b, packed, pair):
-    pair[0], pair[1] = quarter[...], far[...]
+def site_step_kernel(
+    a0, b0, a1, b1, units, far, kept_a, came_a, kept_b, came_b, a, b, pair, sent_a, sent_b, own_a, own_b
+):
+    pair[0], pair[1] = units[...], far[...]
     a[0], a[1], b[0], b[1] = a0[...], a1[...], b0[...], b1[...]
-    pieces = column_pieces(shard[...])
-    for tap in range(stem.shape[0]):
-        pieces += column_pieces(stem[tap])
-    pack_rows(packed, pieces + [ref[i] for ref in (a0, b0, a1, b1) for i in range(3)])
+    for kept, came, own, sent in ((kept_a, came_a, own_a, sent_a), (kept_b, came_b, own_b, sent_b)):
+        own[...] = kept[0] + came[0].astype(F32)
+        sent[...] = (kept[1] + came[1].astype(F32)).astype(BF16)
 
 
 def collect_kernel(a, b, c, out):
     out[0], out[1], out[2] = a[...], b[...], c[...]
 
 
-def three_kernel(pair, near, a2, b2, quarters, units, packed):
-    pieces = [ref[j, i] for ref in (a2, b2) for j in range(2) for i in range(3)]
+def three_kernel(pair, near, a, b, a2, b2, quarters, units, packed):
+    pieces = [ref[j, i] for ref in (a, b, a2, b2) for j in range(2) for i in range(3)]
     for i, piece in enumerate((pair[1], near[0], near[1])):
         quarters[i] = piece[: len(QUARTER_TAPS)]
         units[i] = piece
@@ -207,7 +204,8 @@
     return centered * inverse, inverse
 
 
-def norm_kernel(scalars, x_ref, out_ref, turned):
+def norm_kernel(scalars, x_ref, *refs):
+    out_ref, turned = refs[-2:]
     core = scalars[1] % 2
     normed, _ = normalise(x_ref[...])
     turned[...] = normed.astype(BF16).T
@@ -217,18 +215,18 @@
         out_ref[pl.ds(z * shard, shard), :] = turned[rows, :]
 
 
-def norm_half(scalars, inputs):
+def norm_half(scalars, inputs, first=()):
     return call(
         norm_kernel, "norm_half", shape((D // 2, ROWS), BF16), (ROWS // BLOCK,),
-        [row_block(BLOCK, D)], pl.BlockSpec((D // 2, BLOCK), lambda i, scalars: (0, i)),
-        [pltpu.VMEM((D, BLOCK), BF16)],
-    )(scalars, inputs)
+        [row_block(BLOCK, D)] + [ANY] * len(first),
+        pl.BlockSpec((D // 2, BLOCK), lambda i, scalars: (0, i)), [pltpu.VMEM((D, BLOCK), BF16)],
+    )(scalars, inputs, *first)
 
 
 OUTER_PLACES = (((0, 0), (0, 0)), ((1, 0), (0, 1)), ((0, 1), (1, 0)), ((1, 1), (1, 1)))
 
 
-def outer_kernel(scalars, na_ref, nb_ref, ca_ref, cb_ref, ka_ref, sa_ref, kb_ref, sb_ref):
+def outer_kernel(scalars, na_ref, nb_ref, ca_ref, cb_ref, _, ka_ref, sa_ref, kb_ref, sb_ref):
     step = pl.program_id(0)
     total = jnp.dot(na_ref[...], ca_ref[...], preferred_element_type=F32)
     total = total + jnp.dot(nb_ref[...], cb_ref[...], preferred_element_type=F32)
@@ -241,27 +239,13 @@
                 ref[i] = value.astype(ref.dtype)
 
 
-def outer_pieces(scalars, normed_a, normed_b, cotangent_a, cotangent_b):
+def outer_pieces(scalars, normed_a, normed_b, cotangent_a, cotangent_b, first):
     dims = (2, D // 4, QUARTER)
     column = pl.BlockSpec((ROWS, QUARTER), lambda i, scalars: (0, lax.bitwise_xor(scalars[0], i)))
     return call(
         outer_kernel, "outer_pieces", (shape(dims, F32), shape(dims, BF16)) * 2, (N_SITE,),
-        [whole((D // 2, ROWS))] * 2 + [column] * 2, (whole(dims),) * 4, [],
-    )(scalars, normed_a, normed_b, cotangent_a, cotangent_b)
-
-
-def half_sum_kernel(scalars, ka_ref, ra_ref, kb_ref, rb_ref, oa_ref, sa_ref, ob_ref, sb_ref):
-    for kept, came, own, sent in ((ka_ref, ra_ref, oa_ref, sa_ref), (kb_ref, rb_ref, ob_ref, sb_ref)):
-        own[...] = kept[0] + came[0].astype(F32)
-        sent[...] = (kept[1] + came[1].astype(F32)).astype(BF16)
-
-
-def half_sum(scalars, *values):
-    dims, out = (2, D // 4, QUARTER), (D // 4, QUARTER)
-    return call(
-        half_sum_kernel, "half_sum", (shape(out, F32), shape(out, BF16)) * 2, (1,),
-        [whole(dims)] * 4, (whole(out),) * 4, [],
-    )(scalars, *values)
+        [whole((D // 2, ROWS))] * 2 + [column] * 2 + [ANY], (whole(dims),) * 4, [],
+    )(scalars, normed_a, normed_b, cotangent_a, cotangent_b, first)
 
 
 def site_sum_kernel(scalars, oa_ref, ra_ref, ob_ref, rb_ref, kept_ref, sent_ref, total):
@@ -348,18 +332,29 @@
     return copies
 
 
+def fetch(source, target, sem):
+    copy = pltpu.make_async_copy(source, target, sem)
+    copy.start()
+    return copy
+
+
 def input_grad_kernel(tables, scalars, *refs):
     n = len(tables)
-    parts, (x_ref, cot_ref, out_ref, weight, normed, inverse, back, sem) = refs[:n], refs[n:]
+    parts, (x_hbm, cot_hbm, out_ref) = refs[:n], refs[n : n + 3]
+    x_ref, cot_ref, weight, normed, inverse, back, sems, sem = refs[n + 3 :]
+    x_copy = fetch(x_hbm, x_ref, sems.at[0])
+    cot_copy = fetch(cot_hbm, cot_ref, sems.at[1])
     copies = weight_copies(tables, scalars, parts, weight, sem)
     for copy in copies:
         copy.start()
+    x_copy.wait()
 
     @pl.loop(0, ROWS // BLOCK)
     def _(i):
         rows = pl.ds(pl.multiple_of(i * BLOCK, BLOCK), BLOCK)
         normed[rows, :], inverse[rows, :] = normalise(x_ref[rows, :])
 
+    cot_copy.wait()
     for copy in copies:
         copy.wait()
 
@@ -385,27 +380,67 @@
     tables, values = split_parts(parts)
     return call(
         lambda *refs: input_grad_kernel(tables, *refs), "input_gradient", shape((ROWS, D), BF16),
-        (1,), [ANY] * len(values) + [whole((ROWS, D))] * 2, whole((ROWS, D)),
+        (1,), [HBM] * (len(values) + 2), whole((ROWS, D)),
         [
+            pltpu.VMEM((ROWS, D), BF16),
+            pltpu.VMEM((ROWS, D), BF16),
             pltpu.VMEM((1, D, D), BF16),
             pltpu.VMEM((ROWS, D), F32),
             pltpu.VMEM((ROWS, 1), F32),
             pltpu.VMEM((ROWS, D), F32),
+            pltpu.SemaphoreType.DMA((2,)),
             pltpu.SemaphoreType.DMA,
         ],
-        vmem=32,
+        vmem=22,
     )(scalars, *values, inputs, cotangent)
 
 
-def starts_of(scalars):
+def held_before(start, holder):
+    return 2 * (start // (2 * N_FSDP)) + jnp.clip(start % (2 * N_FSDP) - 2 * holder, 0, 2)
+
+
+SLOTS_AT = 2
+SEGMENTS_AT = SLOTS_AT + HOLD
+COUNT_AT = SEGMENTS_AT + OWN_SEG
+
+
+def plan_kernel(scalars, plan):
+    site, index = scalars[0], scalars[1]
+    plan[0], plan[1] = site, index
     starts = [jnp.int32(0)]
     for owner in range(N_FSDP):
         starts.append(starts[-1] + scalars[2 + owner])
-    return starts
-
-
-def held_before(start, holder):
-    return 2 * (start // (2 * N_FSDP)) + jnp.clip(start % (2 * N_FSDP) - 2 * holder, 0, 2)
+
+    @pl.loop(0, HOLD)
+    def _(slot):
+        item = 2 * (slot // 2 * N_FSDP + index) + slot % 2
+        owner = jnp.int32(0)
+        start = jnp.int32(0)
+        for other in range(1, N_FSDP):
+            passed = item >= starts[other]
+            owner = jnp.where(passed, other, owner)
+            start = jnp.where(passed, starts[other], start)
+        plan[SLOTS_AT + slot] = lax.bitwise_xor(owner, index) * CAP + slot - held_before(start, index)
+
+    start = jnp.int32(0)
+    for owner in range(N_FSDP):
+        start = start + jnp.where(owner < index, scalars[2 + owner], 0)
+    count = scalars[2 + index]
+    plan[COUNT_AT] = count
+
+    @pl.loop(0, OWN_SEG)
+    def _(segment):
+        item = start + jnp.minimum(segment, count - 1)
+        holder = item // 2 % N_FSDP
+        rank = 2 * (item // (2 * N_FSDP)) + item % 2 - held_before(start, holder)
+        plan[SEGMENTS_AT + segment] = lax.bitwise_xor(holder, index) * CAP + rank
+
+
+def plan_of(scalars):
+    return call(
+        plan_kernel, "plan", shape((COUNT_AT + 1,), jnp.int32), (1,), [],
+        pl.BlockSpec(memory_space=pltpu.SMEM), [],
+    )(scalars)
 
 
 def stem_kernel(tables, scalars, *refs):
@@ -418,36 +453,28 @@
     for copy in copies:
         copy.wait()
     index = scalars[1]
-    for lane in range(0, CS, COLUMNS):
-        span = pl.ds(lane, COLUMNS)
+    for lane in range(0, CS, CS // 2):
+        span = pl.ds(lane, CS // 2)
         even = dot_nt(grad_ref[...], weight[1, span, :])
         first = dot_nt(grad_ref[...], weight[0, span, :])
         leading[:, span] = first
         row = lax.broadcasted_iota(jnp.int32, first.shape, 0)
         following = jnp.where(row % SEG == SEG - 1, 0.0, pltpu.roll(first, ROWS - 1, 0))
         odd = dot_nt(grad_ref[...], weight[2, span, :]) + following
-        for part in range(COLUMNS // LANES):
+        for part in range(CS // 2 // LANES):
             at = lane // LANES + part
             columns = slice(part * LANES, (part + 1) * LANES)
             mixed[at, pl.ds(0, ROWS, stride=2), :] = even[:, columns]
             mixed[at, pl.ds(1, ROWS, stride=2), :] = odd[:, columns]
-    starts = starts_of(scalars)
-
-    @pl.loop(0, HOLD, unroll=4)
+
+    @pl.loop(0, HOLD, unroll=8)
     def _(slot):
-        item = 2 * (slot // 2 * N_FSDP + index) + slot % 2
-        owner = jnp.int32(0)
-        start = jnp.int32(0)
-        for other in range(1, N_FSDP):
-            passed = item >= starts[other]
-            owner = jnp.where(passed, other, owner)
-            start = jnp.where(passed, starts[other], start)
-        rank = slot - held_before(start, index)
-        place = lax.bitwise_xor(owner, index)
+        block = scalars[SLOTS_AT + slot]
+        place, rank = block // CAP, block % CAP
         rows = pl.ds(pl.multiple_of(slot * 2 * SEG, 2 * SEG), 2 * SEG)
         for lane in range(CS // LANES):
             packed[place, rank, :, pl.ds(lane * LANES, LANES)] = mixed[lane, rows, :].astype(BF16)
-        firsts[pl.ds(place * CAP + rank, 1), :] = leading[pl.ds(slot * SEG, 1), :]
+        firsts[pl.ds(block, 1), :] = leading[pl.ds(slot * SEG, 1), :]
 
     packed[:, CAP] = firsts[...].reshape(N_FSDP, CAP, CS).astype(BF16)
     copies = [
@@ -476,15 +503,13 @@
             pltpu.SemaphoreType.DMA,
             pltpu.SemaphoreType.DMA((N_FSDP,)),
         ],
-        vmem=32,
+        vmem=18,
     )(scalars, *values, grad)
 
 
 def owner_kernel(scalars, *refs):
-    payloads, out_ref = refs[:N_FSDP], refs[N_FSDP]
-    packed, firsts, sem = refs[N_FSDP + 1 :]
+    payloads, (out_ref, packed, firsts, sem) = refs[:N_FSDP], refs[N_FSDP:]
     step = pl.program_id(0)
-    index = scalars[1]
 
     @pl.when(step == 0)
     def _():
@@ -498,40 +523,20 @@
             copy.wait()
         firsts[...] = packed[:, CAP].astype(F32).reshape(N_FSDP * CAP, CS)
 
-    start = jnp.int32(0)
-    for owner in range(N_FSDP):
-        start = start + jnp.where(owner < index, scalars[2 + owner], 0)
-    count = scalars[2 + index]
-
-    def place_of(segment):
-        item = start + segment
-        holder = item // 2 % N_FSDP
-        slot = 2 * (item // (2 * N_FSDP)) + item % 2
-        return lax.bitwise_xor(holder, index), slot - held_before(start, holder)
-
+    count = scalars[COUNT_AT]
     per_step = OWN_SEG // 4
     last_row = lax.broadcasted_iota(jnp.int32, (2 * SEG, CS), 0) == 2 * SEG - 1
 
-    def one(local, carry):
+    @pl.loop(0, per_step, unroll=4)
+    def _(local):
         segment = step * per_step + local
-        rows = pl.ds(pl.multiple_of(local * 2 * SEG, 2 * SEG), 2 * SEG)
-
-        @pl.when(segment < count)
-        def _():
-            place, rank = place_of(segment)
-            follows = segment + 1 < count
-            next_place, next_rank = place_of(jnp.where(follows, segment + 1, segment))
-            first = firsts[pl.ds(next_place * CAP + next_rank, 1), :]
-            extra = jnp.where(last_row & follows, jnp.broadcast_to(first, (2 * SEG, CS)), 0.0)
-            out_ref[rows, :] = (packed[place, rank].astype(F32) + extra).astype(BF16)
-
-        @pl.when(segment >= count)
-        def _():
-            out_ref[rows, :] = jnp.zeros((2 * SEG, CS), BF16)
-
-        return carry
-
-    lax.fori_loop(0, per_step, one, 0)
+        block = scalars[SEGMENTS_AT + segment]
+        follower = scalars[SEGMENTS_AT + jnp.minimum(segment + 1, OWN_SEG - 1)]
+        first = jnp.broadcast_to(firsts[pl.ds(follower, 1), :], (2 * SEG, CS))
+        first = jnp.where(last_row & (segment + 1 < count), first, 0.0)
+        rows = packed[block // CAP, block % CAP].astype(F32) + first
+        to = pl.ds(pl.multiple_of(local * 2 * SEG, 2 * SEG), 2 * SEG)
+        out_ref[to, :] = jnp.where(segment < count, rows, 0.0).astype(BF16)
 
 
 def owner_rows(scalars, payloads):
@@ -553,83 +558,83 @@
     scalars = jnp.concatenate([jnp.stack([site, index]).astype(jnp.int32), seg_counts[0]])
     inputs, cotangent = held_input[0], held_cotangent[0]
 
+    plan = plan_of(scalars)
     piece = (D // N_FSDP, QUARTER)
     half = (3, HALF, QUARTER)
     units = (UNITS, STEM_ROWS, QUARTER)
     quarters = (len(QUARTER_TAPS), STEM_ROWS, QUARTER)
 
-    normed_own = norm_half(scalars, inputs)
-    normed_theirs = norm_half(scalars, swap_core(inputs))
+    (proj_quarter,) = join(cut_proj_kernel, "cut_proj", [piece], [proj_weight])
+    far = swap_z(proj_quarter, 2)
+    normed_own = norm_half(scalars, inputs, [proj_quarter])
+    normed_theirs = norm_half(scalars, swap_core(inputs), [normed_own])
+    cotangent_theirs = swap_core(cotangent)
+    proj_swapped, stem_swapped = swap_core(proj_weight), swap_core(stem_weight)
+    (pair,) = join(
+        pair_kernel, "pair", [(2, *piece)], [proj_quarter, far],
+        [normed_theirs, cotangent_theirs, proj_swapped, stem_swapped],
+    )
+
+    near = swap_z(pair, 1)
     kept_a, sent_a, kept_b, sent_b = outer_pieces(
-        scalars, normed_own, normed_theirs, cotangent, swap_core(cotangent)
-    )
-    (proj_quarter,) = join(cut_proj_kernel, "cut_proj", [piece], [proj_weight], [normed_own])
-    far = swap_z(proj_quarter, 2)
-    (pair,) = join(pair_kernel, "pair", [(2, *piece)], [proj_quarter, far], [sent_a])
-
-    near = swap_z(pair, 1)
-    came_a, came_b = swap_site(sent_a, 1), swap_site(sent_b, 2)
-    a0, b0 = join(halves_kernel, "halves", [half, half], [pair, near])
-
-    a1, b1 = swap_site(a0, 1), swap_site(b0, 2)
-    own_a, sent_a, own_b, sent_b = half_sum(scalars, kept_a, came_a, kept_b, came_b)
-    (stem_quarter,) = join(cut_stem_kernel, "cut_stem", [units], [stem_weight], [near])
-    far = swap_z(stem_quarter, 2)
-    kept, sent = site_sum(scalars, own_a, swap_site(sent_a, 2), own_b, swap_site(sent_b, 1))
-    a, b, packed, stem_pair = join(
-        site_step_kernel, "site_step", [(2, *half)] * 2 + [(D // 2 + TAPS * N_SITE * STEM_ROWS + 12 * HALF, QUARTER), (2, *units)],
-        [proj_weight, stem_weight, a0, b0, a1, b1, stem_quarter, far], [kept],
+        scalars, normed_own, normed_theirs, cotangent, cotangent_theirs, pair
+    )
+    terms = (D // 4, QUARTER)
+    a0, b0, sent_a, sent_b, stem_units = join(
+        halves_kernel, "halves", [half, half, (2, *terms), (2, *terms), units],
+        [pair, near, sent_a, sent_b, stem_weight],
+    )
+
+    a, b, stem_pair, sent_a, sent_b, own_a, own_b = join(
+        site_step_kernel, "site_step", [(2, *half), (2, *half), (2, *units), terms, terms],
+        [
+            a0, b0, swap_site(a0, 1), swap_site(b0, 2), stem_units, swap_z(stem_units, 2),
+            kept_a, swap_site(sent_a, 1), kept_b, swap_site(sent_b, 2),
+        ],
+        [plan],
+        wide_dims=[terms, terms],
     )
 
     a2, b2 = swap_site(a, 2), swap_site(b, 1)
     near = swap_z(stem_pair, 1)
+    kept, sent = site_sum(scalars, own_a, swap_site(sent_a, 2), own_b, swap_site(sent_b, 1))
+    n = 3 * UNITS * STEM_ROWS
+    others, all_others, packed = join(
+        three_kernel, "three", [(3, *quarters), (3, *units), (24 * HALF + n, QUARTER)],
+        [stem_pair, near, a, b, a2, b2], [kept],
+    )
+
+    over = [swap_site(others, distance) for distance in (1, 2, 3)]
     packed = swap_core(packed)
-    n = 3 * UNITS * STEM_ROWS
-    others, all_others, late = join(
-        three_kernel, "three", [(3, *quarters), (3, *units), (12 * HALF + n, QUARTER)],
-        [stem_pair, near, a2, b2], [packed],
-    )
-
-    over = [swap_site(others, distance) for distance in (1, 2, 3)]
-    late = swap_core(late)
     whole_proj = [(0, 0, ("all", 0), 0, D // N_FSDP)]
-    first = [half_places(0, 0), half_places(0, HALF), half_places(1, 0), half_places(2, HALF)]
+    first = [half_places(0, 0) + half_places(1, 0), half_places(0, HALF) + half_places(2, HALF)]
     last = [half_places(2, 0) + half_places(3, 0), half_places(1, HALF) + half_places(3, HALF)]
     proj_parts = [
-        (proj_weight, whole_proj, 0),
-        (rows_of(a0), first[0], 0), (rows_of(b0), first[1], 0),
-        (rows_of(a1), first[2], 0), (rows_of(b1), first[3], 0),
+        (proj_weight, whole_proj, 0), (proj_swapped, whole_proj, 1),
+        (rows_of(a), first[0], 0), (rows_of(b), first[1], 0),
         (rows_of(a2), last[0], 0), (rows_of(b2), last[1], 0),
-        (packed, shard_places(0, D // N_FSDP) + [TAPS * N_SITE * STEM_ROWS] + sum(first, []), 1),
-        (late, sum(last, []) + [n], 1),
+        (packed, sum(first + last, []) + [n], 1),
     ]
     grad = input_gradient(scalars, proj_parts, inputs, cotangent)
-    own, sent = near_sum(scalars, kept, swap_z(hold(sent, others), 1), [grad])
+    own, sent = near_sum(scalars, kept, swap_z(sent, 1), [grad])
     (over,) = join(collect_kernel, "collect", [(3, 3, *quarters)], over, [grad, sent])
     over = rows_of(over)
     last = sum((unit_places(d) for d in (1, 2, 3)), [])
+    whole_stem = [(tap, 0, ("all", 0), 0, STEM_ROWS) for tap in range(TAPS)]
     stem_parts = [
-        (stem_weight.reshape(-1, D), [(tap, 0, ("all", 0), 0, STEM_ROWS) for tap in range(TAPS)], 0),
-        (rows_of(all_others), all_places(), 0),
-        (over, last, 0),
-        (
-            packed,
-            [D // 2] + sum((shard_places(tap, STEM_ROWS) for tap in range(TAPS)), []) + [12 * HALF],
-            1,
-        ),
-        (late, [12 * HALF] + all_places(), 1),
-        (swap_core(over), last, 1),
+        (stem_weight.reshape(-1, D), whole_stem, 0), (stem_swapped.reshape(-1, D), whole_stem, 1),
+        (rows_of(all_others), all_places(), 0), (over, last, 0),
+        (packed, [24 * HALF] + all_places(), 1), (swap_core(over), last, 1),
     ]
 
-    payloads = stem_payloads(scalars, stem_parts, grad)
+    payloads = stem_payloads(plan, stem_parts, grad)
     received = {0: payloads[0]}
     for d in PAYLOAD_ORDER[1:]:
         received[d] = lax.ppermute(payloads[d], "fsdp", [(i, i ^ d) for i in range(N_FSDP)])
     scale = 1.0 / math.sqrt(N_SITE * N_FSDP * ROWS)
-    first = [received[d] for d in (4, 5, 2, 3)]
-    terms = far_sum(scalars, own, swap_z(sent, 2), scale, first)
+    terms = far_sum(scalars, own, swap_z(sent, 2), scale, [received[4]])
     weight_grad = lay_columns(scalars, [terms] + [swap_site(terms, d) for d in (1, 2, 3)])
-    stem_grad = owner_rows(scalars, [received[d] for d in PAYLOAD_ORDER])
+    stem_grad = owner_rows(plan, [received[d] for d in PAYLOAD_ORDER])
     return (stem_grad[None], weight_grad)
 
 

time: 163 us -> 148 us (0.908)
  waiting for transfers between devices: 78.9 us -> 57.4 us
  starting transfers between devices: 31.7 us -> 44 us
  local copies, waits for them, and re-layouts: 10 us -> 3.56 us
    ppermute x7, waiting for transfers between devices: 41.6 us -> 27 us  [body(): lax.ppermute(payloads[d], 'fsdp', [(i, i ^ d) for i in range(N_FSDP)])]
    ppermute x7, starting transfers between devices: 7.27 us -> 20.6 us  [body(): lax.ppermute(payloads[d], 'fsdp', [(i, i ^ d) for i in range(N_FSDP)])]
    ppermute x6, waiting for transfers between devices: 18.5 us -> 7.1 us  [swap_z(): lax.ppermute(value, 'fsdp', [(i, i ^ 2 * distance) for i in range(N_FSDP)])]
    unnamed x44 -> x12, local copies, waits for them, and re-layouts: 10 us -> 3.56 us
    pallas_call x2 -> x1, Pallas kernels: 0.74 us -> 6.34 us  [plan_of(): call(plan_kernel, 'plan', shape((COUNT_AT + 1,), jnp.int32), (1,), [], pl...]
    ppermute x14, waiting for transfers between devices: 18.8 us -> 21.9 us  [swap_site(): lax.ppermute(value, 'site', [(i, i ^ distance) for i in range(N_SITE)])]
    pallas_call x1, Pallas kernels: 6.73 us -> 4.15 us  [owner_rows(): call(owner_kernel, 'owner_rows', shape((rows, CS), BF16), (4,), [ANY] * N...]
    ppermute x5 -> x6, starting transfers between devices: 4.13 us -> 3.83 us  [swap_core(): return lax.ppermute(value, 'fsdp', [(i, i ^ 1) for i in range(N_FSDP)])]
  transfers between devices with their start and end apart: 32 -> 33, of which waited for: 13 -> 11; matrix products, arithmetic and copies ran while one was open for 0% -> 0% of each run, Pallas kernels for 19% -> 26%
where the time goes in v3:
time: 148 us; the launch traced here: 147 us
  waiting for transfers between devices  57.4 us (39%)
  starting transfers between devices  44 us (30%)
  Pallas kernels  40.6 us (27%)
  local copies, waits for them, and re-layouts  3.56 us (2%)
    ppermute x7, waiting for transfers between devices, body(): lax.ppermute(payloads[d], 'fsdp', [(i, i ^ d) for i in range(N_FSDP)])  27 us
    ppermute x14, waiting for transfers between devices, swap_site(): lax.ppermute(value, 'site', [(i, i ^ distance) for i in range(N_SITE)])  21.9 us
    ppermute x7, starting transfers between devices, body(): lax.ppermute(payloads[d], 'fsdp', [(i, i ^ d) for i in range(N_FSDP)])  20.6 us
    ppermute x14, starting transfers between devices, swap_site(): lax.ppermute(value, 'site', [(i, i ^ distance) for i in range(N_SITE)])  10.4 us
    ppermute x6, starting transfers between devices, swap_z(): lax.ppermute(value, 'fsdp', [(i, i ^ 2 * distance) for i in range(N_FSDP)])  9.23 us
    pallas_call x1, Pallas kernels, input_gradient(): call(lambda *refs: input_grad_kernel(tables, *refs), 'input_gradient', sh...  7.1 us
    ppermute x6, waiting for transfers between devices, swap_z(): lax.ppermute(value, 'fsdp', [(i, i ^ 2 * distance) for i in range(N_FSDP)])  7.1 us
    pallas_call x2, Pallas kernels, norm_half(): call(norm_kernel, 'norm_half', shape((D // 2, ROWS), BF16), (ROWS // BLOC...  6.83 us
  transfers between devices with their start and end apart: 33, of which 11 were waited for; matrix products, arithmetic and copies ran while one was open for 0% of the time, Pallas kernels for 26%

profile of v3, /device:TPU:9, one launch (start us, length us, event | category | flops | bytes accessed | tf_op | source)
XLA Modules:
  0.0 147.2 jit_solution(8204013906116301011)
XLA Ops:
  0.6 0.7 collective-permute-start.2
  1.5 0.4 collective-permute-start
  2.0 1.1 copy-done.4
  3.0 2.4 %collective-permute-start.1 = (bf16[192,384]{1,0:T(8,128)(2,1)S(1)}, bf16[192,384]{1,0:T(8,128)(2,1)S(1)}, u32[]{:S(2)}, u32[]{:S(2)}) collective-permute-start(bf16[192,384]{1,0:T(8,128)(2,1)S(1)} %cut_proj.1.refs_0_), channel_id=1, source_target_pairs={{0,4},{1,5},{2,6},{3,7},{4,0},{5,1},{6,2},{7,3},{8,12},{9,13},{10,... | collective-permute-start | bytes 442376 | tf_op jit(solution)/shard_map/ppermute | solution.py:37
  5.4 0.7 pad_add_fusion.scalars.refs_0_
  6.2 1.4 copy-done
  7.6 2.7 %norm_half.2.refs_0_.na_ref = bf16[768,512]{1,0:T(8,128)(2,1)S(1)} custom-call(s32[10]{0:T(128)S(1)} %pad_add_fusion.scalars.refs_0_, bf16[512,1536]{1,0:T(8,128)(2,1)S(1)} %bitcast.15, bf16[192,384]{1,0:T(8,128)(2,1)S(1)} %cut_proj.1.refs_0_), custom_call_target="tpu_custom_call" | custom-call | tf_op jit(solution)/shard_map/norm_half/pallas_call | solution.py:219
  10.2 4.2 %norm_half.3.refs_2_.nb_ref = bf16[768,512]{1,0:T(8,128)(2,1)S(1)} custom-call(s32[10]{0:T(128)S(1)} %pad_add_fusion.scalars.refs_0_, bf16[512,1536]{1,0:T(8,128)(2,1)} %collective-permute-done.2.x_ref, bf16[768,512]{1,0:T(8,128)(2,1)S(1)} %norm_half.2.refs_0_.na_ref), custom_call_target="tpu_custom_call" | custom-call | tf_op jit(solution)/shard_map/norm_half/pallas_call | solution.py:219
  14.8 1.1 copy-done.2
  15.8 5.2 %outer_pieces.1 = (f32[2,384,384]{2,1,0:T(8,128)S(1)}, bf16[2,384,384]{2,1,0:T(8,128)(2,1)S(1)}, f32[2,384,384]{2,1,0:T(8,128)S(1)}, bf16[2,384,384]{2,1,0:T(8,128)(2,1)S(1)}) custom-call(s32[10]{0:T(128)S(1)} %pad_add_fusion.scalars.refs_0_, bf16[768,512]{1,0:T(8,128)(2,1)S(1)} %norm_half.2.refs_0_.na_ref, bf16[768,512]{1,0:T(8,128)(2,1)S(1)} %norm_half.3.refs_2_.nb_ref, ...), custom_call_target="tpu_custom_call" | custom-call | tf_op jit(solution)/shard_map/outer_pieces/pallas_call | solution.py:245
  21.1 1.3 collective-permute-done.5.refs_1_
  22.6 1.3 collective-permute-start.10
  23.9 1.2 collective-permute-start.9
  25.1 0.9 collective-permute-start.8
  26.6 6.3 %plan.1.refs_10_.refs_0_.scalars = s32[195]{0:T(256)S(1)} custom-call(s32[10]{0:T(128)S(1)} %pad_add_fusion.scalars.refs_0_), custom_call_target="tpu_custom_call" | custom-call | tf_op jit(solution)/shard_map/plan/pallas_call | solution.py:440
  32.9 8.7 %collective-permute-done.6.refs_2_ = bf16[3,96,384]{2,1,0:T(8,128)(2,1)S(1)} collective-permute-done((bf16[3,96,384]{2,1,0:T(8,128)(2,1)S(1)}, bf16[3,96,384]{2,1,0:T(8,128)(2,1)S(1)}, u32[]{:S(2)}, u32[]{:S(2)}) %collective-permute-start.6) | collective-permute-done | bytes 221216 | tf_op jit(solution)/shard_map/ppermute | solution.py:41
  41.6 3.8 %collective-permute-done.8.refs_5_ = bf16[9,64,384]{2,1,0:T(8,128)(2,1)S(1)} collective-permute-done((bf16[9,64,384]{2,1,0:T(8,128)(2,1)S(1)}, bf16[9,64,384]{2,1,0:T(8,128)(2,1)S(1)}, u32[]{:S(2)}, u32[]{:S(2)}) %collective-permute-start.8) | collective-permute-done | bytes 442400 | tf_op jit(solution)/shard_map/ppermute | solution.py:37
  45.4 0.3 site_step.1
  45.8 1.3 collective-permute-start.11
  47.6 1.2 collective-permute-start.14
  48.8 1.2 collective-permute-start.15
  50.0 13.2 %collective-permute-done.14.ra_ref = bf16[384,384]{1,0:T(8,128)(2,1)S(1)} collective-permute-done((bf16[384,384]{1,0:T(8,128)(2,1)S(1)}, bf16[384,384]{1,0:T(8,128)(2,1)S(1)}, u32[]{:S(2)}, u32[]{:S(2)}) %collective-permute-start.14) | collective-permute-done | bytes 294944 | tf_op jit(solution)/shard_map/ppermute | solution.py:41
  63.2 0.7 site_sum.1
  64.0 1.9 %collective-permute-done.11.refs_1_ = bf16[2,9,64,384]{3,2,1,0:T(8,128)(2,1)S(1)} collective-permute-done((bf16[2,9,64,384]{3,2,1,0:T(8,128)(2,1)S(1)}, bf16[2,9,64,384]{3,2,1,0:T(8,128)(2,1)S(1)}, u32[]{:S(2)}, u32[]{:S(2)}) %collective-permute-start.11) | collective-permute-done | bytes 884768 | tf_op jit(solution)/shard_map/ppermute | solution.py:37
  65.9 0.4 three.1
  66.3 2.1 %collective-permute-start.19 = (bf16[4032,384]{1,0:T(8,128)(2,1)S(1)}, bf16[4032,384]{1,0:T(8,128)(2,1)S(1)}, u32[]{:S(2)}, u32[]{:S(2)}) collective-permute-start(bf16[4032,384]{1,0:T(8,128)(2,1)S(1)} %get-tuple-element.52), channel_id=1, source_target_pairs={{0,1},{1,0},{2,3},{3,2},{4,5},{5,4},{6,7},{7,6},{8,9},{9,8},{10,11... | collective-permute-start | bytes 9289736 | tf_op jit(solution)/shard_map/ppermute | solution.py:33
  68.4 1.3 collective-permute-start.20
  70.1 2.2 %collective-permute-start.18 = (bf16[3,1,64,384]{3,2,1,0:T(8,128)(2,1)S(1)}, bf16[3,1,64,384]{3,2,1,0:T(8,128)(2,1)S(1)}, u32[]{:S(2)}, u32[]{:S(2)}) collective-permute-start(bf16[3,1,64,384]{3,2,1,0:T(8,128)(2,1)S(1)} %get-tuple-element.51), channel_id=1, source_target_pairs={{0,24},{8,16},{16,8},{24,0},{1,25},{9,17},{17,9},{25,1},{2,26},{10... | collective-permute-start | bytes 442376 | tf_op jit(solution)/shard_map/ppermute | solution.py:41
  72.3 1.3 collective-permute-done.19.refs_7_.refs_5_
  73.6 7.1 %input_gradient.1.refs_0_.refs_3_.refs_7_ = bf16[512,1536]{1,0:T(8,128)(2,1)S(1)} custom-call(s32[10]{0:T(128)S(1)} %pad_add_fusion.scalars.refs_0_, bf16[192,1536]{1,0:T(8,128)(2,1)S(1)} %copy-done.5, bf16[192,1536]{1,0:T(8,128)(2,1)S(1)} %collective-permute-done.4.refs_4_.refs_2_, bf16[576,384]{1,0:T(8,128)(2,1)S(1)} %bitcast.24, ...), custom_call_target="tpu_custom_call" | custom-call | tf_op jit(solution)/shard_map/input_gradient/pallas_call | solution.py:381
  80.7 0.6 near_sum.1
  81.4 0.4 collective-permute-start.21
  81.8 3.1 %collective-permute-start.29 = (bf16[192,384]{1,0:T(8,128)(2,1)S(1)}, bf16[192,384]{1,0:T(8,128)(2,1)S(1)}, u32[]{:S(2)}, u32[]{:S(2)}) collective-permute-start(bf16[192,384]{1,0:T(8,128)(2,1)S(1)} %get-tuple-element.54.refs_4_), channel_id=1, source_target_pairs={{0,4},{1,5},{2,6},{3,7},{4,0},{5,1},{6,2},{7,3},{8,12},{9,13},{10,... | collective-permute-start | bytes 442376 | tf_op jit(solution)/shard_map/ppermute | solution.py:37
  85.0 6.4 %stem_payloads.1 = (bf16[17,16,512]{2,1,0:T(8,128)(2,1)S(1)}, bf16[17,16,512]{2,1,0:T(8,128)(2,1)S(1)}, bf16[17,16,512]{2,1,0:T(8,128)(2,1)S(1)}, bf16[17,16,512...) custom-call(s32[195]{0:T(256)S(1)} %plan.1.refs_10_.refs_0_.scalars,, ...), custom_call_target="tpu_custom_call" | custom-call | tf_op jit(solution)/shard_map/stem_payloads/pallas_call | solution.py:493
  91.4 1.5 %collective-permute-start.22 = (bf16[17,16,512]{2,1,0:T(8,128)(2,1)S(1)}, bf16[17,16,512]{2,1,0:T(8,128)(2,1)S(1)}, u32[]{:S(2)}, u32[]{:S(2)}) collective-permute-start(bf16[17,16,512]{2,1,0:T(8,128)(2,1)S(1)} %get-tuple-element.56), channel_id=1, source_target_pairs={{0,4},{1,5},{2,6},{3,7},{4,0},{5,1},{6,2},{7,3},{8,12},{9,13},{10,... | collective-permute-start | bytes 835592 | tf_op jit(solution)/shard_map/ppermute | solution.py:633
  92.8 1.5 %collective-permute-start.23 = (bf16[17,16,512]{2,1,0:T(8,128)(2,1)S(1)}, bf16[17,16,512]{2,1,0:T(8,128)(2,1)S(1)}, u32[]{:S(2)}, u32[]{:S(2)}) collective-permute-start(bf16[17,16,512]{2,1,0:T(8,128)(2,1)S(1)} %get-tuple-element.57), channel_id=1, source_target_pairs={{0,5},{1,4},{2,7},{3,6},{4,1},{5,0},{6,3},{7,2},{8,13},{9,12},{10,... | collective-permute-start | bytes 835592 | tf_op jit(solution)/shard_map/ppermute | solution.py:633
  94.4 1.4 collective-permute-start.25
  96.1 14.8 %collective-permute-done.22.refs_1_.refs_3_ = bf16[17,16,512]{2,1,0:T(8,128)(2,1)S(1)} collective-permute-done((bf16[17,16,512]{2,1,0:T(8,128)(2,1)S(1)}, bf16[17,16,512]{2,1,0:T(8,128)(2,1)S(1)}, u32[]{:S(2)}, u32[]{:S(2)}) %collective-permute-start.22) | collective-permute-done | bytes 278560 | tf_op jit(solution)/shard_map/ppermute | solution.py:633
  110.9 0.6 far_sum.1.a_ref
  111.5 0.3 collective-permute-start.30
  111.9 5.3 %collective-permute-done.23.refs_2_ = bf16[17,16,512]{2,1,0:T(8,128)(2,1)S(1)} collective-permute-done((bf16[17,16,512]{2,1,0:T(8,128)(2,1)S(1)}, bf16[17,16,512]{2,1,0:T(8,128)(2,1)S(1)}, u32[]{:S(2)}, u32[]{:S(2)}) %collective-permute-start.23) | collective-permute-done | bytes 278560 | tf_op jit(solution)/shard_map/ppermute | solution.py:633
  117.4 1.2 collective-permute-start.32
  118.8 7.8 %collective-permute-start.27 = (bf16[17,16,512]{2,1,0:T(8,128)(2,1)S(1)}, bf16[17,16,512]{2,1,0:T(8,128)(2,1)S(1)}, u32[]{:S(2)}, u32[]{:S(2)}) collective-permute-start(bf16[17,16,512]{2,1,0:T(8,128)(2,1)S(1)} %get-tuple-element.61), channel_id=1, source_target_pairs={{0,7},{1,6},{2,5},{3,4},{4,3},{5,2},{6,1},{7,0},{8,15},{9,14},{10,... | collective-permute-start | bytes 835592 | tf_op jit(solution)/shard_map/ppermute | solution.py:633
  126.6 2.3 %collective-permute-done.26.refs_5_ = bf16[17,16,512]{2,1,0:T(8,128)(2,1)S(1)} collective-permute-done((bf16[17,16,512]{2,1,0:T(8,128)(2,1)S(1)}, bf16[17,16,512]{2,1,0:T(8,128)(2,1)S(1)}, u32[]{:S(2)}, u32[]{:S(2)}) %collective-permute-start.26) | collective-permute-done | bytes 278560 | tf_op jit(solution)/shard_map/ppermute | solution.py:633
  128.8 8.1 %collective-permute-start.28 = (bf16[17,16,512]{2,1,0:T(8,128)(2,1)S(1)}, bf16[17,16,512]{2,1,0:T(8,128)(2,1)S(1)}, u32[]{:S(2)}, u32[]{:S(2)}) collective-permute-start(bf16[17,16,512]{2,1,0:T(8,128)(2,1)S(1)} %get-tuple-element.62), channel_id=1, source_target_pairs={{0,1},{1,0},{2,3},{3,2},{4,5},{5,4},{6,7},{7,6},{8,9},{9,8},{10,11... | collective-permute-start | bytes 835592 | tf_op jit(solution)/shard_map/ppermute | solution.py:633
  137.0 4.4 %collective-permute-done.27.refs_6_ = bf16[17,16,512]{2,1,0:T(8,128)(2,1)S(1)} collective-permute-done((bf16[17,16,512]{2,1,0:T(8,128)(2,1)S(1)}, bf16[17,16,512]{2,1,0:T(8,128)(2,1)S(1)}, u32[]{:S(2)}, u32[]{:S(2)}) %collective-permute-start.27) | collective-permute-done | bytes 278560 | tf_op jit(solution)/shard_map/ppermute | solution.py:633
  141.4 4.2 %owner_rows.1 = bf16[2048,512]{1,0:T(8,128)(2,1)} custom-call(s32[195]{0:T(256)S(1)} %plan.1.refs_10_.refs_0_.scalars, bf16[17,16,512]{2,1,0:T(8,128)(2,1)S(1)} %get-tuple-element.55.refs_0_, bf16[17,16,512]{2,1,0:T(8,128)(2,1)S(1)} %collective-permute-done.22.refs_1_.refs_3_, bf16[17,16,512]{2,1,0:T(8,128)(2,1)S(1)} %collective-permute-done.23.refs_2_, ...), custom_call_target="tpu_custom_call" | custom-call | tf_op jit(solution)/shard_map/owner_rows/pallas_call | solution.py:545
  145.5 1.6 %lay_columns.1 = f32[192,1536]{1,0:T(8,128)} custom-call(s32[10]{0:T(128)S(1)} %pad_add_fusion.scalars.refs_0_, f32[192,384]{1,0:T(8,128)S(1)} %far_sum.1.a_ref, f32[192,384]{1,0:T(8,128)S(1)} %collective-permute-done.30.b_ref, f32[192,384]{1,0:T(8,128)S(1)} %collective-permute-done.31.c_ref, f32[192,384]{1,0:T(8,128)S(1)} %collective-permute-done.32.d_ref), custom_call_target="tpu_custom_call" | custom-call | tf_op jit(solution)/shard_map/lay_columns/pallas_call | solution.py:303
  (48 shorter events, 2.9 us)
Async XLA Ops:
  0.6 9.6 %collective-permute-start.2 = (bf16[512,1536]{1,0:T(8,128)(2,1)}, bf16[512,1536]{1,0:T(8,128)(2,1)}, u32[]{:S(2)}, u32[]{:S(2)}) collective-permute-start(bf16[512,1536]{1,0:T(8,128)(2,1)} %bitcast.14), channel_id=1, source_target_pairs={{0,1},{1,0},{2,3},{3,2},{4,5},{5,4},{6,7},{7,6},{8,9},{9,8},{10,11... | collective-permute-start | bytes 4718600 | tf_op jit(solution)/shard_map/ppermute | solution.py:33
  1.4 13.1 %collective-permute-start.3 = (bf16[512,1536]{1,0:T(8,128)(2,1)}, bf16[512,1536]{1,0:T(8,128)(2,1)S(1)}, u32[]{:S(2)}, u32[]{:S(2)}) collective-permute-start(bf16[512,1536]{1,0:T(8,128)(2,1)} %bitcast.17), channel_id=1, source_target_pairs={{0,1},{1,0},{2,3},{3,2},{4,5},{5,4},{6,7},{7,6},{8,9},{9,8},{10,11... | collective-permute-start | bytes 4718600 | tf_op jit(solution)/shard_map/ppermute | solution.py:33
  1.5 13.0 %collective-permute-start = (bf16[3,64,1536]{2,1,0:T(8,128)(2,1)}, bf16[3,64,1536]{2,1,0:T(8,128)(2,1)S(1)}, u32[]{:S(2)}, u32[]{:S(2)}) collective-permute-start(bf16[3,64,1536]{2,1,0:T(8,128)(2,1)} %refs_4_.1), channel_id=1, source_target_pairs={{0,1},{1,0},{2,3},{3,2},{4,5},{5,4},{6,7},{7,6},{8,9},{9,8},{10,11... | collective-permute-start | bytes 1769480 | tf_op jit(solution)/shard_map/ppermute | solution.py:33
  1.9 12.6 %collective-permute-start.4 = (bf16[192,1536]{1,0:T(8,128)(2,1)}, bf16[192,1536]{1,0:T(8,128)(2,1)S(1)}, u32[]{:S(2)}, u32[]{:S(2)}) collective-permute-start(bf16[192,1536]{1,0:T(8,128)(2,1)} %refs_1_.1), channel_id=1, source_target_pairs={{0,1},{1,0},{2,3},{3,2},{4,5},{5,4},{6,7},{7,6},{8,9},{9,8},{10,11... | collective-permute-start | bytes 1769480 | tf_op jit(solution)/shard_map/ppermute | solution.py:33
  2.0 1.1 copy-start.4
  3.0 11.4 %collective-permute-start.1 = (bf16[192,384]{1,0:T(8,128)(2,1)S(1)}, bf16[192,384]{1,0:T(8,128)(2,1)S(1)}, u32[]{:S(2)}, u32[]{:S(2)}) collective-permute-start(bf16[192,384]{1,0:T(8,128)(2,1)S(1)} %cut_proj.1.refs_0_), channel_id=1, source_target_pairs={{0,4},{1,5},{2,6},{3,7},{4,0},{5,1},{6,2},{7,3},{8,12},{9,13},{10,... | collective-permute-start | bytes 442376 | tf_op jit(solution)/shard_map/ppermute | solution.py:37
  6.1 1.4 copy-start
  14.4 1.4 copy-start.2
  14.5 7.9 %copy-start.3 = (bf16[3,64,1536]{2,1,0:T(8,128)(2,1)S(1)}, bf16[3,64,1536]{2,1,0:T(8,128)(2,1)}, u32[]{:S(2)}) copy-start(bf16[3,64,1536]{2,1,0:T(8,128)(2,1)} %refs_4_.1) | copy-start | bytes 1769476
  14.5 7.9 %collective-permute-start.5 = (bf16[2,192,384]{2,1,0:T(8,128)(2,1)S(1)}, bf16[2,192,384]{2,1,0:T(8,128)(2,1)S(1)}, u32[]{:S(2)}, u32[]{:S(2)}) collective-permute-start(bf16[2,192,384]{2,1,0:T(8,128)(2,1)S(1)} %pair.1._.refs_0_), channel_id=1, source_target_pairs={{0,2},{1,3},{2,0},{3,1},{4,6},{5,7},{6,4},{7,5},{8,10},{9,11},{10,... | collective-permute-start | bytes 884744 | tf_op jit(solution)/shard_map/ppermute | solution.py:37
  22.6 22.8 %collective-permute-start.10 = (bf16[2,384,384]{2,1,0:T(8,128)(2,1)S(1)}, bf16[2,384,384]{2,1,0:T(8,128)(2,1)S(1)}, u32[]{:S(2)}, u32[]{:S(2)}) collective-permute-start(bf16[2,384,384]{2,1,0:T(8,128)(2,1)S(1)} %get-tuple-element.41), channel_id=1, source_target_pairs={{0,16},{8,24},{16,0},{24,8},{1,17},{9,25},{17,1},{25,9},{2,18},{10... | collective-permute-start | bytes 1769480 | tf_op jit(solution)/shard_map/ppermute | solution.py:41
  23.9 21.5 %collective-permute-start.9 = (bf16[2,384,384]{2,1,0:T(8,128)(2,1)S(1)}, bf16[2,384,384]{2,1,0:T(8,128)(2,1)S(1)}, u32[]{:S(2)}, u32[]{:S(2)}) collective-permute-start(bf16[2,384,384]{2,1,0:T(8,128)(2,1)S(1)} %get-tuple-element.39), channel_id=1, source_target_pairs={{0,8},{8,0},{16,24},{24,16},{1,9},{9,1},{17,25},{25,17},{2,10},{10... | collective-permute-start | bytes 1769480 | tf_op jit(solution)/shard_map/ppermute | solution.py:41
  25.1 20.3 %collective-permute-start.8 = (bf16[9,64,384]{2,1,0:T(8,128)(2,1)S(1)}, bf16[9,64,384]{2,1,0:T(8,128)(2,1)S(1)}, u32[]{:S(2)}, u32[]{:S(2)}) collective-permute-start(bf16[9,64,384]{2,1,0:T(8,128)(2,1)S(1)} %get-tuple-element.37.refs_4_), channel_id=1, source_target_pairs={{0,4},{1,5},{2,6},{3,7},{4,0},{5,1},{6,2},{7,3},{8,12},{9,13},{10,... | collective-permute-start | bytes 1327112 | tf_op jit(solution)/shard_map/ppermute | solution.py:37
  26.1 15.5 %collective-permute-start.6 = (bf16[3,96,384]{2,1,0:T(8,128)(2,1)S(1)}, bf16[3,96,384]{2,1,0:T(8,128)(2,1)S(1)}, u32[]{:S(2)}, u32[]{:S(2)}) collective-permute-start(bf16[3,96,384]{2,1,0:T(8,128)(2,1)S(1)} %get-tuple-element.35.refs_0_), channel_id=1, source_target_pairs={{0,8},{8,0},{16,24},{24,16},{1,9},{9,1},{17,25},{25,17},{2,10},{10... | collective-permute-start | bytes 663560 | tf_op jit(solution)/shard_map/ppermute | solution.py:41
  26.3 15.3 %collective-permute-start.7 = (bf16[3,96,384]{2,1,0:T(8,128)(2,1)S(1)}, bf16[3,96,384]{2,1,0:T(8,128)(2,1)S(1)}, u32[]{:S(2)}, u32[]{:S(2)}) collective-permute-start(bf16[3,96,384]{2,1,0:T(8,128)(2,1)S(1)} %get-tuple-element.36.refs_1_), channel_id=1, source_target_pairs={{0,16},{8,24},{16,0},{24,8},{1,17},{9,25},{17,1},{25,9},{2,18},{10... | collective-permute-start | bytes 663560 | tf_op jit(solution)/shard_map/ppermute | solution.py:41
  45.8 20.1 %collective-permute-start.11 = (bf16[2,9,64,384]{3,2,1,0:T(8,128)(2,1)S(1)}, bf16[2,9,64,384]{3,2,1,0:T(8,128)(2,1)S(1)}, u32[]{:S(2)}, u32[]{:S(2)}) collective-permute-start(bf16[2,9,64,384]{3,2,1,0:T(8,128)(2,1)S(1)} %get-tuple-element.42.refs_0_), channel_id=1, source_target_pairs={{0,2},{1,3},{2,0},{3,1},{4,6},{5,7},{6,4},{7,5},{8,10},{9,11},{10,... | collective-permute-start | bytes 2654216 | tf_op jit(solution)/shard_map/ppermute | solution.py:37
  47.1 16.9 %collective-permute-start.12 = (bf16[2,3,96,384]{3,2,1,0:T(8,128)(2,1)S(1)}, bf16[2,3,96,384]{3,2,1,0:T(8,128)(2,1)S(1)}, u32[]{:S(2)}, u32[]{:S(2)}) collective-permute-start(bf16[2,3,96,384]{3,2,1,0:T(8,128)(2,1)S(1)} %get-tuple-element.43.refs_2_), channel_id=1, source_target_pairs={{0,16},{8,24},{16,0},{24,8},{1,17},{9,25},{17,1},{25,9},{2,18},{10... | collective-permute-start | bytes 1327112 | tf_op jit(solution)/shard_map/ppermute | solution.py:41
  47.3 16.7 %collective-permute-start.13 = (bf16[2,3,96,384]{3,2,1,0:T(8,128)(2,1)S(1)}, bf16[2,3,96,384]{3,2,1,0:T(8,128)(2,1)S(1)}, u32[]{:S(2)}, u32[]{:S(2)}) collective-permute-start(bf16[2,3,96,384]{3,2,1,0:T(8,128)(2,1)S(1)} %get-tuple-element.44.refs_3_), channel_id=1, source_target_pairs={{0,8},{8,0},{16,24},{24,16},{1,9},{9,1},{17,25},{25,17},{2,10},{10... | collective-permute-start | bytes 1327112 | tf_op jit(solution)/shard_map/ppermute | solution.py:41
  47.6 15.6 %collective-permute-start.14 = (bf16[384,384]{1,0:T(8,128)(2,1)S(1)}, bf16[384,384]{1,0:T(8,128)(2,1)S(1)}, u32[]{:S(2)}, u32[]{:S(2)}) collective-permute-start(bf16[384,384]{1,0:T(8,128)(2,1)S(1)} %get-tuple-element.46), channel_id=1, source_target_pairs={{0,16},{8,24},{16,0},{24,8},{1,17},{9,25},{17,1},{25,9},{2,18},{10... | collective-permute-start | bytes 884744 | tf_op jit(solution)/shard_map/ppermute | solution.py:41
  48.8 14.4 %collective-permute-start.15 = (bf16[384,384]{1,0:T(8,128)(2,1)S(1)}, bf16[384,384]{1,0:T(8,128)(2,1)S(1)}, u32[]{:S(2)}, u32[]{:S(2)}) collective-permute-start(bf16[384,384]{1,0:T(8,128)(2,1)S(1)} %get-tuple-element.48), channel_id=1, source_target_pairs={{0,8},{8,0},{16,24},{24,16},{1,9},{9,1},{17,25},{25,17},{2,10},{10... | collective-permute-start | bytes 884744 | tf_op jit(solution)/shard_map/ppermute | solution.py:41
  65.9 7.7 %copy-start.1 = (bf16[1,512,1536]{2,1,0:T(8,128)(2,1)S(1)}, bf16[1,512,1536]{2,1,0:T(8,128)(2,1)}, u32[]{:S(2)}) copy-start(bf16[1,512,1536]{2,1,0:T(8,128)(2,1)} %param.5) | copy-start | bytes 4718596
  65.9 7.7 %copy-start.5 = (bf16[192,1536]{1,0:T(8,128)(2,1)S(1)}, bf16[192,1536]{1,0:T(8,128)(2,1)}, u32[]{:S(2)}) copy-start(bf16[192,1536]{1,0:T(8,128)(2,1)} %refs_1_.1) | copy-start | bytes 1769476
  66.3 7.3 %collective-permute-start.19 = (bf16[4032,384]{1,0:T(8,128)(2,1)S(1)}, bf16[4032,384]{1,0:T(8,128)(2,1)S(1)}, u32[]{:S(2)}, u32[]{:S(2)}) collective-permute-start(bf16[4032,384]{1,0:T(8,128)(2,1)S(1)} %get-tuple-element.52), channel_id=1, source_target_pairs={{0,1},{1,0},{2,3},{3,2},{4,5},{5,4},{6,7},{7,6},{8,9},{9,8},{10,11... | collective-permute-start | bytes 9289736 | tf_op jit(solution)/shard_map/ppermute | solution.py:33
  68.4 12.3 %collective-permute-start.20 = (bf16[2,192,384]{2,1,0:T(8,128)(2,1)S(1)}, bf16[2,192,384]{2,1,0:T(8,128)(2,1)S(1)}, u32[]{:S(2)}, u32[]{:S(2)}) collective-permute-start(bf16[2,192,384]{2,1,0:T(8,128)(2,1)S(1)} %get-tuple-element.53), channel_id=1, source_target_pairs={{0,2},{1,3},{2,0},{3,1},{4,6},{5,7},{6,4},{7,5},{8,10},{9,11},{10,... | collective-permute-start | bytes 884744 | tf_op jit(solution)/shard_map/ppermute | solution.py:37
  69.7 11.7 %collective-permute-start.16 = (bf16[3,1,64,384]{3,2,1,0:T(8,128)(2,1)S(1)}, bf16[3,1,64,384]{3,2,1,0:T(8,128)(2,1)S(1)}, u32[]{:S(2)}, u32[]{:S(2)}) collective-permute-start(bf16[3,1,64,384]{3,2,1,0:T(8,128)(2,1)S(1)} %get-tuple-element.51), channel_id=1, source_target_pairs={{0,8},{8,0},{16,24},{24,16},{1,9},{9,1},{17,25},{25,17},{2,10},{10... | collective-permute-start | bytes 442376 | tf_op jit(solution)/shard_map/ppermute | solution.py:41
  69.9 11.4 %collective-permute-start.17 = (bf16[3,1,64,384]{3,2,1,0:T(8,128)(2,1)S(1)}, bf16[3,1,64,384]{3,2,1,0:T(8,128)(2,1)S(1)}, u32[]{:S(2)}, u32[]{:S(2)}) collective-permute-start(bf16[3,1,64,384]{3,2,1,0:T(8,128)(2,1)S(1)} %get-tuple-element.51), channel_id=1, source_target_pairs={{0,16},{8,24},{16,0},{24,8},{1,17},{9,25},{17,1},{25,9},{2,18},{10... | collective-permute-start | bytes 442376 | tf_op jit(solution)/shard_map/ppermute | solution.py:41
  70.1 11.2 %collective-permute-start.18 = (bf16[3,1,64,384]{3,2,1,0:T(8,128)(2,1)S(1)}, bf16[3,1,64,384]{3,2,1,0:T(8,128)(2,1)S(1)}, u32[]{:S(2)}, u32[]{:S(2)}) collective-permute-start(bf16[3,1,64,384]{3,2,1,0:T(8,128)(2,1)S(1)} %get-tuple-element.51), channel_id=1, source_target_pairs={{0,24},{8,16},{16,8},{24,0},{1,25},{9,17},{17,9},{25,1},{2,26},{10... | collective-permute-start | bytes 442376 | tf_op jit(solution)/shard_map/ppermute | solution.py:41
  81.4 3.5 %collective-permute-start.21 = (bf16[576,384]{1,0:T(8,128)(2,1)S(1)}, bf16[576,384]{1,0:T(8,128)(2,1)S(1)}, u32[]{:S(2)}, u32[]{:S(2)}) collective-permute-start(bf16[576,384]{1,0:T(8,128)(2,1)S(1)} %bitcast.22), channel_id=1, source_target_pairs={{0,1},{1,0},{2,3},{3,2},{4,5},{5,4},{6,7},{7,6},{8,9},{9,8},{10,11... | collective-permute-start | bytes 1327112 | tf_op jit(solution)/shard_map/ppermute | solution.py:33
  81.8 14.0 %collective-permute-start.29 = (bf16[192,384]{1,0:T(8,128)(2,1)S(1)}, bf16[192,384]{1,0:T(8,128)(2,1)S(1)}, u32[]{:S(2)}, u32[]{:S(2)}) collective-permute-start(bf16[192,384]{1,0:T(8,128)(2,1)S(1)} %get-tuple-element.54.refs_4_), channel_id=1, source_target_pairs={{0,4},{1,5},{2,6},{3,7},{4,0},{5,1},{6,2},{7,3},{8,12},{9,13},{10,... | collective-permute-start | bytes 442376 | tf_op jit(solution)/shard_map/ppermute | solution.py:37
  91.4 19.6 %collective-permute-start.22 = (bf16[17,16,512]{2,1,0:T(8,128)(2,1)S(1)}, bf16[17,16,512]{2,1,0:T(8,128)(2,1)S(1)}, u32[]{:S(2)}, u32[]{:S(2)}) collective-permute-start(bf16[17,16,512]{2,1,0:T(8,128)(2,1)S(1)} %get-tuple-element.56), channel_id=1, source_target_pairs={{0,4},{1,5},{2,6},{3,7},{4,0},{5,1},{6,2},{7,3},{8,12},{9,13},{10,... | collective-permute-start | bytes 835592 | tf_op jit(solution)/shard_map/ppermute | solution.py:633
  92.8 24.3 %collective-permute-start.23 = (bf16[17,16,512]{2,1,0:T(8,128)(2,1)S(1)}, bf16[17,16,512]{2,1,0:T(8,128)(2,1)S(1)}, u32[]{:S(2)}, u32[]{:S(2)}) collective-permute-start(bf16[17,16,512]{2,1,0:T(8,128)(2,1)S(1)} %get-tuple-element.57), channel_id=1, source_target_pairs={{0,5},{1,4},{2,7},{3,6},{4,1},{5,0},{6,3},{7,2},{8,13},{9,12},{10,... | collective-permute-start | bytes 835592 | tf_op jit(solution)/shard_map/ppermute | solution.py:633
  94.4 23.0 %collective-permute-start.24 = (bf16[17,16,512]{2,1,0:T(8,128)(2,1)S(1)}, bf16[17,16,512]{2,1,0:T(8,128)(2,1)S(1)}, u32[]{:S(2)}, u32[]{:S(2)}) collective-permute-start(bf16[17,16,512]{2,1,0:T(8,128)(2,1)S(1)} %get-tuple-element.58), channel_id=1, source_target_pairs={{0,2},{1,3},{2,0},{3,1},{4,6},{5,7},{6,4},{7,5},{8,10},{9,11},{10,... | collective-permute-start | bytes 835592 | tf_op jit(solution)/shard_map/ppermute | solution.py:633
  94.4 24.4 %collective-permute-start.25 = (bf16[17,16,512]{2,1,0:T(8,128)(2,1)S(1)}, bf16[17,16,512]{2,1,0:T(8,128)(2,1)S(1)}, u32[]{:S(2)}, u32[]{:S(2)}) collective-permute-start(bf16[17,16,512]{2,1,0:T(8,128)(2,1)S(1)} %get-tuple-element.59), channel_id=1, source_target_pairs={{0,3},{1,2},{2,1},{3,0},{4,7},{5,6},{6,5},{7,4},{8,11},{9,10},{10,... | collective-permute-start | bytes 835592 | tf_op jit(solution)/shard_map/ppermute | solution.py:633
  95.8 33.0 %collective-permute-start.26 = (bf16[17,16,512]{2,1,0:T(8,128)(2,1)S(1)}, bf16[17,16,512]{2,1,0:T(8,128)(2,1)S(1)}, u32[]{:S(2)}, u32[]{:S(2)}) collective-permute-start(bf16[17,16,512]{2,1,0:T(8,128)(2,1)S(1)} %get-tuple-element.60), channel_id=1, source_target_pairs={{0,6},{1,7},{2,4},{3,5},{4,2},{5,3},{6,0},{7,1},{8,14},{9,15},{10,... | collective-permute-start | bytes 835592 | tf_op jit(solution)/shard_map/ppermute | solution.py:633
  111.5 34.0 %collective-permute-start.30 = (f32[192,384]{1,0:T(8,128)S(1)}, f32[192,384]{1,0:T(8,128)S(1)}, u32[]{:S(2)}, u32[]{:S(2)}) collective-permute-start(f32[192,384]{1,0:T(8,128)S(1)} %far_sum.1.a_ref), channel_id=1, source_target_pairs={{0,8},{8,0},{16,24},{24,16},{1,9},{9,1},{17,25},{25,17},{2,10},{10... | collective-permute-start | bytes 884744 | tf_op jit(solution)/shard_map/ppermute | solution.py:41
  117.1 28.4 %collective-permute-start.31 = (f32[192,384]{1,0:T(8,128)S(1)}, f32[192,384]{1,0:T(8,128)S(1)}, u32[]{:S(2)}, u32[]{:S(2)}) collective-permute-start(f32[192,384]{1,0:T(8,128)S(1)} %far_sum.1.a_ref), channel_id=1, source_target_pairs={{0,16},{8,24},{16,0},{24,8},{1,17},{9,25},{17,1},{25,9},{2,18},{10... | collective-permute-start | bytes 884744 | tf_op jit(solution)/shard_map/ppermute | solution.py:41
  117.4 28.1 %collective-permute-start.32 = (f32[192,384]{1,0:T(8,128)S(1)}, f32[192,384]{1,0:T(8,128)S(1)}, u32[]{:S(2)}, u32[]{:S(2)}) collective-permute-start(f32[192,384]{1,0:T(8,128)S(1)} %far_sum.1.a_ref), channel_id=1, source_target_pairs={{0,24},{8,16},{16,8},{24,0},{1,25},{9,17},{17,9},{25,1},{2,26},{10... | collective-permute-start | bytes 884744 | tf_op jit(solution)/shard_map/ppermute | solution.py:41
  118.8 22.5 %collective-permute-start.27 = (bf16[17,16,512]{2,1,0:T(8,128)(2,1)S(1)}, bf16[17,16,512]{2,1,0:T(8,128)(2,1)S(1)}, u32[]{:S(2)}, u32[]{:S(2)}) collective-permute-start(bf16[17,16,512]{2,1,0:T(8,128)(2,1)S(1)} %get-tuple-element.61), channel_id=1, source_target_pairs={{0,7},{1,6},{2,5},{3,4},{4,3},{5,2},{6,1},{7,0},{8,15},{9,14},{10,... | collective-permute-start | bytes 835592 | tf_op jit(solution)/shard_map/ppermute | solution.py:633
  128.8 12.5 %collective-permute-start.28 = (bf16[17,16,512]{2,1,0:T(8,128)(2,1)S(1)}, bf16[17,16,512]{2,1,0:T(8,128)(2,1)S(1)}, u32[]{:S(2)}, u32[]{:S(2)}) collective-permute-start(bf16[17,16,512]{2,1,0:T(8,128)(2,1)S(1)} %get-tuple-element.62), channel_id=1, source_target_pairs={{0,1},{1,0},{2,3},{3,2},{4,5},{5,4},{6,7},{7,6},{8,9},{9,8},{10,11... | collective-permute-start | bytes 835592 | tf_op jit(solution)/shard_map/ppermute | solution.py:633

commit v4 on v3

--- a/solution.py
+++ b/solution.py
@@ -57,23 +57,27 @@
 HALF = D // N_FSDP // 2
 STEM_ROWS = CS // N_FSDP
 TAPS = 3
-QUARTER_TAPS = (1,)
-WHOLE_TAPS = (0, 2)
-UNITS = len(QUARTER_TAPS) + len(WHOLE_TAPS) * N_SITE
 
 
 def half_places(site, low):
     return [(0, z, ("xor", site), low, HALF) for z in Z_ORDER]
 
 
+SPLIT = STEM_ROWS // 2
+QUARTER_BLOCKS = ((1, 0, STEM_ROWS), (0, 0, SPLIT))
+WHOLE_BLOCKS = ((2, 0, STEM_ROWS), (0, SPLIT, STEM_ROWS - SPLIT))
+QUARTER_ROWS = sum(count for _, _, count in QUARTER_BLOCKS)
+UNIT_ROWS = QUARTER_ROWS + N_SITE * sum(count for _, _, count in WHOLE_BLOCKS)
+
+
 def unit_places(site):
-    return [(tap, z, ("xor", site), 0, STEM_ROWS) for z in Z_ORDER for tap in QUARTER_TAPS]
+    return [(tap, z, ("xor", site), low, count) for z in Z_ORDER for tap, low, count in QUARTER_BLOCKS]
 
 
 def all_places():
-    whole_tap = [(tap, ("abs", j)) for tap in WHOLE_TAPS for j in range(N_SITE)]
-    columns = [(tap, ("xor", 0)) for tap in QUARTER_TAPS] + whole_tap
-    return [(tap, z, kind, 0, STEM_ROWS) for z in Z_ORDER for tap, kind in columns]
+    blocks = [(tap, ("xor", 0), low, count) for tap, low, count in QUARTER_BLOCKS]
+    blocks += [(tap, ("abs", j), low, count) for tap, low, count in WHOLE_BLOCKS for j in range(N_SITE)]
+    return [(tap, z, kind, low, count) for z in Z_ORDER for tap, kind, low, count in blocks]
 
 
 def shard_places(tap, count):
@@ -137,7 +141,7 @@
         out_shape=out,
         in_specs=[vmem] * n + [ANY] * len(first),
         out_specs=(vmem,) * len(out),
-        compiler_params=pltpu.CompilerParams(vmem_limit_bytes=16 * MIB),
+        compiler_params=pltpu.CompilerParams(vmem_limit_bytes=14 * MIB),
         cost_estimate=pl.CostEstimate(flops=0, bytes_accessed=0, transcendentals=0),
     )(*values, *first)
 
@@ -147,23 +151,18 @@
     out[...] = shard[:, pl.ds(at, QUARTER)]
 
 
-def pair_kernel(a, b, out):
-    out[0] = a[...]
-    out[1] = b[...]
-
-
-def halves_kernel(pair, near, sent_a, sent_b, stem, a, b, out_a, out_b, units):
-    out_a[...], out_b[...] = sent_a[...], sent_b[...]
-    for i, piece in enumerate((pair.at[1], near.at[0], near.at[1])):
-        a[i] = piece[:HALF, :]
-        b[i] = piece[HALF:, :]
+def halves_kernel(far, near, farthest, sent_a, sent_b, stem, a, b, units):
+    for i, piece in enumerate((far, near, farthest)):
+        a[i * HALF : (i + 1) * HALF, :] = piece[:HALF, :]
+        b[i * HALF : (i + 1) * HALF, :] = piece[HALF:, :]
+    for out, sent in ((a, sent_a), (b, sent_b)):
+        out[3 * HALF : 3 * HALF + D // 4, :] = sent[0]
+        out[3 * HALF + D // 4 :, :] = sent[1]
     at = pl.multiple_of(lax.axis_index("site") * QUARTER, QUARTER)
-    for i, tap in enumerate(QUARTER_TAPS):
-        units[i] = stem[tap, :, pl.ds(at, QUARTER)]
-    for i, tap in enumerate(WHOLE_TAPS):
-        for j in range(N_SITE):
-            columns = slice(j * QUARTER, (j + 1) * QUARTER)
-            units[len(QUARTER_TAPS) + N_SITE * i + j] = stem[tap, :, columns]
+    pieces = [stem[tap, low : low + count, pl.ds(at, QUARTER)] for tap, low, count in QUARTER_BLOCKS]
+    for tap, low, count in WHOLE_BLOCKS:
+        pieces += column_pieces(stem[tap, low : low + count, :])
+    pack_rows(units, pieces)
 
 
 def pack_rows(out, pieces):
@@ -173,27 +172,36 @@
         at += piece.shape[0]
 
 
+def column_pieces(rows):
+    return [rows[:, i * QUARTER : (i + 1) * QUARTER] for i in range(N_SITE)]
+
+
 def site_step_kernel(
-    a0, b0, a1, b1, units, far, kept_a, came_a, kept_b, came_b, a, b, pair, sent_a, sent_b, own_a, own_b
+    shard, stem, a0, b0, a1, b1, units, far, kept_a, kept_b, a, b, packed, pair, own_a, own_b
 ):
     pair[0], pair[1] = units[...], far[...]
-    a[0], a[1], b[0], b[1] = a0[...], a1[...], b0[...], b1[...]
-    for kept, came, own, sent in ((kept_a, came_a, own_a, sent_a), (kept_b, came_b, own_b, sent_b)):
-        own[...] = kept[0] + came[0].astype(F32)
-        sent[...] = (kept[1] + came[1].astype(F32)).astype(BF16)
+    n, m = 3 * HALF, D // 4
+    for sent, came, kept, out, own in ((a0, a1, kept_a, a, own_a), (b0, b1, kept_b, b, own_b)):
+        for j, source in enumerate((sent, came)):
+            out[j * n : (j + 1) * n, :] = source[:n, :]
+        own[...] = kept[0] + came[n : n + m, :].astype(F32)
+        out[2 * n :, :] = (kept[1] + came[n + m :, :].astype(F32)).astype(BF16)
+    pieces = column_pieces(shard[...])
+    for tap in range(TAPS):
+        pieces += column_pieces(stem[tap])
+    pack_rows(packed, pieces + [ref[:n, :] for ref in (a0, a1, b0, b1)])
 
 
 def collect_kernel(a, b, c, out):
     out[0], out[1], out[2] = a[...], b[...], c[...]
 
 
-def three_kernel(pair, near, a, b, a2, b2, quarters, units, packed):
-    pieces = [ref[j, i] for ref in (a, b, a2, b2) for j in range(2) for i in range(3)]
-    for i, piece in enumerate((pair[1], near[0], near[1])):
-        quarters[i] = piece[: len(QUARTER_TAPS)]
-        units[i] = piece
-        pieces += [piece[j] for j in range(UNITS)]
-    pack_rows(packed, pieces)
+def three_kernel(pair, near, a2, b2, quarters, units, packed):
+    n = 6 * HALF
+    packed[:n, :], packed[n:, :] = a2[:n, :], b2[:n, :]
+    for i, piece in enumerate((pair.at[1], near.at[0], near.at[1])):
+        quarters[i] = piece[:QUARTER_ROWS, :]
+        units[i] = piece[...]
 
 
 def normalise(inputs):
@@ -226,7 +234,7 @@
 OUTER_PLACES = (((0, 0), (0, 0)), ((1, 0), (0, 1)), ((0, 1), (1, 0)), ((1, 1), (1, 1)))
 
 
-def outer_kernel(scalars, na_ref, nb_ref, ca_ref, cb_ref, _, ka_ref, sa_ref, kb_ref, sb_ref):
+def outer_kernel(scalars, na_ref, nb_ref, ca_ref, cb_ref, ka_ref, sa_ref, kb_ref, sb_ref):
     step = pl.program_id(0)
     total = jnp.dot(na_ref[...], ca_ref[...], preferred_element_type=F32)
     total = total + jnp.dot(nb_ref[...], cb_ref[...], preferred_element_type=F32)
@@ -239,30 +247,30 @@
                 ref[i] = value.astype(ref.dtype)
 
 
-def outer_pieces(scalars, normed_a, normed_b, cotangent_a, cotangent_b, first):
+def outer_pieces(scalars, normed_a, normed_b, cotangent_a, cotangent_b):
     dims = (2, D // 4, QUARTER)
     column = pl.BlockSpec((ROWS, QUARTER), lambda i, scalars: (0, lax.bitwise_xor(scalars[0], i)))
     return call(
         outer_kernel, "outer_pieces", (shape(dims, F32), shape(dims, BF16)) * 2, (N_SITE,),
-        [whole((D // 2, ROWS))] * 2 + [column] * 2 + [ANY], (whole(dims),) * 4, [],
-    )(scalars, normed_a, normed_b, cotangent_a, cotangent_b, first)
+        [whole((D // 2, ROWS))] * 2 + [column] * 2, (whole(dims),) * 4, [],
+    )(scalars, normed_a, normed_b, cotangent_a, cotangent_b)
 
 
 def site_sum_kernel(scalars, oa_ref, ra_ref, ob_ref, rb_ref, kept_ref, sent_ref, total):
     shard = D // N_FSDP
     z = scalars[1] // 2
-    total[: D // 4, :] = oa_ref[...] + ra_ref[...].astype(F32)
-    total[D // 4 :, :] = ob_ref[...] + rb_ref[...].astype(F32)
+    total[: D // 4, :] = oa_ref[...] + ra_ref[6 * HALF :, :].astype(F32)
+    total[D // 4 :, :] = ob_ref[...] + rb_ref[6 * HALF :, :].astype(F32)
     for distance, (ref, i) in enumerate(((kept_ref, 0), (sent_ref, 0), (kept_ref, 1), (sent_ref, 1))):
         rows = pl.ds(pl.multiple_of(lax.bitwise_xor(z, distance) * shard, shard), shard)
         ref[i] = total[rows, :].astype(ref.dtype)
 
 
 def site_sum(scalars, *values):
-    dims, out = (D // 4, QUARTER), (2, D // N_FSDP, QUARTER)
+    out = (2, D // N_FSDP, QUARTER)
     return call(
         site_sum_kernel, "site_sum", (shape(out, F32), shape(out, BF16)), (1,),
-        [whole(dims)] * 4, (whole(out),) * 2, [pltpu.VMEM((D // 2, QUARTER), F32)],
+        [whole(value.shape) for value in values], (whole(out),) * 2, [pltpu.VMEM((D // 2, QUARTER), F32)],
     )(scalars, *values)
 
 
@@ -290,20 +298,6 @@
         lambda *refs: far_sum_kernel(scale, *refs), "far_sum", shape(dims, F32), (1,),
         [whole(dims)] * 2 + [ANY] * len(first), whole(dims), [],
     )(scalars, own, came, *first)
-
-
-def lay_columns_kernel(scalars, a_ref, b_ref, c_ref, d_ref, out_ref):
-    for distance, ref in enumerate((a_ref, b_ref, c_ref, d_ref)):
-        at = pl.multiple_of(lax.bitwise_xor(scalars[0], distance) * QUARTER, QUARTER)
-        out_ref[:, pl.ds(at, QUARTER)] = ref[...]
-
-
-def lay_columns(scalars, parts):
-    out = (D // N_FSDP, D)
-    return call(
-        lay_columns_kernel, "lay_columns", shape(out, F32), (1,), [whole(parts[0].shape)] * N_SITE,
-        whole(out), [],
-    )(scalars, *parts)
 
 
 def weight_copies(tables, scalars, refs, weight, sem):
@@ -508,8 +502,21 @@
 
 
 def owner_kernel(scalars, *refs):
-    payloads, (out_ref, packed, firsts, sem) = refs[:N_FSDP], refs[N_FSDP:]
+    payloads, terms, (out_ref, total), (packed, firsts, sem, total_sem) = (
+        refs[:N_FSDP], refs[N_FSDP : N_FSDP + N_SITE], refs[-6:-4], refs[-4:]
+    )
     step = pl.program_id(0)
+    total_copies = []
+    for distance, term in enumerate(terms):
+        at = pl.multiple_of(lax.bitwise_xor(scalars[0], distance) * QUARTER, QUARTER)
+        total_copies.append(
+            pltpu.make_async_copy(term, total.at[:, pl.ds(at, QUARTER)], total_sem.at[distance])
+        )
+
+    @pl.when(step == 0)
+    def _():
+        for copy in total_copies:
+            copy.start()
 
     @pl.when(step == 0)
     def _():
@@ -538,19 +545,25 @@
         to = pl.ds(pl.multiple_of(local * 2 * SEG, 2 * SEG), 2 * SEG)
         out_ref[to, :] = jnp.where(segment < count, rows, 0.0).astype(BF16)
 
-
-def owner_rows(scalars, payloads):
+    @pl.when(step == pl.num_programs(0) - 1)
+    def _():
+        for copy in total_copies:
+            copy.wait()
+
+
+def owner_rows(scalars, payloads, terms):
     payload = (CAP + 1, 2 * SEG, CS)
     rows = 2 * OWN_SEG * SEG
     return call(
-        owner_kernel, "owner_rows", shape((rows, CS), BF16), (4,), [ANY] * N_FSDP,
-        row_block(rows // 4, CS),
+        owner_kernel, "owner_rows", (shape((rows, CS), BF16), shape((D // N_FSDP, D), F32)), (4,),
+        [ANY] * (N_FSDP + N_SITE), (row_block(rows // 4, CS), HBM),
         [
             pltpu.VMEM((N_FSDP,) + payload, BF16),
             pltpu.VMEM((N_FSDP * CAP, CS), F32),
             pltpu.SemaphoreType.DMA((N_FSDP,)),
+            pltpu.SemaphoreType.DMA((N_SITE,)),
         ],
-    )(scalars, *payloads)
+    )(scalars, *payloads, *terms)
 
 
 def body(held_input, held_cotangent, proj_weight, stem_weight, seg_counts):
@@ -561,70 +574,66 @@
     plan = plan_of(scalars)
     piece = (D // N_FSDP, QUARTER)
     half = (3, HALF, QUARTER)
-    units = (UNITS, STEM_ROWS, QUARTER)
-    quarters = (len(QUARTER_TAPS), STEM_ROWS, QUARTER)
+    units = (UNIT_ROWS, QUARTER)
+    quarters = (QUARTER_ROWS, QUARTER)
 
     (proj_quarter,) = join(cut_proj_kernel, "cut_proj", [piece], [proj_weight])
-    far = swap_z(proj_quarter, 2)
+    around = [swap_z(proj_quarter, distance) for distance in Z_ORDER]
     normed_own = norm_half(scalars, inputs, [proj_quarter])
     normed_theirs = norm_half(scalars, swap_core(inputs), [normed_own])
-    cotangent_theirs = swap_core(cotangent)
-    proj_swapped, stem_swapped = swap_core(proj_weight), swap_core(stem_weight)
-    (pair,) = join(
-        pair_kernel, "pair", [(2, *piece)], [proj_quarter, far],
-        [normed_theirs, cotangent_theirs, proj_swapped, stem_swapped],
-    )
-
-    near = swap_z(pair, 1)
     kept_a, sent_a, kept_b, sent_b = outer_pieces(
-        scalars, normed_own, normed_theirs, cotangent, cotangent_theirs, pair
-    )
-    terms = (D // 4, QUARTER)
-    a0, b0, sent_a, sent_b, stem_units = join(
-        halves_kernel, "halves", [half, half, (2, *terms), (2, *terms), units],
-        [pair, near, sent_a, sent_b, stem_weight],
-    )
-
-    a, b, stem_pair, sent_a, sent_b, own_a, own_b = join(
-        site_step_kernel, "site_step", [(2, *half), (2, *half), (2, *units), terms, terms],
+        scalars, normed_own, normed_theirs, cotangent, swap_core(cotangent)
+    )
+    n, m = 3 * HALF, D // 4
+    a0, b0, stem_units = join(
+        halves_kernel, "halves", [(n + 2 * m, QUARTER)] * 2 + [units],
+        [*around, sent_a, sent_b, stem_weight],
+    )
+
+    a, b, packed, stem_pair, own_a, own_b = join(
+        site_step_kernel, "site_step", [(2 * n + m, QUARTER)] * 2 + [(D + 4 * n, QUARTER), (2, *units)],
         [
-            a0, b0, swap_site(a0, 1), swap_site(b0, 2), stem_units, swap_z(stem_units, 2),
-            kept_a, swap_site(sent_a, 1), kept_b, swap_site(sent_b, 2),
+            proj_weight, stem_weight, a0, b0, swap_site(a0, 1), swap_site(b0, 2),
+            stem_units, swap_z(stem_units, 2), kept_a, kept_b,
         ],
         [plan],
-        wide_dims=[terms, terms],
+        wide_dims=[(m, QUARTER)] * 2,
     )
 
     a2, b2 = swap_site(a, 2), swap_site(b, 1)
     near = swap_z(stem_pair, 1)
-    kept, sent = site_sum(scalars, own_a, swap_site(sent_a, 2), own_b, swap_site(sent_b, 1))
-    n = 3 * UNITS * STEM_ROWS
-    others, all_others, packed = join(
-        three_kernel, "three", [(3, *quarters), (3, *units), (24 * HALF + n, QUARTER)],
-        [stem_pair, near, a, b, a2, b2], [kept],
+    packed = swap_core(packed)
+    kept, sent = site_sum(scalars, own_a, a2, own_b, b2)
+    others, all_others, late = join(
+        three_kernel, "three", [(3, *quarters), (3, *units), (4 * n, QUARTER)],
+        [stem_pair, near, a2, b2], [kept, packed],
     )
 
     over = [swap_site(others, distance) for distance in (1, 2, 3)]
-    packed = swap_core(packed)
+    late, late_stem = swap_core(late), swap_core(rows_of(all_others))
     whole_proj = [(0, 0, ("all", 0), 0, D // N_FSDP)]
     first = [half_places(0, 0) + half_places(1, 0), half_places(0, HALF) + half_places(2, HALF)]
     last = [half_places(2, 0) + half_places(3, 0), half_places(1, HALF) + half_places(3, HALF)]
     proj_parts = [
-        (proj_weight, whole_proj, 0), (proj_swapped, whole_proj, 1),
-        (rows_of(a), first[0], 0), (rows_of(b), first[1], 0),
-        (rows_of(a2), last[0], 0), (rows_of(b2), last[1], 0),
-        (packed, sum(first + last, []) + [n], 1),
+        (proj_weight, whole_proj, 0),
+        (a, first[0] + [m], 0), (b, first[1] + [m], 0),
+        (a2, last[0] + [m], 0), (b2, last[1] + [m], 0),
+        (packed, shard_places(0, D // N_FSDP) + [D // 2] + sum(first, []), 1), (late, sum(last, []), 1),
     ]
     grad = input_gradient(scalars, proj_parts, inputs, cotangent)
     own, sent = near_sum(scalars, kept, swap_z(sent, 1), [grad])
-    (over,) = join(collect_kernel, "collect", [(3, 3, *quarters)], over, [grad, sent])
+    (over,) = join(collect_kernel, "collect", [(3, 3, *quarters)], over, [grad, sent, late_stem])
     over = rows_of(over)
     last = sum((unit_places(d) for d in (1, 2, 3)), [])
     whole_stem = [(tap, 0, ("all", 0), 0, STEM_ROWS) for tap in range(TAPS)]
     stem_parts = [
-        (stem_weight.reshape(-1, D), whole_stem, 0), (stem_swapped.reshape(-1, D), whole_stem, 1),
+        (stem_weight.reshape(-1, D), whole_stem, 0),
+        (
+            packed,
+            [D // 2] + sum((shard_places(tap, STEM_ROWS) for tap in range(TAPS)), []) + [4 * n], 1,
+        ),
         (rows_of(all_others), all_places(), 0), (over, last, 0),
-        (packed, [24 * HALF] + all_places(), 1), (swap_core(over), last, 1),
+        (late_stem, all_places(), 1), (swap_core(over), last, 1),
     ]
 
     payloads = stem_payloads(plan, stem_parts, grad)
@@ -633,8 +642,8 @@
         received[d] = lax.ppermute(payloads[d], "fsdp", [(i, i ^ d) for i in range(N_FSDP)])
     scale = 1.0 / math.sqrt(N_SITE * N_FSDP * ROWS)
     terms = far_sum(scalars, own, swap_z(sent, 2), scale, [received[4]])
-    weight_grad = lay_columns(scalars, [terms] + [swap_site(terms, d) for d in (1, 2, 3)])
-    stem_grad = owner_rows(plan, [received[d] for d in PAYLOAD_ORDER])
+    terms = [terms] + [swap_site(terms, d) for d in (1, 2, 3)]
+    stem_grad, weight_grad = owner_rows(plan, [received[d] for d in PAYLOAD_ORDER], terms)
     return (stem_grad[None], weight_grad)
 
 

time: 148 us -> 142 us (0.959)
  starting transfers between devices: 44 us -> 33.5 us
  waiting for transfers between devices: 57.4 us -> 65.7 us
  Pallas kernels: 40.6 us -> 38.1 us
    ppermute x7, waiting for transfers between devices: 27 us -> 36.3 us  [body(): lax.ppermute(payloads[d], 'fsdp', [(i, i ^ d) for i in range(N_FSDP)])]
    ppermute x7, starting transfers between devices: 20.6 us -> 12.3 us  [body(): lax.ppermute(payloads[d], 'fsdp', [(i, i ^ d) for i in range(N_FSDP)])]
    ppermute x6 -> x7, waiting for transfers between devices: 7.1 us -> 9.6 us  [swap_z(): lax.ppermute(value, 'fsdp', [(i, i ^ 2 * distance) for i in range(N_FSDP)])]
    ppermute x14 -> x10, waiting for transfers between devices: 21.9 us -> 19.8 us  [swap_site(): lax.ppermute(value, 'site', [(i, i ^ distance) for i in range(N_SITE)])]
    pallas_call x2 -> x1, Pallas kernels: 5.79 us -> 4.2 us  [owner_rows(): call(owner_kernel, 'owner_rows', (shape((rows, CS), BF16), shape((D // N_...]
    ppermute x14 -> x10, starting transfers between devices: 10.4 us -> 8.85 us  [swap_site(): lax.ppermute(value, 'site', [(i, i ^ distance) for i in range(N_SITE)])]
    pallas_call x2, Pallas kernels: 6.83 us -> 5.34 us  [norm_half(): call(norm_kernel, 'norm_half', shape((D // 2, ROWS), BF16), (ROWS // BLOC...]
    ppermute x6 -> x7, starting transfers between devices: 9.23 us -> 8.66 us  [swap_z(): lax.ppermute(value, 'fsdp', [(i, i ^ 2 * distance) for i in range(N_FSDP)])]
  transfers between devices with their start and end apart: 33 -> 30, of which waited for: 11 -> 9; matrix products, arithmetic and copies ran while one was open for 0% -> 1% of each run, Pallas kernels for 26% -> 22%
where the time goes in v4:
time: 142 us; the launch traced here: 141 us
  waiting for transfers between devices  65.7 us (46%)
  Pallas kernels  38.1 us (27%)
  starting transfers between devices  33.5 us (24%)
  local copies, waits for them, and re-layouts  2.5 us (2%)
    ppermute x7, waiting for transfers between devices, body(): lax.ppermute(payloads[d], 'fsdp', [(i, i ^ d) for i in range(N_FSDP)])  36.3 us
    ppermute x10, waiting for transfers between devices, swap_site(): lax.ppermute(value, 'site', [(i, i ^ distance) for i in range(N_SITE)])  19.8 us
    ppermute x7, starting transfers between devices, body(): lax.ppermute(payloads[d], 'fsdp', [(i, i ^ d) for i in range(N_FSDP)])  12.3 us
    ppermute x7, waiting for transfers between devices, swap_z(): lax.ppermute(value, 'fsdp', [(i, i ^ 2 * distance) for i in range(N_FSDP)])  9.6 us
    ppermute x10, starting transfers between devices, swap_site(): lax.ppermute(value, 'site', [(i, i ^ distance) for i in range(N_SITE)])  8.85 us
    ppermute x7, starting transfers between devices, swap_z(): lax.ppermute(value, 'fsdp', [(i, i ^ 2 * distance) for i in range(N_FSDP)])  8.66 us
    pallas_call x1, Pallas kernels, input_gradient(): call(lambda *refs: input_grad_kernel(tables, *refs), 'input_gradient', sh...  7.01 us
    pallas_call x1, Pallas kernels, plan_of(): call(plan_kernel, 'plan', shape((COUNT_AT + 1,), jnp.int32), (1,), [], pl...  6.34 us
  transfers between devices with their start and end apart: 30, of which 9 were waited for; matrix products, arithmetic and copies ran while one was open for 1% of the time, Pallas kernels for 22%

profile of v4, /device:TPU:9, one launch (start us, length us, event | category | flops | bytes accessed | tf_op | source)
XLA Modules:
  0.0 141.4 jit_solution(14604013404429853090)
XLA Ops:
  0.6 0.7 collective-permute-start.3
  1.5 1.1 copy-done.3
  2.5 1.4 collective-permute-start.2
  3.9 2.2 %collective-permute-start.1 = (bf16[192,384]{1,0:T(8,128)(2,1)S(1)}, bf16[192,384]{1,0:T(8,128)(2,1)}, u32[]{:S(2)}, u32[]{:S(2)}) collective-permute-start(bf16[192,384]{1,0:T(8,128)(2,1)S(1)} %cut_proj.1.refs_0_), channel_id=1, source_target_pairs={{0,2},{1,3},{2,0},{3,1},{4,6},{5,7},{6,4},{7,5},{8,10},{9,11},{10,... | collective-permute-start | bytes 442376 | tf_op jit(solution)/shard_map/ppermute | solution.py:37
  6.1 0.7 pad_add_fusion.scalars.refs_0_
  6.8 1.4 copy-done.1
  8.2 2.7 %norm_half.2.refs_0_.na_ref = bf16[768,512]{1,0:T(8,128)(2,1)S(1)} custom-call(s32[10]{0:T(128)S(1)} %pad_add_fusion.scalars.refs_0_, bf16[512,1536]{1,0:T(8,128)(2,1)S(1)} %bitcast.13, bf16[192,384]{1,0:T(8,128)(2,1)S(1)} %cut_proj.1.refs_0_), custom_call_target="tpu_custom_call" | custom-call | tf_op jit(solution)/shard_map/norm_half/pallas_call | solution.py:227
  10.9 2.7 %norm_half.3.nb_ref = bf16[768,512]{1,0:T(8,128)(2,1)S(1)} custom-call(s32[10]{0:T(128)S(1)} %pad_add_fusion.scalars.refs_0_, bf16[512,1536]{1,0:T(8,128)(2,1)S(1)} %collective-permute-done.3.x_ref, bf16[768,512]{1,0:T(8,128)(2,1)S(1)} %norm_half.2.refs_0_.na_ref), custom_call_target="tpu_custom_call" | custom-call | tf_op jit(solution)/shard_map/norm_half/pallas_call | solution.py:227
  13.6 5.2 %outer_pieces.1 = (f32[2,384,384]{2,1,0:T(8,128)S(1)}, bf16[2,384,384]{2,1,0:T(8,128)(2,1)S(1)}, f32[2,384,384]{2,1,0:T(8,128)S(1)}, bf16[2,384,384]{2,1,0:T(8,128)(2,1)S(1)}) custom-call(s32[10]{0:T(128)S(1)} %pad_add_fusion.scalars.refs_0_, bf16[768,512]{1,0:T(8,128)(2,1)S(1)} %norm_half.2.refs_0_.na_ref, bf16[768,512]{1,0:T(8,128)(2,1)S(1)} %norm_half.3.nb_ref, ...), custom_call_target="tpu_custom_call" | custom-call | tf_op jit(solution)/shard_map/outer_pieces/pallas_call | solution.py:253
  19.0 1.2 halves.1
  20.2 1.3 collective-permute-start.5
  21.4 1.2 collective-permute-start.6
  22.7 2.4 %collective-permute-start.7 = (bf16[480,384]{1,0:T(8,128)(2,1)S(1)}, bf16[480,384]{1,0:T(8,128)(2,1)S(1)}, u32[]{:S(2)}, u32[]{:S(2)}) collective-permute-start(bf16[480,384]{1,0:T(8,128)(2,1)S(1)} %get-tuple-element.36.refs_6_), channel_id=1, source_target_pairs={{0,4},{1,5},{2,6},{3,7},{4,0},{5,1},{6,2},{7,3},{8,12},{9,13},{10,... | collective-permute-start | bytes 1105928 | tf_op jit(solution)/shard_map/ppermute | solution.py:37
  25.0 6.3 %plan.1.refs_10_.refs_0_.scalars = s32[195]{0:T(256)S(1)} custom-call(s32[10]{0:T(128)S(1)} %pad_add_fusion.scalars.refs_0_), custom_call_target="tpu_custom_call" | custom-call | tf_op jit(solution)/shard_map/plan/pallas_call | solution.py:434
  31.4 9.6 %collective-permute-done.7.refs_7_ = bf16[480,384]{1,0:T(8,128)(2,1)S(1)} collective-permute-done((bf16[480,384]{1,0:T(8,128)(2,1)S(1)}, bf16[480,384]{1,0:T(8,128)(2,1)S(1)}, u32[]{:S(2)}, u32[]{:S(2)}) %collective-permute-start.7) | collective-permute-done | bytes 368672 | tf_op jit(solution)/shard_map/ppermute | solution.py:37
  41.0 0.6 site_step.1
  41.6 1.0 collective-permute-start.8
  42.6 1.3 collective-permute-start.10
  44.1 0.4 collective-permute-start.9
  44.5 16.2 %collective-permute-done.10.ra_ref.refs_2_.refs_4_ = bf16[960,384]{1,0:T(8,128)(2,1)S(1)} collective-permute-done((bf16[960,384]{1,0:T(8,128)(2,1)S(1)}, bf16[960,384]{1,0:T(8,128)(2,1)S(1)}, u32[]{:S(2)}, u32[]{:S(2)}) %collective-permute-start.10) | collective-permute-done | bytes 737312 | tf_op jit(solution)/shard_map/ppermute | solution.py:41
  60.7 0.9 collective-permute-done.11.rb_ref.refs_3_.refs_5_
  61.6 0.7 site_sum.1
  62.6 1.2 collective-permute-start.15
  63.9 0.4 collective-permute-start.16
  64.2 1.2 collective-permute-start.14
  65.4 0.7 collective-permute-start.13
  66.1 0.8 collective-permute-start.12
  66.9 7.0 %input_gradient.1.refs_0_.refs_3_.refs_7_ = bf16[512,1536]{1,0:T(8,128)(2,1)S(1)} custom-call(s32[10]{0:T(128)S(1)} %pad_add_fusion.scalars.refs_0_, bf16[192,1536]{1,0:T(8,128)(2,1)S(1)} %copy-done.4, bf16[960,384]{1,0:T(8,128)(2,1)S(1)} %get-tuple-element.41.refs_2_, bf16[960,384]{1,0:T(8,128)(2,1)S(1)} %get-tuple-element.42.refs_3_, ...), custom_call_target="tpu_custom_call" | custom-call | tf_op jit(solution)/shard_map/input_gradient/pallas_call | solution.py:375
  73.9 0.6 near_sum.1
  74.5 2.7 %collective-permute-done.13.refs_1_ = bf16[3,96,384]{2,1,0:T(8,128)(2,1)S(1)} collective-permute-done((bf16[3,96,384]{2,1,0:T(8,128)(2,1)S(1)}, bf16[3,96,384]{2,1,0:T(8,128)(2,1)S(1)}, u32[]{:S(2)}, u32[]{:S(2)}) %collective-permute-start.13) | collective-permute-done | bytes 221216 | tf_op jit(solution)/shard_map/ppermute | solution.py:41
  77.3 0.6 collective-permute-start.18
  77.9 2.0 %collective-permute-start.26 = (bf16[192,384]{1,0:T(8,128)(2,1)S(1)}, bf16[192,384]{1,0:T(8,128)(2,1)S(1)}, u32[]{:S(2)}, u32[]{:S(2)}) collective-permute-start(bf16[192,384]{1,0:T(8,128)(2,1)S(1)} %get-tuple-element.50.refs_4_), channel_id=1, source_target_pairs={{0,4},{1,5},{2,6},{3,7},{4,0},{5,1},{6,2},{7,3},{8,12},{9,13},{10,... | collective-permute-start | bytes 442376 | tf_op jit(solution)/shard_map/ppermute | solution.py:37
  79.9 5.9 %stem_payloads.1 = (bf16[17,16,512]{2,1,0:T(8,128)(2,1)S(1)}, bf16[17,16,512]{2,1,0:T(8,128)(2,1)S(1)}, bf16[17,16,512]{2,1,0:T(8,128)(2,1)S(1)}, bf16[17,16,512...) custom-call(s32[195]{0:T(256)S(1)} %plan.1.refs_10_.refs_0_.scalars,, ...), custom_call_target="tpu_custom_call" | custom-call | tf_op jit(solution)/shard_map/stem_payloads/pallas_call | solution.py:487
  85.8 1.8 %collective-permute-start.19 = (bf16[17,16,512]{2,1,0:T(8,128)(2,1)S(1)}, bf16[17,16,512]{2,1,0:T(8,128)(2,1)S(1)}, u32[]{:S(2)}, u32[]{:S(2)}) collective-permute-start(bf16[17,16,512]{2,1,0:T(8,128)(2,1)S(1)} %get-tuple-element.52), channel_id=1, source_target_pairs={{0,4},{1,5},{2,6},{3,7},{4,0},{5,1},{6,2},{7,3},{8,12},{9,13},{10,... | collective-permute-start | bytes 835592 | tf_op jit(solution)/shard_map/ppermute | solution.py:642
  87.6 1.2 collective-permute-start.20
  88.8 1.5 %collective-permute-start.21 = (bf16[17,16,512]{2,1,0:T(8,128)(2,1)S(1)}, bf16[17,16,512]{2,1,0:T(8,128)(2,1)S(1)}, u32[]{:S(2)}, u32[]{:S(2)}) collective-permute-start(bf16[17,16,512]{2,1,0:T(8,128)(2,1)S(1)} %get-tuple-element.54), channel_id=1, source_target_pairs={{0,2},{1,3},{2,0},{3,1},{4,6},{5,7},{6,4},{7,5},{8,10},{9,11},{10,... | collective-permute-start | bytes 835592 | tf_op jit(solution)/shard_map/ppermute | solution.py:642
  90.3 2.0 %collective-permute-start.23 = (bf16[17,16,512]{2,1,0:T(8,128)(2,1)S(1)}, bf16[17,16,512]{2,1,0:T(8,128)(2,1)S(1)}, u32[]{:S(2)}, u32[]{:S(2)}) collective-permute-start(bf16[17,16,512]{2,1,0:T(8,128)(2,1)S(1)} %get-tuple-element.56), channel_id=1, source_target_pairs={{0,6},{1,7},{2,4},{3,5},{4,2},{5,3},{6,0},{7,1},{8,14},{9,15},{10,... | collective-permute-start | bytes 835592 | tf_op jit(solution)/shard_map/ppermute | solution.py:642
  92.3 13.0 %collective-permute-done.19.refs_3_.refs_1_ = bf16[17,16,512]{2,1,0:T(8,128)(2,1)S(1)} collective-permute-done((bf16[17,16,512]{2,1,0:T(8,128)(2,1)S(1)}, bf16[17,16,512]{2,1,0:T(8,128)(2,1)S(1)}, u32[]{:S(2)}, u32[]{:S(2)}) %collective-permute-start.19) | collective-permute-done | bytes 278560 | tf_op jit(solution)/shard_map/ppermute | solution.py:642
  105.3 0.6 far_sum.1.refs_8_
  105.8 1.0 collective-permute-start.29
  106.8 4.4 %collective-permute-done.20.refs_2_ = bf16[17,16,512]{2,1,0:T(8,128)(2,1)S(1)} collective-permute-done((bf16[17,16,512]{2,1,0:T(8,128)(2,1)S(1)}, bf16[17,16,512]{2,1,0:T(8,128)(2,1)S(1)}, u32[]{:S(2)}, u32[]{:S(2)}) %collective-permute-start.20) | collective-permute-done | bytes 278560 | tf_op jit(solution)/shard_map/ppermute | solution.py:642
  111.2 0.5 collective-permute-start.28
  111.8 0.7 collective-permute-start.27
  112.4 7.7 %collective-permute-done.22.refs_4_ = bf16[17,16,512]{2,1,0:T(8,128)(2,1)S(1)} collective-permute-done((bf16[17,16,512]{2,1,0:T(8,128)(2,1)S(1)}, bf16[17,16,512]{2,1,0:T(8,128)(2,1)S(1)}, u32[]{:S(2)}, u32[]{:S(2)}) %collective-permute-start.22) | collective-permute-done | bytes 278560 | tf_op jit(solution)/shard_map/ppermute | solution.py:642
  120.2 5.1 %collective-permute-done.23.refs_5_ = bf16[17,16,512]{2,1,0:T(8,128)(2,1)S(1)} collective-permute-done((bf16[17,16,512]{2,1,0:T(8,128)(2,1)S(1)}, bf16[17,16,512]{2,1,0:T(8,128)(2,1)S(1)}, u32[]{:S(2)}, u32[]{:S(2)}) %collective-permute-start.23) | collective-permute-done | bytes 278560 | tf_op jit(solution)/shard_map/ppermute | solution.py:642
  125.3 5.9 %collective-permute-start.25 = (bf16[17,16,512]{2,1,0:T(8,128)(2,1)S(1)}, bf16[17,16,512]{2,1,0:T(8,128)(2,1)S(1)}, u32[]{:S(2)}, u32[]{:S(2)}) collective-permute-start(bf16[17,16,512]{2,1,0:T(8,128)(2,1)S(1)} %get-tuple-element.58), channel_id=1, source_target_pairs={{0,1},{1,0},{2,3},{3,2},{4,5},{5,4},{6,7},{7,6},{8,9},{9,8},{10,11... | collective-permute-start | bytes 835592 | tf_op jit(solution)/shard_map/ppermute | solution.py:642
  131.1 6.1 %collective-permute-done.24.refs_6_ = bf16[17,16,512]{2,1,0:T(8,128)(2,1)S(1)} collective-permute-done((bf16[17,16,512]{2,1,0:T(8,128)(2,1)S(1)}, bf16[17,16,512]{2,1,0:T(8,128)(2,1)S(1)}, u32[]{:S(2)}, u32[]{:S(2)}) %collective-permute-start.24) | collective-permute-done | bytes 278560 | tf_op jit(solution)/shard_map/ppermute | solution.py:642
  137.3 4.2 %owner_rows.1 = (bf16[2048,512]{1,0:T(8,128)(2,1)}, f32[192,1536]{1,0:T(8,128)}) custom-call(s32[195]{0:T(256)S(1)} %plan.1.refs_10_.refs_0_.scalars, bf16[17,16,512]{2,1,0:T(8,128)(2,1)S(1)} %get-tuple-element.51.refs_0_, bf16[17,16,512]{2,1,0:T(8,128)(2,1)S(1)} %collective-permute-done.19.refs_3_.refs_1_, ...), custom_call_target="tpu_custom_call" | custom-call | tf_op jit(solution)/shard_map/owner_rows/pallas_call | solution.py:557
  (40 shorter events, 0.8 us)
Async XLA Ops:
  0.6 10.3 %collective-permute-start.3 = (bf16[512,1536]{1,0:T(8,128)(2,1)}, bf16[512,1536]{1,0:T(8,128)(2,1)S(1)}, u32[]{:S(2)}, u32[]{:S(2)}) collective-permute-start(bf16[512,1536]{1,0:T(8,128)(2,1)} %bitcast.12), channel_id=1, source_target_pairs={{0,1},{1,0},{2,3},{3,2},{4,5},{5,4},{6,7},{7,6},{8,9},{9,8},{10,11... | collective-permute-start | bytes 4718600 | tf_op jit(solution)/shard_map/ppermute | solution.py:33
  1.4 12.3 %collective-permute-start.4 = (bf16[512,1536]{1,0:T(8,128)(2,1)}, bf16[512,1536]{1,0:T(8,128)(2,1)S(1)}, u32[]{:S(2)}, u32[]{:S(2)}) collective-permute-start(bf16[512,1536]{1,0:T(8,128)(2,1)} %bitcast.9), channel_id=1, source_target_pairs={{0,1},{1,0},{2,3},{3,2},{4,5},{5,4},{6,7},{7,6},{8,9},{9,8},{10,11... | collective-permute-start | bytes 4718600 | tf_op jit(solution)/shard_map/ppermute | solution.py:33
  1.5 1.1 copy-start.3
  2.5 16.4 %collective-permute-start.2 = (bf16[192,384]{1,0:T(8,128)(2,1)S(1)}, bf16[192,384]{1,0:T(8,128)(2,1)S(1)}, u32[]{:S(2)}, u32[]{:S(2)}) collective-permute-start(bf16[192,384]{1,0:T(8,128)(2,1)S(1)} %cut_proj.1.refs_0_), channel_id=1, source_target_pairs={{0,6},{1,7},{2,4},{3,5},{4,2},{5,3},{6,0},{7,1},{8,14},{9,15},{10,... | collective-permute-start | bytes 442376 | tf_op jit(solution)/shard_map/ppermute | solution.py:37
  3.9 15.0 %collective-permute-start.1 = (bf16[192,384]{1,0:T(8,128)(2,1)S(1)}, bf16[192,384]{1,0:T(8,128)(2,1)}, u32[]{:S(2)}, u32[]{:S(2)}) collective-permute-start(bf16[192,384]{1,0:T(8,128)(2,1)S(1)} %cut_proj.1.refs_0_), channel_id=1, source_target_pairs={{0,2},{1,3},{2,0},{3,1},{4,6},{5,7},{6,4},{7,5},{8,10},{9,11},{10,... | collective-permute-start | bytes 442376 | tf_op jit(solution)/shard_map/ppermute | solution.py:37
  6.1 12.8 %collective-permute-start = (bf16[192,384]{1,0:T(8,128)(2,1)S(1)}, bf16[192,384]{1,0:T(8,128)(2,1)}, u32[]{:S(2)}, u32[]{:S(2)}) collective-permute-start(bf16[192,384]{1,0:T(8,128)(2,1)S(1)} %cut_proj.1.refs_0_), channel_id=1, source_target_pairs={{0,4},{1,5},{2,6},{3,7},{4,0},{5,1},{6,2},{7,3},{8,12},{9,13},{10,... | collective-permute-start | bytes 442376 | tf_op jit(solution)/shard_map/ppermute | solution.py:37
  6.8 1.4 copy-start.1
  10.9 2.7 %copy-start = (bf16[1,512,1536]{2,1,0:T(8,128)(2,1)S(1)}, bf16[1,512,1536]{2,1,0:T(8,128)(2,1)}, u32[]{:S(2)}) copy-start(bf16[1,512,1536]{2,1,0:T(8,128)(2,1)} %param.6) | copy-start | bytes 4718596
  13.6 5.3 %copy-start.5 = (bf16[3,64,1536]{2,1,0:T(8,128)(2,1)S(1)}, bf16[3,64,1536]{2,1,0:T(8,128)(2,1)}, u32[]{:S(2)}) copy-start(bf16[3,64,1536]{2,1,0:T(8,128)(2,1)} %refs_1_.2) | copy-start | bytes 1769476
  18.9 22.1 %copy-start.4 = (bf16[192,1536]{1,0:T(8,128)(2,1)S(1)}, bf16[192,1536]{1,0:T(8,128)(2,1)}, u32[]{:S(2)}) copy-start(bf16[192,1536]{1,0:T(8,128)(2,1)} %refs_1_.3) | copy-start | bytes 1769476
  20.2 20.8 %collective-permute-start.5 = (bf16[1056,384]{1,0:T(8,128)(2,1)S(1)}, bf16[1056,384]{1,0:T(8,128)(2,1)S(1)}, u32[]{:S(2)}, u32[]{:S(2)}) collective-permute-start(bf16[1056,384]{1,0:T(8,128)(2,1)S(1)} %get-tuple-element.34.refs_2_), channel_id=1, source_target_pairs={{0,8},{8,0},{16,24},{24,16},{1,9},{9,1},{17,25},{25,17},{2,10},{10... | collective-permute-start | bytes 2433032 | tf_op jit(solution)/shard_map/ppermute | solution.py:41
  21.4 19.5 %collective-permute-start.6 = (bf16[1056,384]{1,0:T(8,128)(2,1)S(1)}, bf16[1056,384]{1,0:T(8,128)(2,1)S(1)}, u32[]{:S(2)}, u32[]{:S(2)}) collective-permute-start(bf16[1056,384]{1,0:T(8,128)(2,1)S(1)} %get-tuple-element.35.refs_3_), channel_id=1, source_target_pairs={{0,16},{8,24},{16,0},{24,8},{1,17},{9,25},{17,1},{25,9},{2,18},{10... | collective-permute-start | bytes 2433032 | tf_op jit(solution)/shard_map/ppermute | solution.py:41
  22.7 18.3 %collective-permute-start.7 = (bf16[480,384]{1,0:T(8,128)(2,1)S(1)}, bf16[480,384]{1,0:T(8,128)(2,1)S(1)}, u32[]{:S(2)}, u32[]{:S(2)}) collective-permute-start(bf16[480,384]{1,0:T(8,128)(2,1)S(1)} %get-tuple-element.36.refs_6_), channel_id=1, source_target_pairs={{0,4},{1,5},{2,6},{3,7},{4,0},{5,1},{6,2},{7,3},{8,12},{9,13},{10,... | collective-permute-start | bytes 1105928 | tf_op jit(solution)/shard_map/ppermute | solution.py:37
  41.6 20.8 %collective-permute-start.8 = (bf16[2688,384]{1,0:T(8,128)(2,1)S(1)}, bf16[2688,384]{1,0:T(8,128)(2,1)S(1)}, u32[]{:S(2)}, u32[]{:S(2)}) collective-permute-start(bf16[2688,384]{1,0:T(8,128)(2,1)S(1)} %get-tuple-element.39), channel_id=1, source_target_pairs={{0,1},{1,0},{2,3},{3,2},{4,5},{5,4},{6,7},{7,6},{8,9},{9,8},{10,11... | collective-permute-start | bytes 6193160 | tf_op jit(solution)/shard_map/ppermute | solution.py:33
  42.6 18.1 %collective-permute-start.10 = (bf16[960,384]{1,0:T(8,128)(2,1)S(1)}, bf16[960,384]{1,0:T(8,128)(2,1)S(1)}, u32[]{:S(2)}, u32[]{:S(2)}) collective-permute-start(bf16[960,384]{1,0:T(8,128)(2,1)S(1)} %get-tuple-element.41.refs_2_), channel_id=1, source_target_pairs={{0,16},{8,24},{16,0},{24,8},{1,17},{9,25},{17,1},{25,9},{2,18},{10... | collective-permute-start | bytes 2211848 | tf_op jit(solution)/shard_map/ppermute | solution.py:41
  43.8 17.7 %collective-permute-start.11 = (bf16[960,384]{1,0:T(8,128)(2,1)S(1)}, bf16[960,384]{1,0:T(8,128)(2,1)S(1)}, u32[]{:S(2)}, u32[]{:S(2)}) collective-permute-start(bf16[960,384]{1,0:T(8,128)(2,1)S(1)} %get-tuple-element.42.refs_3_), channel_id=1, source_target_pairs={{0,8},{8,0},{16,24},{24,16},{1,9},{9,1},{17,25},{25,17},{2,10},{10... | collective-permute-start | bytes 2211848 | tf_op jit(solution)/shard_map/ppermute | solution.py:41
  44.1 18.2 %collective-permute-start.9 = (bf16[2,480,384]{2,1,0:T(8,128)(2,1)S(1)}, bf16[2,480,384]{2,1,0:T(8,128)(2,1)S(1)}, u32[]{:S(2)}, u32[]{:S(2)}) collective-permute-start(bf16[2,480,384]{2,1,0:T(8,128)(2,1)S(1)} %get-tuple-element.40.refs_0_), channel_id=1, source_target_pairs={{0,2},{1,3},{2,0},{3,1},{4,6},{5,7},{6,4},{7,5},{8,10},{9,11},{10,... | collective-permute-start | bytes 2211848 | tf_op jit(solution)/shard_map/ppermute | solution.py:37
  62.3 4.5 %copy-start.2 = (bf16[1,512,1536]{2,1,0:T(8,128)(2,1)S(1)}, bf16[1,512,1536]{2,1,0:T(8,128)(2,1)}, u32[]{:S(2)}) copy-start(bf16[1,512,1536]{2,1,0:T(8,128)(2,1)} %param.5) | copy-start | bytes 4718596
  62.6 3.5 %collective-permute-start.15 = (bf16[1152,384]{1,0:T(8,128)(2,1)S(1)}, bf16[1152,384]{1,0:T(8,128)(2,1)S(1)}, u32[]{:S(2)}, u32[]{:S(2)}) collective-permute-start(bf16[1152,384]{1,0:T(8,128)(2,1)S(1)} %get-tuple-element.48), channel_id=1, source_target_pairs={{0,1},{1,0},{2,3},{3,2},{4,5},{5,4},{6,7},{7,6},{8,9},{9,8},{10,11... | collective-permute-start | bytes 2654216 | tf_op jit(solution)/shard_map/ppermute | solution.py:33
  63.8 13.4 %collective-permute-start.17 = (bf16[1440,384]{1,0:T(8,128)(2,1)S(1)}, bf16[1440,384]{1,0:T(8,128)(2,1)S(1)}, u32[]{:S(2)}, u32[]{:S(2)}) collective-permute-start(bf16[1440,384]{1,0:T(8,128)(2,1)S(1)} %bitcast.18), channel_id=1, source_target_pairs={{0,1},{1,0},{2,3},{3,2},{4,5},{5,4},{6,7},{7,6},{8,9},{9,8},{10,11... | collective-permute-start | bytes 3317768 | tf_op jit(solution)/shard_map/ppermute | solution.py:33
  63.9 10.0 %collective-permute-start.16 = (bf16[2,192,384]{2,1,0:T(8,128)(2,1)S(1)}, bf16[2,192,384]{2,1,0:T(8,128)(2,1)S(1)}, u32[]{:S(2)}, u32[]{:S(2)}) collective-permute-start(bf16[2,192,384]{2,1,0:T(8,128)(2,1)S(1)} %get-tuple-element.49), channel_id=1, source_target_pairs={{0,2},{1,3},{2,0},{3,1},{4,6},{5,7},{6,4},{7,5},{8,10},{9,11},{10,... | collective-permute-start | bytes 884744 | tf_op jit(solution)/shard_map/ppermute | solution.py:37
  64.2 10.3 %collective-permute-start.14 = (bf16[3,96,384]{2,1,0:T(8,128)(2,1)S(1)}, bf16[3,96,384]{2,1,0:T(8,128)(2,1)S(1)}, u32[]{:S(2)}, u32[]{:S(2)}) collective-permute-start(bf16[3,96,384]{2,1,0:T(8,128)(2,1)S(1)} %get-tuple-element.47), channel_id=1, source_target_pairs={{0,24},{8,16},{16,8},{24,0},{1,25},{9,17},{17,9},{25,1},{2,26},{10... | collective-permute-start | bytes 663560 | tf_op jit(solution)/shard_map/ppermute | solution.py:41
  65.4 11.8 %collective-permute-start.13 = (bf16[3,96,384]{2,1,0:T(8,128)(2,1)S(1)}, bf16[3,96,384]{2,1,0:T(8,128)(2,1)S(1)}, u32[]{:S(2)}, u32[]{:S(2)}) collective-permute-start(bf16[3,96,384]{2,1,0:T(8,128)(2,1)S(1)} %get-tuple-element.47), channel_id=1, source_target_pairs={{0,16},{8,24},{16,0},{24,8},{1,17},{9,25},{17,1},{25,9},{2,18},{10... | collective-permute-start | bytes 663560 | tf_op jit(solution)/shard_map/ppermute | solution.py:41
  66.1 11.1 %collective-permute-start.12 = (bf16[3,96,384]{2,1,0:T(8,128)(2,1)S(1)}, bf16[3,96,384]{2,1,0:T(8,128)(2,1)S(1)}, u32[]{:S(2)}, u32[]{:S(2)}) collective-permute-start(bf16[3,96,384]{2,1,0:T(8,128)(2,1)S(1)} %get-tuple-element.47), channel_id=1, source_target_pairs={{0,8},{8,0},{16,24},{24,16},{1,9},{9,1},{17,25},{25,17},{2,10},{10... | collective-permute-start | bytes 663560 | tf_op jit(solution)/shard_map/ppermute | solution.py:41
  77.3 2.6 %collective-permute-start.18 = (bf16[864,384]{1,0:T(8,128)(2,1)S(1)}, bf16[864,384]{1,0:T(8,128)(2,1)S(1)}, u32[]{:S(2)}, u32[]{:S(2)}) collective-permute-start(bf16[864,384]{1,0:T(8,128)(2,1)S(1)} %bitcast.16), channel_id=1, source_target_pairs={{0,1},{1,0},{2,3},{3,2},{4,5},{5,4},{6,7},{7,6},{8,9},{9,8},{10,11... | collective-permute-start | bytes 1990664 | tf_op jit(solution)/shard_map/ppermute | solution.py:33
  77.9 12.5 %collective-permute-start.26 = (bf16[192,384]{1,0:T(8,128)(2,1)S(1)}, bf16[192,384]{1,0:T(8,128)(2,1)S(1)}, u32[]{:S(2)}, u32[]{:S(2)}) collective-permute-start(bf16[192,384]{1,0:T(8,128)(2,1)S(1)} %get-tuple-element.50.refs_4_), channel_id=1, source_target_pairs={{0,4},{1,5},{2,6},{3,7},{4,0},{5,1},{6,2},{7,3},{8,12},{9,13},{10,... | collective-permute-start | bytes 442376 | tf_op jit(solution)/shard_map/ppermute | solution.py:37
  85.8 19.4 %collective-permute-start.19 = (bf16[17,16,512]{2,1,0:T(8,128)(2,1)S(1)}, bf16[17,16,512]{2,1,0:T(8,128)(2,1)S(1)}, u32[]{:S(2)}, u32[]{:S(2)}) collective-permute-start(bf16[17,16,512]{2,1,0:T(8,128)(2,1)S(1)} %get-tuple-element.52), channel_id=1, source_target_pairs={{0,4},{1,5},{2,6},{3,7},{4,0},{5,1},{6,2},{7,3},{8,12},{9,13},{10,... | collective-permute-start | bytes 835592 | tf_op jit(solution)/shard_map/ppermute | solution.py:642
  87.6 23.6 %collective-permute-start.20 = (bf16[17,16,512]{2,1,0:T(8,128)(2,1)S(1)}, bf16[17,16,512]{2,1,0:T(8,128)(2,1)S(1)}, u32[]{:S(2)}, u32[]{:S(2)}) collective-permute-start(bf16[17,16,512]{2,1,0:T(8,128)(2,1)S(1)} %get-tuple-element.53), channel_id=1, source_target_pairs={{0,5},{1,4},{2,7},{3,6},{4,1},{5,0},{6,3},{7,2},{8,13},{9,12},{10,... | collective-permute-start | bytes 835592 | tf_op jit(solution)/shard_map/ppermute | solution.py:642
  88.8 23.0 %collective-permute-start.21 = (bf16[17,16,512]{2,1,0:T(8,128)(2,1)S(1)}, bf16[17,16,512]{2,1,0:T(8,128)(2,1)S(1)}, u32[]{:S(2)}, u32[]{:S(2)}) collective-permute-start(bf16[17,16,512]{2,1,0:T(8,128)(2,1)S(1)} %get-tuple-element.54), channel_id=1, source_target_pairs={{0,2},{1,3},{2,0},{3,1},{4,6},{5,7},{6,4},{7,5},{8,10},{9,11},{10,... | collective-permute-start | bytes 835592 | tf_op jit(solution)/shard_map/ppermute | solution.py:642
  90.2 29.9 %collective-permute-start.22 = (bf16[17,16,512]{2,1,0:T(8,128)(2,1)S(1)}, bf16[17,16,512]{2,1,0:T(8,128)(2,1)S(1)}, u32[]{:S(2)}, u32[]{:S(2)}) collective-permute-start(bf16[17,16,512]{2,1,0:T(8,128)(2,1)S(1)} %get-tuple-element.55), channel_id=1, source_target_pairs={{0,3},{1,2},{2,1},{3,0},{4,7},{5,6},{6,5},{7,4},{8,11},{9,10},{10,... | collective-permute-start | bytes 835592 | tf_op jit(solution)/shard_map/ppermute | solution.py:642
  90.3 35.0 %collective-permute-start.23 = (bf16[17,16,512]{2,1,0:T(8,128)(2,1)S(1)}, bf16[17,16,512]{2,1,0:T(8,128)(2,1)S(1)}, u32[]{:S(2)}, u32[]{:S(2)}) collective-permute-start(bf16[17,16,512]{2,1,0:T(8,128)(2,1)S(1)} %get-tuple-element.56), channel_id=1, source_target_pairs={{0,6},{1,7},{2,4},{3,5},{4,2},{5,3},{6,0},{7,1},{8,14},{9,15},{10,... | collective-permute-start | bytes 835592 | tf_op jit(solution)/shard_map/ppermute | solution.py:642
  105.8 31.4 %collective-permute-start.29 = (f32[192,384]{1,0:T(8,128)S(1)}, f32[192,384]{1,0:T(8,128)S(1)}, u32[]{:S(2)}, u32[]{:S(2)}) collective-permute-start(f32[192,384]{1,0:T(8,128)S(1)} %far_sum.1.refs_8_), channel_id=1, source_target_pairs={{0,24},{8,16},{16,8},{24,0},{1,25},{9,17},{17,9},{25,1},{2,26},{10... | collective-permute-start | bytes 884744 | tf_op jit(solution)/shard_map/ppermute | solution.py:41
  111.2 26.0 %collective-permute-start.28 = (f32[192,384]{1,0:T(8,128)S(1)}, f32[192,384]{1,0:T(8,128)S(1)}, u32[]{:S(2)}, u32[]{:S(2)}) collective-permute-start(f32[192,384]{1,0:T(8,128)S(1)} %far_sum.1.refs_8_), channel_id=1, source_target_pairs={{0,16},{8,24},{16,0},{24,8},{1,17},{9,25},{17,1},{25,9},{2,18},{10... | collective-permute-start | bytes 884744 | tf_op jit(solution)/shard_map/ppermute | solution.py:41
  111.8 25.5 %collective-permute-start.27 = (f32[192,384]{1,0:T(8,128)S(1)}, f32[192,384]{1,0:T(8,128)S(1)}, u32[]{:S(2)}, u32[]{:S(2)}) collective-permute-start(f32[192,384]{1,0:T(8,128)S(1)} %far_sum.1.refs_8_), channel_id=1, source_target_pairs={{0,8},{8,0},{16,24},{24,16},{1,9},{9,1},{17,25},{25,17},{2,10},{10... | collective-permute-start | bytes 884744 | tf_op jit(solution)/shard_map/ppermute | solution.py:41
  120.1 17.1 %collective-permute-start.24 = (bf16[17,16,512]{2,1,0:T(8,128)(2,1)S(1)}, bf16[17,16,512]{2,1,0:T(8,128)(2,1)S(1)}, u32[]{:S(2)}, u32[]{:S(2)}) collective-permute-start(bf16[17,16,512]{2,1,0:T(8,128)(2,1)S(1)} %get-tuple-element.57), channel_id=1, source_target_pairs={{0,7},{1,6},{2,5},{3,4},{4,3},{5,2},{6,1},{7,0},{8,15},{9,14},{10,... | collective-permute-start | bytes 835592 | tf_op jit(solution)/shard_map/ppermute | solution.py:642
  125.3 11.9 %collective-permute-start.25 = (bf16[17,16,512]{2,1,0:T(8,128)(2,1)S(1)}, bf16[17,16,512]{2,1,0:T(8,128)(2,1)S(1)}, u32[]{:S(2)}, u32[]{:S(2)}) collective-permute-start(bf16[17,16,512]{2,1,0:T(8,128)(2,1)S(1)} %get-tuple-element.58), channel_id=1, source_target_pairs={{0,1},{1,0},{2,3},{3,2},{4,5},{5,4},{6,7},{7,6},{8,9},{9,8},{10,11... | collective-permute-start | bytes 835592 | tf_op jit(solution)/shard_map/ppermute | solution.py:642

commit v5 on v4

--- a/solution.py
+++ b/solution.py
@@ -18,9 +18,9 @@
 CAP = OWN_SEG // N_FSDP
 CS = 512
 ROWS = HOLD * SEG
-BLOCK = 128
+BLOCK = 256
 LANES = 128
-COLUMNS = 768
+COLUMNS = 512
 PAYLOAD_ORDER = (0, 4, 5, 2, 3, 6, 7, 1)
 MIB = 1024 * 1024
 
@@ -127,7 +127,7 @@
     return lax.dot_general(a, b, (((1,), (1,)), ((), ())), preferred_element_type=F32)
 
 
-def join(kernel, name, out_dims, values, first=(), wide_dims=()):
+def join(kernel, name, out_dims, values, first=(), wide_dims=(), aliases=None):
     n = len(values)
 
     def wrapped(*refs):
@@ -141,6 +141,7 @@
         out_shape=out,
         in_specs=[vmem] * n + [ANY] * len(first),
         out_specs=(vmem,) * len(out),
+        input_output_aliases=aliases or {},
         compiler_params=pltpu.CompilerParams(vmem_limit_bytes=14 * MIB),
         cost_estimate=pl.CostEstimate(flops=0, bytes_accessed=0, transcendentals=0),
     )(*values, *first)
@@ -151,13 +152,10 @@
     out[...] = shard[:, pl.ds(at, QUARTER)]
 
 
-def halves_kernel(far, near, farthest, sent_a, sent_b, stem, a, b, units):
+def halves_kernel(_, __, far, near, farthest, stem, a, b, units):
     for i, piece in enumerate((far, near, farthest)):
         a[i * HALF : (i + 1) * HALF, :] = piece[:HALF, :]
         b[i * HALF : (i + 1) * HALF, :] = piece[HALF:, :]
-    for out, sent in ((a, sent_a), (b, sent_b)):
-        out[3 * HALF : 3 * HALF + D // 4, :] = sent[0]
-        out[3 * HALF + D // 4 :, :] = sent[1]
     at = pl.multiple_of(lax.axis_index("site") * QUARTER, QUARTER)
     pieces = [stem[tap, low : low + count, pl.ds(at, QUARTER)] for tap, low, count in QUARTER_BLOCKS]
     for tap, low, count in WHOLE_BLOCKS:
@@ -234,26 +232,33 @@
 OUTER_PLACES = (((0, 0), (0, 0)), ((1, 0), (0, 1)), ((0, 1), (1, 0)), ((1, 1), (1, 1)))
 
 
-def outer_kernel(scalars, na_ref, nb_ref, ca_ref, cb_ref, ka_ref, sa_ref, kb_ref, sb_ref):
-    step = pl.program_id(0)
-    total = jnp.dot(na_ref[...], ca_ref[...], preferred_element_type=F32)
-    total = total + jnp.dot(nb_ref[...], cb_ref[...], preferred_element_type=F32)
-    low, high = total[: D // 4, :], total[D // 4 :, :]
-    for at, (a, b) in enumerate(OUTER_PLACES):
-
-        @pl.when(step == at)
-        def _(a=a, b=b):
-            for (ref, i), value in (((ka_ref, sa_ref)[a[0]], a[1]), low), (((kb_ref, sb_ref)[b[0]], b[1]), high):
-                ref[i] = value.astype(ref.dtype)
+def outer_kernel(scalars, na_ref, nb_ref, ca_ref, cb_ref, ka_ref, a_ref, kb_ref, b_ref):
+    site = scalars[0]
+    n, m = 3 * HALF, D // 4
+    for half in range(2):
+        start = lax.bitwise_xor(site // 2, half) * 2 * QUARTER
+        columns = pl.ds(pl.multiple_of(start, 2 * QUARTER), 2 * QUARTER)
+        total = jnp.dot(na_ref[...], ca_ref[:, columns], preferred_element_type=F32)
+        total = total + jnp.dot(nb_ref[...], cb_ref[:, columns], preferred_element_type=F32)
+        low, high = total[:, :QUARTER], total[:, QUARTER:]
+        odd = site % 2 == 1
+        for at, value in ((2 * half, jnp.where(odd, high, low)), (2 * half + 1, jnp.where(odd, low, high))):
+            for (goes, i), kept, sent, rows in zip(
+                OUTER_PLACES[at], (ka_ref, kb_ref), (a_ref, b_ref), (value[:m, :], value[m:, :]), strict=True
+            ):
+                if goes:
+                    sent[n + i * m : n + (i + 1) * m, :] = rows.astype(BF16)
+                else:
+                    kept[i] = rows
 
 
 def outer_pieces(scalars, normed_a, normed_b, cotangent_a, cotangent_b):
-    dims = (2, D // 4, QUARTER)
-    column = pl.BlockSpec((ROWS, QUARTER), lambda i, scalars: (0, lax.bitwise_xor(scalars[0], i)))
-    return call(
-        outer_kernel, "outer_pieces", (shape(dims, F32), shape(dims, BF16)) * 2, (N_SITE,),
-        [whole((D // 2, ROWS))] * 2 + [column] * 2, (whole(dims),) * 4, [],
-    )(scalars, normed_a, normed_b, cotangent_a, cotangent_b)
+    kept, sent = (2, D // 4, QUARTER), (3 * HALF + D // 2, QUARTER)
+    values = (normed_a, normed_b, cotangent_a, cotangent_b)
+    return call(
+        outer_kernel, "outer_pieces", (shape(kept, F32), shape(sent, BF16)) * 2, (1,),
+        [whole(value.shape) for value in values], (whole(kept), whole(sent)) * 2, [], vmem=24,
+    )(scalars, *values)
 
 
 def site_sum_kernel(scalars, oa_ref, ra_ref, ob_ref, rb_ref, kept_ref, sent_ref, total):
@@ -352,18 +357,23 @@
     for copy in copies:
         copy.wait()
 
-    @pl.loop(0, D // COLUMNS)
-    def _(i):
-        rows = pl.ds(pl.multiple_of(i * COLUMNS, COLUMNS), COLUMNS)
-        back[:, rows] = dot_nt(cot_ref[...], weight[0, rows, :])
-
-    @pl.loop(0, ROWS // BLOCK)
-    def _(i):
-        rows = pl.ds(pl.multiple_of(i * BLOCK, BLOCK), BLOCK)
+    def finish(rows):
         term, row_normed = back[rows, :], normed[rows, :]
         inner = term - jnp.mean(term, axis=-1, keepdims=True)
         inner = inner - row_normed * jnp.mean(term * row_normed, axis=-1, keepdims=True)
         out_ref[rows, :] = (cot_ref[rows, :].astype(F32) + inverse[rows, :] * inner).astype(BF16)
+
+    half = ROWS // 2
+    for i in range(3):
+        if i < 2:
+            rows = slice(i * half, (i + 1) * half)
+            for j in range(D // COLUMNS):
+                columns = slice(j * COLUMNS, (j + 1) * COLUMNS)
+                back[rows, columns] = dot_nt(cot_ref[rows, :], weight[0, columns, :])
+        if i > 0:
+            for j in range(4):
+                start = (i - 1) * half + j * half // 4
+                finish(slice(start, start + half // 4))
 
 
 def split_parts(parts):
@@ -587,7 +597,7 @@
     n, m = 3 * HALF, D // 4
     a0, b0, stem_units = join(
         halves_kernel, "halves", [(n + 2 * m, QUARTER)] * 2 + [units],
-        [*around, sent_a, sent_b, stem_weight],
+        [sent_a, sent_b, *around, stem_weight], aliases={0: 0, 1: 1},
     )
 
     a, b, packed, stem_pair, own_a, own_b = join(

time: 142 us -> 140 us (0.986)
  Pallas kernels: 38.1 us -> 33.4 us
  starting transfers between devices: 33.5 us -> 35.1 us
    ppermute x7, starting transfers between devices: 8.66 us -> 12.5 us  [swap_z(): lax.ppermute(value, 'fsdp', [(i, i ^ 2 * distance) for i in range(N_FSDP)])]
    ppermute x7, starting transfers between devices: 12.3 us -> 10.3 us  [body(): lax.ppermute(payloads[d], 'fsdp', [(i, i ^ d) for i in range(N_FSDP)])]
    pallas_call x1, Pallas kernels: 5.24 us -> 3.24 us  [outer_pieces(): call(outer_kernel, 'outer_pieces', (shape(kept, F32), shape(sent, BF16))...]
  transfers between devices with their start and end apart: 30 -> 30, of which waited for: 9 -> 11; matrix products, arithmetic and copies ran while one was open for 1% -> 1% of each run, Pallas kernels for 22% -> 20%
where the time goes in v5:
time: 140 us; the launch traced here: 139 us
  waiting for transfers between devices  66.6 us (48%)
  starting transfers between devices  35.1 us (25%)
  Pallas kernels  33.4 us (24%)
  local copies, waits for them, and re-layouts  2.5 us (2%)
    ppermute x7, waiting for transfers between devices, body(): lax.ppermute(payloads[d], 'fsdp', [(i, i ^ d) for i in range(N_FSDP)])  37.3 us
    ppermute x10, waiting for transfers between devices, swap_site(): lax.ppermute(value, 'site', [(i, i ^ distance) for i in range(N_SITE)])  19 us
    ppermute x7, starting transfers between devices, swap_z(): lax.ppermute(value, 'fsdp', [(i, i ^ 2 * distance) for i in range(N_FSDP)])  12.5 us
    ppermute x7, starting transfers between devices, body(): lax.ppermute(payloads[d], 'fsdp', [(i, i ^ d) for i in range(N_FSDP)])  10.3 us
    ppermute x7, waiting for transfers between devices, swap_z(): lax.ppermute(value, 'fsdp', [(i, i ^ 2 * distance) for i in range(N_FSDP)])  9.37 us
    ppermute x10, starting transfers between devices, swap_site(): lax.ppermute(value, 'site', [(i, i ^ distance) for i in range(N_SITE)])  9 us
    pallas_call x1, Pallas kernels, plan_of(): call(plan_kernel, 'plan', shape((COUNT_AT + 1,), jnp.int32), (1,), [], pl...  6.34 us
    pallas_call x1, Pallas kernels, stem_payloads(): call(lambda *refs: stem_kernel(tables, *refs), 'stem_payloads', (shape(pa...  6.12 us
  transfers between devices with their start and end apart: 30, of which 11 were waited for; matrix products, arithmetic and copies ran while one was open for 1% of the time, Pallas kernels for 20%

profile of v5, /device:TPU:9, one launch (start us, length us, event | category | flops | bytes accessed | tf_op | source)
XLA Modules:
  0.0 139.4 jit_solution(13468377594381437596)
XLA Ops:
  0.6 0.7 collective-permute-start
  1.5 1.1 copy-done.3
  2.5 1.4 collective-permute-start.4
  3.9 2.2 %collective-permute-start.3 = (bf16[192,384]{1,0:T(8,128)(2,1)S(1)}, bf16[192,384]{1,0:T(8,128)(2,1)}, u32[]{:S(2)}, u32[]{:S(2)}) collective-permute-start(bf16[192,384]{1,0:T(8,128)(2,1)S(1)} %cut_proj.1.refs_0_), channel_id=1, source_target_pairs={{0,2},{1,3},{2,0},{3,1},{4,6},{5,7},{6,4},{7,5},{8,10},{9,11},{10,... | collective-permute-start | bytes 442376 | tf_op jit(solution)/shard_map/ppermute | solution.py:37
  6.1 0.7 pad_add_fusion.scalars.refs_0_
  6.8 1.4 %copy-done.1 = bf16[1,512,1536]{2,1,0:T(8,128)(2,1)S(1)} copy-done((bf16[1,512,1536]{2,1,0:T(8,128)(2,1)S(1)}, bf16[1,512,1536]{2,1,0:T(8,128)(2,1)}, u32[]{:S(2)}) %copy-start.1) | copy-done | bytes 1572888
  8.2 2.1 %norm_half.2.refs_0_.na_ref = bf16[768,512]{1,0:T(8,128)(2,1)S(1)} custom-call(s32[10]{0:T(128)S(1)} %pad_add_fusion.scalars.refs_0_, bf16[512,1536]{1,0:T(8,128)(2,1)S(1)} %bitcast.13, bf16[192,384]{1,0:T(8,128)(2,1)S(1)} %cut_proj.1.refs_0_), custom_call_target="tpu_custom_call" | custom-call | tf_op jit(solution)/shard_map/norm_half/pallas_call | solution.py:225
  10.3 2.1 %norm_half.3.nb_ref = bf16[768,512]{1,0:T(8,128)(2,1)S(1)} custom-call(s32[10]{0:T(128)S(1)} %pad_add_fusion.scalars.refs_0_, bf16[512,1536]{1,0:T(8,128)(2,1)S(1)} %collective-permute-done.x_ref, bf16[768,512]{1,0:T(8,128)(2,1)S(1)} %norm_half.2.refs_0_.na_ref), custom_call_target="tpu_custom_call" | custom-call | tf_op jit(solution)/shard_map/norm_half/pallas_call | solution.py:225
  12.4 3.2 %outer_pieces.1 = (f32[2,384,384]{2,1,0:T(8,128)S(1)}, bf16[1056,384]{1,0:T(8,128)(2,1)S(1)}, f32[2,384,384]{2,1,0:T(8,128)S(1)}, bf16[1056,384]{1,0:T(8,128)(2,1)S(1)}) custom-call(s32[10]{0:T(128)S(1)} %pad_add_fusion.scalars.refs_0_, bf16[768,512]{1,0:T(8,128)(2,1)S(1)} %norm_half.2.refs_0_.na_ref, bf16[768,512]{1,0:T(8,128)(2,1)S(1)} %norm_half.3.nb_ref, ...), custom_call_target="tpu_custom_call" | custom-call | tf_op jit(solution)/shard_map/outer_pieces/pallas_call | solution.py:258
  15.7 1.1 halves.1
  16.8 1.3 collective-permute-start.5
  18.1 1.2 collective-permute-start.6
  19.3 3.6 %collective-permute-start.7 = (bf16[480,384]{1,0:T(8,128)(2,1)S(1)}, bf16[480,384]{1,0:T(8,128)(2,1)S(1)}, u32[]{:S(2)}, u32[]{:S(2)}) collective-permute-start(bf16[480,384]{1,0:T(8,128)(2,1)S(1)} %get-tuple-element.36.refs_6_), channel_id=1, source_target_pairs={{0,4},{1,5},{2,6},{3,7},{4,0},{5,1},{6,2},{7,3},{8,12},{9,13},{10,... | collective-permute-start | bytes 1105928 | tf_op jit(solution)/shard_map/ppermute | solution.py:37
  22.9 6.3 %plan.1.refs_10_.refs_0_.scalars = s32[195]{0:T(256)S(1)} custom-call(s32[10]{0:T(128)S(1)} %pad_add_fusion.scalars.refs_0_), custom_call_target="tpu_custom_call" | custom-call | tf_op jit(solution)/shard_map/plan/pallas_call | solution.py:444
  29.3 8.7 %collective-permute-done.7.refs_7_ = bf16[480,384]{1,0:T(8,128)(2,1)S(1)} collective-permute-done((bf16[480,384]{1,0:T(8,128)(2,1)S(1)}, bf16[480,384]{1,0:T(8,128)(2,1)S(1)}, u32[]{:S(2)}, u32[]{:S(2)}) %collective-permute-start.7) | collective-permute-done | bytes 368672 | tf_op jit(solution)/shard_map/ppermute | solution.py:37
  38.5 0.6 collective-permute-start.8
  39.2 1.2 collective-permute-start.10
  40.7 2.6 %collective-permute-start.9 = (bf16[2,480,384]{2,1,0:T(8,128)(2,1)S(1)}, bf16[2,480,384]{2,1,0:T(8,128)(2,1)S(1)}, u32[]{:S(2)}, u32[]{:S(2)}) collective-permute-start(bf16[2,480,384]{2,1,0:T(8,128)(2,1)S(1)} %get-tuple-element.40.refs_0_), channel_id=1, source_target_pairs={{0,2},{1,3},{2,0},{3,1},{4,6},{5,7},{6,4},{7,5},{8,10},{9,11},{10,... | collective-permute-start | bytes 2211848 | tf_op jit(solution)/shard_map/ppermute | solution.py:37
  43.3 14.0 %collective-permute-done.10.ra_ref.refs_2_.refs_4_ = bf16[960,384]{1,0:T(8,128)(2,1)S(1)} collective-permute-done((bf16[960,384]{1,0:T(8,128)(2,1)S(1)}, bf16[960,384]{1,0:T(8,128)(2,1)S(1)}, u32[]{:S(2)}, u32[]{:S(2)}) %collective-permute-start.10) | collective-permute-done | bytes 737312 | tf_op jit(solution)/shard_map/ppermute | solution.py:41
  57.2 0.9 collective-permute-done.11.rb_ref.refs_3_.refs_5_
  58.2 0.7 site_sum.1
  58.9 0.6 collective-permute-done.9.refs_1_
  59.8 1.2 collective-permute-start.15
  61.1 2.0 %collective-permute-start.16 = (bf16[2,192,384]{2,1,0:T(8,128)(2,1)S(1)}, bf16[2,192,384]{2,1,0:T(8,128)(2,1)S(1)}, u32[]{:S(2)}, u32[]{:S(2)}) collective-permute-start(bf16[2,192,384]{2,1,0:T(8,128)(2,1)S(1)} %get-tuple-element.49), channel_id=1, source_target_pairs={{0,2},{1,3},{2,0},{3,1},{4,6},{5,7},{6,4},{7,5},{8,10},{9,11},{10,... | collective-permute-start | bytes 884744 | tf_op jit(solution)/shard_map/ppermute | solution.py:37
  63.1 1.0 collective-permute-start.14
  64.1 0.8 collective-permute-start.13
  64.9 0.8 collective-permute-start.12
  65.7 5.6 %input_gradient.1.refs_0_.refs_3_.refs_7_ = bf16[512,1536]{1,0:T(8,128)(2,1)S(1)} custom-call(s32[10]{0:T(128)S(1)} %pad_add_fusion.scalars.refs_0_, bf16[192,1536]{1,0:T(8,128)(2,1)S(1)} %copy-done.4, bf16[960,384]{1,0:T(8,128)(2,1)S(1)} %get-tuple-element.41.refs_2_, bf16[960,384]{1,0:T(8,128)(2,1)S(1)} %get-tuple-element.42.refs_3_, ...), custom_call_target="tpu_custom_call" | custom-call | tf_op jit(solution)/shard_map/input_gradient/pallas_call | solution.py:385
  71.3 0.6 near_sum.1
  72.0 4.1 %collective-permute-done.13.refs_1_ = bf16[3,96,384]{2,1,0:T(8,128)(2,1)S(1)} collective-permute-done((bf16[3,96,384]{2,1,0:T(8,128)(2,1)S(1)}, bf16[3,96,384]{2,1,0:T(8,128)(2,1)S(1)}, u32[]{:S(2)}, u32[]{:S(2)}) %collective-permute-start.13) | collective-permute-done | bytes 221216 | tf_op jit(solution)/shard_map/ppermute | solution.py:41
  76.7 0.7 collective-permute-start.26
  77.4 1.0 collective-permute-done.18.refs_6_
  78.4 6.1 %stem_payloads.1 = (bf16[17,16,512]{2,1,0:T(8,128)(2,1)S(1)}, bf16[17,16,512]{2,1,0:T(8,128)(2,1)S(1)}, bf16[17,16,512]{2,1,0:T(8,128)(2,1)S(1)}, bf16[17,16,512...) custom-call(s32[195]{0:T(256)S(1)} %plan.1.refs_10_.refs_0_.scalars,, ...), custom_call_target="tpu_custom_call" | custom-call | tf_op jit(solution)/shard_map/stem_payloads/pallas_call | solution.py:497
  84.5 0.8 collective-permute-start.19
  85.3 2.2 %collective-permute-start.20 = (bf16[17,16,512]{2,1,0:T(8,128)(2,1)S(1)}, bf16[17,16,512]{2,1,0:T(8,128)(2,1)S(1)}, u32[]{:S(2)}, u32[]{:S(2)}) collective-permute-start(bf16[17,16,512]{2,1,0:T(8,128)(2,1)S(1)} %get-tuple-element.53), channel_id=1, source_target_pairs={{0,5},{1,4},{2,7},{3,6},{4,1},{5,0},{6,3},{7,2},{8,13},{9,12},{10,... | collective-permute-start | bytes 835592 | tf_op jit(solution)/shard_map/ppermute | solution.py:652
  88.0 1.1 collective-permute-start.22
  89.0 1.0 collective-permute-start.23
  90.0 13.0 %collective-permute-done.19.refs_3_.refs_1_ = bf16[17,16,512]{2,1,0:T(8,128)(2,1)S(1)} collective-permute-done((bf16[17,16,512]{2,1,0:T(8,128)(2,1)S(1)}, bf16[17,16,512]{2,1,0:T(8,128)(2,1)S(1)}, u32[]{:S(2)}, u32[]{:S(2)}) %collective-permute-start.19) | collective-permute-done | bytes 278560 | tf_op jit(solution)/shard_map/ppermute | solution.py:652
  103.6 1.1 collective-permute-start.29
  104.6 4.3 %collective-permute-done.20.refs_2_ = bf16[17,16,512]{2,1,0:T(8,128)(2,1)S(1)} collective-permute-done((bf16[17,16,512]{2,1,0:T(8,128)(2,1)S(1)}, bf16[17,16,512]{2,1,0:T(8,128)(2,1)S(1)}, u32[]{:S(2)}, u32[]{:S(2)}) %collective-permute-start.20) | collective-permute-done | bytes 278560 | tf_op jit(solution)/shard_map/ppermute | solution.py:652
  109.0 0.6 collective-permute-start.28
  109.6 0.7 collective-permute-start.27
  110.2 2.5 %collective-permute-done.22.refs_4_ = bf16[17,16,512]{2,1,0:T(8,128)(2,1)S(1)} collective-permute-done((bf16[17,16,512]{2,1,0:T(8,128)(2,1)S(1)}, bf16[17,16,512]{2,1,0:T(8,128)(2,1)S(1)}, u32[]{:S(2)}, u32[]{:S(2)}) %collective-permute-start.22) | collective-permute-done | bytes 278560 | tf_op jit(solution)/shard_map/ppermute | solution.py:652
  112.8 1.2 collective-permute-start.24
  113.9 12.9 %collective-permute-done.23.refs_5_ = bf16[17,16,512]{2,1,0:T(8,128)(2,1)S(1)} collective-permute-done((bf16[17,16,512]{2,1,0:T(8,128)(2,1)S(1)}, bf16[17,16,512]{2,1,0:T(8,128)(2,1)S(1)}, u32[]{:S(2)}, u32[]{:S(2)}) %collective-permute-start.23) | collective-permute-done | bytes 278560 | tf_op jit(solution)/shard_map/ppermute | solution.py:652
  126.9 3.6 %collective-permute-start.25 = (bf16[17,16,512]{2,1,0:T(8,128)(2,1)S(1)}, bf16[17,16,512]{2,1,0:T(8,128)(2,1)S(1)}, u32[]{:S(2)}, u32[]{:S(2)}) collective-permute-start(bf16[17,16,512]{2,1,0:T(8,128)(2,1)S(1)} %get-tuple-element.58), channel_id=1, source_target_pairs={{0,1},{1,0},{2,3},{3,2},{4,5},{5,4},{6,7},{7,6},{8,9},{9,8},{10,11... | collective-permute-start | bytes 835592 | tf_op jit(solution)/shard_map/ppermute | solution.py:652
  130.5 4.5 %collective-permute-done.24.refs_6_ = bf16[17,16,512]{2,1,0:T(8,128)(2,1)S(1)} collective-permute-done((bf16[17,16,512]{2,1,0:T(8,128)(2,1)S(1)}, bf16[17,16,512]{2,1,0:T(8,128)(2,1)S(1)}, u32[]{:S(2)}, u32[]{:S(2)}) %collective-permute-start.24) | collective-permute-done | bytes 278560 | tf_op jit(solution)/shard_map/ppermute | solution.py:652
  135.0 4.2 %owner_rows.1 = (bf16[2048,512]{1,0:T(8,128)(2,1)}, f32[192,1536]{1,0:T(8,128)}) custom-call(s32[195]{0:T(256)S(1)} %plan.1.refs_10_.refs_0_.scalars, bf16[17,16,512]{2,1,0:T(8,128)(2,1)S(1)} %get-tuple-element.51.refs_0_, bf16[17,16,512]{2,1,0:T(8,128)(2,1)S(1)} %collective-permute-done.19.refs_3_.refs_1_, ...), custom_call_target="tpu_custom_call" | custom-call | tf_op jit(solution)/shard_map/owner_rows/pallas_call | solution.py:567
  (40 shorter events, 2.8 us)
Async XLA Ops:
  0.6 9.7 %collective-permute-start = (bf16[512,1536]{1,0:T(8,128)(2,1)}, bf16[512,1536]{1,0:T(8,128)(2,1)S(1)}, u32[]{:S(2)}, u32[]{:S(2)}) collective-permute-start(bf16[512,1536]{1,0:T(8,128)(2,1)} %bitcast.12), channel_id=1, source_target_pairs={{0,1},{1,0},{2,3},{3,2},{4,5},{5,4},{6,7},{7,6},{8,9},{9,8},{10,11... | collective-permute-start | bytes 4718600 | tf_op jit(solution)/shard_map/ppermute | solution.py:33
  1.4 11.0 %collective-permute-start.1 = (bf16[512,1536]{1,0:T(8,128)(2,1)}, bf16[512,1536]{1,0:T(8,128)(2,1)S(1)}, u32[]{:S(2)}, u32[]{:S(2)}) collective-permute-start(bf16[512,1536]{1,0:T(8,128)(2,1)} %bitcast.9), channel_id=1, source_target_pairs={{0,1},{1,0},{2,3},{3,2},{4,5},{5,4},{6,7},{7,6},{8,9},{9,8},{10,11... | collective-permute-start | bytes 4718600 | tf_op jit(solution)/shard_map/ppermute | solution.py:33
  1.5 1.1 copy-start.3
  2.5 13.1 %collective-permute-start.4 = (bf16[192,384]{1,0:T(8,128)(2,1)S(1)}, bf16[192,384]{1,0:T(8,128)(2,1)S(1)}, u32[]{:S(2)}, u32[]{:S(2)}) collective-permute-start(bf16[192,384]{1,0:T(8,128)(2,1)S(1)} %cut_proj.1.refs_0_), channel_id=1, source_target_pairs={{0,6},{1,7},{2,4},{3,5},{4,2},{5,3},{6,0},{7,1},{8,14},{9,15},{10,... | collective-permute-start | bytes 442376 | tf_op jit(solution)/shard_map/ppermute | solution.py:37
  3.9 11.8 %collective-permute-start.3 = (bf16[192,384]{1,0:T(8,128)(2,1)S(1)}, bf16[192,384]{1,0:T(8,128)(2,1)}, u32[]{:S(2)}, u32[]{:S(2)}) collective-permute-start(bf16[192,384]{1,0:T(8,128)(2,1)S(1)} %cut_proj.1.refs_0_), channel_id=1, source_target_pairs={{0,2},{1,3},{2,0},{3,1},{4,6},{5,7},{6,4},{7,5},{8,10},{9,11},{10,... | collective-permute-start | bytes 442376 | tf_op jit(solution)/shard_map/ppermute | solution.py:37
  6.1 9.6 %collective-permute-start.2 = (bf16[192,384]{1,0:T(8,128)(2,1)S(1)}, bf16[192,384]{1,0:T(8,128)(2,1)}, u32[]{:S(2)}, u32[]{:S(2)}) collective-permute-start(bf16[192,384]{1,0:T(8,128)(2,1)S(1)} %cut_proj.1.refs_0_), channel_id=1, source_target_pairs={{0,4},{1,5},{2,6},{3,7},{4,0},{5,1},{6,2},{7,3},{8,12},{9,13},{10,... | collective-permute-start | bytes 442376 | tf_op jit(solution)/shard_map/ppermute | solution.py:37
  6.8 1.4 %copy-start.1 = (bf16[1,512,1536]{2,1,0:T(8,128)(2,1)S(1)}, bf16[1,512,1536]{2,1,0:T(8,128)(2,1)}, u32[]{:S(2)}) copy-start(bf16[1,512,1536]{2,1,0:T(8,128)(2,1)} %param.5) | copy-start | bytes 4718596
  10.3 2.1 %copy-start = (bf16[1,512,1536]{2,1,0:T(8,128)(2,1)S(1)}, bf16[1,512,1536]{2,1,0:T(8,128)(2,1)}, u32[]{:S(2)}) copy-start(bf16[1,512,1536]{2,1,0:T(8,128)(2,1)} %param.6) | copy-start | bytes 4718596
  12.4 3.3 %copy-start.5 = (bf16[3,64,1536]{2,1,0:T(8,128)(2,1)S(1)}, bf16[3,64,1536]{2,1,0:T(8,128)(2,1)}, u32[]{:S(2)}) copy-start(bf16[3,64,1536]{2,1,0:T(8,128)(2,1)} %refs_1_.2) | copy-start | bytes 1769476
  15.7 22.3 %copy-start.4 = (bf16[192,1536]{1,0:T(8,128)(2,1)S(1)}, bf16[192,1536]{1,0:T(8,128)(2,1)}, u32[]{:S(2)}) copy-start(bf16[192,1536]{1,0:T(8,128)(2,1)} %refs_1_.3) | copy-start | bytes 1769476
  16.8 21.2 %collective-permute-start.5 = (bf16[1056,384]{1,0:T(8,128)(2,1)S(1)}, bf16[1056,384]{1,0:T(8,128)(2,1)S(1)}, u32[]{:S(2)}, u32[]{:S(2)}) collective-permute-start(bf16[1056,384]{1,0:T(8,128)(2,1)S(1)} %get-tuple-element.34.refs_2_), channel_id=1, source_target_pairs={{0,8},{8,0},{16,24},{24,16},{1,9},{9,1},{17,25},{25,17},{2,10},{10... | collective-permute-start | bytes 2433032 | tf_op jit(solution)/shard_map/ppermute | solution.py:41
  18.1 19.9 %collective-permute-start.6 = (bf16[1056,384]{1,0:T(8,128)(2,1)S(1)}, bf16[1056,384]{1,0:T(8,128)(2,1)S(1)}, u32[]{:S(2)}, u32[]{:S(2)}) collective-permute-start(bf16[1056,384]{1,0:T(8,128)(2,1)S(1)} %get-tuple-element.35.refs_3_), channel_id=1, source_target_pairs={{0,16},{8,24},{16,0},{24,8},{1,17},{9,25},{17,1},{25,9},{2,18},{10... | collective-permute-start | bytes 2433032 | tf_op jit(solution)/shard_map/ppermute | solution.py:41
  19.3 18.7 %collective-permute-start.7 = (bf16[480,384]{1,0:T(8,128)(2,1)S(1)}, bf16[480,384]{1,0:T(8,128)(2,1)S(1)}, u32[]{:S(2)}, u32[]{:S(2)}) collective-permute-start(bf16[480,384]{1,0:T(8,128)(2,1)S(1)} %get-tuple-element.36.refs_6_), channel_id=1, source_target_pairs={{0,4},{1,5},{2,6},{3,7},{4,0},{5,1},{6,2},{7,3},{8,12},{9,13},{10,... | collective-permute-start | bytes 1105928 | tf_op jit(solution)/shard_map/ppermute | solution.py:37
  38.5 21.0 %collective-permute-start.8 = (bf16[2688,384]{1,0:T(8,128)(2,1)S(1)}, bf16[2688,384]{1,0:T(8,128)(2,1)S(1)}, u32[]{:S(2)}, u32[]{:S(2)}) collective-permute-start(bf16[2688,384]{1,0:T(8,128)(2,1)S(1)} %get-tuple-element.39), channel_id=1, source_target_pairs={{0,1},{1,0},{2,3},{3,2},{4,5},{5,4},{6,7},{7,6},{8,9},{9,8},{10,11... | collective-permute-start | bytes 6193160 | tf_op jit(solution)/shard_map/ppermute | solution.py:33
  39.2 18.1 %collective-permute-start.10 = (bf16[960,384]{1,0:T(8,128)(2,1)S(1)}, bf16[960,384]{1,0:T(8,128)(2,1)S(1)}, u32[]{:S(2)}, u32[]{:S(2)}) collective-permute-start(bf16[960,384]{1,0:T(8,128)(2,1)S(1)} %get-tuple-element.41.refs_2_), channel_id=1, source_target_pairs={{0,16},{8,24},{16,0},{24,8},{1,17},{9,25},{17,1},{25,9},{2,18},{10... | collective-permute-start | bytes 2211848 | tf_op jit(solution)/shard_map/ppermute | solution.py:41
  40.4 17.7 %collective-permute-start.11 = (bf16[960,384]{1,0:T(8,128)(2,1)S(1)}, bf16[960,384]{1,0:T(8,128)(2,1)S(1)}, u32[]{:S(2)}, u32[]{:S(2)}) collective-permute-start(bf16[960,384]{1,0:T(8,128)(2,1)S(1)} %get-tuple-element.42.refs_3_), channel_id=1, source_target_pairs={{0,8},{8,0},{16,24},{24,16},{1,9},{9,1},{17,25},{25,17},{2,10},{10... | collective-permute-start | bytes 2211848 | tf_op jit(solution)/shard_map/ppermute | solution.py:41
  40.7 18.9 %collective-permute-start.9 = (bf16[2,480,384]{2,1,0:T(8,128)(2,1)S(1)}, bf16[2,480,384]{2,1,0:T(8,128)(2,1)S(1)}, u32[]{:S(2)}, u32[]{:S(2)}) collective-permute-start(bf16[2,480,384]{2,1,0:T(8,128)(2,1)S(1)} %get-tuple-element.40.refs_0_), channel_id=1, source_target_pairs={{0,2},{1,3},{2,0},{3,1},{4,6},{5,7},{6,4},{7,5},{8,10},{9,11},{10,... | collective-permute-start | bytes 2211848 | tf_op jit(solution)/shard_map/ppermute | solution.py:37
  59.6 6.2 %copy-start.2 = (bf16[1,512,1536]{2,1,0:T(8,128)(2,1)S(1)}, bf16[1,512,1536]{2,1,0:T(8,128)(2,1)}, u32[]{:S(2)}) copy-start(bf16[1,512,1536]{2,1,0:T(8,128)(2,1)} %param.5) | copy-start | bytes 4718596
  59.8 5.2 %collective-permute-start.15 = (bf16[1152,384]{1,0:T(8,128)(2,1)S(1)}, bf16[1152,384]{1,0:T(8,128)(2,1)S(1)}, u32[]{:S(2)}, u32[]{:S(2)}) collective-permute-start(bf16[1152,384]{1,0:T(8,128)(2,1)S(1)} %get-tuple-element.48), channel_id=1, source_target_pairs={{0,1},{1,0},{2,3},{3,2},{4,5},{5,4},{6,7},{7,6},{8,9},{9,8},{10,11... | collective-permute-start | bytes 2654216 | tf_op jit(solution)/shard_map/ppermute | solution.py:33
  61.0 15.1 %collective-permute-start.17 = (bf16[1440,384]{1,0:T(8,128)(2,1)S(1)}, bf16[1440,384]{1,0:T(8,128)(2,1)S(1)}, u32[]{:S(2)}, u32[]{:S(2)}) collective-permute-start(bf16[1440,384]{1,0:T(8,128)(2,1)S(1)} %bitcast.18), channel_id=1, source_target_pairs={{0,1},{1,0},{2,3},{3,2},{4,5},{5,4},{6,7},{7,6},{8,9},{9,8},{10,11... | collective-permute-start | bytes 3317768 | tf_op jit(solution)/shard_map/ppermute | solution.py:33
  61.1 10.3 %collective-permute-start.16 = (bf16[2,192,384]{2,1,0:T(8,128)(2,1)S(1)}, bf16[2,192,384]{2,1,0:T(8,128)(2,1)S(1)}, u32[]{:S(2)}, u32[]{:S(2)}) collective-permute-start(bf16[2,192,384]{2,1,0:T(8,128)(2,1)S(1)} %get-tuple-element.49), channel_id=1, source_target_pairs={{0,2},{1,3},{2,0},{3,1},{4,6},{5,7},{6,4},{7,5},{8,10},{9,11},{10,... | collective-permute-start | bytes 884744 | tf_op jit(solution)/shard_map/ppermute | solution.py:37
  63.1 8.9 %collective-permute-start.14 = (bf16[3,96,384]{2,1,0:T(8,128)(2,1)S(1)}, bf16[3,96,384]{2,1,0:T(8,128)(2,1)S(1)}, u32[]{:S(2)}, u32[]{:S(2)}) collective-permute-start(bf16[3,96,384]{2,1,0:T(8,128)(2,1)S(1)} %get-tuple-element.47), channel_id=1, source_target_pairs={{0,24},{8,16},{16,8},{24,0},{1,25},{9,17},{17,9},{25,1},{2,26},{10... | collective-permute-start | bytes 663560 | tf_op jit(solution)/shard_map/ppermute | solution.py:41
  64.1 12.0 %collective-permute-start.13 = (bf16[3,96,384]{2,1,0:T(8,128)(2,1)S(1)}, bf16[3,96,384]{2,1,0:T(8,128)(2,1)S(1)}, u32[]{:S(2)}, u32[]{:S(2)}) collective-permute-start(bf16[3,96,384]{2,1,0:T(8,128)(2,1)S(1)} %get-tuple-element.47), channel_id=1, source_target_pairs={{0,16},{8,24},{16,0},{24,8},{1,17},{9,25},{17,1},{25,9},{2,18},{10... | collective-permute-start | bytes 663560 | tf_op jit(solution)/shard_map/ppermute | solution.py:41
  64.9 11.1 %collective-permute-start.12 = (bf16[3,96,384]{2,1,0:T(8,128)(2,1)S(1)}, bf16[3,96,384]{2,1,0:T(8,128)(2,1)S(1)}, u32[]{:S(2)}, u32[]{:S(2)}) collective-permute-start(bf16[3,96,384]{2,1,0:T(8,128)(2,1)S(1)} %get-tuple-element.47), channel_id=1, source_target_pairs={{0,8},{8,0},{16,24},{24,16},{1,9},{9,1},{17,25},{25,17},{2,10},{10... | collective-permute-start | bytes 663560 | tf_op jit(solution)/shard_map/ppermute | solution.py:41
  76.1 2.3 %collective-permute-start.18 = (bf16[864,384]{1,0:T(8,128)(2,1)S(1)}, bf16[864,384]{1,0:T(8,128)(2,1)S(1)}, u32[]{:S(2)}, u32[]{:S(2)}) collective-permute-start(bf16[864,384]{1,0:T(8,128)(2,1)S(1)} %bitcast.16), channel_id=1, source_target_pairs={{0,1},{1,0},{2,3},{3,2},{4,5},{5,4},{6,7},{7,6},{8,9},{9,8},{10,11... | collective-permute-start | bytes 1990664 | tf_op jit(solution)/shard_map/ppermute | solution.py:33
  76.7 12.3 %collective-permute-start.26 = (bf16[192,384]{1,0:T(8,128)(2,1)S(1)}, bf16[192,384]{1,0:T(8,128)(2,1)S(1)}, u32[]{:S(2)}, u32[]{:S(2)}) collective-permute-start(bf16[192,384]{1,0:T(8,128)(2,1)S(1)} %get-tuple-element.50.refs_4_), channel_id=1, source_target_pairs={{0,4},{1,5},{2,6},{3,7},{4,0},{5,1},{6,2},{7,3},{8,12},{9,13},{10,... | collective-permute-start | bytes 442376 | tf_op jit(solution)/shard_map/ppermute | solution.py:37
  84.5 18.4 %collective-permute-start.19 = (bf16[17,16,512]{2,1,0:T(8,128)(2,1)S(1)}, bf16[17,16,512]{2,1,0:T(8,128)(2,1)S(1)}, u32[]{:S(2)}, u32[]{:S(2)}) collective-permute-start(bf16[17,16,512]{2,1,0:T(8,128)(2,1)S(1)} %get-tuple-element.52), channel_id=1, source_target_pairs={{0,4},{1,5},{2,6},{3,7},{4,0},{5,1},{6,2},{7,3},{8,12},{9,13},{10,... | collective-permute-start | bytes 835592 | tf_op jit(solution)/shard_map/ppermute | solution.py:652
  85.3 23.6 %collective-permute-start.20 = (bf16[17,16,512]{2,1,0:T(8,128)(2,1)S(1)}, bf16[17,16,512]{2,1,0:T(8,128)(2,1)S(1)}, u32[]{:S(2)}, u32[]{:S(2)}) collective-permute-start(bf16[17,16,512]{2,1,0:T(8,128)(2,1)S(1)} %get-tuple-element.53), channel_id=1, source_target_pairs={{0,5},{1,4},{2,7},{3,6},{4,1},{5,0},{6,3},{7,2},{8,13},{9,12},{10,... | collective-permute-start | bytes 835592 | tf_op jit(solution)/shard_map/ppermute | solution.py:652
  87.5 22.1 %collective-permute-start.21 = (bf16[17,16,512]{2,1,0:T(8,128)(2,1)S(1)}, bf16[17,16,512]{2,1,0:T(8,128)(2,1)S(1)}, u32[]{:S(2)}, u32[]{:S(2)}) collective-permute-start(bf16[17,16,512]{2,1,0:T(8,128)(2,1)S(1)} %get-tuple-element.54), channel_id=1, source_target_pairs={{0,2},{1,3},{2,0},{3,1},{4,6},{5,7},{6,4},{7,5},{8,10},{9,11},{10,... | collective-permute-start | bytes 835592 | tf_op jit(solution)/shard_map/ppermute | solution.py:652
  88.0 24.8 %collective-permute-start.22 = (bf16[17,16,512]{2,1,0:T(8,128)(2,1)S(1)}, bf16[17,16,512]{2,1,0:T(8,128)(2,1)S(1)}, u32[]{:S(2)}, u32[]{:S(2)}) collective-permute-start(bf16[17,16,512]{2,1,0:T(8,128)(2,1)S(1)} %get-tuple-element.55), channel_id=1, source_target_pairs={{0,3},{1,2},{2,1},{3,0},{4,7},{5,6},{6,5},{7,4},{8,11},{9,10},{10,... | collective-permute-start | bytes 835592 | tf_op jit(solution)/shard_map/ppermute | solution.py:652
  89.0 37.8 %collective-permute-start.23 = (bf16[17,16,512]{2,1,0:T(8,128)(2,1)S(1)}, bf16[17,16,512]{2,1,0:T(8,128)(2,1)S(1)}, u32[]{:S(2)}, u32[]{:S(2)}) collective-permute-start(bf16[17,16,512]{2,1,0:T(8,128)(2,1)S(1)} %get-tuple-element.56), channel_id=1, source_target_pairs={{0,6},{1,7},{2,4},{3,5},{4,2},{5,3},{6,0},{7,1},{8,14},{9,15},{10,... | collective-permute-start | bytes 835592 | tf_op jit(solution)/shard_map/ppermute | solution.py:652
  103.6 31.5 %collective-permute-start.29 = (f32[192,384]{1,0:T(8,128)S(1)}, f32[192,384]{1,0:T(8,128)S(1)}, u32[]{:S(2)}, u32[]{:S(2)}) collective-permute-start(f32[192,384]{1,0:T(8,128)S(1)} %far_sum.1.refs_8_), channel_id=1, source_target_pairs={{0,24},{8,16},{16,8},{24,0},{1,25},{9,17},{17,9},{25,1},{2,26},{10... | collective-permute-start | bytes 884744 | tf_op jit(solution)/shard_map/ppermute | solution.py:41
  109.0 26.1 %collective-permute-start.28 = (f32[192,384]{1,0:T(8,128)S(1)}, f32[192,384]{1,0:T(8,128)S(1)}, u32[]{:S(2)}, u32[]{:S(2)}) collective-permute-start(f32[192,384]{1,0:T(8,128)S(1)} %far_sum.1.refs_8_), channel_id=1, source_target_pairs={{0,16},{8,24},{16,0},{24,8},{1,17},{9,25},{17,1},{25,9},{2,18},{10... | collective-permute-start | bytes 884744 | tf_op jit(solution)/shard_map/ppermute | solution.py:41
  109.6 25.5 %collective-permute-start.27 = (f32[192,384]{1,0:T(8,128)S(1)}, f32[192,384]{1,0:T(8,128)S(1)}, u32[]{:S(2)}, u32[]{:S(2)}) collective-permute-start(f32[192,384]{1,0:T(8,128)S(1)} %far_sum.1.refs_8_), channel_id=1, source_target_pairs={{0,8},{8,0},{16,24},{24,16},{1,9},{9,1},{17,25},{25,17},{2,10},{10... | collective-permute-start | bytes 884744 | tf_op jit(solution)/shard_map/ppermute | solution.py:41
  112.8 22.2 %collective-permute-start.24 = (bf16[17,16,512]{2,1,0:T(8,128)(2,1)S(1)}, bf16[17,16,512]{2,1,0:T(8,128)(2,1)S(1)}, u32[]{:S(2)}, u32[]{:S(2)}) collective-permute-start(bf16[17,16,512]{2,1,0:T(8,128)(2,1)S(1)} %get-tuple-element.57), channel_id=1, source_target_pairs={{0,7},{1,6},{2,5},{3,4},{4,3},{5,2},{6,1},{7,0},{8,15},{9,14},{10,... | collective-permute-start | bytes 835592 | tf_op jit(solution)/shard_map/ppermute | solution.py:652
  126.9 8.2 %collective-permute-start.25 = (bf16[17,16,512]{2,1,0:T(8,128)(2,1)S(1)}, bf16[17,16,512]{2,1,0:T(8,128)(2,1)S(1)}, u32[]{:S(2)}, u32[]{:S(2)}) collective-permute-start(bf16[17,16,512]{2,1,0:T(8,128)(2,1)S(1)} %get-tuple-element.58), channel_id=1, source_target_pairs={{0,1},{1,0},{2,3},{3,2},{4,5},{5,4},{6,7},{7,6},{8,9},{9,8},{10,11... | collective-permute-start | bytes 835592 | tf_op jit(solution)/shard_map/ppermute | solution.py:652

commit v6 on v5

--- a/solution.py
+++ b/solution.py
@@ -403,41 +403,34 @@
     return 2 * (start // (2 * N_FSDP)) + jnp.clip(start % (2 * N_FSDP) - 2 * holder, 0, 2)
 
 
-SLOTS_AT = 2
-SEGMENTS_AT = SLOTS_AT + HOLD
-COUNT_AT = SEGMENTS_AT + OWN_SEG
+BASES_AT = 2
+SEGMENTS_AT = BASES_AT + N_FSDP
+BEFORE_AT = SEGMENTS_AT + N_FSDP * CAP
+COUNT_AT = BEFORE_AT + N_FSDP * CAP
 
 
 def plan_kernel(scalars, plan):
     site, index = scalars[0], scalars[1]
     plan[0], plan[1] = site, index
+    count = scalars[2 + index]
+    plan[COUNT_AT] = count
     starts = [jnp.int32(0)]
     for owner in range(N_FSDP):
         starts.append(starts[-1] + scalars[2 + owner])
-
-    @pl.loop(0, HOLD)
-    def _(slot):
-        item = 2 * (slot // 2 * N_FSDP + index) + slot % 2
-        owner = jnp.int32(0)
-        start = jnp.int32(0)
-        for other in range(1, N_FSDP):
-            passed = item >= starts[other]
-            owner = jnp.where(passed, other, owner)
-            start = jnp.where(passed, starts[other], start)
-        plan[SLOTS_AT + slot] = lax.bitwise_xor(owner, index) * CAP + slot - held_before(start, index)
-
-    start = jnp.int32(0)
+    my_start = jnp.int32(0)
     for owner in range(N_FSDP):
-        start = start + jnp.where(owner < index, scalars[2 + owner], 0)
-    count = scalars[2 + index]
-    plan[COUNT_AT] = count
-
-    @pl.loop(0, OWN_SEG)
-    def _(segment):
-        item = start + jnp.minimum(segment, count - 1)
-        holder = item // 2 % N_FSDP
-        rank = 2 * (item // (2 * N_FSDP)) + item % 2 - held_before(start, holder)
-        plan[SEGMENTS_AT + segment] = lax.bitwise_xor(holder, index) * CAP + rank
+        place = lax.bitwise_xor(index, owner)
+        plan[BASES_AT + place] = held_before(starts[owner], index)
+        my_start = my_start + jnp.where(owner < index, scalars[2 + owner], 0)
+
+    @pl.loop(0, N_FSDP * CAP)
+    def _(block):
+        holder = lax.bitwise_xor(index, block // CAP)
+        slot = held_before(my_start, holder) + block % CAP
+        segment = 2 * (slot // 2 * N_FSDP + holder) + slot % 2 - my_start
+        held = (segment >= 0) & (segment < count)
+        plan[SEGMENTS_AT + block] = jnp.where(held, segment, OWN_SEG)
+        plan[BEFORE_AT + block] = jnp.where(held & (segment > 0), segment - 1, OWN_SEG)
 
 
 def plan_of(scalars):
@@ -450,7 +443,7 @@
 def stem_kernel(tables, scalars, *refs):
     n = len(tables)
     parts, grad_ref, outs = refs[:n], refs[n], refs[n + 1 : n + 1 + N_FSDP]
-    weight, mixed, leading, packed, firsts, sem, out_sem = refs[n + 1 + N_FSDP :]
+    weight, mixed, leading, firsts, sem = refs[n + 1 + N_FSDP :]
     copies = weight_copies(tables, scalars, parts, weight, sem)
     for copy in copies:
         copy.start()
@@ -471,24 +464,18 @@
             mixed[at, pl.ds(0, ROWS, stride=2), :] = even[:, columns]
             mixed[at, pl.ds(1, ROWS, stride=2), :] = odd[:, columns]
 
-    @pl.loop(0, HOLD, unroll=8)
-    def _(slot):
-        block = scalars[SLOTS_AT + slot]
-        place, rank = block // CAP, block % CAP
-        rows = pl.ds(pl.multiple_of(slot * 2 * SEG, 2 * SEG), 2 * SEG)
-        for lane in range(CS // LANES):
-            packed[place, rank, :, pl.ds(lane * LANES, LANES)] = mixed[lane, rows, :].astype(BF16)
-        firsts[pl.ds(block, 1), :] = leading[pl.ds(slot * SEG, 1), :]
-
-    packed[:, CAP] = firsts[...].reshape(N_FSDP, CAP, CS).astype(BF16)
-    copies = [
-        pltpu.make_async_copy(packed.at[place], outs[place], out_sem.at[place])
-        for place in range(N_FSDP)
-    ]
-    for copy in copies:
-        copy.start()
-    for copy in copies:
-        copy.wait()
+    for place, out in enumerate(outs):
+        base = scalars[BASES_AT + place]
+        for rank in range(CAP):
+            slot = jnp.minimum(base + rank, HOLD - 1)
+            rows = pl.ds(pl.multiple_of(slot * 2 * SEG, 2 * SEG), 2 * SEG)
+            for lane in range(CS // LANES):
+                out[rank, :, lane * LANES : (lane + 1) * LANES] = mixed[lane, rows, :].astype(BF16)
+            firsts[rank : rank + 1, :] = leading[pl.ds(slot * SEG, 1), :]
+        out[CAP] = firsts[...].astype(BF16)
+
+
+VMEM = pl.BlockSpec(memory_space=pltpu.VMEM)
 
 
 def stem_payloads(scalars, parts, grad):
@@ -497,80 +484,63 @@
     return call(
         lambda *refs: stem_kernel(tables, *refs), "stem_payloads",
         (shape(payload, BF16),) * N_FSDP, (1,),
-        [ANY] * len(values) + [whole((ROWS, D))], (HBM,) * N_FSDP,
+        [ANY] * len(values) + [whole((ROWS, D))], (VMEM,) * N_FSDP,
         [
             pltpu.VMEM((3, CS, D), BF16),
             pltpu.VMEM((CS // LANES, 2 * ROWS, LANES), F32),
             pltpu.VMEM((ROWS, CS), F32),
-            pltpu.VMEM((N_FSDP,) + payload, BF16),
-            pltpu.VMEM((N_FSDP * CAP, CS), F32),
+            pltpu.VMEM((CAP, CS), F32),
             pltpu.SemaphoreType.DMA,
-            pltpu.SemaphoreType.DMA((N_FSDP,)),
         ],
         vmem=18,
     )(scalars, *values, grad)
 
 
 def owner_kernel(scalars, *refs):
-    payloads, terms, (out_ref, total), (packed, firsts, sem, total_sem) = (
-        refs[:N_FSDP], refs[N_FSDP : N_FSDP + N_SITE], refs[-6:-4], refs[-4:]
-    )
-    step = pl.program_id(0)
-    total_copies = []
+    payloads, terms, (out_hbm, total), (out, sem, total_sem) = (
+        refs[:N_FSDP], refs[N_FSDP : N_FSDP + N_SITE], refs[-5:-3], refs[-3:]
+    )
+    copies = []
     for distance, term in enumerate(terms):
         at = pl.multiple_of(lax.bitwise_xor(scalars[0], distance) * QUARTER, QUARTER)
-        total_copies.append(
+        copies.append(
             pltpu.make_async_copy(term, total.at[:, pl.ds(at, QUARTER)], total_sem.at[distance])
         )
-
-    @pl.when(step == 0)
-    def _():
-        for copy in total_copies:
-            copy.start()
-
-    @pl.when(step == 0)
-    def _():
-        copies = [
-            pltpu.make_async_copy(payloads[i], packed.at[place], sem.at[place])
-            for i, place in enumerate(PAYLOAD_ORDER)
-        ]
-        for copy in copies:
-            copy.start()
-        for copy in copies:
-            copy.wait()
-        firsts[...] = packed[:, CAP].astype(F32).reshape(N_FSDP * CAP, CS)
-
-    count = scalars[COUNT_AT]
-    per_step = OWN_SEG // 4
+    for copy in copies:
+        copy.start()
+
+    def rows_of_segment(segment):
+        return pl.ds(pl.multiple_of(segment * 2 * SEG, 2 * SEG), 2 * SEG)
+
+    @pl.loop(scalars[COUNT_AT], OWN_SEG)
+    def _(segment):
+        out[rows_of_segment(segment), :] = jnp.zeros((2 * SEG, CS), BF16)
+
+    for i, place in enumerate(PAYLOAD_ORDER):
+        for rank in range(CAP):
+            segment = scalars[SEGMENTS_AT + place * CAP + rank]
+            out[rows_of_segment(segment), :] = payloads[i][rank]
     last_row = lax.broadcasted_iota(jnp.int32, (2 * SEG, CS), 0) == 2 * SEG - 1
-
-    @pl.loop(0, per_step, unroll=4)
-    def _(local):
-        segment = step * per_step + local
-        block = scalars[SEGMENTS_AT + segment]
-        follower = scalars[SEGMENTS_AT + jnp.minimum(segment + 1, OWN_SEG - 1)]
-        first = jnp.broadcast_to(firsts[pl.ds(follower, 1), :], (2 * SEG, CS))
-        first = jnp.where(last_row & (segment + 1 < count), first, 0.0)
-        rows = packed[block // CAP, block % CAP].astype(F32) + first
-        to = pl.ds(pl.multiple_of(local * 2 * SEG, 2 * SEG), 2 * SEG)
-        out_ref[to, :] = jnp.where(segment < count, rows, 0.0).astype(BF16)
-
-    @pl.when(step == pl.num_programs(0) - 1)
-    def _():
-        for copy in total_copies:
-            copy.wait()
+    for i, place in enumerate(PAYLOAD_ORDER):
+        firsts = payloads[i][CAP].astype(F32)
+        for rank in range(CAP):
+            rows = rows_of_segment(scalars[BEFORE_AT + place * CAP + rank])
+            first = jnp.broadcast_to(firsts[rank : rank + 1, :], (2 * SEG, CS))
+            term = jnp.where(last_row, first, 0.0)
+            out[rows, :] = (out[rows, :].astype(F32) + term).astype(BF16)
+    copies.append(fetch(out.at[pl.ds(0, out_hbm.shape[0]), :], out_hbm, sem))
+    for copy in copies:
+        copy.wait()
 
 
 def owner_rows(scalars, payloads, terms):
-    payload = (CAP + 1, 2 * SEG, CS)
     rows = 2 * OWN_SEG * SEG
     return call(
-        owner_kernel, "owner_rows", (shape((rows, CS), BF16), shape((D // N_FSDP, D), F32)), (4,),
-        [ANY] * (N_FSDP + N_SITE), (row_block(rows // 4, CS), HBM),
+        owner_kernel, "owner_rows", (shape((rows, CS), BF16), shape((D // N_FSDP, D), F32)), (1,),
+        [VMEM] * N_FSDP + [ANY] * N_SITE, (HBM, HBM),
         [
-            pltpu.VMEM((N_FSDP,) + payload, BF16),
-            pltpu.VMEM((N_FSDP * CAP, CS), F32),
-            pltpu.SemaphoreType.DMA((N_FSDP,)),
+            pltpu.VMEM((rows + 2 * SEG, CS), BF16),
+            pltpu.SemaphoreType.DMA,
             pltpu.SemaphoreType.DMA((N_SITE,)),
         ],
     )(scalars, *payloads, *terms)

time: 140 us -> 138 us (0.986)
  Pallas kernels: 33.4 us -> 30 us
  waiting for transfers between devices: 66.6 us -> 68.1 us
    ppermute x7, waiting for transfers between devices: 9.37 us -> 10.9 us  [swap_z(): lax.ppermute(value, 'fsdp', [(i, i ^ 2 * distance) for i in range(N_FSDP)])]
    pallas_call x1, Pallas kernels: 6.34 us -> 4.79 us  [plan_of(): call(plan_kernel, 'plan', shape((COUNT_AT + 1,), jnp.int32), (1,), [], pl...]
  transfers between devices with their start and end apart: 30 -> 30, of which waited for: 11 -> 11; matrix products, arithmetic and copies ran while one was open for 1% -> 1% of each run, Pallas kernels for 20% -> 18%
where the time goes in v6:
time: 138 us
  waiting for transfers between devices  68.1 us (49%)
  starting transfers between devices  35.2 us (26%)
  Pallas kernels  30 us (22%)
  local copies, waits for them, and re-layouts  2.5 us (2%)
    ppermute x7, waiting for transfers between devices, body(): lax.ppermute(payloads[d], 'fsdp', [(i, i ^ d) for i in range(N_FSDP)])  37.2 us
    ppermute x10, waiting for transfers between devices, swap_site(): lax.ppermute(value, 'site', [(i, i ^ distance) for i in range(N_SITE)])  19 us
    ppermute x7, starting transfers between devices, swap_z(): lax.ppermute(value, 'fsdp', [(i, i ^ 2 * distance) for i in range(N_FSDP)])  12.5 us
    ppermute x7, waiting for transfers between devices, swap_z(): lax.ppermute(value, 'fsdp', [(i, i ^ 2 * distance) for i in range(N_FSDP)])  10.9 us
    ppermute x7, starting transfers between devices, body(): lax.ppermute(payloads[d], 'fsdp', [(i, i ^ d) for i in range(N_FSDP)])  10.3 us
    ppermute x10, starting transfers between devices, swap_site(): lax.ppermute(value, 'site', [(i, i ^ distance) for i in range(N_SITE)])  9.01 us
    pallas_call x1, Pallas kernels, input_gradient(): call(lambda *refs: input_grad_kernel(tables, *refs), 'input_gradient', sh...  5.6 us
    pallas_call x1, Pallas kernels, stem_payloads(): call(lambda *refs: stem_kernel(tables, *refs), 'stem_payloads', (shape(pa...  5.48 us
  transfers between devices with their start and end apart: 30, of which 11 were waited for; matrix products, arithmetic and copies ran while one was open for 1% of the time, Pallas kernels for 18%

profile of v6, /device:TPU:9, one launch (start us, length us, event | category | flops | bytes accessed | tf_op | source)
XLA Modules:
  0.0 137.5 jit_solution(4557617397312964754)
XLA Ops:
  0.6 0.7 collective-permute-start
  1.5 1.1 copy-done.3
  2.5 1.4 collective-permute-start.4
  3.9 2.2 %collective-permute-start.3 = (bf16[192,384]{1,0:T(8,128)(2,1)S(1)}, bf16[192,384]{1,0:T(8,128)(2,1)}, u32[]{:S(2)}, u32[]{:S(2)}) collective-permute-start(bf16[192,384]{1,0:T(8,128)(2,1)S(1)} %cut_proj.1.refs_0_), channel_id=1, source_target_pairs={{0,2},{1,3},{2,0},{3,1},{4,6},{5,7},{6,4},{7,5},{8,10},{9,11},{10,... | collective-permute-start | bytes 442376 | tf_op jit(solution)/shard_map/ppermute | solution.py:37
  6.1 0.7 pad_add_fusion.scalars.refs_0_
  6.8 1.4 %copy-done.1 = bf16[1,512,1536]{2,1,0:T(8,128)(2,1)S(1)} copy-done((bf16[1,512,1536]{2,1,0:T(8,128)(2,1)S(1)}, bf16[1,512,1536]{2,1,0:T(8,128)(2,1)}, u32[]{:S(2)}) %copy-start.1) | copy-done | bytes 1572888
  8.2 2.1 %norm_half.2.refs_0_.na_ref = bf16[768,512]{1,0:T(8,128)(2,1)S(1)} custom-call(s32[10]{0:T(128)S(1)} %pad_add_fusion.scalars.refs_0_, bf16[512,1536]{1,0:T(8,128)(2,1)S(1)} %bitcast.13, bf16[192,384]{1,0:T(8,128)(2,1)S(1)} %cut_proj.1.refs_0_), custom_call_target="tpu_custom_call" | custom-call | tf_op jit(solution)/shard_map/norm_half/pallas_call | solution.py:225
  10.3 2.1 %norm_half.3.nb_ref = bf16[768,512]{1,0:T(8,128)(2,1)S(1)} custom-call(s32[10]{0:T(128)S(1)} %pad_add_fusion.scalars.refs_0_, bf16[512,1536]{1,0:T(8,128)(2,1)S(1)} %collective-permute-done.x_ref, bf16[768,512]{1,0:T(8,128)(2,1)S(1)} %norm_half.2.refs_0_.na_ref), custom_call_target="tpu_custom_call" | custom-call | tf_op jit(solution)/shard_map/norm_half/pallas_call | solution.py:225
  12.4 3.2 %outer_pieces.1 = (f32[2,384,384]{2,1,0:T(8,128)S(1)}, bf16[1056,384]{1,0:T(8,128)(2,1)S(1)}, f32[2,384,384]{2,1,0:T(8,128)S(1)}, bf16[1056,384]{1,0:T(8,128)(2,1)S(1)}) custom-call(s32[10]{0:T(128)S(1)} %pad_add_fusion.scalars.refs_0_, bf16[768,512]{1,0:T(8,128)(2,1)S(1)} %norm_half.2.refs_0_.na_ref, bf16[768,512]{1,0:T(8,128)(2,1)S(1)} %norm_half.3.nb_ref, ...), custom_call_target="tpu_custom_call" | custom-call | tf_op jit(solution)/shard_map/outer_pieces/pallas_call | solution.py:258
  15.7 1.1 halves.1
  16.8 1.3 collective-permute-start.5
  18.1 1.2 collective-permute-start.6
  19.3 3.6 %collective-permute-start.7 = (bf16[480,384]{1,0:T(8,128)(2,1)S(1)}, bf16[480,384]{1,0:T(8,128)(2,1)S(1)}, u32[]{:S(2)}, u32[]{:S(2)}) collective-permute-start(bf16[480,384]{1,0:T(8,128)(2,1)S(1)} %get-tuple-element.36.refs_6_), channel_id=1, source_target_pairs={{0,4},{1,5},{2,6},{3,7},{4,0},{5,1},{6,2},{7,3},{8,12},{9,13},{10,... | collective-permute-start | bytes 1105928 | tf_op jit(solution)/shard_map/ppermute | solution.py:37
  22.9 4.8 %plan.1.refs_10_.refs_0_.scalars = s32[267]{0:T(512)S(1)} custom-call(s32[10]{0:T(128)S(1)} %pad_add_fusion.scalars.refs_0_), custom_call_target="tpu_custom_call" | custom-call | tf_op jit(solution)/shard_map/plan/pallas_call | solution.py:437
  27.7 10.3 %collective-permute-done.7.refs_7_ = bf16[480,384]{1,0:T(8,128)(2,1)S(1)} collective-permute-done((bf16[480,384]{1,0:T(8,128)(2,1)S(1)}, bf16[480,384]{1,0:T(8,128)(2,1)S(1)}, u32[]{:S(2)}, u32[]{:S(2)}) %collective-permute-start.7) | collective-permute-done | bytes 368672 | tf_op jit(solution)/shard_map/ppermute | solution.py:37
  38.5 0.6 collective-permute-start.8
  39.2 1.2 collective-permute-start.10
  40.7 2.6 %collective-permute-start.9 = (bf16[2,480,384]{2,1,0:T(8,128)(2,1)S(1)}, bf16[2,480,384]{2,1,0:T(8,128)(2,1)S(1)}, u32[]{:S(2)}, u32[]{:S(2)}) collective-permute-start(bf16[2,480,384]{2,1,0:T(8,128)(2,1)S(1)} %get-tuple-element.40.refs_0_), channel_id=1, source_target_pairs={{0,2},{1,3},{2,0},{3,1},{4,6},{5,7},{6,4},{7,5},{8,10},{9,11},{10,... | collective-permute-start | bytes 2211848 | tf_op jit(solution)/shard_map/ppermute | solution.py:37
  43.3 14.0 %collective-permute-done.10.ra_ref.refs_2_.refs_4_ = bf16[960,384]{1,0:T(8,128)(2,1)S(1)} collective-permute-done((bf16[960,384]{1,0:T(8,128)(2,1)S(1)}, bf16[960,384]{1,0:T(8,128)(2,1)S(1)}, u32[]{:S(2)}, u32[]{:S(2)}) %collective-permute-start.10) | collective-permute-done | bytes 737312 | tf_op jit(solution)/shard_map/ppermute | solution.py:41
  57.2 0.9 collective-permute-done.11.rb_ref.refs_3_.refs_5_
  58.2 0.7 site_sum.1
  58.9 0.6 collective-permute-done.9.refs_1_
  59.8 1.2 collective-permute-start.15
  61.1 2.0 %collective-permute-start.16 = (bf16[2,192,384]{2,1,0:T(8,128)(2,1)S(1)}, bf16[2,192,384]{2,1,0:T(8,128)(2,1)S(1)}, u32[]{:S(2)}, u32[]{:S(2)}) collective-permute-start(bf16[2,192,384]{2,1,0:T(8,128)(2,1)S(1)} %get-tuple-element.49), channel_id=1, source_target_pairs={{0,2},{1,3},{2,0},{3,1},{4,6},{5,7},{6,4},{7,5},{8,10},{9,11},{10,... | collective-permute-start | bytes 884744 | tf_op jit(solution)/shard_map/ppermute | solution.py:37
  63.1 1.0 collective-permute-start.14
  64.1 0.8 collective-permute-start.13
  64.9 0.8 collective-permute-start.12
  65.7 5.6 %input_gradient.1.refs_0_.refs_3_.refs_7_ = bf16[512,1536]{1,0:T(8,128)(2,1)S(1)} custom-call(s32[10]{0:T(128)S(1)} %pad_add_fusion.scalars.refs_0_, bf16[192,1536]{1,0:T(8,128)(2,1)S(1)} %copy-done.4, bf16[960,384]{1,0:T(8,128)(2,1)S(1)} %get-tuple-element.41.refs_2_, bf16[960,384]{1,0:T(8,128)(2,1)S(1)} %get-tuple-element.42.refs_3_, ...), custom_call_target="tpu_custom_call" | custom-call | tf_op jit(solution)/shard_map/input_gradient/pallas_call | solution.py:385
  71.3 0.6 near_sum.1
  72.0 4.1 %collective-permute-done.13.refs_1_ = bf16[3,96,384]{2,1,0:T(8,128)(2,1)S(1)} collective-permute-done((bf16[3,96,384]{2,1,0:T(8,128)(2,1)S(1)}, bf16[3,96,384]{2,1,0:T(8,128)(2,1)S(1)}, u32[]{:S(2)}, u32[]{:S(2)}) %collective-permute-start.13) | collective-permute-done | bytes 221216 | tf_op jit(solution)/shard_map/ppermute | solution.py:41
  76.7 0.7 collective-permute-start.26
  77.4 1.0 collective-permute-done.18.refs_6_
  78.4 5.5 %stem_payloads.1 = (bf16[17,16,512]{2,1,0:T(8,128)(2,1)S(1)}, bf16[17,16,512]{2,1,0:T(8,128)(2,1)S(1)}, bf16[17,16,512]{2,1,0:T(8,128)(2,1)S(1)}, bf16[17,16,512...) custom-call(s32[267]{0:T(512)S(1)} %plan.1.refs_10_.refs_0_.scalars,, ...), custom_call_target="tpu_custom_call" | custom-call | tf_op jit(solution)/shard_map/stem_payloads/pallas_call | solution.py:484
  83.9 0.8 collective-permute-start.19
  84.7 2.2 %collective-permute-start.20 = (bf16[17,16,512]{2,1,0:T(8,128)(2,1)S(1)}, bf16[17,16,512]{2,1,0:T(8,128)(2,1)S(1)}, u32[]{:S(2)}, u32[]{:S(2)}) collective-permute-start(bf16[17,16,512]{2,1,0:T(8,128)(2,1)S(1)} %get-tuple-element.53), channel_id=1, source_target_pairs={{0,5},{1,4},{2,7},{3,6},{4,1},{5,0},{6,3},{7,2},{8,13},{9,12},{10,... | collective-permute-start | bytes 835592 | tf_op jit(solution)/shard_map/ppermute | solution.py:622
  87.3 1.1 collective-permute-start.22
  88.4 1.0 collective-permute-start.23
  89.4 13.0 %collective-permute-done.19.refs_3_.refs_1_ = bf16[17,16,512]{2,1,0:T(8,128)(2,1)S(1)} collective-permute-done((bf16[17,16,512]{2,1,0:T(8,128)(2,1)S(1)}, bf16[17,16,512]{2,1,0:T(8,128)(2,1)S(1)}, u32[]{:S(2)}, u32[]{:S(2)}) %collective-permute-start.19) | collective-permute-done | bytes 278560 | tf_op jit(solution)/shard_map/ppermute | solution.py:622
  102.9 1.1 collective-permute-start.29
  104.0 4.3 %collective-permute-done.20.refs_2_ = bf16[17,16,512]{2,1,0:T(8,128)(2,1)S(1)} collective-permute-done((bf16[17,16,512]{2,1,0:T(8,128)(2,1)S(1)}, bf16[17,16,512]{2,1,0:T(8,128)(2,1)S(1)}, u32[]{:S(2)}, u32[]{:S(2)}) %collective-permute-start.20) | collective-permute-done | bytes 278560 | tf_op jit(solution)/shard_map/ppermute | solution.py:622
  108.3 0.6 collective-permute-start.28
  108.9 0.7 collective-permute-start.27
  109.6 2.5 %collective-permute-done.22.refs_4_ = bf16[17,16,512]{2,1,0:T(8,128)(2,1)S(1)} collective-permute-done((bf16[17,16,512]{2,1,0:T(8,128)(2,1)S(1)}, bf16[17,16,512]{2,1,0:T(8,128)(2,1)S(1)}, u32[]{:S(2)}, u32[]{:S(2)}) %collective-permute-start.22) | collective-permute-done | bytes 278560 | tf_op jit(solution)/shard_map/ppermute | solution.py:622
  112.1 1.2 collective-permute-start.24
  113.3 12.9 %collective-permute-done.23.refs_5_ = bf16[17,16,512]{2,1,0:T(8,128)(2,1)S(1)} collective-permute-done((bf16[17,16,512]{2,1,0:T(8,128)(2,1)S(1)}, bf16[17,16,512]{2,1,0:T(8,128)(2,1)S(1)}, u32[]{:S(2)}, u32[]{:S(2)}) %collective-permute-start.23) | collective-permute-done | bytes 278560 | tf_op jit(solution)/shard_map/ppermute | solution.py:622
  126.2 3.6 %collective-permute-start.25 = (bf16[17,16,512]{2,1,0:T(8,128)(2,1)S(1)}, bf16[17,16,512]{2,1,0:T(8,128)(2,1)S(1)}, u32[]{:S(2)}, u32[]{:S(2)}) collective-permute-start(bf16[17,16,512]{2,1,0:T(8,128)(2,1)S(1)} %get-tuple-element.58), channel_id=1, source_target_pairs={{0,1},{1,0},{2,3},{3,2},{4,5},{5,4},{6,7},{7,6},{8,9},{9,8},{10,11... | collective-permute-start | bytes 835592 | tf_op jit(solution)/shard_map/ppermute | solution.py:622
  129.9 4.5 %collective-permute-done.24.refs_6_ = bf16[17,16,512]{2,1,0:T(8,128)(2,1)S(1)} collective-permute-done((bf16[17,16,512]{2,1,0:T(8,128)(2,1)S(1)}, bf16[17,16,512]{2,1,0:T(8,128)(2,1)S(1)}, u32[]{:S(2)}, u32[]{:S(2)}) %collective-permute-start.24) | collective-permute-done | bytes 278560 | tf_op jit(solution)/shard_map/ppermute | solution.py:622
  134.4 2.9 %owner_rows.1 = (bf16[2048,512]{1,0:T(8,128)(2,1)}, f32[192,1536]{1,0:T(8,128)}) custom-call(s32[267]{0:T(512)S(1)} %plan.1.refs_10_.refs_0_.scalars, bf16[17,16,512]{2,1,0:T(8,128)(2,1)S(1)} %get-tuple-element.51.refs_0_, bf16[17,16,512]{2,1,0:T(8,128)(2,1)S(1)} %collective-permute-done.19.refs_3_.refs_1_, ...), custom_call_target="tpu_custom_call" | custom-call | tf_op jit(solution)/shard_map/owner_rows/pallas_call | solution.py:538
  (40 shorter events, 2.8 us)
Async XLA Ops:
  0.6 9.7 %collective-permute-start = (bf16[512,1536]{1,0:T(8,128)(2,1)}, bf16[512,1536]{1,0:T(8,128)(2,1)S(1)}, u32[]{:S(2)}, u32[]{:S(2)}) collective-permute-start(bf16[512,1536]{1,0:T(8,128)(2,1)} %bitcast.12), channel_id=1, source_target_pairs={{0,1},{1,0},{2,3},{3,2},{4,5},{5,4},{6,7},{7,6},{8,9},{9,8},{10,11... | collective-permute-start | bytes 4718600 | tf_op jit(solution)/shard_map/ppermute | solution.py:33
  1.4 11.0 %collective-permute-start.1 = (bf16[512,1536]{1,0:T(8,128)(2,1)}, bf16[512,1536]{1,0:T(8,128)(2,1)S(1)}, u32[]{:S(2)}, u32[]{:S(2)}) collective-permute-start(bf16[512,1536]{1,0:T(8,128)(2,1)} %bitcast.9), channel_id=1, source_target_pairs={{0,1},{1,0},{2,3},{3,2},{4,5},{5,4},{6,7},{7,6},{8,9},{9,8},{10,11... | collective-permute-start | bytes 4718600 | tf_op jit(solution)/shard_map/ppermute | solution.py:33
  1.5 1.1 copy-start.3
  2.5 13.1 %collective-permute-start.4 = (bf16[192,384]{1,0:T(8,128)(2,1)S(1)}, bf16[192,384]{1,0:T(8,128)(2,1)S(1)}, u32[]{:S(2)}, u32[]{:S(2)}) collective-permute-start(bf16[192,384]{1,0:T(8,128)(2,1)S(1)} %cut_proj.1.refs_0_), channel_id=1, source_target_pairs={{0,6},{1,7},{2,4},{3,5},{4,2},{5,3},{6,0},{7,1},{8,14},{9,15},{10,... | collective-permute-start | bytes 442376 | tf_op jit(solution)/shard_map/ppermute | solution.py:37
  3.9 11.8 %collective-permute-start.3 = (bf16[192,384]{1,0:T(8,128)(2,1)S(1)}, bf16[192,384]{1,0:T(8,128)(2,1)}, u32[]{:S(2)}, u32[]{:S(2)}) collective-permute-start(bf16[192,384]{1,0:T(8,128)(2,1)S(1)} %cut_proj.1.refs_0_), channel_id=1, source_target_pairs={{0,2},{1,3},{2,0},{3,1},{4,6},{5,7},{6,4},{7,5},{8,10},{9,11},{10,... | collective-permute-start | bytes 442376 | tf_op jit(solution)/shard_map/ppermute | solution.py:37
  6.1 9.6 %collective-permute-start.2 = (bf16[192,384]{1,0:T(8,128)(2,1)S(1)}, bf16[192,384]{1,0:T(8,128)(2,1)}, u32[]{:S(2)}, u32[]{:S(2)}) collective-permute-start(bf16[192,384]{1,0:T(8,128)(2,1)S(1)} %cut_proj.1.refs_0_), channel_id=1, source_target_pairs={{0,4},{1,5},{2,6},{3,7},{4,0},{5,1},{6,2},{7,3},{8,12},{9,13},{10,... | collective-permute-start | bytes 442376 | tf_op jit(solution)/shard_map/ppermute | solution.py:37
  6.8 1.4 %copy-start.1 = (bf16[1,512,1536]{2,1,0:T(8,128)(2,1)S(1)}, bf16[1,512,1536]{2,1,0:T(8,128)(2,1)}, u32[]{:S(2)}) copy-start(bf16[1,512,1536]{2,1,0:T(8,128)(2,1)} %param.5) | copy-start | bytes 4718596
  10.3 2.1 %copy-start = (bf16[1,512,1536]{2,1,0:T(8,128)(2,1)S(1)}, bf16[1,512,1536]{2,1,0:T(8,128)(2,1)}, u32[]{:S(2)}) copy-start(bf16[1,512,1536]{2,1,0:T(8,128)(2,1)} %param.6) | copy-start | bytes 4718596
  12.4 3.3 %copy-start.5 = (bf16[3,64,1536]{2,1,0:T(8,128)(2,1)S(1)}, bf16[3,64,1536]{2,1,0:T(8,128)(2,1)}, u32[]{:S(2)}) copy-start(bf16[3,64,1536]{2,1,0:T(8,128)(2,1)} %refs_1_.2) | copy-start | bytes 1769476
  15.7 22.3 %copy-start.4 = (bf16[192,1536]{1,0:T(8,128)(2,1)S(1)}, bf16[192,1536]{1,0:T(8,128)(2,1)}, u32[]{:S(2)}) copy-start(bf16[192,1536]{1,0:T(8,128)(2,1)} %refs_1_.3) | copy-start | bytes 1769476
  16.8 21.2 %collective-permute-start.5 = (bf16[1056,384]{1,0:T(8,128)(2,1)S(1)}, bf16[1056,384]{1,0:T(8,128)(2,1)S(1)}, u32[]{:S(2)}, u32[]{:S(2)}) collective-permute-start(bf16[1056,384]{1,0:T(8,128)(2,1)S(1)} %get-tuple-element.34.refs_2_), channel_id=1, source_target_pairs={{0,8},{8,0},{16,24},{24,16},{1,9},{9,1},{17,25},{25,17},{2,10},{10... | collective-permute-start | bytes 2433032 | tf_op jit(solution)/shard_map/ppermute | solution.py:41
  18.1 19.9 %collective-permute-start.6 = (bf16[1056,384]{1,0:T(8,128)(2,1)S(1)}, bf16[1056,384]{1,0:T(8,128)(2,1)S(1)}, u32[]{:S(2)}, u32[]{:S(2)}) collective-permute-start(bf16[1056,384]{1,0:T(8,128)(2,1)S(1)} %get-tuple-element.35.refs_3_), channel_id=1, source_target_pairs={{0,16},{8,24},{16,0},{24,8},{1,17},{9,25},{17,1},{25,9},{2,18},{10... | collective-permute-start | bytes 2433032 | tf_op jit(solution)/shard_map/ppermute | solution.py:41
  19.3 18.7 %collective-permute-start.7 = (bf16[480,384]{1,0:T(8,128)(2,1)S(1)}, bf16[480,384]{1,0:T(8,128)(2,1)S(1)}, u32[]{:S(2)}, u32[]{:S(2)}) collective-permute-start(bf16[480,384]{1,0:T(8,128)(2,1)S(1)} %get-tuple-element.36.refs_6_), channel_id=1, source_target_pairs={{0,4},{1,5},{2,6},{3,7},{4,0},{5,1},{6,2},{7,3},{8,12},{9,13},{10,... | collective-permute-start | bytes 1105928 | tf_op jit(solution)/shard_map/ppermute | solution.py:37
  38.5 21.0 %collective-permute-start.8 = (bf16[2688,384]{1,0:T(8,128)(2,1)S(1)}, bf16[2688,384]{1,0:T(8,128)(2,1)S(1)}, u32[]{:S(2)}, u32[]{:S(2)}) collective-permute-start(bf16[2688,384]{1,0:T(8,128)(2,1)S(1)} %get-tuple-element.39), channel_id=1, source_target_pairs={{0,1},{1,0},{2,3},{3,2},{4,5},{5,4},{6,7},{7,6},{8,9},{9,8},{10,11... | collective-permute-start | bytes 6193160 | tf_op jit(solution)/shard_map/ppermute | solution.py:33
  39.2 18.1 %collective-permute-start.10 = (bf16[960,384]{1,0:T(8,128)(2,1)S(1)}, bf16[960,384]{1,0:T(8,128)(2,1)S(1)}, u32[]{:S(2)}, u32[]{:S(2)}) collective-permute-start(bf16[960,384]{1,0:T(8,128)(2,1)S(1)} %get-tuple-element.41.refs_2_), channel_id=1, source_target_pairs={{0,16},{8,24},{16,0},{24,8},{1,17},{9,25},{17,1},{25,9},{2,18},{10... | collective-permute-start | bytes 2211848 | tf_op jit(solution)/shard_map/ppermute | solution.py:41
  40.4 17.7 %collective-permute-start.11 = (bf16[960,384]{1,0:T(8,128)(2,1)S(1)}, bf16[960,384]{1,0:T(8,128)(2,1)S(1)}, u32[]{:S(2)}, u32[]{:S(2)}) collective-permute-start(bf16[960,384]{1,0:T(8,128)(2,1)S(1)} %get-tuple-element.42.refs_3_), channel_id=1, source_target_pairs={{0,8},{8,0},{16,24},{24,16},{1,9},{9,1},{17,25},{25,17},{2,10},{10... | collective-permute-start | bytes 2211848 | tf_op jit(solution)/shard_map/ppermute | solution.py:41
  40.7 18.9 %collective-permute-start.9 = (bf16[2,480,384]{2,1,0:T(8,128)(2,1)S(1)}, bf16[2,480,384]{2,1,0:T(8,128)(2,1)S(1)}, u32[]{:S(2)}, u32[]{:S(2)}) collective-permute-start(bf16[2,480,384]{2,1,0:T(8,128)(2,1)S(1)} %get-tuple-element.40.refs_0_), channel_id=1, source_target_pairs={{0,2},{1,3},{2,0},{3,1},{4,6},{5,7},{6,4},{7,5},{8,10},{9,11},{10,... | collective-permute-start | bytes 2211848 | tf_op jit(solution)/shard_map/ppermute | solution.py:37
  59.6 6.2 %copy-start.2 = (bf16[1,512,1536]{2,1,0:T(8,128)(2,1)S(1)}, bf16[1,512,1536]{2,1,0:T(8,128)(2,1)}, u32[]{:S(2)}) copy-start(bf16[1,512,1536]{2,1,0:T(8,128)(2,1)} %param.5) | copy-start | bytes 4718596
  59.8 5.2 %collective-permute-start.15 = (bf16[1152,384]{1,0:T(8,128)(2,1)S(1)}, bf16[1152,384]{1,0:T(8,128)(2,1)S(1)}, u32[]{:S(2)}, u32[]{:S(2)}) collective-permute-start(bf16[1152,384]{1,0:T(8,128)(2,1)S(1)} %get-tuple-element.48), channel_id=1, source_target_pairs={{0,1},{1,0},{2,3},{3,2},{4,5},{5,4},{6,7},{7,6},{8,9},{9,8},{10,11... | collective-permute-start | bytes 2654216 | tf_op jit(solution)/shard_map/ppermute | solution.py:33
  61.0 15.1 %collective-permute-start.17 = (bf16[1440,384]{1,0:T(8,128)(2,1)S(1)}, bf16[1440,384]{1,0:T(8,128)(2,1)S(1)}, u32[]{:S(2)}, u32[]{:S(2)}) collective-permute-start(bf16[1440,384]{1,0:T(8,128)(2,1)S(1)} %bitcast.18), channel_id=1, source_target_pairs={{0,1},{1,0},{2,3},{3,2},{4,5},{5,4},{6,7},{7,6},{8,9},{9,8},{10,11... | collective-permute-start | bytes 3317768 | tf_op jit(solution)/shard_map/ppermute | solution.py:33
  61.1 10.3 %collective-permute-start.16 = (bf16[2,192,384]{2,1,0:T(8,128)(2,1)S(1)}, bf16[2,192,384]{2,1,0:T(8,128)(2,1)S(1)}, u32[]{:S(2)}, u32[]{:S(2)}) collective-permute-start(bf16[2,192,384]{2,1,0:T(8,128)(2,1)S(1)} %get-tuple-element.49), channel_id=1, source_target_pairs={{0,2},{1,3},{2,0},{3,1},{4,6},{5,7},{6,4},{7,5},{8,10},{9,11},{10,... | collective-permute-start | bytes 884744 | tf_op jit(solution)/shard_map/ppermute | solution.py:37
  63.1 8.9 %collective-permute-start.14 = (bf16[3,96,384]{2,1,0:T(8,128)(2,1)S(1)}, bf16[3,96,384]{2,1,0:T(8,128)(2,1)S(1)}, u32[]{:S(2)}, u32[]{:S(2)}) collective-permute-start(bf16[3,96,384]{2,1,0:T(8,128)(2,1)S(1)} %get-tuple-element.47), channel_id=1, source_target_pairs={{0,24},{8,16},{16,8},{24,0},{1,25},{9,17},{17,9},{25,1},{2,26},{10... | collective-permute-start | bytes 663560 | tf_op jit(solution)/shard_map/ppermute | solution.py:41
  64.1 12.0 %collective-permute-start.13 = (bf16[3,96,384]{2,1,0:T(8,128)(2,1)S(1)}, bf16[3,96,384]{2,1,0:T(8,128)(2,1)S(1)}, u32[]{:S(2)}, u32[]{:S(2)}) collective-permute-start(bf16[3,96,384]{2,1,0:T(8,128)(2,1)S(1)} %get-tuple-element.47), channel_id=1, source_target_pairs={{0,16},{8,24},{16,0},{24,8},{1,17},{9,25},{17,1},{25,9},{2,18},{10... | collective-permute-start | bytes 663560 | tf_op jit(solution)/shard_map/ppermute | solution.py:41
  64.9 11.1 %collective-permute-start.12 = (bf16[3,96,384]{2,1,0:T(8,128)(2,1)S(1)}, bf16[3,96,384]{2,1,0:T(8,128)(2,1)S(1)}, u32[]{:S(2)}, u32[]{:S(2)}) collective-permute-start(bf16[3,96,384]{2,1,0:T(8,128)(2,1)S(1)} %get-tuple-element.47), channel_id=1, source_target_pairs={{0,8},{8,0},{16,24},{24,16},{1,9},{9,1},{17,25},{25,17},{2,10},{10... | collective-permute-start | bytes 663560 | tf_op jit(solution)/shard_map/ppermute | solution.py:41
  76.1 2.3 %collective-permute-start.18 = (bf16[864,384]{1,0:T(8,128)(2,1)S(1)}, bf16[864,384]{1,0:T(8,128)(2,1)S(1)}, u32[]{:S(2)}, u32[]{:S(2)}) collective-permute-start(bf16[864,384]{1,0:T(8,128)(2,1)S(1)} %bitcast.16), channel_id=1, source_target_pairs={{0,1},{1,0},{2,3},{3,2},{4,5},{5,4},{6,7},{7,6},{8,9},{9,8},{10,11... | collective-permute-start | bytes 1990664 | tf_op jit(solution)/shard_map/ppermute | solution.py:33
  76.7 11.7 %collective-permute-start.26 = (bf16[192,384]{1,0:T(8,128)(2,1)S(1)}, bf16[192,384]{1,0:T(8,128)(2,1)S(1)}, u32[]{:S(2)}, u32[]{:S(2)}) collective-permute-start(bf16[192,384]{1,0:T(8,128)(2,1)S(1)} %get-tuple-element.50.refs_4_), channel_id=1, source_target_pairs={{0,4},{1,5},{2,6},{3,7},{4,0},{5,1},{6,2},{7,3},{8,12},{9,13},{10,... | collective-permute-start | bytes 442376 | tf_op jit(solution)/shard_map/ppermute | solution.py:37
  83.9 18.4 %collective-permute-start.19 = (bf16[17,16,512]{2,1,0:T(8,128)(2,1)S(1)}, bf16[17,16,512]{2,1,0:T(8,128)(2,1)S(1)}, u32[]{:S(2)}, u32[]{:S(2)}) collective-permute-start(bf16[17,16,512]{2,1,0:T(8,128)(2,1)S(1)} %get-tuple-element.52), channel_id=1, source_target_pairs={{0,4},{1,5},{2,6},{3,7},{4,0},{5,1},{6,2},{7,3},{8,12},{9,13},{10,... | collective-permute-start | bytes 835592 | tf_op jit(solution)/shard_map/ppermute | solution.py:622
  84.7 23.6 %collective-permute-start.20 = (bf16[17,16,512]{2,1,0:T(8,128)(2,1)S(1)}, bf16[17,16,512]{2,1,0:T(8,128)(2,1)S(1)}, u32[]{:S(2)}, u32[]{:S(2)}) collective-permute-start(bf16[17,16,512]{2,1,0:T(8,128)(2,1)S(1)} %get-tuple-element.53), channel_id=1, source_target_pairs={{0,5},{1,4},{2,7},{3,6},{4,1},{5,0},{6,3},{7,2},{8,13},{9,12},{10,... | collective-permute-start | bytes 835592 | tf_op jit(solution)/shard_map/ppermute | solution.py:622
  86.9 22.1 %collective-permute-start.21 = (bf16[17,16,512]{2,1,0:T(8,128)(2,1)S(1)}, bf16[17,16,512]{2,1,0:T(8,128)(2,1)S(1)}, u32[]{:S(2)}, u32[]{:S(2)}) collective-permute-start(bf16[17,16,512]{2,1,0:T(8,128)(2,1)S(1)} %get-tuple-element.54), channel_id=1, source_target_pairs={{0,2},{1,3},{2,0},{3,1},{4,6},{5,7},{6,4},{7,5},{8,10},{9,11},{10,... | collective-permute-start | bytes 835592 | tf_op jit(solution)/shard_map/ppermute | solution.py:622
  87.3 24.8 %collective-permute-start.22 = (bf16[17,16,512]{2,1,0:T(8,128)(2,1)S(1)}, bf16[17,16,512]{2,1,0:T(8,128)(2,1)S(1)}, u32[]{:S(2)}, u32[]{:S(2)}) collective-permute-start(bf16[17,16,512]{2,1,0:T(8,128)(2,1)S(1)} %get-tuple-element.55), channel_id=1, source_target_pairs={{0,3},{1,2},{2,1},{3,0},{4,7},{5,6},{6,5},{7,4},{8,11},{9,10},{10,... | collective-permute-start | bytes 835592 | tf_op jit(solution)/shard_map/ppermute | solution.py:622
  88.4 37.8 %collective-permute-start.23 = (bf16[17,16,512]{2,1,0:T(8,128)(2,1)S(1)}, bf16[17,16,512]{2,1,0:T(8,128)(2,1)S(1)}, u32[]{:S(2)}, u32[]{:S(2)}) collective-permute-start(bf16[17,16,512]{2,1,0:T(8,128)(2,1)S(1)} %get-tuple-element.56), channel_id=1, source_target_pairs={{0,6},{1,7},{2,4},{3,5},{4,2},{5,3},{6,0},{7,1},{8,14},{9,15},{10,... | collective-permute-start | bytes 835592 | tf_op jit(solution)/shard_map/ppermute | solution.py:622
  102.9 31.4 %collective-permute-start.29 = (f32[192,384]{1,0:T(8,128)S(1)}, f32[192,384]{1,0:T(8,128)S(1)}, u32[]{:S(2)}, u32[]{:S(2)}) collective-permute-start(f32[192,384]{1,0:T(8,128)S(1)} %far_sum.1.refs_8_), channel_id=1, source_target_pairs={{0,24},{8,16},{16,8},{24,0},{1,25},{9,17},{17,9},{25,1},{2,26},{10... | collective-permute-start | bytes 884744 | tf_op jit(solution)/shard_map/ppermute | solution.py:41
  108.3 26.1 %collective-permute-start.28 = (f32[192,384]{1,0:T(8,128)S(1)}, f32[192,384]{1,0:T(8,128)S(1)}, u32[]{:S(2)}, u32[]{:S(2)}) collective-permute-start(f32[192,384]{1,0:T(8,128)S(1)} %far_sum.1.refs_8_), channel_id=1, source_target_pairs={{0,16},{8,24},{16,0},{24,8},{1,17},{9,25},{17,1},{25,9},{2,18},{10... | collective-permute-start | bytes 884744 | tf_op jit(solution)/shard_map/ppermute | solution.py:41
  108.9 25.5 %collective-permute-start.27 = (f32[192,384]{1,0:T(8,128)S(1)}, f32[192,384]{1,0:T(8,128)S(1)}, u32[]{:S(2)}, u32[]{:S(2)}) collective-permute-start(f32[192,384]{1,0:T(8,128)S(1)} %far_sum.1.refs_8_), channel_id=1, source_target_pairs={{0,8},{8,0},{16,24},{24,16},{1,9},{9,1},{17,25},{25,17},{2,10},{10... | collective-permute-start | bytes 884744 | tf_op jit(solution)/shard_map/ppermute | solution.py:41
  112.1 22.2 %collective-permute-start.24 = (bf16[17,16,512]{2,1,0:T(8,128)(2,1)S(1)}, bf16[17,16,512]{2,1,0:T(8,128)(2,1)S(1)}, u32[]{:S(2)}, u32[]{:S(2)}) collective-permute-start(bf16[17,16,512]{2,1,0:T(8,128)(2,1)S(1)} %get-tuple-element.57), channel_id=1, source_target_pairs={{0,7},{1,6},{2,5},{3,4},{4,3},{5,2},{6,1},{7,0},{8,15},{9,14},{10,... | collective-permute-start | bytes 835592 | tf_op jit(solution)/shard_map/ppermute | solution.py:622
  126.2 8.1 %collective-permute-start.25 = (bf16[17,16,512]{2,1,0:T(8,128)(2,1)S(1)}, bf16[17,16,512]{2,1,0:T(8,128)(2,1)S(1)}, u32[]{:S(2)}, u32[]{:S(2)}) collective-permute-start(bf16[17,16,512]{2,1,0:T(8,128)(2,1)S(1)} %get-tuple-element.58), channel_id=1, source_target_pairs={{0,1},{1,0},{2,3},{3,2},{4,5},{5,4},{6,7},{7,6},{8,9},{9,8},{10,11... | collective-permute-start | bytes 835592 | tf_op jit(solution)/shard_map/ppermute | solution.py:622

commit v7 on v6

--- a/solution.py
+++ b/solution.py
@@ -403,10 +403,12 @@
     return 2 * (start // (2 * N_FSDP)) + jnp.clip(start % (2 * N_FSDP) - 2 * holder, 0, 2)
 
 
+PAIRS = CAP // 2
 BASES_AT = 2
-SEGMENTS_AT = BASES_AT + N_FSDP
+SPLITS_AT = BASES_AT + N_FSDP
+SEGMENTS_AT = SPLITS_AT + N_FSDP
 BEFORE_AT = SEGMENTS_AT + N_FSDP * CAP
-COUNT_AT = BEFORE_AT + N_FSDP * CAP
+COUNT_AT = BEFORE_AT + N_FSDP * PAIRS
 
 
 def plan_kernel(scalars, plan):
@@ -419,9 +421,11 @@
         starts.append(starts[-1] + scalars[2 + owner])
     my_start = jnp.int32(0)
     for owner in range(N_FSDP):
-        place = lax.bitwise_xor(index, owner)
-        plan[BASES_AT + place] = held_before(starts[owner], index)
+        start = starts[owner]
+        plan[BASES_AT + lax.bitwise_xor(index, owner)] = held_before(start, index)
         my_start = my_start + jnp.where(owner < index, scalars[2 + owner], 0)
+        splits = (start % 2 == 1) & (start // 2 % N_FSDP == index)
+        plan[SPLITS_AT + owner] = jnp.where(splits, 2 * (start // (2 * N_FSDP)) * SEG + SEG - 1, -1)
 
     @pl.loop(0, N_FSDP * CAP)
     def _(block):
@@ -430,7 +434,17 @@
         segment = 2 * (slot // 2 * N_FSDP + holder) + slot % 2 - my_start
         held = (segment >= 0) & (segment < count)
         plan[SEGMENTS_AT + block] = jnp.where(held, segment, OWN_SEG)
-        plan[BEFORE_AT + block] = jnp.where(held & (segment > 0), segment - 1, OWN_SEG)
+
+    @pl.loop(0, N_FSDP * PAIRS)
+    def _(block):
+        holder = lax.bitwise_xor(index, block // PAIRS)
+        segment = 2 * (even_slot(held_before(my_start, holder), block % PAIRS) // 2 * N_FSDP + holder) - my_start
+        held = (segment > 0) & (segment < count)
+        plan[BEFORE_AT + block] = jnp.where(held, segment - 1, OWN_SEG)
+
+
+def even_slot(base, i):
+    return base + base % 2 + 2 * i
 
 
 def plan_of(scalars):
@@ -449,20 +463,25 @@
         copy.start()
     for copy in copies:
         copy.wait()
-    index = scalars[1]
+    row = lax.broadcasted_iota(jnp.int32, (ROWS, LANES), 0)
+    inside = row % (2 * SEG) == SEG - 1
+    for owner in range(1, N_FSDP):
+        inside = inside & (row != scalars[SPLITS_AT + owner])
+    inside = inside | (row % SEG != SEG - 1)
     for lane in range(0, CS, CS // 2):
         span = pl.ds(lane, CS // 2)
         even = dot_nt(grad_ref[...], weight[1, span, :])
         first = dot_nt(grad_ref[...], weight[0, span, :])
         leading[:, span] = first
-        row = lax.broadcasted_iota(jnp.int32, first.shape, 0)
-        following = jnp.where(row % SEG == SEG - 1, 0.0, pltpu.roll(first, ROWS - 1, 0))
-        odd = dot_nt(grad_ref[...], weight[2, span, :]) + following
+        following = pltpu.roll(first, ROWS - 1, 0)
+        odd = dot_nt(grad_ref[...], weight[2, span, :])
         for part in range(CS // 2 // LANES):
             at = lane // LANES + part
             columns = slice(part * LANES, (part + 1) * LANES)
             mixed[at, pl.ds(0, ROWS, stride=2), :] = even[:, columns]
-            mixed[at, pl.ds(1, ROWS, stride=2), :] = odd[:, columns]
+            mixed[at, pl.ds(1, ROWS, stride=2), :] = odd[:, columns] + jnp.where(
+                inside, following[:, columns], 0.0
+            )
 
     for place, out in enumerate(outs):
         base = scalars[BASES_AT + place]
@@ -470,9 +489,14 @@
             slot = jnp.minimum(base + rank, HOLD - 1)
             rows = pl.ds(pl.multiple_of(slot * 2 * SEG, 2 * SEG), 2 * SEG)
             for lane in range(CS // LANES):
-                out[rank, :, lane * LANES : (lane + 1) * LANES] = mixed[lane, rows, :].astype(BF16)
-            firsts[rank : rank + 1, :] = leading[pl.ds(slot * SEG, 1), :]
-        out[CAP] = firsts[...].astype(BF16)
+                at, columns = divmod(lane * LANES, CS // 2)
+                out[2 * rank + at, :, columns : columns + LANES] = mixed[lane, rows, :].astype(BF16)
+        for i in range(PAIRS):
+            slot = jnp.minimum(even_slot(base, i), HOLD - 1)
+            first = leading[pl.ds(slot * SEG, 1), :]
+            for at in range(2):
+                firsts[at * PAIRS + i : at * PAIRS + i + 1, :] = first[:, at * CS // 2 : (at + 1) * CS // 2]
+        out[2 * CAP] = firsts[...].astype(BF16)
 
 
 VMEM = pl.BlockSpec(memory_space=pltpu.VMEM)
@@ -480,7 +504,7 @@
 
 def stem_payloads(scalars, parts, grad):
     tables, values = split_parts(parts)
-    payload = (CAP + 1, 2 * SEG, CS)
+    payload = (2 * CAP + 1, 2 * PAIRS, CS // 2)
     return call(
         lambda *refs: stem_kernel(tables, *refs), "stem_payloads",
         (shape(payload, BF16),) * N_FSDP, (1,),
@@ -489,7 +513,7 @@
             pltpu.VMEM((3, CS, D), BF16),
             pltpu.VMEM((CS // LANES, 2 * ROWS, LANES), F32),
             pltpu.VMEM((ROWS, CS), F32),
-            pltpu.VMEM((CAP, CS), F32),
+            pltpu.VMEM((2 * PAIRS, CS // 2), F32),
             pltpu.SemaphoreType.DMA,
         ],
         vmem=18,
@@ -516,18 +540,21 @@
     def _(segment):
         out[rows_of_segment(segment), :] = jnp.zeros((2 * SEG, CS), BF16)
 
+    halves = [slice(0, CS // 2), slice(CS // 2, CS)]
     for i, place in enumerate(PAYLOAD_ORDER):
         for rank in range(CAP):
-            segment = scalars[SEGMENTS_AT + place * CAP + rank]
-            out[rows_of_segment(segment), :] = payloads[i][rank]
-    last_row = lax.broadcasted_iota(jnp.int32, (2 * SEG, CS), 0) == 2 * SEG - 1
+            rows = rows_of_segment(scalars[SEGMENTS_AT + place * CAP + rank])
+            for at, columns in enumerate(halves):
+                out[rows, columns] = payloads[i][2 * rank + at]
+    last_row = lax.broadcasted_iota(jnp.int32, (2 * SEG, CS // 2), 0) == 2 * SEG - 1
     for i, place in enumerate(PAYLOAD_ORDER):
-        firsts = payloads[i][CAP].astype(F32)
-        for rank in range(CAP):
-            rows = rows_of_segment(scalars[BEFORE_AT + place * CAP + rank])
-            first = jnp.broadcast_to(firsts[rank : rank + 1, :], (2 * SEG, CS))
-            term = jnp.where(last_row, first, 0.0)
-            out[rows, :] = (out[rows, :].astype(F32) + term).astype(BF16)
+        firsts = payloads[i][2 * CAP].astype(F32)
+        for pair in range(PAIRS):
+            rows = rows_of_segment(scalars[BEFORE_AT + place * PAIRS + pair])
+            for at, columns in enumerate(halves):
+                first = firsts[at * PAIRS + pair : at * PAIRS + pair + 1, :]
+                term = jnp.where(last_row, jnp.broadcast_to(first, last_row.shape), 0.0)
+                out[rows, columns] = (out[rows, columns].astype(F32) + term).astype(BF16)
     copies.append(fetch(out.at[pl.ds(0, out_hbm.shape[0]), :], out_hbm, sem))
     for copy in copies:
         copy.wait()

time: 138 us -> 136 us (0.986)
  waiting for transfers between devices: 68.1 us -> 65.1 us
  Pallas kernels: 30 us -> 31.7 us
    ppermute x7, waiting for transfers between devices: 37.2 us -> 35.7 us  [body(): lax.ppermute(payloads[d], 'fsdp', [(i, i ^ d) for i in range(N_FSDP)])]
    ppermute x7, waiting for transfers between devices: 10.9 us -> 9.42 us  [swap_z(): lax.ppermute(value, 'fsdp', [(i, i ^ 2 * distance) for i in range(N_FSDP)])]
    pallas_call x1, Pallas kernels: 4.79 us -> 6.28 us  [plan_of(): call(plan_kernel, 'plan', shape((COUNT_AT + 1,), jnp.int32), (1,), [], pl...]
  transfers between devices with their start and end apart: 30 -> 30, of which waited for: 11 -> 11; matrix products, arithmetic and copies ran while one was open for 1% -> 1% of each run, Pallas kernels for 18% -> 20%
where the time goes in v7:
time: 136 us
  waiting for transfers between devices  65.1 us (48%)
  starting transfers between devices  35.3 us (26%)
  Pallas kernels  31.7 us (23%)
  local copies, waits for them, and re-layouts  2.5 us (2%)
    ppermute x7, waiting for transfers between devices, body(): lax.ppermute(payloads[d], 'fsdp', [(i, i ^ d) for i in range(N_FSDP)])  35.7 us
    ppermute x10, waiting for transfers between devices, swap_site(): lax.ppermute(value, 'site', [(i, i ^ distance) for i in range(N_SITE)])  19 us
    ppermute x7, starting transfers between devices, swap_z(): lax.ppermute(value, 'fsdp', [(i, i ^ 2 * distance) for i in range(N_FSDP)])  12.5 us
    ppermute x7, starting transfers between devices, body(): lax.ppermute(payloads[d], 'fsdp', [(i, i ^ d) for i in range(N_FSDP)])  10.4 us
    ppermute x7, waiting for transfers between devices, swap_z(): lax.ppermute(value, 'fsdp', [(i, i ^ 2 * distance) for i in range(N_FSDP)])  9.42 us
    ppermute x10, starting transfers between devices, swap_site(): lax.ppermute(value, 'site', [(i, i ^ distance) for i in range(N_SITE)])  9.04 us
    pallas_call x1, Pallas kernels, plan_of(): call(plan_kernel, 'plan', shape((COUNT_AT + 1,), jnp.int32), (1,), [], pl...  6.28 us
    pallas_call x1, Pallas kernels, input_gradient(): call(lambda *refs: input_grad_kernel(tables, *refs), 'input_gradient', sh...  5.6 us
  transfers between devices with their start and end apart: 30, of which 11 were waited for; matrix products, arithmetic and copies ran while one was open for 1% of the time, Pallas kernels for 20%

profile of v7, /device:TPU:9, one launch (start us, length us, event | category | flops | bytes accessed | tf_op | source)
XLA Modules:
  0.0 136.3 jit_solution(14121312633492775584)
XLA Ops:
  0.6 0.7 collective-permute-start
  1.5 1.1 copy-done.3
  2.5 1.4 collective-permute-start.4
  3.9 2.2 %collective-permute-start.3 = (bf16[192,384]{1,0:T(8,128)(2,1)S(1)}, bf16[192,384]{1,0:T(8,128)(2,1)}, u32[]{:S(2)}, u32[]{:S(2)}) collective-permute-start(bf16[192,384]{1,0:T(8,128)(2,1)S(1)} %cut_proj.1.refs_0_), channel_id=1, source_target_pairs={{0,2},{1,3},{2,0},{3,1},{4,6},{5,7},{6,4},{7,5},{8,10},{9,11},{10,... | collective-permute-start | bytes 442376 | tf_op jit(solution)/shard_map/ppermute | solution.py:37
  6.1 0.7 pad_add_fusion.scalars.refs_0_
  6.8 1.4 %copy-done.1 = bf16[1,512,1536]{2,1,0:T(8,128)(2,1)S(1)} copy-done((bf16[1,512,1536]{2,1,0:T(8,128)(2,1)S(1)}, bf16[1,512,1536]{2,1,0:T(8,128)(2,1)}, u32[]{:S(2)}) %copy-start.1) | copy-done | bytes 1572888
  8.2 2.1 %norm_half.2.refs_0_.na_ref = bf16[768,512]{1,0:T(8,128)(2,1)S(1)} custom-call(s32[10]{0:T(128)S(1)} %pad_add_fusion.scalars.refs_0_, bf16[512,1536]{1,0:T(8,128)(2,1)S(1)} %bitcast.13, bf16[192,384]{1,0:T(8,128)(2,1)S(1)} %cut_proj.1.refs_0_), custom_call_target="tpu_custom_call" | custom-call | tf_op jit(solution)/shard_map/norm_half/pallas_call | solution.py:225
  10.3 2.1 %norm_half.3.nb_ref = bf16[768,512]{1,0:T(8,128)(2,1)S(1)} custom-call(s32[10]{0:T(128)S(1)} %pad_add_fusion.scalars.refs_0_, bf16[512,1536]{1,0:T(8,128)(2,1)S(1)} %collective-permute-done.x_ref, bf16[768,512]{1,0:T(8,128)(2,1)S(1)} %norm_half.2.refs_0_.na_ref), custom_call_target="tpu_custom_call" | custom-call | tf_op jit(solution)/shard_map/norm_half/pallas_call | solution.py:225
  12.4 3.2 %outer_pieces.1 = (f32[2,384,384]{2,1,0:T(8,128)S(1)}, bf16[1056,384]{1,0:T(8,128)(2,1)S(1)}, f32[2,384,384]{2,1,0:T(8,128)S(1)}, bf16[1056,384]{1,0:T(8,128)(2,1)S(1)}) custom-call(s32[10]{0:T(128)S(1)} %pad_add_fusion.scalars.refs_0_, bf16[768,512]{1,0:T(8,128)(2,1)S(1)} %norm_half.2.refs_0_.na_ref, bf16[768,512]{1,0:T(8,128)(2,1)S(1)} %norm_half.3.nb_ref, ...), custom_call_target="tpu_custom_call" | custom-call | tf_op jit(solution)/shard_map/outer_pieces/pallas_call | solution.py:258
  15.7 1.1 halves.1
  16.8 1.3 collective-permute-start.5
  18.1 1.2 collective-permute-start.6
  19.3 3.6 %collective-permute-start.7 = (bf16[480,384]{1,0:T(8,128)(2,1)S(1)}, bf16[480,384]{1,0:T(8,128)(2,1)S(1)}, u32[]{:S(2)}, u32[]{:S(2)}) collective-permute-start(bf16[480,384]{1,0:T(8,128)(2,1)S(1)} %get-tuple-element.36.refs_6_), channel_id=1, source_target_pairs={{0,4},{1,5},{2,6},{3,7},{4,0},{5,1},{6,2},{7,3},{8,12},{9,13},{10,... | collective-permute-start | bytes 1105928 | tf_op jit(solution)/shard_map/ppermute | solution.py:37
  22.9 6.3 %plan.1.refs_10_.refs_0_.scalars = s32[211]{0:T(256)S(1)} custom-call(s32[10]{0:T(128)S(1)} %pad_add_fusion.scalars.refs_0_), custom_call_target="tpu_custom_call" | custom-call | tf_op jit(solution)/shard_map/plan/pallas_call | solution.py:451
  29.2 8.8 %collective-permute-done.7.refs_7_ = bf16[480,384]{1,0:T(8,128)(2,1)S(1)} collective-permute-done((bf16[480,384]{1,0:T(8,128)(2,1)S(1)}, bf16[480,384]{1,0:T(8,128)(2,1)S(1)}, u32[]{:S(2)}, u32[]{:S(2)}) %collective-permute-start.7) | collective-permute-done | bytes 368672 | tf_op jit(solution)/shard_map/ppermute | solution.py:37
  38.5 0.6 collective-permute-start.8
  39.2 1.2 collective-permute-start.10
  40.7 2.6 %collective-permute-start.9 = (bf16[2,480,384]{2,1,0:T(8,128)(2,1)S(1)}, bf16[2,480,384]{2,1,0:T(8,128)(2,1)S(1)}, u32[]{:S(2)}, u32[]{:S(2)}) collective-permute-start(bf16[2,480,384]{2,1,0:T(8,128)(2,1)S(1)} %get-tuple-element.40.refs_0_), channel_id=1, source_target_pairs={{0,2},{1,3},{2,0},{3,1},{4,6},{5,7},{6,4},{7,5},{8,10},{9,11},{10,... | collective-permute-start | bytes 2211848 | tf_op jit(solution)/shard_map/ppermute | solution.py:37
  43.3 14.0 %collective-permute-done.10.ra_ref.refs_2_.refs_4_ = bf16[960,384]{1,0:T(8,128)(2,1)S(1)} collective-permute-done((bf16[960,384]{1,0:T(8,128)(2,1)S(1)}, bf16[960,384]{1,0:T(8,128)(2,1)S(1)}, u32[]{:S(2)}, u32[]{:S(2)}) %collective-permute-start.10) | collective-permute-done | bytes 737312 | tf_op jit(solution)/shard_map/ppermute | solution.py:41
  57.2 0.9 collective-permute-done.11.rb_ref.refs_3_.refs_5_
  58.2 0.7 site_sum.1
  58.9 0.6 collective-permute-done.9.refs_1_
  59.8 1.2 collective-permute-start.15
  61.1 2.0 %collective-permute-start.16 = (bf16[2,192,384]{2,1,0:T(8,128)(2,1)S(1)}, bf16[2,192,384]{2,1,0:T(8,128)(2,1)S(1)}, u32[]{:S(2)}, u32[]{:S(2)}) collective-permute-start(bf16[2,192,384]{2,1,0:T(8,128)(2,1)S(1)} %get-tuple-element.49), channel_id=1, source_target_pairs={{0,2},{1,3},{2,0},{3,1},{4,6},{5,7},{6,4},{7,5},{8,10},{9,11},{10,... | collective-permute-start | bytes 884744 | tf_op jit(solution)/shard_map/ppermute | solution.py:37
  63.1 1.0 collective-permute-start.14
  64.1 0.8 collective-permute-start.13
  64.9 0.8 collective-permute-start.12
  65.7 5.6 %input_gradient.1.refs_0_.refs_3_.refs_7_ = bf16[512,1536]{1,0:T(8,128)(2,1)S(1)} custom-call(s32[10]{0:T(128)S(1)} %pad_add_fusion.scalars.refs_0_, bf16[192,1536]{1,0:T(8,128)(2,1)S(1)} %copy-done.4, bf16[960,384]{1,0:T(8,128)(2,1)S(1)} %get-tuple-element.41.refs_2_, bf16[960,384]{1,0:T(8,128)(2,1)S(1)} %get-tuple-element.42.refs_3_, ...), custom_call_target="tpu_custom_call" | custom-call | tf_op jit(solution)/shard_map/input_gradient/pallas_call | solution.py:385
  71.3 0.6 near_sum.1
  72.0 4.1 %collective-permute-done.13.refs_1_ = bf16[3,96,384]{2,1,0:T(8,128)(2,1)S(1)} collective-permute-done((bf16[3,96,384]{2,1,0:T(8,128)(2,1)S(1)}, bf16[3,96,384]{2,1,0:T(8,128)(2,1)S(1)}, u32[]{:S(2)}, u32[]{:S(2)}) %collective-permute-start.13) | collective-permute-done | bytes 221216 | tf_op jit(solution)/shard_map/ppermute | solution.py:41
  76.7 0.7 collective-permute-start.26
  77.4 1.0 collective-permute-done.18.refs_6_
  78.4 5.5 %stem_payloads.1 = (bf16[33,16,256]{2,1,0:T(8,128)(2,1)S(1)}, bf16[33,16,256]{2,1,0:T(8,128)(2,1)S(1)}, bf16[33,16,256]{2,1,0:T(8,128)(2,1)S(1)}, bf16[33,16,256...) custom-call(s32[211]{0:T(256)S(1)} %plan.1.refs_10_.refs_0_.scalars,, ...), custom_call_target="tpu_custom_call" | custom-call | tf_op jit(solution)/shard_map/stem_payloads/pallas_call | solution.py:508
  83.9 0.8 collective-permute-start.19
  84.7 2.2 %collective-permute-start.20 = (bf16[33,16,256]{2,1,0:T(8,128)(2,1)S(1)}, bf16[33,16,256]{2,1,0:T(8,128)(2,1)S(1)}, u32[]{:S(2)}, u32[]{:S(2)}) collective-permute-start(bf16[33,16,256]{2,1,0:T(8,128)(2,1)S(1)} %get-tuple-element.53), channel_id=1, source_target_pairs={{0,5},{1,4},{2,7},{3,6},{4,1},{5,0},{6,3},{7,2},{8,13},{9,12},{10,... | collective-permute-start | bytes 811016 | tf_op jit(solution)/shard_map/ppermute | solution.py:649
  87.3 1.1 collective-permute-start.22
  88.4 1.0 collective-permute-start.23
  89.4 12.4 %collective-permute-done.19.refs_3_.refs_1_ = bf16[33,16,256]{2,1,0:T(8,128)(2,1)S(1)} collective-permute-done((bf16[33,16,256]{2,1,0:T(8,128)(2,1)S(1)}, bf16[33,16,256]{2,1,0:T(8,128)(2,1)S(1)}, u32[]{:S(2)}, u32[]{:S(2)}) %collective-permute-start.19) | collective-permute-done | bytes 270368 | tf_op jit(solution)/shard_map/ppermute | solution.py:649
  102.4 1.1 collective-permute-start.29
  103.5 4.1 %collective-permute-done.20.refs_2_ = bf16[33,16,256]{2,1,0:T(8,128)(2,1)S(1)} collective-permute-done((bf16[33,16,256]{2,1,0:T(8,128)(2,1)S(1)}, bf16[33,16,256]{2,1,0:T(8,128)(2,1)S(1)}, u32[]{:S(2)}, u32[]{:S(2)}) %collective-permute-start.20) | collective-permute-done | bytes 270368 | tf_op jit(solution)/shard_map/ppermute | solution.py:649
  107.6 0.6 collective-permute-start.28
  108.2 0.7 collective-permute-start.27
  108.9 2.5 %collective-permute-done.22.refs_4_ = bf16[33,16,256]{2,1,0:T(8,128)(2,1)S(1)} collective-permute-done((bf16[33,16,256]{2,1,0:T(8,128)(2,1)S(1)}, bf16[33,16,256]{2,1,0:T(8,128)(2,1)S(1)}, u32[]{:S(2)}, u32[]{:S(2)}) %collective-permute-start.22) | collective-permute-done | bytes 270368 | tf_op jit(solution)/shard_map/ppermute | solution.py:649
  111.4 1.2 collective-permute-start.24
  112.6 12.3 %collective-permute-done.23.refs_5_ = bf16[33,16,256]{2,1,0:T(8,128)(2,1)S(1)} collective-permute-done((bf16[33,16,256]{2,1,0:T(8,128)(2,1)S(1)}, bf16[33,16,256]{2,1,0:T(8,128)(2,1)S(1)}, u32[]{:S(2)}, u32[]{:S(2)}) %collective-permute-start.23) | collective-permute-done | bytes 270368 | tf_op jit(solution)/shard_map/ppermute | solution.py:649
  124.8 3.8 %collective-permute-start.25 = (bf16[33,16,256]{2,1,0:T(8,128)(2,1)S(1)}, bf16[33,16,256]{2,1,0:T(8,128)(2,1)S(1)}, u32[]{:S(2)}, u32[]{:S(2)}) collective-permute-start(bf16[33,16,256]{2,1,0:T(8,128)(2,1)S(1)} %get-tuple-element.58), channel_id=1, source_target_pairs={{0,1},{1,0},{2,3},{3,2},{4,5},{5,4},{6,7},{7,6},{8,9},{9,8},{10,11... | collective-permute-start | bytes 811016 | tf_op jit(solution)/shard_map/ppermute | solution.py:649
  128.6 4.4 %collective-permute-done.24.refs_6_ = bf16[33,16,256]{2,1,0:T(8,128)(2,1)S(1)} collective-permute-done((bf16[33,16,256]{2,1,0:T(8,128)(2,1)S(1)}, bf16[33,16,256]{2,1,0:T(8,128)(2,1)S(1)}, u32[]{:S(2)}, u32[]{:S(2)}) %collective-permute-start.24) | collective-permute-done | bytes 270368 | tf_op jit(solution)/shard_map/ppermute | solution.py:649
  133.0 3.2 %owner_rows.1 = (bf16[2048,512]{1,0:T(8,128)(2,1)}, f32[192,1536]{1,0:T(8,128)}) custom-call(s32[211]{0:T(256)S(1)} %plan.1.refs_10_.refs_0_.scalars, bf16[33,16,256]{2,1,0:T(8,128)(2,1)S(1)} %get-tuple-element.51.refs_0_, bf16[33,16,256]{2,1,0:T(8,128)(2,1)S(1)} %collective-permute-done.19.refs_3_.refs_1_, ...), custom_call_target="tpu_custom_call" | custom-call | tf_op jit(solution)/shard_map/owner_rows/pallas_call | solution.py:565
  (40 shorter events, 2.9 us)
Async XLA Ops:
  0.6 9.7 %collective-permute-start = (bf16[512,1536]{1,0:T(8,128)(2,1)}, bf16[512,1536]{1,0:T(8,128)(2,1)S(1)}, u32[]{:S(2)}, u32[]{:S(2)}) collective-permute-start(bf16[512,1536]{1,0:T(8,128)(2,1)} %bitcast.12), channel_id=1, source_target_pairs={{0,1},{1,0},{2,3},{3,2},{4,5},{5,4},{6,7},{7,6},{8,9},{9,8},{10,11... | collective-permute-start | bytes 4718600 | tf_op jit(solution)/shard_map/ppermute | solution.py:33
  1.4 11.0 %collective-permute-start.1 = (bf16[512,1536]{1,0:T(8,128)(2,1)}, bf16[512,1536]{1,0:T(8,128)(2,1)S(1)}, u32[]{:S(2)}, u32[]{:S(2)}) collective-permute-start(bf16[512,1536]{1,0:T(8,128)(2,1)} %bitcast.9), channel_id=1, source_target_pairs={{0,1},{1,0},{2,3},{3,2},{4,5},{5,4},{6,7},{7,6},{8,9},{9,8},{10,11... | collective-permute-start | bytes 4718600 | tf_op jit(solution)/shard_map/ppermute | solution.py:33
  1.5 1.1 copy-start.3
  2.5 13.1 %collective-permute-start.4 = (bf16[192,384]{1,0:T(8,128)(2,1)S(1)}, bf16[192,384]{1,0:T(8,128)(2,1)S(1)}, u32[]{:S(2)}, u32[]{:S(2)}) collective-permute-start(bf16[192,384]{1,0:T(8,128)(2,1)S(1)} %cut_proj.1.refs_0_), channel_id=1, source_target_pairs={{0,6},{1,7},{2,4},{3,5},{4,2},{5,3},{6,0},{7,1},{8,14},{9,15},{10,... | collective-permute-start | bytes 442376 | tf_op jit(solution)/shard_map/ppermute | solution.py:37
  3.9 11.8 %collective-permute-start.3 = (bf16[192,384]{1,0:T(8,128)(2,1)S(1)}, bf16[192,384]{1,0:T(8,128)(2,1)}, u32[]{:S(2)}, u32[]{:S(2)}) collective-permute-start(bf16[192,384]{1,0:T(8,128)(2,1)S(1)} %cut_proj.1.refs_0_), channel_id=1, source_target_pairs={{0,2},{1,3},{2,0},{3,1},{4,6},{5,7},{6,4},{7,5},{8,10},{9,11},{10,... | collective-permute-start | bytes 442376 | tf_op jit(solution)/shard_map/ppermute | solution.py:37
  6.1 9.6 %collective-permute-start.2 = (bf16[192,384]{1,0:T(8,128)(2,1)S(1)}, bf16[192,384]{1,0:T(8,128)(2,1)}, u32[]{:S(2)}, u32[]{:S(2)}) collective-permute-start(bf16[192,384]{1,0:T(8,128)(2,1)S(1)} %cut_proj.1.refs_0_), channel_id=1, source_target_pairs={{0,4},{1,5},{2,6},{3,7},{4,0},{5,1},{6,2},{7,3},{8,12},{9,13},{10,... | collective-permute-start | bytes 442376 | tf_op jit(solution)/shard_map/ppermute | solution.py:37
  6.8 1.4 %copy-start.1 = (bf16[1,512,1536]{2,1,0:T(8,128)(2,1)S(1)}, bf16[1,512,1536]{2,1,0:T(8,128)(2,1)}, u32[]{:S(2)}) copy-start(bf16[1,512,1536]{2,1,0:T(8,128)(2,1)} %param.5) | copy-start | bytes 4718596
  10.3 2.1 %copy-start = (bf16[1,512,1536]{2,1,0:T(8,128)(2,1)S(1)}, bf16[1,512,1536]{2,1,0:T(8,128)(2,1)}, u32[]{:S(2)}) copy-start(bf16[1,512,1536]{2,1,0:T(8,128)(2,1)} %param.6) | copy-start | bytes 4718596
  12.4 3.3 %copy-start.5 = (bf16[3,64,1536]{2,1,0:T(8,128)(2,1)S(1)}, bf16[3,64,1536]{2,1,0:T(8,128)(2,1)}, u32[]{:S(2)}) copy-start(bf16[3,64,1536]{2,1,0:T(8,128)(2,1)} %refs_1_.2) | copy-start | bytes 1769476
  15.7 22.3 %copy-start.4 = (bf16[192,1536]{1,0:T(8,128)(2,1)S(1)}, bf16[192,1536]{1,0:T(8,128)(2,1)}, u32[]{:S(2)}) copy-start(bf16[192,1536]{1,0:T(8,128)(2,1)} %refs_1_.3) | copy-start | bytes 1769476
  16.8 21.2 %collective-permute-start.5 = (bf16[1056,384]{1,0:T(8,128)(2,1)S(1)}, bf16[1056,384]{1,0:T(8,128)(2,1)S(1)}, u32[]{:S(2)}, u32[]{:S(2)}) collective-permute-start(bf16[1056,384]{1,0:T(8,128)(2,1)S(1)} %get-tuple-element.34.refs_2_), channel_id=1, source_target_pairs={{0,8},{8,0},{16,24},{24,16},{1,9},{9,1},{17,25},{25,17},{2,10},{10... | collective-permute-start | bytes 2433032 | tf_op jit(solution)/shard_map/ppermute | solution.py:41
  18.1 19.9 %collective-permute-start.6 = (bf16[1056,384]{1,0:T(8,128)(2,1)S(1)}, bf16[1056,384]{1,0:T(8,128)(2,1)S(1)}, u32[]{:S(2)}, u32[]{:S(2)}) collective-permute-start(bf16[1056,384]{1,0:T(8,128)(2,1)S(1)} %get-tuple-element.35.refs_3_), channel_id=1, source_target_pairs={{0,16},{8,24},{16,0},{24,8},{1,17},{9,25},{17,1},{25,9},{2,18},{10... | collective-permute-start | bytes 2433032 | tf_op jit(solution)/shard_map/ppermute | solution.py:41
  19.3 18.7 %collective-permute-start.7 = (bf16[480,384]{1,0:T(8,128)(2,1)S(1)}, bf16[480,384]{1,0:T(8,128)(2,1)S(1)}, u32[]{:S(2)}, u32[]{:S(2)}) collective-permute-start(bf16[480,384]{1,0:T(8,128)(2,1)S(1)} %get-tuple-element.36.refs_6_), channel_id=1, source_target_pairs={{0,4},{1,5},{2,6},{3,7},{4,0},{5,1},{6,2},{7,3},{8,12},{9,13},{10,... | collective-permute-start | bytes 1105928 | tf_op jit(solution)/shard_map/ppermute | solution.py:37
  38.5 21.0 %collective-permute-start.8 = (bf16[2688,384]{1,0:T(8,128)(2,1)S(1)}, bf16[2688,384]{1,0:T(8,128)(2,1)S(1)}, u32[]{:S(2)}, u32[]{:S(2)}) collective-permute-start(bf16[2688,384]{1,0:T(8,128)(2,1)S(1)} %get-tuple-element.39), channel_id=1, source_target_pairs={{0,1},{1,0},{2,3},{3,2},{4,5},{5,4},{6,7},{7,6},{8,9},{9,8},{10,11... | collective-permute-start | bytes 6193160 | tf_op jit(solution)/shard_map/ppermute | solution.py:33
  39.2 18.1 %collective-permute-start.10 = (bf16[960,384]{1,0:T(8,128)(2,1)S(1)}, bf16[960,384]{1,0:T(8,128)(2,1)S(1)}, u32[]{:S(2)}, u32[]{:S(2)}) collective-permute-start(bf16[960,384]{1,0:T(8,128)(2,1)S(1)} %get-tuple-element.41.refs_2_), channel_id=1, source_target_pairs={{0,16},{8,24},{16,0},{24,8},{1,17},{9,25},{17,1},{25,9},{2,18},{10... | collective-permute-start | bytes 2211848 | tf_op jit(solution)/shard_map/ppermute | solution.py:41
  40.4 17.7 %collective-permute-start.11 = (bf16[960,384]{1,0:T(8,128)(2,1)S(1)}, bf16[960,384]{1,0:T(8,128)(2,1)S(1)}, u32[]{:S(2)}, u32[]{:S(2)}) collective-permute-start(bf16[960,384]{1,0:T(8,128)(2,1)S(1)} %get-tuple-element.42.refs_3_), channel_id=1, source_target_pairs={{0,8},{8,0},{16,24},{24,16},{1,9},{9,1},{17,25},{25,17},{2,10},{10... | collective-permute-start | bytes 2211848 | tf_op jit(solution)/shard_map/ppermute | solution.py:41
  40.7 18.9 %collective-permute-start.9 = (bf16[2,480,384]{2,1,0:T(8,128)(2,1)S(1)}, bf16[2,480,384]{2,1,0:T(8,128)(2,1)S(1)}, u32[]{:S(2)}, u32[]{:S(2)}) collective-permute-start(bf16[2,480,384]{2,1,0:T(8,128)(2,1)S(1)} %get-tuple-element.40.refs_0_), channel_id=1, source_target_pairs={{0,2},{1,3},{2,0},{3,1},{4,6},{5,7},{6,4},{7,5},{8,10},{9,11},{10,... | collective-permute-start | bytes 2211848 | tf_op jit(solution)/shard_map/ppermute | solution.py:37
  59.6 6.2 %copy-start.2 = (bf16[1,512,1536]{2,1,0:T(8,128)(2,1)S(1)}, bf16[1,512,1536]{2,1,0:T(8,128)(2,1)}, u32[]{:S(2)}) copy-start(bf16[1,512,1536]{2,1,0:T(8,128)(2,1)} %param.5) | copy-start | bytes 4718596
  59.8 5.2 %collective-permute-start.15 = (bf16[1152,384]{1,0:T(8,128)(2,1)S(1)}, bf16[1152,384]{1,0:T(8,128)(2,1)S(1)}, u32[]{:S(2)}, u32[]{:S(2)}) collective-permute-start(bf16[1152,384]{1,0:T(8,128)(2,1)S(1)} %get-tuple-element.48), channel_id=1, source_target_pairs={{0,1},{1,0},{2,3},{3,2},{4,5},{5,4},{6,7},{7,6},{8,9},{9,8},{10,11... | collective-permute-start | bytes 2654216 | tf_op jit(solution)/shard_map/ppermute | solution.py:33
  61.0 15.1 %collective-permute-start.17 = (bf16[1440,384]{1,0:T(8,128)(2,1)S(1)}, bf16[1440,384]{1,0:T(8,128)(2,1)S(1)}, u32[]{:S(2)}, u32[]{:S(2)}) collective-permute-start(bf16[1440,384]{1,0:T(8,128)(2,1)S(1)} %bitcast.18), channel_id=1, source_target_pairs={{0,1},{1,0},{2,3},{3,2},{4,5},{5,4},{6,7},{7,6},{8,9},{9,8},{10,11... | collective-permute-start | bytes 3317768 | tf_op jit(solution)/shard_map/ppermute | solution.py:33
  61.1 10.3 %collective-permute-start.16 = (bf16[2,192,384]{2,1,0:T(8,128)(2,1)S(1)}, bf16[2,192,384]{2,1,0:T(8,128)(2,1)S(1)}, u32[]{:S(2)}, u32[]{:S(2)}) collective-permute-start(bf16[2,192,384]{2,1,0:T(8,128)(2,1)S(1)} %get-tuple-element.49), channel_id=1, source_target_pairs={{0,2},{1,3},{2,0},{3,1},{4,6},{5,7},{6,4},{7,5},{8,10},{9,11},{10,... | collective-permute-start | bytes 884744 | tf_op jit(solution)/shard_map/ppermute | solution.py:37
  63.1 8.9 %collective-permute-start.14 = (bf16[3,96,384]{2,1,0:T(8,128)(2,1)S(1)}, bf16[3,96,384]{2,1,0:T(8,128)(2,1)S(1)}, u32[]{:S(2)}, u32[]{:S(2)}) collective-permute-start(bf16[3,96,384]{2,1,0:T(8,128)(2,1)S(1)} %get-tuple-element.47), channel_id=1, source_target_pairs={{0,24},{8,16},{16,8},{24,0},{1,25},{9,17},{17,9},{25,1},{2,26},{10... | collective-permute-start | bytes 663560 | tf_op jit(solution)/shard_map/ppermute | solution.py:41
  64.1 12.0 %collective-permute-start.13 = (bf16[3,96,384]{2,1,0:T(8,128)(2,1)S(1)}, bf16[3,96,384]{2,1,0:T(8,128)(2,1)S(1)}, u32[]{:S(2)}, u32[]{:S(2)}) collective-permute-start(bf16[3,96,384]{2,1,0:T(8,128)(2,1)S(1)} %get-tuple-element.47), channel_id=1, source_target_pairs={{0,16},{8,24},{16,0},{24,8},{1,17},{9,25},{17,1},{25,9},{2,18},{10... | collective-permute-start | bytes 663560 | tf_op jit(solution)/shard_map/ppermute | solution.py:41
  64.9 11.1 %collective-permute-start.12 = (bf16[3,96,384]{2,1,0:T(8,128)(2,1)S(1)}, bf16[3,96,384]{2,1,0:T(8,128)(2,1)S(1)}, u32[]{:S(2)}, u32[]{:S(2)}) collective-permute-start(bf16[3,96,384]{2,1,0:T(8,128)(2,1)S(1)} %get-tuple-element.47), channel_id=1, source_target_pairs={{0,8},{8,0},{16,24},{24,16},{1,9},{9,1},{17,25},{25,17},{2,10},{10... | collective-permute-start | bytes 663560 | tf_op jit(solution)/shard_map/ppermute | solution.py:41
  76.1 2.3 %collective-permute-start.18 = (bf16[864,384]{1,0:T(8,128)(2,1)S(1)}, bf16[864,384]{1,0:T(8,128)(2,1)S(1)}, u32[]{:S(2)}, u32[]{:S(2)}) collective-permute-start(bf16[864,384]{1,0:T(8,128)(2,1)S(1)} %bitcast.16), channel_id=1, source_target_pairs={{0,1},{1,0},{2,3},{3,2},{4,5},{5,4},{6,7},{7,6},{8,9},{9,8},{10,11... | collective-permute-start | bytes 1990664 | tf_op jit(solution)/shard_map/ppermute | solution.py:33
  76.7 11.7 %collective-permute-start.26 = (bf16[192,384]{1,0:T(8,128)(2,1)S(1)}, bf16[192,384]{1,0:T(8,128)(2,1)S(1)}, u32[]{:S(2)}, u32[]{:S(2)}) collective-permute-start(bf16[192,384]{1,0:T(8,128)(2,1)S(1)} %get-tuple-element.50.refs_4_), channel_id=1, source_target_pairs={{0,4},{1,5},{2,6},{3,7},{4,0},{5,1},{6,2},{7,3},{8,12},{9,13},{10,... | collective-permute-start | bytes 442376 | tf_op jit(solution)/shard_map/ppermute | solution.py:37
  83.9 17.9 %collective-permute-start.19 = (bf16[33,16,256]{2,1,0:T(8,128)(2,1)S(1)}, bf16[33,16,256]{2,1,0:T(8,128)(2,1)S(1)}, u32[]{:S(2)}, u32[]{:S(2)}) collective-permute-start(bf16[33,16,256]{2,1,0:T(8,128)(2,1)S(1)} %get-tuple-element.52), channel_id=1, source_target_pairs={{0,4},{1,5},{2,6},{3,7},{4,0},{5,1},{6,2},{7,3},{8,12},{9,13},{10,... | collective-permute-start | bytes 811016 | tf_op jit(solution)/shard_map/ppermute | solution.py:649
  84.7 22.9 %collective-permute-start.20 = (bf16[33,16,256]{2,1,0:T(8,128)(2,1)S(1)}, bf16[33,16,256]{2,1,0:T(8,128)(2,1)S(1)}, u32[]{:S(2)}, u32[]{:S(2)}) collective-permute-start(bf16[33,16,256]{2,1,0:T(8,128)(2,1)S(1)} %get-tuple-element.53), channel_id=1, source_target_pairs={{0,5},{1,4},{2,7},{3,6},{4,1},{5,0},{6,3},{7,2},{8,13},{9,12},{10,... | collective-permute-start | bytes 811016 | tf_op jit(solution)/shard_map/ppermute | solution.py:649
  86.8 21.3 %collective-permute-start.21 = (bf16[33,16,256]{2,1,0:T(8,128)(2,1)S(1)}, bf16[33,16,256]{2,1,0:T(8,128)(2,1)S(1)}, u32[]{:S(2)}, u32[]{:S(2)}) collective-permute-start(bf16[33,16,256]{2,1,0:T(8,128)(2,1)S(1)} %get-tuple-element.54), channel_id=1, source_target_pairs={{0,2},{1,3},{2,0},{3,1},{4,6},{5,7},{6,4},{7,5},{8,10},{9,11},{10,... | collective-permute-start | bytes 811016 | tf_op jit(solution)/shard_map/ppermute | solution.py:649
  87.3 24.1 %collective-permute-start.22 = (bf16[33,16,256]{2,1,0:T(8,128)(2,1)S(1)}, bf16[33,16,256]{2,1,0:T(8,128)(2,1)S(1)}, u32[]{:S(2)}, u32[]{:S(2)}) collective-permute-start(bf16[33,16,256]{2,1,0:T(8,128)(2,1)S(1)} %get-tuple-element.55), channel_id=1, source_target_pairs={{0,3},{1,2},{2,1},{3,0},{4,7},{5,6},{6,5},{7,4},{8,11},{9,10},{10,... | collective-permute-start | bytes 811016 | tf_op jit(solution)/shard_map/ppermute | solution.py:649
  88.4 36.5 %collective-permute-start.23 = (bf16[33,16,256]{2,1,0:T(8,128)(2,1)S(1)}, bf16[33,16,256]{2,1,0:T(8,128)(2,1)S(1)}, u32[]{:S(2)}, u32[]{:S(2)}) collective-permute-start(bf16[33,16,256]{2,1,0:T(8,128)(2,1)S(1)} %get-tuple-element.56), channel_id=1, source_target_pairs={{0,6},{1,7},{2,4},{3,5},{4,2},{5,3},{6,0},{7,1},{8,14},{9,15},{10,... | collective-permute-start | bytes 811016 | tf_op jit(solution)/shard_map/ppermute | solution.py:649
  102.4 30.6 %collective-permute-start.29 = (f32[192,384]{1,0:T(8,128)S(1)}, f32[192,384]{1,0:T(8,128)S(1)}, u32[]{:S(2)}, u32[]{:S(2)}) collective-permute-start(f32[192,384]{1,0:T(8,128)S(1)} %far_sum.1.refs_8_), channel_id=1, source_target_pairs={{0,24},{8,16},{16,8},{24,0},{1,25},{9,17},{17,9},{25,1},{2,26},{10... | collective-permute-start | bytes 884744 | tf_op jit(solution)/shard_map/ppermute | solution.py:41
  107.6 25.4 %collective-permute-start.28 = (f32[192,384]{1,0:T(8,128)S(1)}, f32[192,384]{1,0:T(8,128)S(1)}, u32[]{:S(2)}, u32[]{:S(2)}) collective-permute-start(f32[192,384]{1,0:T(8,128)S(1)} %far_sum.1.refs_8_), channel_id=1, source_target_pairs={{0,16},{8,24},{16,0},{24,8},{1,17},{9,25},{17,1},{25,9},{2,18},{10... | collective-permute-start | bytes 884744 | tf_op jit(solution)/shard_map/ppermute | solution.py:41
  108.2 24.8 %collective-permute-start.27 = (f32[192,384]{1,0:T(8,128)S(1)}, f32[192,384]{1,0:T(8,128)S(1)}, u32[]{:S(2)}, u32[]{:S(2)}) collective-permute-start(f32[192,384]{1,0:T(8,128)S(1)} %far_sum.1.refs_8_), channel_id=1, source_target_pairs={{0,8},{8,0},{16,24},{24,16},{1,9},{9,1},{17,25},{25,17},{2,10},{10... | collective-permute-start | bytes 884744 | tf_op jit(solution)/shard_map/ppermute | solution.py:41
  111.4 21.5 %collective-permute-start.24 = (bf16[33,16,256]{2,1,0:T(8,128)(2,1)S(1)}, bf16[33,16,256]{2,1,0:T(8,128)(2,1)S(1)}, u32[]{:S(2)}, u32[]{:S(2)}) collective-permute-start(bf16[33,16,256]{2,1,0:T(8,128)(2,1)S(1)} %get-tuple-element.57), channel_id=1, source_target_pairs={{0,7},{1,6},{2,5},{3,4},{4,3},{5,2},{6,1},{7,0},{8,15},{9,14},{10,... | collective-permute-start | bytes 811016 | tf_op jit(solution)/shard_map/ppermute | solution.py:649
  124.8 8.1 %collective-permute-start.25 = (bf16[33,16,256]{2,1,0:T(8,128)(2,1)S(1)}, bf16[33,16,256]{2,1,0:T(8,128)(2,1)S(1)}, u32[]{:S(2)}, u32[]{:S(2)}) collective-permute-start(bf16[33,16,256]{2,1,0:T(8,128)(2,1)S(1)} %get-tuple-element.58), channel_id=1, source_target_pairs={{0,1},{1,0},{2,3},{3,2},{4,5},{5,4},{6,7},{7,6},{8,9},{9,8},{10,11... | collective-permute-start | bytes 811016 | tf_op jit(solution)/shard_map/ppermute | solution.py:649

commit v8 on v7

--- a/solution.py
+++ b/solution.py
@@ -63,7 +63,7 @@
     return [(0, z, ("xor", site), low, HALF) for z in Z_ORDER]
 
 
-SPLIT = STEM_ROWS // 2
+SPLIT = STEM_ROWS // 4
 QUARTER_BLOCKS = ((1, 0, STEM_ROWS), (0, 0, SPLIT))
 WHOLE_BLOCKS = ((2, 0, STEM_ROWS), (0, SPLIT, STEM_ROWS - SPLIT))
 QUARTER_ROWS = sum(count for _, _, count in QUARTER_BLOCKS)

time: 136 us -> 137 us (level)
  waiting for transfers between devices: 65.1 us -> 67.1 us
  starting transfers between devices: 35.3 us -> 33.8 us
    ppermute x10, starting transfers between devices: 9.04 us -> 7.25 us  [swap_site(): lax.ppermute(value, 'site', [(i, i ^ distance) for i in range(N_SITE)])]
  transfers between devices with their start and end apart: 30 -> 30, of which waited for: 11 -> 10; matrix products, arithmetic and copies ran while one was open for 1% -> 1% of each run, Pallas kernels for 20% -> 19%
where the time goes in v8:
time: 137 us
  waiting for transfers between devices  67.1 us (49%)
  starting transfers between devices  33.8 us (25%)
  Pallas kernels  31.7 us (23%)
  local copies, waits for them, and re-layouts  2.5 us (2%)
    ppermute x7, waiting for transfers between devices, body(): lax.ppermute(payloads[d], 'fsdp', [(i, i ^ d) for i in range(N_FSDP)])  36.2 us
    ppermute x10, waiting for transfers between devices, swap_site(): lax.ppermute(value, 'site', [(i, i ^ distance) for i in range(N_SITE)])  18.5 us
    ppermute x7, starting transfers between devices, swap_z(): lax.ppermute(value, 'fsdp', [(i, i ^ 2 * distance) for i in range(N_FSDP)])  12.1 us
    ppermute x7, starting transfers between devices, body(): lax.ppermute(payloads[d], 'fsdp', [(i, i ^ d) for i in range(N_FSDP)])  10.6 us
    ppermute x7, waiting for transfers between devices, swap_z(): lax.ppermute(value, 'fsdp', [(i, i ^ 2 * distance) for i in range(N_FSDP)])  10.4 us
    ppermute x10, starting transfers between devices, swap_site(): lax.ppermute(value, 'site', [(i, i ^ distance) for i in range(N_SITE)])  7.25 us
    pallas_call x1, Pallas kernels, plan_of(): call(plan_kernel, 'plan', shape((COUNT_AT + 1,), jnp.int32), (1,), [], pl...  6.28 us
    pallas_call x1, Pallas kernels, input_gradient(): call(lambda *refs: input_grad_kernel(tables, *refs), 'input_gradient', sh...  5.6 us
  transfers between devices with their start and end apart: 30, of which 10 were waited for; matrix products, arithmetic and copies ran while one was open for 1% of the time, Pallas kernels for 19%

profile of v8, /device:TPU:9, one launch (start us, length us, event | category | flops | bytes accessed | tf_op | source)
XLA Modules:
  0.0 136.8 jit_solution(7326566984543305886)
XLA Ops:
  0.6 0.7 collective-permute-start
  1.5 1.1 copy-done.3
  2.5 1.4 collective-permute-start.4
  3.9 2.2 %collective-permute-start.3 = (bf16[192,384]{1,0:T(8,128)(2,1)S(1)}, bf16[192,384]{1,0:T(8,128)(2,1)}, u32[]{:S(2)}, u32[]{:S(2)}) collective-permute-start(bf16[192,384]{1,0:T(8,128)(2,1)S(1)} %cut_proj.1.refs_0_), channel_id=1, source_target_pairs={{0,2},{1,3},{2,0},{3,1},{4,6},{5,7},{6,4},{7,5},{8,10},{9,11},{10,... | collective-permute-start | bytes 442376 | tf_op jit(solution)/shard_map/ppermute | solution.py:37
  6.1 0.7 pad_add_fusion.scalars.refs_0_
  6.8 1.4 %copy-done.1 = bf16[1,512,1536]{2,1,0:T(8,128)(2,1)S(1)} copy-done((bf16[1,512,1536]{2,1,0:T(8,128)(2,1)S(1)}, bf16[1,512,1536]{2,1,0:T(8,128)(2,1)}, u32[]{:S(2)}) %copy-start.1) | copy-done | bytes 1572888
  8.2 2.1 %norm_half.2.refs_0_.na_ref = bf16[768,512]{1,0:T(8,128)(2,1)S(1)} custom-call(s32[10]{0:T(128)S(1)} %pad_add_fusion.scalars.refs_0_, bf16[512,1536]{1,0:T(8,128)(2,1)S(1)} %bitcast.13, bf16[192,384]{1,0:T(8,128)(2,1)S(1)} %cut_proj.1.refs_0_), custom_call_target="tpu_custom_call" | custom-call | tf_op jit(solution)/shard_map/norm_half/pallas_call | solution.py:225
  10.3 2.1 %norm_half.3.nb_ref = bf16[768,512]{1,0:T(8,128)(2,1)S(1)} custom-call(s32[10]{0:T(128)S(1)} %pad_add_fusion.scalars.refs_0_, bf16[512,1536]{1,0:T(8,128)(2,1)S(1)} %collective-permute-done.x_ref, bf16[768,512]{1,0:T(8,128)(2,1)S(1)} %norm_half.2.refs_0_.na_ref), custom_call_target="tpu_custom_call" | custom-call | tf_op jit(solution)/shard_map/norm_half/pallas_call | solution.py:225
  12.4 3.2 %outer_pieces.1 = (f32[2,384,384]{2,1,0:T(8,128)S(1)}, bf16[1056,384]{1,0:T(8,128)(2,1)S(1)}, f32[2,384,384]{2,1,0:T(8,128)S(1)}, bf16[1056,384]{1,0:T(8,128)(2,1)S(1)}) custom-call(s32[10]{0:T(128)S(1)} %pad_add_fusion.scalars.refs_0_, bf16[768,512]{1,0:T(8,128)(2,1)S(1)} %norm_half.2.refs_0_.na_ref, bf16[768,512]{1,0:T(8,128)(2,1)S(1)} %norm_half.3.nb_ref, ...), custom_call_target="tpu_custom_call" | custom-call | tf_op jit(solution)/shard_map/outer_pieces/pallas_call | solution.py:258
  15.7 1.1 halves.1
  16.8 1.3 collective-permute-start.5
  18.1 1.2 collective-permute-start.6
  19.3 3.6 %collective-permute-start.7 = (bf16[528,384]{1,0:T(8,128)(2,1)S(1)}, bf16[528,384]{1,0:T(8,128)(2,1)S(1)}, u32[]{:S(2)}, u32[]{:S(2)}) collective-permute-start(bf16[528,384]{1,0:T(8,128)(2,1)S(1)} %get-tuple-element.36.refs_6_), channel_id=1, source_target_pairs={{0,4},{1,5},{2,6},{3,7},{4,0},{5,1},{6,2},{7,3},{8,12},{9,13},{10,... | collective-permute-start | bytes 1216520 | tf_op jit(solution)/shard_map/ppermute | solution.py:37
  22.9 6.3 %plan.1.refs_10_.refs_0_.scalars = s32[211]{0:T(256)S(1)} custom-call(s32[10]{0:T(128)S(1)} %pad_add_fusion.scalars.refs_0_), custom_call_target="tpu_custom_call" | custom-call | tf_op jit(solution)/shard_map/plan/pallas_call | solution.py:451
  29.2 10.3 %collective-permute-done.7.refs_7_ = bf16[528,384]{1,0:T(8,128)(2,1)S(1)} collective-permute-done((bf16[528,384]{1,0:T(8,128)(2,1)S(1)}, bf16[528,384]{1,0:T(8,128)(2,1)S(1)}, u32[]{:S(2)}, u32[]{:S(2)}) %collective-permute-start.7) | collective-permute-done | bytes 405536 | tf_op jit(solution)/shard_map/ppermute | solution.py:37
  39.6 0.5 site_step.1
  40.1 0.6 collective-permute-start.8
  40.7 3.1 %collective-permute-start.9 = (bf16[2,528,384]{2,1,0:T(8,128)(2,1)S(1)}, bf16[2,528,384]{2,1,0:T(8,128)(2,1)S(1)}, u32[]{:S(2)}, u32[]{:S(2)}) collective-permute-start(bf16[2,528,384]{2,1,0:T(8,128)(2,1)S(1)} %get-tuple-element.40.refs_0_), channel_id=1, source_target_pairs={{0,2},{1,3},{2,0},{3,1},{4,6},{5,7},{6,4},{7,5},{8,10},{9,11},{10,... | collective-permute-start | bytes 2433032 | tf_op jit(solution)/shard_map/ppermute | solution.py:37
  44.3 17.2 %collective-permute-done.10.ra_ref.refs_2_.refs_4_ = bf16[960,384]{1,0:T(8,128)(2,1)S(1)} collective-permute-done((bf16[960,384]{1,0:T(8,128)(2,1)S(1)}, bf16[960,384]{1,0:T(8,128)(2,1)S(1)}, u32[]{:S(2)}, u32[]{:S(2)}) %collective-permute-start.10) | collective-permute-done | bytes 737312 | tf_op jit(solution)/shard_map/ppermute | solution.py:41
  61.5 0.7 site_sum.1
  62.5 1.5 %collective-permute-start.17 = (bf16[1584,384]{1,0:T(8,128)(2,1)S(1)}, bf16[1584,384]{1,0:T(8,128)(2,1)S(1)}, u32[]{:S(2)}, u32[]{:S(2)}) collective-permute-start(bf16[1584,384]{1,0:T(8,128)(2,1)S(1)} %bitcast.18), channel_id=1, source_target_pairs={{0,1},{1,0},{2,3},{3,2},{4,5},{5,4},{6,7},{7,6},{8,9},{9,8},{10,11... | collective-permute-start | bytes 3649544 | tf_op jit(solution)/shard_map/ppermute | solution.py:33
  64.1 0.6 collective-permute-start.16
  64.6 0.6 collective-permute-start.14
  65.3 0.8 collective-permute-start.13
  66.1 1.7 %collective-permute-done.15.refs_7_ = bf16[1152,384]{1,0:T(8,128)(2,1)S(1)} collective-permute-done((bf16[1152,384]{1,0:T(8,128)(2,1)S(1)}, bf16[1152,384]{1,0:T(8,128)(2,1)S(1)}, u32[]{:S(2)}, u32[]{:S(2)}) %collective-permute-start.15) | collective-permute-done | bytes 884768 | tf_op jit(solution)/shard_map/ppermute | solution.py:33
  68.0 5.6 %input_gradient.1.refs_0_.refs_3_.refs_7_ = bf16[512,1536]{1,0:T(8,128)(2,1)S(1)} custom-call(s32[10]{0:T(128)S(1)} %pad_add_fusion.scalars.refs_0_, bf16[192,1536]{1,0:T(8,128)(2,1)S(1)} %copy-done.4, bf16[960,384]{1,0:T(8,128)(2,1)S(1)} %get-tuple-element.41.refs_2_, bf16[960,384]{1,0:T(8,128)(2,1)S(1)} %get-tuple-element.42.refs_3_, ...), custom_call_target="tpu_custom_call" | custom-call | tf_op jit(solution)/shard_map/input_gradient/pallas_call | solution.py:385
  73.6 0.6 near_sum.1
  74.3 1.2 collective-permute-done.13.refs_1_
  75.5 0.9 collective-permute-start.18
  76.4 1.3 collective-permute-start.26
  77.7 0.3 collective-permute-done.18.refs_6_
  78.0 5.5 %stem_payloads.1 = (bf16[33,16,256]{2,1,0:T(8,128)(2,1)S(1)}, bf16[33,16,256]{2,1,0:T(8,128)(2,1)S(1)}, bf16[33,16,256]{2,1,0:T(8,128)(2,1)S(1)}, bf16[33,16,256...) custom-call(s32[211]{0:T(256)S(1)} %plan.1.refs_10_.refs_0_.scalars,, ...), custom_call_target="tpu_custom_call" | custom-call | tf_op jit(solution)/shard_map/stem_payloads/pallas_call | solution.py:508
  83.5 1.3 collective-permute-start.19
  84.8 1.6 %collective-permute-start.20 = (bf16[33,16,256]{2,1,0:T(8,128)(2,1)S(1)}, bf16[33,16,256]{2,1,0:T(8,128)(2,1)S(1)}, u32[]{:S(2)}, u32[]{:S(2)}) collective-permute-start(bf16[33,16,256]{2,1,0:T(8,128)(2,1)S(1)} %get-tuple-element.53), channel_id=1, source_target_pairs={{0,5},{1,4},{2,7},{3,6},{4,1},{5,0},{6,3},{7,2},{8,13},{9,12},{10,... | collective-permute-start | bytes 811016 | tf_op jit(solution)/shard_map/ppermute | solution.py:649
  86.5 1.3 collective-permute-start.21
  88.0 0.9 collective-permute-start.23
  88.8 13.4 %collective-permute-done.19.refs_3_.refs_1_ = bf16[33,16,256]{2,1,0:T(8,128)(2,1)S(1)} collective-permute-done((bf16[33,16,256]{2,1,0:T(8,128)(2,1)S(1)}, bf16[33,16,256]{2,1,0:T(8,128)(2,1)S(1)}, u32[]{:S(2)}, u32[]{:S(2)}) %collective-permute-start.19) | collective-permute-done | bytes 270368 | tf_op jit(solution)/shard_map/ppermute | solution.py:649
  102.2 0.6 far_sum.1.refs_8_
  102.8 1.2 collective-permute-start.29
  103.9 4.0 %collective-permute-done.20.refs_2_ = bf16[33,16,256]{2,1,0:T(8,128)(2,1)S(1)} collective-permute-done((bf16[33,16,256]{2,1,0:T(8,128)(2,1)S(1)}, bf16[33,16,256]{2,1,0:T(8,128)(2,1)S(1)}, u32[]{:S(2)}, u32[]{:S(2)}) %collective-permute-start.20) | collective-permute-done | bytes 270368 | tf_op jit(solution)/shard_map/ppermute | solution.py:649
  108.0 0.5 collective-permute-start.28
  108.5 0.9 collective-permute-start.27
  109.4 7.4 %collective-permute-done.22.refs_4_ = bf16[33,16,256]{2,1,0:T(8,128)(2,1)S(1)} collective-permute-done((bf16[33,16,256]{2,1,0:T(8,128)(2,1)S(1)}, bf16[33,16,256]{2,1,0:T(8,128)(2,1)S(1)}, u32[]{:S(2)}, u32[]{:S(2)}) %collective-permute-start.22) | collective-permute-done | bytes 270368 | tf_op jit(solution)/shard_map/ppermute | solution.py:649
  116.8 0.4 collective-permute-start.24
  117.2 4.7 %collective-permute-done.23.refs_5_ = bf16[33,16,256]{2,1,0:T(8,128)(2,1)S(1)} collective-permute-done((bf16[33,16,256]{2,1,0:T(8,128)(2,1)S(1)}, bf16[33,16,256]{2,1,0:T(8,128)(2,1)S(1)}, u32[]{:S(2)}, u32[]{:S(2)}) %collective-permute-start.23) | collective-permute-done | bytes 270368 | tf_op jit(solution)/shard_map/ppermute | solution.py:649
  121.9 4.9 %collective-permute-start.25 = (bf16[33,16,256]{2,1,0:T(8,128)(2,1)S(1)}, bf16[33,16,256]{2,1,0:T(8,128)(2,1)S(1)}, u32[]{:S(2)}, u32[]{:S(2)}) collective-permute-start(bf16[33,16,256]{2,1,0:T(8,128)(2,1)S(1)} %get-tuple-element.58), channel_id=1, source_target_pairs={{0,1},{1,0},{2,3},{3,2},{4,5},{5,4},{6,7},{7,6},{8,9},{9,8},{10,11... | collective-permute-start | bytes 811016 | tf_op jit(solution)/shard_map/ppermute | solution.py:649
  126.7 6.7 %collective-permute-done.24.refs_6_ = bf16[33,16,256]{2,1,0:T(8,128)(2,1)S(1)} collective-permute-done((bf16[33,16,256]{2,1,0:T(8,128)(2,1)S(1)}, bf16[33,16,256]{2,1,0:T(8,128)(2,1)S(1)}, u32[]{:S(2)}, u32[]{:S(2)}) %collective-permute-start.24) | collective-permute-done | bytes 270368 | tf_op jit(solution)/shard_map/ppermute | solution.py:649
  133.5 3.1 %owner_rows.1 = (bf16[2048,512]{1,0:T(8,128)(2,1)}, f32[192,1536]{1,0:T(8,128)}) custom-call(s32[211]{0:T(256)S(1)} %plan.1.refs_10_.refs_0_.scalars, bf16[33,16,256]{2,1,0:T(8,128)(2,1)S(1)} %get-tuple-element.51.refs_0_, bf16[33,16,256]{2,1,0:T(8,128)(2,1)S(1)} %collective-permute-done.19.refs_3_.refs_1_, ...), custom_call_target="tpu_custom_call" | custom-call | tf_op jit(solution)/shard_map/owner_rows/pallas_call | solution.py:565
  (40 shorter events, 1.5 us)
Async XLA Ops:
  0.6 9.7 %collective-permute-start = (bf16[512,1536]{1,0:T(8,128)(2,1)}, bf16[512,1536]{1,0:T(8,128)(2,1)S(1)}, u32[]{:S(2)}, u32[]{:S(2)}) collective-permute-start(bf16[512,1536]{1,0:T(8,128)(2,1)} %bitcast.12), channel_id=1, source_target_pairs={{0,1},{1,0},{2,3},{3,2},{4,5},{5,4},{6,7},{7,6},{8,9},{9,8},{10,11... | collective-permute-start | bytes 4718600 | tf_op jit(solution)/shard_map/ppermute | solution.py:33
  1.4 11.0 %collective-permute-start.1 = (bf16[512,1536]{1,0:T(8,128)(2,1)}, bf16[512,1536]{1,0:T(8,128)(2,1)S(1)}, u32[]{:S(2)}, u32[]{:S(2)}) collective-permute-start(bf16[512,1536]{1,0:T(8,128)(2,1)} %bitcast.9), channel_id=1, source_target_pairs={{0,1},{1,0},{2,3},{3,2},{4,5},{5,4},{6,7},{7,6},{8,9},{9,8},{10,11... | collective-permute-start | bytes 4718600 | tf_op jit(solution)/shard_map/ppermute | solution.py:33
  1.5 1.1 copy-start.3
  2.5 13.1 %collective-permute-start.4 = (bf16[192,384]{1,0:T(8,128)(2,1)S(1)}, bf16[192,384]{1,0:T(8,128)(2,1)S(1)}, u32[]{:S(2)}, u32[]{:S(2)}) collective-permute-start(bf16[192,384]{1,0:T(8,128)(2,1)S(1)} %cut_proj.1.refs_0_), channel_id=1, source_target_pairs={{0,6},{1,7},{2,4},{3,5},{4,2},{5,3},{6,0},{7,1},{8,14},{9,15},{10,... | collective-permute-start | bytes 442376 | tf_op jit(solution)/shard_map/ppermute | solution.py:37
  3.9 11.8 %collective-permute-start.3 = (bf16[192,384]{1,0:T(8,128)(2,1)S(1)}, bf16[192,384]{1,0:T(8,128)(2,1)}, u32[]{:S(2)}, u32[]{:S(2)}) collective-permute-start(bf16[192,384]{1,0:T(8,128)(2,1)S(1)} %cut_proj.1.refs_0_), channel_id=1, source_target_pairs={{0,2},{1,3},{2,0},{3,1},{4,6},{5,7},{6,4},{7,5},{8,10},{9,11},{10,... | collective-permute-start | bytes 442376 | tf_op jit(solution)/shard_map/ppermute | solution.py:37
  6.1 9.6 %collective-permute-start.2 = (bf16[192,384]{1,0:T(8,128)(2,1)S(1)}, bf16[192,384]{1,0:T(8,128)(2,1)}, u32[]{:S(2)}, u32[]{:S(2)}) collective-permute-start(bf16[192,384]{1,0:T(8,128)(2,1)S(1)} %cut_proj.1.refs_0_), channel_id=1, source_target_pairs={{0,4},{1,5},{2,6},{3,7},{4,0},{5,1},{6,2},{7,3},{8,12},{9,13},{10,... | collective-permute-start | bytes 442376 | tf_op jit(solution)/shard_map/ppermute | solution.py:37
  6.8 1.4 %copy-start.1 = (bf16[1,512,1536]{2,1,0:T(8,128)(2,1)S(1)}, bf16[1,512,1536]{2,1,0:T(8,128)(2,1)}, u32[]{:S(2)}) copy-start(bf16[1,512,1536]{2,1,0:T(8,128)(2,1)} %param.5) | copy-start | bytes 4718596
  10.3 2.1 %copy-start = (bf16[1,512,1536]{2,1,0:T(8,128)(2,1)S(1)}, bf16[1,512,1536]{2,1,0:T(8,128)(2,1)}, u32[]{:S(2)}) copy-start(bf16[1,512,1536]{2,1,0:T(8,128)(2,1)} %param.6) | copy-start | bytes 4718596
  12.4 3.3 %copy-start.5 = (bf16[3,64,1536]{2,1,0:T(8,128)(2,1)S(1)}, bf16[3,64,1536]{2,1,0:T(8,128)(2,1)}, u32[]{:S(2)}) copy-start(bf16[3,64,1536]{2,1,0:T(8,128)(2,1)} %refs_1_.2) | copy-start | bytes 1769476
  15.7 23.9 %copy-start.4 = (bf16[192,1536]{1,0:T(8,128)(2,1)S(1)}, bf16[192,1536]{1,0:T(8,128)(2,1)}, u32[]{:S(2)}) copy-start(bf16[192,1536]{1,0:T(8,128)(2,1)} %refs_1_.3) | copy-start | bytes 1769476
  16.8 22.8 %collective-permute-start.5 = (bf16[1056,384]{1,0:T(8,128)(2,1)S(1)}, bf16[1056,384]{1,0:T(8,128)(2,1)S(1)}, u32[]{:S(2)}, u32[]{:S(2)}) collective-permute-start(bf16[1056,384]{1,0:T(8,128)(2,1)S(1)} %get-tuple-element.34.refs_2_), channel_id=1, source_target_pairs={{0,8},{8,0},{16,24},{24,16},{1,9},{9,1},{17,25},{25,17},{2,10},{10... | collective-permute-start | bytes 2433032 | tf_op jit(solution)/shard_map/ppermute | solution.py:41
  18.1 21.5 %collective-permute-start.6 = (bf16[1056,384]{1,0:T(8,128)(2,1)S(1)}, bf16[1056,384]{1,0:T(8,128)(2,1)S(1)}, u32[]{:S(2)}, u32[]{:S(2)}) collective-permute-start(bf16[1056,384]{1,0:T(8,128)(2,1)S(1)} %get-tuple-element.35.refs_3_), channel_id=1, source_target_pairs={{0,16},{8,24},{16,0},{24,8},{1,17},{9,25},{17,1},{25,9},{2,18},{10... | collective-permute-start | bytes 2433032 | tf_op jit(solution)/shard_map/ppermute | solution.py:41
  19.3 20.2 %collective-permute-start.7 = (bf16[528,384]{1,0:T(8,128)(2,1)S(1)}, bf16[528,384]{1,0:T(8,128)(2,1)S(1)}, u32[]{:S(2)}, u32[]{:S(2)}) collective-permute-start(bf16[528,384]{1,0:T(8,128)(2,1)S(1)} %get-tuple-element.36.refs_6_), channel_id=1, source_target_pairs={{0,4},{1,5},{2,6},{3,7},{4,0},{5,1},{6,2},{7,3},{8,12},{9,13},{10,... | collective-permute-start | bytes 1216520 | tf_op jit(solution)/shard_map/ppermute | solution.py:37
  40.1 22.1 %collective-permute-start.8 = (bf16[2688,384]{1,0:T(8,128)(2,1)S(1)}, bf16[2688,384]{1,0:T(8,128)(2,1)S(1)}, u32[]{:S(2)}, u32[]{:S(2)}) collective-permute-start(bf16[2688,384]{1,0:T(8,128)(2,1)S(1)} %get-tuple-element.39), channel_id=1, source_target_pairs={{0,1},{1,0},{2,3},{3,2},{4,5},{5,4},{6,7},{7,6},{8,9},{9,8},{10,11... | collective-permute-start | bytes 6193160 | tf_op jit(solution)/shard_map/ppermute | solution.py:33
  40.7 21.6 %collective-permute-start.9 = (bf16[2,528,384]{2,1,0:T(8,128)(2,1)S(1)}, bf16[2,528,384]{2,1,0:T(8,128)(2,1)S(1)}, u32[]{:S(2)}, u32[]{:S(2)}) collective-permute-start(bf16[2,528,384]{2,1,0:T(8,128)(2,1)S(1)} %get-tuple-element.40.refs_0_), channel_id=1, source_target_pairs={{0,2},{1,3},{2,0},{3,1},{4,6},{5,7},{6,4},{7,5},{8,10},{9,11},{10,... | collective-permute-start | bytes 2433032 | tf_op jit(solution)/shard_map/ppermute | solution.py:37
  43.8 17.7 %collective-permute-start.10 = (bf16[960,384]{1,0:T(8,128)(2,1)S(1)}, bf16[960,384]{1,0:T(8,128)(2,1)S(1)}, u32[]{:S(2)}, u32[]{:S(2)}) collective-permute-start(bf16[960,384]{1,0:T(8,128)(2,1)S(1)} %get-tuple-element.41.refs_2_), channel_id=1, source_target_pairs={{0,16},{8,24},{16,0},{24,8},{1,17},{9,25},{17,1},{25,9},{2,18},{10... | collective-permute-start | bytes 2211848 | tf_op jit(solution)/shard_map/ppermute | solution.py:41
  44.0 17.5 %collective-permute-start.11 = (bf16[960,384]{1,0:T(8,128)(2,1)S(1)}, bf16[960,384]{1,0:T(8,128)(2,1)S(1)}, u32[]{:S(2)}, u32[]{:S(2)}) collective-permute-start(bf16[960,384]{1,0:T(8,128)(2,1)S(1)} %get-tuple-element.42.refs_3_), channel_id=1, source_target_pairs={{0,8},{8,0},{16,24},{24,16},{1,9},{9,1},{17,25},{25,17},{2,10},{10... | collective-permute-start | bytes 2211848 | tf_op jit(solution)/shard_map/ppermute | solution.py:41
  62.3 5.7 %copy-start.2 = (bf16[1,512,1536]{2,1,0:T(8,128)(2,1)S(1)}, bf16[1,512,1536]{2,1,0:T(8,128)(2,1)}, u32[]{:S(2)}) copy-start(bf16[1,512,1536]{2,1,0:T(8,128)(2,1)} %param.5) | copy-start | bytes 4718596
  62.5 13.0 %collective-permute-start.17 = (bf16[1584,384]{1,0:T(8,128)(2,1)S(1)}, bf16[1584,384]{1,0:T(8,128)(2,1)S(1)}, u32[]{:S(2)}, u32[]{:S(2)}) collective-permute-start(bf16[1584,384]{1,0:T(8,128)(2,1)S(1)} %bitcast.18), channel_id=1, source_target_pairs={{0,1},{1,0},{2,3},{3,2},{4,5},{5,4},{6,7},{7,6},{8,9},{9,8},{10,11... | collective-permute-start | bytes 3649544 | tf_op jit(solution)/shard_map/ppermute | solution.py:33
  64.0 3.8 %collective-permute-start.15 = (bf16[1152,384]{1,0:T(8,128)(2,1)S(1)}, bf16[1152,384]{1,0:T(8,128)(2,1)S(1)}, u32[]{:S(2)}, u32[]{:S(2)}) collective-permute-start(bf16[1152,384]{1,0:T(8,128)(2,1)S(1)} %get-tuple-element.48), channel_id=1, source_target_pairs={{0,1},{1,0},{2,3},{3,2},{4,5},{5,4},{6,7},{7,6},{8,9},{9,8},{10,11... | collective-permute-start | bytes 2654216 | tf_op jit(solution)/shard_map/ppermute | solution.py:33
  64.1 9.6 %collective-permute-start.16 = (bf16[2,192,384]{2,1,0:T(8,128)(2,1)S(1)}, bf16[2,192,384]{2,1,0:T(8,128)(2,1)S(1)}, u32[]{:S(2)}, u32[]{:S(2)}) collective-permute-start(bf16[2,192,384]{2,1,0:T(8,128)(2,1)S(1)} %get-tuple-element.49), channel_id=1, source_target_pairs={{0,2},{1,3},{2,0},{3,1},{4,6},{5,7},{6,4},{7,5},{8,10},{9,11},{10,... | collective-permute-start | bytes 884744 | tf_op jit(solution)/shard_map/ppermute | solution.py:37
  64.6 9.6 %collective-permute-start.14 = (bf16[3,80,384]{2,1,0:T(8,128)(2,1)S(1)}, bf16[3,80,384]{2,1,0:T(8,128)(2,1)S(1)}, u32[]{:S(2)}, u32[]{:S(2)}) collective-permute-start(bf16[3,80,384]{2,1,0:T(8,128)(2,1)S(1)} %get-tuple-element.47), channel_id=1, source_target_pairs={{0,24},{8,16},{16,8},{24,0},{1,25},{9,17},{17,9},{25,1},{2,26},{10... | collective-permute-start | bytes 552968 | tf_op jit(solution)/shard_map/ppermute | solution.py:41
  65.3 10.2 %collective-permute-start.13 = (bf16[3,80,384]{2,1,0:T(8,128)(2,1)S(1)}, bf16[3,80,384]{2,1,0:T(8,128)(2,1)S(1)}, u32[]{:S(2)}, u32[]{:S(2)}) collective-permute-start(bf16[3,80,384]{2,1,0:T(8,128)(2,1)S(1)} %get-tuple-element.47), channel_id=1, source_target_pairs={{0,16},{8,24},{16,0},{24,8},{1,17},{9,25},{17,1},{25,9},{2,18},{10... | collective-permute-start | bytes 552968 | tf_op jit(solution)/shard_map/ppermute | solution.py:41
  67.8 7.7 %collective-permute-start.12 = (bf16[3,80,384]{2,1,0:T(8,128)(2,1)S(1)}, bf16[3,80,384]{2,1,0:T(8,128)(2,1)S(1)}, u32[]{:S(2)}, u32[]{:S(2)}) collective-permute-start(bf16[3,80,384]{2,1,0:T(8,128)(2,1)S(1)} %get-tuple-element.47), channel_id=1, source_target_pairs={{0,8},{8,0},{16,24},{24,16},{1,9},{9,1},{17,25},{25,17},{2,10},{10... | collective-permute-start | bytes 552968 | tf_op jit(solution)/shard_map/ppermute | solution.py:41
  75.5 2.5 %collective-permute-start.18 = (bf16[720,384]{1,0:T(8,128)(2,1)S(1)}, bf16[720,384]{1,0:T(8,128)(2,1)S(1)}, u32[]{:S(2)}, u32[]{:S(2)}) collective-permute-start(bf16[720,384]{1,0:T(8,128)(2,1)S(1)} %bitcast.16), channel_id=1, source_target_pairs={{0,1},{1,0},{2,3},{3,2},{4,5},{5,4},{6,7},{7,6},{8,9},{9,8},{10,11... | collective-permute-start | bytes 1658888 | tf_op jit(solution)/shard_map/ppermute | solution.py:33
  76.4 11.6 %collective-permute-start.26 = (bf16[192,384]{1,0:T(8,128)(2,1)S(1)}, bf16[192,384]{1,0:T(8,128)(2,1)S(1)}, u32[]{:S(2)}, u32[]{:S(2)}) collective-permute-start(bf16[192,384]{1,0:T(8,128)(2,1)S(1)} %get-tuple-element.50.refs_4_), channel_id=1, source_target_pairs={{0,4},{1,5},{2,6},{3,7},{4,0},{5,1},{6,2},{7,3},{8,12},{9,13},{10,... | collective-permute-start | bytes 442376 | tf_op jit(solution)/shard_map/ppermute | solution.py:37
  83.5 18.7 %collective-permute-start.19 = (bf16[33,16,256]{2,1,0:T(8,128)(2,1)S(1)}, bf16[33,16,256]{2,1,0:T(8,128)(2,1)S(1)}, u32[]{:S(2)}, u32[]{:S(2)}) collective-permute-start(bf16[33,16,256]{2,1,0:T(8,128)(2,1)S(1)} %get-tuple-element.52), channel_id=1, source_target_pairs={{0,4},{1,5},{2,6},{3,7},{4,0},{5,1},{6,2},{7,3},{8,12},{9,13},{10,... | collective-permute-start | bytes 811016 | tf_op jit(solution)/shard_map/ppermute | solution.py:649
  84.8 23.2 %collective-permute-start.20 = (bf16[33,16,256]{2,1,0:T(8,128)(2,1)S(1)}, bf16[33,16,256]{2,1,0:T(8,128)(2,1)S(1)}, u32[]{:S(2)}, u32[]{:S(2)}) collective-permute-start(bf16[33,16,256]{2,1,0:T(8,128)(2,1)S(1)} %get-tuple-element.53), channel_id=1, source_target_pairs={{0,5},{1,4},{2,7},{3,6},{4,1},{5,0},{6,3},{7,2},{8,13},{9,12},{10,... | collective-permute-start | bytes 811016 | tf_op jit(solution)/shard_map/ppermute | solution.py:649
  86.5 22.0 %collective-permute-start.21 = (bf16[33,16,256]{2,1,0:T(8,128)(2,1)S(1)}, bf16[33,16,256]{2,1,0:T(8,128)(2,1)S(1)}, u32[]{:S(2)}, u32[]{:S(2)}) collective-permute-start(bf16[33,16,256]{2,1,0:T(8,128)(2,1)S(1)} %get-tuple-element.54), channel_id=1, source_target_pairs={{0,2},{1,3},{2,0},{3,1},{4,6},{5,7},{6,4},{7,5},{8,10},{9,11},{10,... | collective-permute-start | bytes 811016 | tf_op jit(solution)/shard_map/ppermute | solution.py:649
  87.7 29.1 %collective-permute-start.22 = (bf16[33,16,256]{2,1,0:T(8,128)(2,1)S(1)}, bf16[33,16,256]{2,1,0:T(8,128)(2,1)S(1)}, u32[]{:S(2)}, u32[]{:S(2)}) collective-permute-start(bf16[33,16,256]{2,1,0:T(8,128)(2,1)S(1)} %get-tuple-element.55), channel_id=1, source_target_pairs={{0,3},{1,2},{2,1},{3,0},{4,7},{5,6},{6,5},{7,4},{8,11},{9,10},{10,... | collective-permute-start | bytes 811016 | tf_op jit(solution)/shard_map/ppermute | solution.py:649
  88.0 33.9 %collective-permute-start.23 = (bf16[33,16,256]{2,1,0:T(8,128)(2,1)S(1)}, bf16[33,16,256]{2,1,0:T(8,128)(2,1)S(1)}, u32[]{:S(2)}, u32[]{:S(2)}) collective-permute-start(bf16[33,16,256]{2,1,0:T(8,128)(2,1)S(1)} %get-tuple-element.56), channel_id=1, source_target_pairs={{0,6},{1,7},{2,4},{3,5},{4,2},{5,3},{6,0},{7,1},{8,14},{9,15},{10,... | collective-permute-start | bytes 811016 | tf_op jit(solution)/shard_map/ppermute | solution.py:649
  102.8 30.7 %collective-permute-start.29 = (f32[192,384]{1,0:T(8,128)S(1)}, f32[192,384]{1,0:T(8,128)S(1)}, u32[]{:S(2)}, u32[]{:S(2)}) collective-permute-start(f32[192,384]{1,0:T(8,128)S(1)} %far_sum.1.refs_8_), channel_id=1, source_target_pairs={{0,24},{8,16},{16,8},{24,0},{1,25},{9,17},{17,9},{25,1},{2,26},{10... | collective-permute-start | bytes 884744 | tf_op jit(solution)/shard_map/ppermute | solution.py:41
  108.0 25.5 %collective-permute-start.28 = (f32[192,384]{1,0:T(8,128)S(1)}, f32[192,384]{1,0:T(8,128)S(1)}, u32[]{:S(2)}, u32[]{:S(2)}) collective-permute-start(f32[192,384]{1,0:T(8,128)S(1)} %far_sum.1.refs_8_), channel_id=1, source_target_pairs={{0,16},{8,24},{16,0},{24,8},{1,17},{9,25},{17,1},{25,9},{2,18},{10... | collective-permute-start | bytes 884744 | tf_op jit(solution)/shard_map/ppermute | solution.py:41
  108.5 25.0 %collective-permute-start.27 = (f32[192,384]{1,0:T(8,128)S(1)}, f32[192,384]{1,0:T(8,128)S(1)}, u32[]{:S(2)}, u32[]{:S(2)}) collective-permute-start(f32[192,384]{1,0:T(8,128)S(1)} %far_sum.1.refs_8_), channel_id=1, source_target_pairs={{0,8},{8,0},{16,24},{24,16},{1,9},{9,1},{17,25},{25,17},{2,10},{10... | collective-permute-start | bytes 884744 | tf_op jit(solution)/shard_map/ppermute | solution.py:41
  116.8 16.7 %collective-permute-start.24 = (bf16[33,16,256]{2,1,0:T(8,128)(2,1)S(1)}, bf16[33,16,256]{2,1,0:T(8,128)(2,1)S(1)}, u32[]{:S(2)}, u32[]{:S(2)}) collective-permute-start(bf16[33,16,256]{2,1,0:T(8,128)(2,1)S(1)} %get-tuple-element.57), channel_id=1, source_target_pairs={{0,7},{1,6},{2,5},{3,4},{4,3},{5,2},{6,1},{7,0},{8,15},{9,14},{10,... | collective-permute-start | bytes 811016 | tf_op jit(solution)/shard_map/ppermute | solution.py:649
  121.9 11.6 %collective-permute-start.25 = (bf16[33,16,256]{2,1,0:T(8,128)(2,1)S(1)}, bf16[33,16,256]{2,1,0:T(8,128)(2,1)S(1)}, u32[]{:S(2)}, u32[]{:S(2)}) collective-permute-start(bf16[33,16,256]{2,1,0:T(8,128)(2,1)S(1)} %get-tuple-element.58), channel_id=1, source_target_pairs={{0,1},{1,0},{2,3},{3,2},{4,5},{5,4},{6,7},{7,6},{8,9},{9,8},{10,11... | collective-permute-start | bytes 811016 | tf_op jit(solution)/shard_map/ppermute | solution.py:649
